TPU v7x, 32 devices: a whole 2x2x4 slice. The times are simulated.
32 devices in a mesh: group: 4 (over z), sub: 8 (over y, x, core).
Axes of the slice: x: 2, y: 2, z: 4, core: 2. Of those that a mesh axis runs over, the one named last changes fastest.
Arguments:
- load: float32 [8, 512, 256], P(None, ('group', 'sub'))
- row_scale: float32 [512, 256], P(('group', 'sub'))
- diag_blocks: bfloat16 [512, 256, 256], P(('group', 'sub')), may hold values from -0.01184082 to 0.01184082
- off_blocks: bfloat16 [512, 256, 256], P(('group', 'sub')), may hold values from -0.01184082 to 0.01184082
- off_pattern: int32 [32, 16], P(('group', 'sub')), may hold values from 0 to 15, each once within a row
- partner: int32 [32, 16], P(('group', 'sub')), may hold values from 0 to 7, as said below
- corner_coupling: bfloat16 [256, 4096], P(('group', 'sub')), may hold values from -0.375 to 0.375
- corner_index: int32 [4, 64], P('group'), may hold values from 0 to 31
- coarse_inverse: float32 [128, 32], P('group'), as said below
Outputs:
- multipliers: float32 [8, 512, 256], P(None, ('group', 'sub'))
- residual: float32 [8, 512, 256], P(None, ('group', 'sub'))
Inputs may be any that keep to these rules, and one draw needn't show every extreme that they name: partner[s, i] is t XOR m for the subdomain s = 8 * grp + t, with m nonzero and depending only on grp and i; so block i of s and block i of its partner share one multiplier. No subdomain shares more than 3 blocks with one other subdomain, and some share exactly 3. `coarse_inverse`: each cluster's block is symmetric and positive definite.
All inputs are finite; a program needn't handle non-finite values.
Results may differ from a plain program's by a relative error of at most 0.012.
The roundings to bfloat16 on the way count: a program that leaves them out, or rounds other values in their place, can miss the bound.
Values sent between devices are 32-bit elements; how exact they have to be, the bound alone decides.
No kernel may reach another device: no remote copies, remote signals or barrier semaphores. Data moves between devices by JAX's collectives and lax.ppermute only.
A program may use at most 64 MiB of HBM per device.

v0:
```python
import jax
import jax.numpy as jnp
from jax import lax
from jax.sharding import PartitionSpec as P

ITERS = 4


HIGH = lax.Precision.HIGHEST


def on_device(
    load,
    row_scale,
    diag_blocks,
    off_blocks,
    off_pattern,
    partner,
    corner_coupling,
    corner_index,
    coarse_inverse,
):
    blocks = diag_blocks.shape[0]
    width = diag_blocks.shape[1]
    columns = load.shape[0]
    corners = corner_coupling.shape[0]
    coarse = coarse_inverse.shape[1]
    peers = lax.axis_size("sub")
    myself = lax.axis_index("sub")
    sigma = off_pattern[0]
    mates = partner[0]
    block_ids = jnp.arange(blocks, dtype=jnp.int32)
    select = sigma[:, None] == block_ids[None, :]
    select_half = select.astype(jnp.bfloat16)
    select_full = select.astype(jnp.float32)
    coarse_ids = jnp.arange(coarse, dtype=jnp.int32)
    own_index = lax.dynamic_slice_in_dim(corner_index[0], myself * corners, corners, 0)
    own_onehot = (own_index[:, None] == coarse_ids[None, :]).astype(jnp.float32)

    def jump(field):
        capacity = (blocks + peers - 2) // (peers - 1)
        same = mates[:, None] == mates[None, :]
        lower = block_ids[:, None] < block_ids[None, :]
        rank = jnp.sum((same & lower).astype(jnp.int32), axis=0)
        peer_ids = jnp.arange(peers, dtype=jnp.int32)
        slot_ids = jnp.arange(capacity, dtype=jnp.int32)
        slots = (
            (mates[None, None, :] == peer_ids[:, None, None])
            & (rank[None, None, :] == slot_ids[None, :, None])
        ).astype(jnp.float32)
        outgoing = jnp.einsum("jcb,nbk->jcnk", slots, field, precision=HIGH)
        incoming = lax.all_to_all(outgoing, "sub", split_axis=0, concat_axis=0, tiled=True)
        other = jnp.einsum("jcb,jcnk->nbk", slots, incoming, precision=HIGH)
        return field - other

    def column(first, second):
        return jnp.sum(first * second, axis=(1, 2))

    def total(value):
        inner = lax.psum(value, "sub")
        return lax.psum(inner, "group")

    def widen(value):
        return value[:, None, None]

    residual = jump(load)
    multipliers = jnp.zeros_like(residual)
    direction = residual
    norm_now = total(column(residual, residual))
    for step in range(ITERS):
        scaled = (row_scale[None] * direction).astype(jnp.bfloat16)
        moved = jnp.einsum(
            "ij,njl->nil", select_half, scaled, preferred_element_type=jnp.float32
        ).astype(jnp.bfloat16)
        coupled = jnp.einsum(
            "ikl,nil->nik", diag_blocks, scaled, preferred_element_type=jnp.float32
        )
        coupled = coupled + jnp.einsum(
            "ilk,nil->nik", diag_blocks, scaled, preferred_element_type=jnp.float32
        )
        coupled = coupled + jnp.einsum(
            "ikl,nil->nik", off_blocks, moved, preferred_element_type=jnp.float32
        )
        back = jnp.einsum("ilk,nil->nik", off_blocks, scaled, preferred_element_type=jnp.float32)
        coupled = coupled + jnp.einsum("ij,nik->njk", select_full, back, precision=HIGH)
        flat = scaled.reshape(columns, blocks * width)
        partial_terms = lax.dot_general(
            flat, corner_coupling, (((1,), (1,)), ((), ())), preferred_element_type=jnp.float32
        )
        spread = jnp.dot(partial_terms, own_onehot, precision=HIGH)
        gathered = lax.psum(spread, "sub")
        solved = jnp.dot(gathered, coarse_inverse.T, precision=HIGH)
        local = jnp.dot(solved, own_onehot.T, precision=HIGH).astype(jnp.bfloat16)
        lifted = jnp.dot(local, corner_coupling, preferred_element_type=jnp.float32).reshape(
            columns, blocks, width
        )
        product = jump(row_scale[None] * (scaled.astype(jnp.float32) + coupled + lifted))
        alpha = norm_now / total(column(direction, product))
        multipliers = multipliers + widen(alpha) * direction
        residual = residual - widen(alpha) * product
        norm_next = total(column(residual, residual))
        direction = residual + widen(norm_next / norm_now) * direction
        norm_now = norm_next
    return (multipliers, residual)


def solution(mesh):
    return jax.shard_map(
        on_device,
        mesh=mesh,
        in_specs=(
            P(None, ("group", "sub"), None),
            P(("group", "sub"), None),
            P(("group", "sub"), None, None),
            P(("group", "sub"), None, None),
            P(("group", "sub"), None),
            P(("group", "sub"), None),
            P(("group", "sub"), None),
            P("group", None),
            P("group", None),
        ),
        out_specs=(P(None, ("group", "sub"), None), P(None, ("group", "sub"), None)),
        check_vma=False,
    )
```

profile of v0, /device:TPU:0, one launch (start us, length us, event | category | flops | bytes accessed | tf_op | source)
XLA Modules:
  0.0 276.9 jit_solution(16478288315978110690)
XLA Ops:
  0.6 0.9 convert_reduce_fusion
  2.2 1.1 fusion.38
  4.1 5.2 %all-to-all-start = ((f32[8,3,8,256]{3,2,1,0:T(8,128)}), f32[8,3,8,256]{3,2,1,0:T(8,128)S(1)}, u32[]{:S(2)}, u32[]{:S(2)}) async-start(f32[8,3,8,256]{3,2,1,0:T(8,128)} %copy.102), calls=%async_computation | async-start | bytes 393216 | tf_op jit(solution)/shard_map/all_to_all | solution.py:52
  10.0 5.5 %all-to-all-done = f32[8,3,8,256]{3,2,1,0:T(8,128)S(1)} async-done(((f32[8,3,8,256]{3,2,1,0:T(8,128)}), f32[8,3,8,256]{3,2,1,0:T(8,128)S(1)}, u32[]{:S(2)}, u32[]{:S(2)}) %all-to-all-start) | async-done | bytes 196640 | tf_op jit(solution)/shard_map/all_to_all | solution.py:52
  15.5 1.2 multiply_convert_fusion.3
  18.1 11.8 %psum.142 = f32[8,32]{1,0:T(8,128)S(1)} all-reduce(f32[8,32]{1,0:T(8,128)S(1)} %fusion.85), channel_id=1, replica_groups=mesh['group'=4,'sub'=8] {'sub'}, use_global_device_ids=true, to_apply=%region_4.0 | all-reduce | flops 256 | bytes 2048 | tf_op jit(solution)/shard_map/psum | solution.py:91
  30.6 2.0 convolution_bitcast_fusion.12
  34.0 8.6 %all_to_all.25 = f32[8,3,8,256]{3,2,1,0:T(8,128)S(1)} all-to-all(f32[8,3,8,256]{3,2,1,0:T(8,128)S(1)} %copy.113), channel_id=1, replica_groups=mesh['group'=4,'sub'=8] {'sub'}, dimensions={0} | all-to-all | bytes 393216 | tf_op jit(solution)/shard_map/all_to_all | solution.py:52
  43.1 11.8 %all-reduce = (f32[8]{0:T(128)S(1)}, f32[8]{0:T(128)S(1)}) all-reduce(f32[8]{0:T(128)S(1)} %get-tuple-element.3, f32[8]{0:T(128)S(1)} %get-tuple-element.2), channel_id=1, replica_groups=mesh['group'=4,'sub'=8] {'sub'}, use_global_device_ids=true, to_apply=%region_2.0 | all-reduce | flops 16 | bytes 128 | tf_op jit(solution)/shard_map/psum | solution.py:60
  54.9 12.0 %all-reduce.1 = (f32[8]{0:T(128)S(1)}, f32[8]{0:T(128)S(1)}) all-reduce(f32[8]{0:T(128)S(1)} %get-tuple-element.4, f32[8]{0:T(128)S(1)} %get-tuple-element.5), channel_id=1, replica_groups=mesh['group'=4,'sub'=8] {'group'}, use_global_device_ids=true, to_apply=%region_3.0 | all-reduce | flops 16 | bytes 128 | tf_op jit(solution)/shard_map/psum | solution.py:61
  67.1 11.8 %psum.145 = f32[8]{0:T(128)S(1)} all-reduce(f32[8]{0:T(128)S(1)} %multiply_reduce_fusion.5), channel_id=1, replica_groups=mesh['group'=4,'sub'=8] {'sub'}, use_global_device_ids=true, to_apply=%region_9.0 | all-reduce | flops 8 | bytes 64 | tf_op jit(solution)/shard_map/psum | solution.py:60
  78.9 8.4 %psum.146 = f32[8]{0:T(128)S(1)} all-reduce(f32[8]{0:T(128)S(1)} %psum.145), channel_id=1, replica_groups=mesh['group'=4,'sub'=8] {'group'}, use_global_device_ids=true, to_apply=%region_10.0 | all-reduce | flops 8 | bytes 64 | tf_op jit(solution)/shard_map/psum | solution.py:61
  90.2 11.8 %psum.147 = f32[8,32]{1,0:T(8,128)S(1)} all-reduce(f32[8,32]{1,0:T(8,128)S(1)} %fusion.84), channel_id=1, replica_groups=mesh['group'=4,'sub'=8] {'sub'}, use_global_device_ids=true, to_apply=%region_11.0 | all-reduce | flops 256 | bytes 2048 | tf_op jit(solution)/shard_map/psum | solution.py:91
  102.4 2.2 fusion.48
  105.4 8.6 %all_to_all.26 = f32[8,3,8,256]{3,2,1,0:T(8,128)S(1)} all-to-all(f32[8,3,8,256]{3,2,1,0:T(8,128)S(1)} %copy.124), channel_id=1, replica_groups=mesh['group'=4,'sub'=8] {'sub'}, dimensions={0} | all-to-all | bytes 393216 | tf_op jit(solution)/shard_map/all_to_all | solution.py:52
  114.4 11.8 %psum.148 = f32[8]{0:T(128)S(1)} all-reduce(f32[8]{0:T(128)S(1)} %get-tuple-element.21), channel_id=1, replica_groups=mesh['group'=4,'sub'=8] {'sub'}, use_global_device_ids=true, to_apply=%region_13.0 | all-reduce | flops 8 | bytes 64 | tf_op jit(solution)/shard_map/psum | solution.py:60
  126.2 10.4 %psum.149 = f32[8]{0:T(128)S(1)} all-reduce(f32[8]{0:T(128)S(1)} %psum.148), channel_id=1, replica_groups=mesh['group'=4,'sub'=8] {'group'}, use_global_device_ids=true, to_apply=%region_14.0 | all-reduce | flops 8 | bytes 64 | tf_op jit(solution)/shard_map/psum | solution.py:61
  136.8 11.8 %psum.150 = f32[8]{0:T(128)S(1)} all-reduce(f32[8]{0:T(128)S(1)} %get-tuple-element.12), channel_id=1, replica_groups=mesh['group'=4,'sub'=8] {'sub'}, use_global_device_ids=true, to_apply=%region_16.0 | all-reduce | flops 8 | bytes 64 | tf_op jit(solution)/shard_map/psum | solution.py:60
  148.6 8.4 %psum.151 = f32[8]{0:T(128)S(1)} all-reduce(f32[8]{0:T(128)S(1)} %psum.150), channel_id=1, replica_groups=mesh['group'=4,'sub'=8] {'group'}, use_global_device_ids=true, to_apply=%region_17.0 | all-reduce | flops 8 | bytes 64 | tf_op jit(solution)/shard_map/psum | solution.py:61
  160.0 11.8 %psum.152 = f32[8,32]{1,0:T(8,128)S(1)} all-reduce(f32[8,32]{1,0:T(8,128)S(1)} %fusion.83), channel_id=1, replica_groups=mesh['group'=4,'sub'=8] {'sub'}, use_global_device_ids=true, to_apply=%region_18.0 | all-reduce | flops 256 | bytes 2048 | tf_op jit(solution)/shard_map/psum | solution.py:91
  172.1 2.2 fusion.46
  175.1 8.6 %all_to_all.27 = f32[8,3,8,256]{3,2,1,0:T(8,128)S(1)} all-to-all(f32[8,3,8,256]{3,2,1,0:T(8,128)S(1)} %copy.135), channel_id=1, replica_groups=mesh['group'=4,'sub'=8] {'sub'}, dimensions={0} | all-to-all | bytes 393216 | tf_op jit(solution)/shard_map/all_to_all | solution.py:52
  184.1 11.8 %psum.153 = f32[8]{0:T(128)S(1)} all-reduce(f32[8]{0:T(128)S(1)} %get-tuple-element.23), channel_id=1, replica_groups=mesh['group'=4,'sub'=8] {'sub'}, use_global_device_ids=true, to_apply=%region_20.0 | all-reduce | flops 8 | bytes 64 | tf_op jit(solution)/shard_map/psum | solution.py:60
  196.0 10.4 %psum.154 = f32[8]{0:T(128)S(1)} all-reduce(f32[8]{0:T(128)S(1)} %psum.153), channel_id=1, replica_groups=mesh['group'=4,'sub'=8] {'group'}, use_global_device_ids=true, to_apply=%region_21.0 | all-reduce | flops 8 | bytes 64 | tf_op jit(solution)/shard_map/psum | solution.py:61
  206.5 11.8 %psum.155 = f32[8]{0:T(128)S(1)} all-reduce(f32[8]{0:T(128)S(1)} %get-tuple-element.8), channel_id=1, replica_groups=mesh['group'=4,'sub'=8] {'sub'}, use_global_device_ids=true, to_apply=%region_23.0 | all-reduce | flops 8 | bytes 64 | tf_op jit(solution)/shard_map/psum | solution.py:60
  218.3 8.4 %psum.156 = f32[8]{0:T(128)S(1)} all-reduce(f32[8]{0:T(128)S(1)} %psum.155), channel_id=1, replica_groups=mesh['group'=4,'sub'=8] {'group'}, use_global_device_ids=true, to_apply=%region_24.0 | all-reduce | flops 8 | bytes 64 | tf_op jit(solution)/shard_map/psum | solution.py:61
  227.4 0.9 copy-done.4
  229.7 11.8 %psum.157 = f32[8,32]{1,0:T(8,128)S(1)} all-reduce(f32[8,32]{1,0:T(8,128)S(1)} %fusion.82), channel_id=1, replica_groups=mesh['group'=4,'sub'=8] {'sub'}, use_global_device_ids=true, to_apply=%region_25.0 | all-reduce | flops 256 | bytes 2048 | tf_op jit(solution)/shard_map/psum | solution.py:91
  241.8 2.2 fusion.44
  244.8 8.6 %all_to_all.28 = f32[8,3,8,256]{3,2,1,0:T(8,128)S(1)} all-to-all(f32[8,3,8,256]{3,2,1,0:T(8,128)S(1)} %copy.146), channel_id=1, replica_groups=mesh['group'=4,'sub'=8] {'sub'}, dimensions={0} | all-to-all | bytes 393216 | tf_op jit(solution)/shard_map/all_to_all | solution.py:52
  253.8 11.8 %psum.158 = f32[8]{0:T(128)S(1)} all-reduce(f32[8]{0:T(128)S(1)} %get-tuple-element.25), channel_id=1, replica_groups=mesh['group'=4,'sub'=8] {'sub'}, use_global_device_ids=true, to_apply=%region_27.0 | all-reduce | flops 8 | bytes 64 | tf_op jit(solution)/shard_map/psum | solution.py:60
  265.7 10.4 %psum.159 = f32[8]{0:T(128)S(1)} all-reduce(f32[8]{0:T(128)S(1)} %psum.158), channel_id=1, replica_groups=mesh['group'=4,'sub'=8] {'group'}, use_global_device_ids=true, to_apply=%region_28.0 | all-reduce | flops 8 | bytes 64 | tf_op jit(solution)/shard_map/psum | solution.py:61
  (91 shorter events, 19.8 us)
Async XLA Ops:
  0.6 16.1 %copy-start = (bf16[16,256,256]{2,1,0:T(8,128)(2,1)S(1)}, bf16[16,256,256]{2,1,0:T(8,128)(2,1)}, u32[]{:S(2)}) copy-start(bf16[16,256,256]{2,1,0:T(8,128)(2,1)} %param.11) | copy-start | bytes 6291460
  4.1 11.4 %all-to-all-start = ((f32[8,3,8,256]{3,2,1,0:T(8,128)}), f32[8,3,8,256]{3,2,1,0:T(8,128)S(1)}, u32[]{:S(2)}, u32[]{:S(2)}) async-start(f32[8,3,8,256]{3,2,1,0:T(8,128)} %copy.102), calls=%async_computation | async-start | bytes 393216 | tf_op jit(solution)/shard_map/all_to_all | solution.py:52
  16.7 1.1 copy-start.5
  16.7 13.3 %copy-start.7 = (f32[32,32]{1,0:T(8,128)S(1)}, f32[32,32]{1,0:T(8,128)}, u32[]{:S(2)}) copy-start(f32[32,32]{1,0:T(8,128)} %param.17) | copy-start | bytes 12292
  16.7 13.6 %copy-start.8 = (s32[1,16]{1,0:T(1,128)S(1)}, s32[1,16]{1,0:T(1,128)}, u32[]{:S(2)}) copy-start(s32[1,16]{1,0:T(1,128)} %param.13) | copy-start | bytes 196
  30.0 2.6 copy-start.1
  30.6 2.9 %copy-start.6 = (f32[16,256]{1,0:T(8,128)S(1)}, f32[16,256]{1,0:T(8,128)}, u32[]{:S(2)}) copy-start(f32[16,256]{1,0:T(8,128)} %param.10) | copy-start | bytes 49156
  87.2 1.6 copy-start.2
  157.0 1.6 copy-start.3
  226.7 1.6 copy-start.4
where the time goes:
time: 278 us; the launch traced here: 277 us
  blocking collectives  233 us (84%)
  matrix products  24.7 us (9%)
  waiting for transfers between devices  5.51 us (2%)
  starting transfers between devices  5.17 us (2%)
  local copies, waits for them, and re-layouts  4.58 us (2%)
  other arithmetic  3.4 us (1%)
    psum x7, blocking collectives, total(): inner = lax.psum(value, 'sub')  82.6 us
    psum x7, blocking collectives, total(): return lax.psum(inner, 'group')  68.1 us
    psum x4, blocking collectives, on_device(): gathered = lax.psum(spread, 'sub')  47.2 us
    all_to_all x4, blocking collectives, jump(): lax.all_to_all(outgoing, 'sub', split_axis=0, concat_axis=0, tiled=True)  34.5 us
    dot_general x4, matrix products, on_device(): jnp.einsum('ikl,nil->nik', off_blocks, moved, preferred_element_type=jnp....  7.38 us
  transfers between devices with their start and end apart: 1, of which 1 were waited for; matrix products, arithmetic and copies ran while one was open for 0% of the time, Pallas kernels for 0%

commit v1 on v0

v1 whole, which is shorter than its diff:
```python
import functools

import jax
import jax.numpy as jnp
from jax import lax
from jax.experimental import pallas as pl
from jax.experimental.pallas import tpu as pltpu
from jax.sharding import PartitionSpec as P

ITERS = 4
HIGH = lax.Precision.HIGHEST
F32 = jnp.float32
BF16 = jnp.bfloat16
VMEM = pl.BlockSpec(memory_space=pltpu.VMEM)
SMEM = pl.BlockSpec(memory_space=pltpu.SMEM)
LIMIT = 24 * 1024 * 1024
PAIRS = [(i, j) for j in range(ITERS) for i in range(j + 1)]
ENTRIES = len(PAIRS) + ITERS
NN = (((1,), (0,)), ((), ()))
NT = (((1,), (1,)), ((), ()))
TN = (((0,), (0,)), ((), ()))


def dot(a, b, dims):
    return lax.dot_general(a, b, dims, preferred_element_type=F32)


def dot_high(a, b, dims):
    return lax.dot_general(a, b, dims, precision=HIGH, preferred_element_type=F32)


def split(a):
    high = a.astype(BF16).astype(F32)
    return jnp.concatenate([high, a - high], axis=0).astype(BF16)


def fold(a):
    half = a.shape[0] // 2
    return a[:half] + a[half:]


def lane_ids(shape):
    return lax.broadcasted_iota(jnp.int32, shape, 1)


class Sizes:
    def __init__(self, load, corner_coupling, coarse_inverse, mesh):
        self.columns = load.shape[0]
        self.blocks = load.shape[1]
        self.width = load.shape[2]
        self.corners = corner_coupling.shape[0]
        self.coarse = coarse_inverse.shape[1]
        self.peers = mesh["sub"]
        self.groups = mesh["group"]
        self.capacity = (self.blocks + self.peers - 2) // (self.peers - 1)
        self.all_corners = self.peers * self.corners
        self.max_lane = self.all_corners
        self.gram_lane = self.max_lane + self.peers
        self.extra_chunks = -(-(self.gram_lane + ENTRIES) // self.width)
        self.extra = self.extra_chunks * self.width
        self.masks = range(1, self.peers)
        self.slots = self.peers * self.capacity


def fill_slots(z, partner, slots, counts):
    me = lax.axis_index("sub")
    for entry in range(z.slots):
        slots[entry] = z.blocks
    for m in range(z.peers):
        counts[m] = 0
    for i in range(z.blocks):
        m = partner[0, i] ^ me
        rank = counts[m]
        slots[m * z.capacity + rank] = i
        counts[m] = rank + 1


def send_slots(z, slots, source, outs):
    for m, out in zip(z.masks, outs):
        for r in range(z.capacity):
            block = jnp.minimum(slots[m * z.capacity + r], z.blocks - 1)
            out[r] = source[block]


def place_slots(z, slots, incs, target):
    for m, inc in zip(z.masks, incs):
        for r in range(z.capacity):
            target[slots[m * z.capacity + r]] = inc[r]


def pack_load(z, partner, load, field, *rest):
    outs, (slots, counts) = rest[:-2], rest[-2:]
    fill_slots(z, partner, slots, counts)
    for i in range(z.blocks):
        field[i] = load[:, i, :]
    send_slots(z, slots, field, outs)


def pack_lift(z, partner, scale, coupling, lift, *rest):
    outs, (slots, counts) = rest[:-2], rest[-2:]
    fill_slots(z, partner, slots, counts)
    for i in range(z.blocks):
        part = coupling[:, i * z.width : (i + 1) * z.width].astype(F32)
        lift[i] = scale[i : i + 1, :] * part
    send_slots(z, slots, lift, outs)


def build_coarse(z, partner, index, inverse, lift, *rest):
    count = len(z.masks)
    incs, (operator, jump_lift), (slots, counts, other) = rest[:count], rest[count : count + 2], rest[count + 2 :]
    fill_slots(z, partner, slots, counts)
    place_slots(z, slots, incs, other)
    me = lax.axis_index("sub")
    rows = lax.broadcasted_iota(jnp.int32, (z.coarse, z.all_corners), 0)
    select = (rows == index[...]).astype(F32)
    operator[...] = dot_high(select, dot_high(inverse[...], select, NN), TN)
    own = operator[pl.ds(me * z.corners, z.corners), :]
    for i in range(z.blocks):
        theirs = operator[pl.ds(partner[0, i] * z.corners, z.corners), :]
        left = jnp.concatenate([own, -theirs], axis=0)
        right = jnp.concatenate([lift[i], other[i]], axis=0)
        jump_lift[i] = split(dot_high(left, right, TN))


def extra_sum(z, own, incs):
    total = own[...]
    for inc in incs:
        total = total + jnp.concatenate(
            [inc[z.capacity + j] for j in range(z.extra_chunks)], axis=1
        )
    return total


def cluster_max(z, total):
    lanes = lane_ids(total.shape)
    own = (lanes >= z.max_lane) & (lanes < z.gram_lane)
    return jnp.max(jnp.where(own, total, 0.0), axis=1, keepdims=True)


def corner_rows(z, total):
    rows = split(total[:, : z.all_corners])
    return jnp.concatenate([rows, rows], axis=1)


def lane_sum(a):
    return jnp.sum(a, axis=1, keepdims=True)


def apply_round(z, step, partner, pattern, *rest):
    count = len(z.masks)
    first, last = step == 1, step == ITERS
    rest = list(rest)
    take = lambda n: [rest.pop(0) for _ in range(n)]
    incs = take(count)
    (before,) = take(1)
    if not first:
        own_extra, jump_lift = take(2)
    scale, diag, off, coupling = take(4)
    older = take(ITERS - 1) if last else []
    field, image = take(2)
    if not first:
        (total_out,) = take(1)
    (extra,) = take(1)
    outs = take(count)
    slots, counts, inverse, other, parts = rest
    fill_slots(z, partner, slots, counts)
    for j in range(z.blocks):
        inverse[pattern[0, j]] = j
    place_slots(z, slots, incs, other)
    if not first:
        total = extra_sum(z, own_extra, incs)
        total_out[...] = total
        rows = corner_rows(z, total)
        shrink = 1.0 / cluster_max(z, total)
    for i in range(z.blocks):
        value = before[i] - other[i]
        if not first:
            value = (value + fold(dot(rows, jump_lift[i], NN))) * shrink
        field[i] = value
        parts[i] = split(scale[i : i + 1, :] * value)
    partial = jnp.zeros((2 * z.columns, z.corners), F32)
    top = jnp.zeros((z.columns, z.width), F32)
    for i in range(z.blocks):
        mine = parts[i]
        partial = partial + dot(mine, coupling[:, i * z.width : (i + 1) * z.width], NT)
        source = inverse[i]
        coupled = dot(mine, diag[i], NT) + dot(mine, diag[i], NN)
        coupled = coupled + dot(parts[pattern[0, i]], off[i], NT)
        coupled = coupled + dot(parts[source], off[source], NN)
        row = scale[i : i + 1, :]
        result = row * (row * field[i] + fold(coupled))
        image[i] = result
        top = jnp.maximum(top, jnp.abs(result))
    send_slots(z, slots, image, outs)
    me = lax.axis_index("sub")
    lanes = lane_ids((z.columns, z.extra))
    sums = fold(partial)
    padded = jnp.concatenate(
        [sums, jnp.zeros((z.columns, z.extra - z.corners), F32)], axis=1
    )
    tile = pltpu.roll(padded, me * z.corners, 1)
    tile = jnp.where(lanes == z.max_lane + me, jnp.max(top, axis=1, keepdims=True), tile)
    if last:
        fields = older + [field]
        products = [(fields[i], fields[j]) for i, j in PAIRS] + [(f, image) for f in fields]
        for entry, (a, b) in enumerate(products):
            acc = a[0] * b[0]
            for i in range(1, z.blocks):
                acc = acc + a[i] * b[i]
            tile = jnp.where(lanes == z.gram_lane + entry, lane_sum(acc), tile)
    extra[...] = tile
    for out in outs:
        for j in range(z.extra_chunks):
            out[z.capacity + j] = tile[:, j * z.width : (j + 1) * z.width]


def cluster_gram(z, operator, own_extra, *rest):
    count = len(z.masks)
    incs, totals, (gram,) = rest[:count], rest[count:-1], rest[-1:]
    total = extra_sum(z, own_extra, incs)
    totals = [t[...] for t in totals]
    partials = [t[:, : z.all_corners] for t in totals + [total]]
    lifted = dot_high(partials[-1], operator[...], NT)
    lanes = lane_ids(gram.shape)
    tile = jnp.zeros(gram.shape, F32)
    for entry in range(ENTRIES):
        lane = z.gram_lane + entry
        value = total[:, lane : lane + 1]
        if entry >= len(PAIRS):
            value = 2.0 * (value + lane_sum(partials[entry - len(PAIRS)] * lifted))
        tile = jnp.where(lanes == entry, value, tile)
    for step, t in enumerate(totals):
        tile = jnp.where(lanes == ENTRIES + step, cluster_max(z, t), tile)
    gram[...] = tile


def finish(z, partner, *rest):
    count = len(z.masks)
    rest = list(rest)
    take = lambda n: [rest.pop(0) for _ in range(n)]
    grams = take(z.groups)
    incs = take(count)
    before, own_extra, jump_lift = take(3)
    fields = take(ITERS)
    multipliers, residual = take(2)
    slots, counts, other, tiles = rest
    here = lax.axis_index("group")
    for k, gram in enumerate(grams):
        tiles[lax.rem(here + z.groups - k, z.groups)] = gram[...]
    total = extra_sum(z, own_extra, incs)
    rows = corner_rows(z, total)
    fill_slots(z, partner, slots, counts)
    place_slots(z, slots, incs, other)

    tables = [tiles[g] for g in range(z.groups)]
    mine = grams[0][...]
    one = jnp.ones((z.columns, 1), F32)
    ratio = [[one] * z.groups]
    own_ratio = [one]
    growth = [None]
    for step in range(1, ITERS + 1):
        if step < ITERS:
            lane = ENTRIES + step - 1
            grown = [q * t[:, lane : lane + 1] for q, t in zip(ratio[-1], tables)]
            own = own_ratio[-1] * mine[:, lane : lane + 1]
        else:
            grown, own = ratio[-1], own_ratio[-1]
        top = functools.reduce(jnp.maximum, grown)
        ratio.append([q / top for q in grown])
        own_ratio.append(own / top)
        growth.append(top)
    gram = {}
    pairs = PAIRS + [(i, ITERS) for i in range(ITERS)]
    for entry, (i, j) in enumerate(pairs):
        value = 0.0
        for g in range(z.groups):
            value = value + ratio[i][g] * ratio[j][g] * tables[g][:, entry : entry + 1]
        gram[i, j] = gram[j, i] = value

    def inner(a, b):
        return sum(a[i] * sum(gram[i, j] * b[j] for j in b) for i in a)

    def add(a, weight, b):
        out = dict(a)
        for i, value in b.items():
            out[i] = out[i] + weight * value if i in out else weight * value
        return out

    rest_of, way, found = {0: one}, {0: one}, {}
    norm = gram[0, 0]
    for step in range(ITERS):
        product = {i + 1: growth[i + 1] * value for i, value in way.items()}
        alpha = norm / inner(way, product)
        found = add(found, alpha, way)
        rest_of = add(rest_of, -alpha, product)
        if step < ITERS - 1:
            following = inner(rest_of, rest_of)
            way = add(rest_of, following / norm, way)
            norm = following
    found = {i: value * own_ratio[i] for i, value in found.items()}
    rest_of = {i: value * own_ratio[i] for i, value in rest_of.items()}
    for i in range(z.blocks):
        newest = before[i] - other[i] + fold(dot(rows, jump_lift[i], NN))
        values = [f[i] for f in fields] + [newest]
        multipliers[:, i, :] = sum(c * values[j] for j, c in found.items())
        residual[:, i, :] = sum(c * values[j] for j, c in rest_of.items())


def call(body, outs, scratch, cost, args, scalars=1):
    specs = [SMEM] * scalars + [VMEM] * (len(args) - scalars)
    return pl.pallas_call(
        body,
        out_shape=[jax.ShapeDtypeStruct(s, t) for s, t in outs],
        in_specs=specs,
        out_specs=[VMEM] * len(outs),
        scratch_shapes=scratch,
        compiler_params=pltpu.CompilerParams(vmem_limit_bytes=LIMIT),
        cost_estimate=pl.CostEstimate(flops=cost, bytes_accessed=cost // 16, transcendentals=0),
    )(*args)


def on_device(
    load,
    row_scale,
    diag_blocks,
    off_blocks,
    off_pattern,
    partner,
    corner_coupling,
    corner_index,
    coarse_inverse,
    *,
    mesh,
):
    z = Sizes(load, corner_coupling, coarse_inverse, mesh)
    cols, blocks, width = z.columns, z.blocks, z.width
    count = len(z.masks)
    field = ((blocks, cols, width), F32)
    tables = [pltpu.SMEM((z.slots,), jnp.int32), pltpu.SMEM((z.peers,), jnp.int32)]
    inverse = pltpu.SMEM((blocks,), jnp.int32)
    other = pltpu.VMEM((blocks + 1, cols, width), F32)
    parts = pltpu.VMEM((blocks, 2 * cols, width), BF16)
    plain = ((z.capacity, cols, width), F32)
    lift_piece = ((z.capacity, z.corners, width), F32)
    full = ((z.capacity + z.extra_chunks, cols, width), F32)
    extra = ((cols, z.extra), F32)
    gram = ((cols, 128), F32)
    light, heavy = 4_000_000, 600_000_000

    def swap(pieces):
        return [
            lax.ppermute(piece, "sub", [(t, t ^ m) for t in range(z.peers)])
            for m, piece in zip(z.masks, pieces)
        ]

    def kernel(body, *extra_args):
        return functools.partial(body, z, *extra_args)

    loaded, *pieces = call(
        kernel(pack_load), [field] + [plain] * count, tables, light,
        [partner, load],
    )
    incs = swap(pieces)
    lift, *pieces = call(
        kernel(pack_lift),
        [((blocks, z.corners, width), F32)] + [lift_piece] * count,
        tables, light, [partner, row_scale, corner_coupling],
    )
    lifts = swap(pieces)

    weights = [row_scale, diag_blocks, off_blocks, corner_coupling]
    scratch = tables + [inverse, other, parts]
    newest, image, own_extra, *pieces = call(
        kernel(apply_round, 1), [field, field, extra] + [full] * count, scratch, heavy,
        [partner, off_pattern, *incs, loaded, *weights], 2,
    )
    incs = swap(pieces)
    operator, jump_lift = call(
        kernel(build_coarse),
        [
            ((z.all_corners, z.all_corners), F32),
            ((blocks, 2 * z.all_corners, width), BF16),
        ],
        tables + [pltpu.VMEM((blocks + 1, z.corners, width), F32)],
        heavy,
        [partner, corner_index, coarse_inverse, lift, *lifts],
    )
    fields, totals = [newest], []
    for step in range(2, ITERS + 1):
        older = fields if step == ITERS else []
        newest, image, total, own_extra, *pieces = call(
            kernel(apply_round, step),
            [field, field, extra, extra] + [full] * count, scratch, heavy,
            [partner, off_pattern, *incs, image, own_extra, jump_lift, *weights, *older], 2,
        )
        fields.append(newest)
        totals.append(total)
        incs = swap(pieces)
    (own_gram,) = call(
        kernel(cluster_gram), [gram], [], light, [operator, own_extra, *incs, *totals], 0
    )
    grams = [own_gram] + [
        lax.ppermute(own_gram, "group", [(a, (a + k) % z.groups) for a in range(z.groups)])
        for k in range(1, z.groups)
    ]
    flat = (load.shape, F32)
    multipliers, residual = call(
        kernel(finish), [flat, flat],
        tables + [other, pltpu.VMEM((z.groups, cols, 128), F32)], light,
        [partner, *grams, *incs, image, own_extra, jump_lift, *fields],
    )
    return multipliers, residual


def solution(mesh):
    return jax.shard_map(
        functools.partial(on_device, mesh=dict(mesh.shape)),
        mesh=mesh,
        in_specs=(
            P(None, ("group", "sub"), None),
            P(("group", "sub"), None),
            P(("group", "sub"), None, None),
            P(("group", "sub"), None, None),
            P(("group", "sub"), None),
            P(("group", "sub"), None),
            P(("group", "sub"), None),
            P("group", None),
            P("group", None),
        ),
        out_specs=(P(None, ("group", "sub"), None), P(None, ("group", "sub"), None)),
        check_vma=False,
    )
```

time: 278 us -> 86 us (0.31)
  blocking collectives: 233 us -> 0 us
  starting transfers between devices: 5.17 us -> 44.5 us
  matrix products: 24.7 us -> 0 us
  Pallas kernels: 0 us -> 16.7 us
  waiting for transfers between devices: 5.51 us -> 16.8 us
  other arithmetic: 3.4 us -> 0 us
    psum x18 -> x0, blocking collectives: 198 us -> none  [the longest x7 82.6 us: total(): inner = lax.psum(value, 'sub')]
    ppermute x0 -> x45, starting transfers between devices: none -> 44.5 us  [the longest x42 39.5 us: swap(): lax.ppermute(piece, 'sub', [(t, t ^ m) for t in range(z.peers)])]
    all_to_all x4 -> x0, blocking collectives: 34.5 us -> none  [jump(): lax.all_to_all(outgoing, 'sub', split_axis=0, concat_axis=0, tiled=True)]
    dot_general x54 -> x0, matrix products: 24.7 us -> none  [the longest x4 7.38 us: on_device(): jnp.einsum('ikl,nil->nik', off_blocks, moved, preferred_element_type=jnp....]
    ppermute x0 -> x45, waiting for transfers between devices: none -> 16.8 us  [the longest x42 12.5 us: swap(): lax.ppermute(piece, 'sub', [(t, t ^ m) for t in range(z.peers)])]
    pallas_call x0 -> x9, Pallas kernels: none -> 16.7 us  [call(): pl.pallas_call(body, out_shape=[jax.ShapeDtypeStruct(s, t) for s, t in ou...]
    all_to_all x1 -> x0, waiting for transfers between devices: 5.51 us -> none  [jump(): lax.all_to_all(outgoing, 'sub', split_axis=0, concat_axis=0, tiled=True)]
    all_to_all x1 -> x0, starting transfers between devices: 5.17 us -> none  [jump(): lax.all_to_all(outgoing, 'sub', split_axis=0, concat_axis=0, tiled=True)]
  transfers between devices with their start and end apart: 1 -> 45, of which waited for: 1 -> 14; matrix products, arithmetic and copies ran while one was open for 0% -> 0% of each run, Pallas kernels for 0% -> 6%
where the time goes in v1:
time: 86 us; the launch traced here: 85.7 us
  starting transfers between devices  44.5 us (52%)
  waiting for transfers between devices  16.8 us (20%)
  Pallas kernels  16.7 us (19%)
  local copies, waits for them, and re-layouts  6.98 us (8%)
    ppermute x42, starting transfers between devices, swap(): lax.ppermute(piece, 'sub', [(t, t ^ m) for t in range(z.peers)])  39.5 us
    pallas_call x9, Pallas kernels, call(): pl.pallas_call(body, out_shape=[jax.ShapeDtypeStruct(s, t) for s, t in ou...  16.7 us
    ppermute x42, waiting for transfers between devices, swap(): lax.ppermute(piece, 'sub', [(t, t ^ m) for t in range(z.peers)])  12.5 us
    unnamed x26, local copies, waits for them, and re-layouts  6.98 us
    ppermute x3, starting transfers between devices, on_device(): lax.ppermute(own_gram, 'group', [(a, (a + k) % z.groups) for a in range(z...  4.95 us
    ppermute x3, waiting for transfers between devices, on_device(): lax.ppermute(own_gram, 'group', [(a, (a + k) % z.groups) for a in range(z...  4.25 us
  transfers between devices with their start and end apart: 45, of which 14 were waited for; matrix products, arithmetic and copies ran while one was open for 0% of the time, Pallas kernels for 6%

profile of v1, /device:TPU:0, one launch (start us, length us, event | category | flops | bytes accessed | tf_op | source)
XLA Modules:
  0.0 85.7 jit_solution(1240776679659625657)
XLA Ops:
  3.4 2.6 %collective-permute-start.8 = (f32[3,8,256]{2,1,0:T(8,128)S(1)}, f32[3,8,256]{2,1,0:T(8,128)S(1)}, u32[]{:S(2)}, u32[]{:S(2)}) collective-permute-start(f32[3,8,256]{2,1,0:T(8,128)S(1)} %get-tuple-element.73), channel_id=1, source_target_pairs={{0,2},{1,3},{2,0},{3,1},{4,6},{5,7},{6,4},{7,5},{8,10},{9,11},{10,... | collective-permute-start | bytes 73736 | tf_op jit(solution)/shard_map/ppermute | solution.py:352
  6.0 1.8 %collective-permute-start.10 = (f32[3,8,256]{2,1,0:T(8,128)S(1)}, f32[3,8,256]{2,1,0:T(8,128)S(1)}, u32[]{:S(2)}, u32[]{:S(2)}) collective-permute-start(f32[3,8,256]{2,1,0:T(8,128)S(1)} %get-tuple-element.75), channel_id=1, source_target_pairs={{0,4},{1,5},{2,6},{3,7},{4,0},{5,1},{6,2},{7,3},{8,12},{9,13},{10,... | collective-permute-start | bytes 73736 | tf_op jit(solution)/shard_map/ppermute | solution.py:352
  7.8 2.6 %collective-permute-start.12 = (f32[3,8,256]{2,1,0:T(8,128)S(1)}, f32[3,8,256]{2,1,0:T(8,128)S(1)}, u32[]{:S(2)}, u32[]{:S(2)}) collective-permute-start(f32[3,8,256]{2,1,0:T(8,128)S(1)} %get-tuple-element.77), channel_id=1, source_target_pairs={{0,6},{1,7},{2,4},{3,5},{4,2},{5,3},{6,0},{7,1},{8,14},{9,15},{10,... | collective-permute-start | bytes 73736 | tf_op jit(solution)/shard_map/ppermute | solution.py:352
  13.4 1.4 %collective-permute-start.1 = (f32[3,8,256]{2,1,0:T(8,128)S(1)}, f32[3,8,256]{2,1,0:T(8,128)S(1)}, u32[]{:S(2)}, u32[]{:S(2)}) collective-permute-start(f32[3,8,256]{2,1,0:T(8,128)S(1)} %get-tuple-element.65), channel_id=1, source_target_pairs={{0,2},{1,3},{2,0},{3,1},{4,6},{5,7},{6,4},{7,5},{8,10},{9,11},{10,... | collective-permute-start | bytes 73736 | tf_op jit(solution)/shard_map/ppermute | solution.py:352
  14.8 1.6 %collective-permute-start.3 = (f32[3,8,256]{2,1,0:T(8,128)S(1)}, f32[3,8,256]{2,1,0:T(8,128)S(1)}, u32[]{:S(2)}, u32[]{:S(2)}) collective-permute-start(f32[3,8,256]{2,1,0:T(8,128)S(1)} %get-tuple-element.67), channel_id=1, source_target_pairs={{0,4},{1,5},{2,6},{3,7},{4,0},{5,1},{6,2},{7,3},{8,12},{9,13},{10,... | collective-permute-start | bytes 73736 | tf_op jit(solution)/shard_map/ppermute | solution.py:352
  16.4 1.6 %copy-done = bf16[16,256,256]{2,1,0:T(8,128)(2,1)S(1)} copy-done((bf16[16,256,256]{2,1,0:T(8,128)(2,1)S(1)}, bf16[16,256,256]{2,1,0:T(8,128)(2,1)}, u32[]{:S(2)}) %copy-start) | copy-done | bytes 2097176
  18.0 1.6 %copy-done.2 = bf16[16,256,256]{2,1,0:T(8,128)(2,1)S(1)} copy-done((bf16[16,256,256]{2,1,0:T(8,128)(2,1)S(1)}, bf16[16,256,256]{2,1,0:T(8,128)(2,1)}, u32[]{:S(2)}) %copy-start.2) | copy-done | bytes 2097176
  20.2 2.6 %shard_map.107 = (f32[16,8,256]{2,1,0:T(8,128)S(1)}, f32[16,8,256]{2,1,0:T(8,128)S(1)}, f32[8,256]{1,0:T(8,128)S(1)}, f32[4,8,256]{2,1,0:T(8,128)S(1)}, f32[4,8,...) custom-call(s32[1,16]{1,0:T(1,128)S(1)} %copy-done.8, ...), custom_call_target="tpu_custom_call" | custom-call | flops 600000000 | bytes 37500000 | tf_op jit(solution)/shard_map/pallas_call | solution.py:311
  23.2 1.5 %collective-permute-start.15 = (f32[4,8,256]{2,1,0:T(8,128)S(1)}, f32[4,8,256]{2,1,0:T(8,128)S(1)}, u32[]{:S(2)}, u32[]{:S(2)}) collective-permute-start(f32[4,8,256]{2,1,0:T(8,128)S(1)} %get-tuple-element.81), channel_id=1, source_target_pairs={{0,2},{1,3},{2,0},{3,1},{4,6},{5,7},{6,4},{7,5},{8,10},{9,11},{10,... | collective-permute-start | bytes 98312 | tf_op jit(solution)/shard_map/ppermute | solution.py:352
  24.8 1.5 %collective-permute-start.5 = (f32[3,8,256]{2,1,0:T(8,128)S(1)}, f32[3,8,256]{2,1,0:T(8,128)S(1)}, u32[]{:S(2)}, u32[]{:S(2)}) collective-permute-start(f32[3,8,256]{2,1,0:T(8,128)S(1)} %get-tuple-element.69), channel_id=1, source_target_pairs={{0,6},{1,7},{2,4},{3,5},{4,2},{5,3},{6,0},{7,1},{8,14},{9,15},{10,... | collective-permute-start | bytes 73736 | tf_op jit(solution)/shard_map/ppermute | solution.py:352
  26.3 1.3 %collective-permute-start.6 = (f32[3,8,256]{2,1,0:T(8,128)S(1)}, f32[3,8,256]{2,1,0:T(8,128)S(1)}, u32[]{:S(2)}, u32[]{:S(2)}) collective-permute-start(f32[3,8,256]{2,1,0:T(8,128)S(1)} %get-tuple-element.70), channel_id=1, source_target_pairs={{0,7},{1,6},{2,5},{3,4},{4,3},{5,2},{6,1},{7,0},{8,15},{9,14},{10,... | collective-permute-start | bytes 73736 | tf_op jit(solution)/shard_map/ppermute | solution.py:352
  28.4 1.1 %collective-permute-done.5.rest_5_ = f32[3,8,256]{2,1,0:T(8,128)S(1)} collective-permute-done((f32[3,8,256]{2,1,0:T(8,128)S(1)}, f32[3,8,256]{2,1,0:T(8,128)S(1)}, u32[]{:S(2)}, u32[]{:S(2)}) %collective-permute-start.5) | collective-permute-done | bytes 24608 | tf_op jit(solution)/shard_map/ppermute | solution.py:352
  29.5 1.7 %collective-permute-start.17 = (f32[4,8,256]{2,1,0:T(8,128)S(1)}, f32[4,8,256]{2,1,0:T(8,128)S(1)}, u32[]{:S(2)}, u32[]{:S(2)}) collective-permute-start(f32[4,8,256]{2,1,0:T(8,128)S(1)} %get-tuple-element.83), channel_id=1, source_target_pairs={{0,4},{1,5},{2,6},{3,7},{4,0},{5,1},{6,2},{7,3},{8,12},{9,13},{10,... | collective-permute-start | bytes 98312 | tf_op jit(solution)/shard_map/ppermute | solution.py:352
  31.2 2.3 %collective-permute-start.19 = (f32[4,8,256]{2,1,0:T(8,128)S(1)}, f32[4,8,256]{2,1,0:T(8,128)S(1)}, u32[]{:S(2)}, u32[]{:S(2)}) collective-permute-start(f32[4,8,256]{2,1,0:T(8,128)S(1)} %get-tuple-element.85), channel_id=1, source_target_pairs={{0,6},{1,7},{2,4},{3,5},{4,2},{5,3},{6,0},{7,1},{8,14},{9,15},{10,... | collective-permute-start | bytes 98312 | tf_op jit(solution)/shard_map/ppermute | solution.py:352
  34.0 1.9 %shard_map.105 = (f32[64,64]{1,0:T(8,128)S(1)}, bf16[16,128,256]{2,1,0:T(8,128)(2,1)S(1)}) custom-call(s32[1,16]{1,0:T(1,128)S(1)} %copy-done.8, s32[1,64]{1,0:T(1,128)S(1)} %copy-done.12, f32[32,32]{1,0:T(8,128)S(1)} %copy-done.11, f32[16,8,256]{2,1,0:T(8,128)S(1)} %get-tuple-element.63.lift, f32[3,8,256]{2,1,0:T(8,128)S(1)} %collective-permute-done.rest_0_, ...), custom_call_target="tpu_custom_call" | custom-call | flops 600000000 | bytes 37500000 | tf_op jit(solution)/shard_map/pallas_call | solution.py:311
  36.1 1.8 %collective-permute-done.20.rest_6_ = f32[4,8,256]{2,1,0:T(8,128)S(1)} collective-permute-done((f32[4,8,256]{2,1,0:T(8,128)S(1)}, f32[4,8,256]{2,1,0:T(8,128)S(1)}, u32[]{:S(2)}, u32[]{:S(2)}) %collective-permute-start.20) | collective-permute-done | bytes 32800 | tf_op jit(solution)/shard_map/ppermute | solution.py:352
  38.0 2.7 %shard_map.108 = (f32[16,8,256]{2,1,0:T(8,128)S(1)}, f32[16,8,256]{2,1,0:T(8,128)S(1)}, f32[8,256]{1,0:T(8,128)S(1)}, f32[8,256]{1,0:T(8,128)S(1)}, f32[4,8,256]...) custom-call(s32[1,16]{1,0:T(1,128)S(1)} %copy-done.8, ...), custom_call_target="tpu_custom_call" | custom-call | flops 600000000 | bytes 37500000 | tf_op jit(solution)/shard_map/pallas_call | solution.py:311
  42.9 1.4 %collective-permute-start.25 = (f32[4,8,256]{2,1,0:T(8,128)S(1)}, f32[4,8,256]{2,1,0:T(8,128)S(1)}, u32[]{:S(2)}, u32[]{:S(2)}) collective-permute-start(f32[4,8,256]{2,1,0:T(8,128)S(1)} %get-tuple-element.94), channel_id=1, source_target_pairs={{0,5},{1,4},{2,7},{3,6},{4,1},{5,0},{6,3},{7,2},{8,13},{9,12},{10,... | collective-permute-start | bytes 98312 | tf_op jit(solution)/shard_map/ppermute | solution.py:352
  45.2 1.8 %collective-permute-start.27 = (f32[4,8,256]{2,1,0:T(8,128)S(1)}, f32[4,8,256]{2,1,0:T(8,128)S(1)}, u32[]{:S(2)}, u32[]{:S(2)}) collective-permute-start(f32[4,8,256]{2,1,0:T(8,128)S(1)} %get-tuple-element.96), channel_id=1, source_target_pairs={{0,7},{1,6},{2,5},{3,4},{4,3},{5,2},{6,1},{7,0},{8,15},{9,14},{10,... | collective-permute-start | bytes 98312 | tf_op jit(solution)/shard_map/ppermute | solution.py:352
  47.0 2.1 %collective-permute-done.26.rest_5_ = f32[4,8,256]{2,1,0:T(8,128)S(1)} collective-permute-done((f32[4,8,256]{2,1,0:T(8,128)S(1)}, f32[4,8,256]{2,1,0:T(8,128)S(1)}, u32[]{:S(2)}, u32[]{:S(2)}) %collective-permute-start.26) | collective-permute-done | bytes 32800 | tf_op jit(solution)/shard_map/ppermute | solution.py:352
  49.5 2.7 %shard_map.109 = (f32[16,8,256]{2,1,0:T(8,128)S(1)}, f32[16,8,256]{2,1,0:T(8,128)S(1)}, f32[8,256]{1,0:T(8,128)S(1)}, f32[8,256]{1,0:T(8,128)S(1)}, f32[4,8,256]...) custom-call(s32[1,16]{1,0:T(1,128)S(1)} %copy-done.8, ...), custom_call_target="tpu_custom_call" | custom-call | flops 600000000 | bytes 37500000 | tf_op jit(solution)/shard_map/pallas_call | solution.py:311
  54.0 1.6 %collective-permute-start.31 = (f32[4,8,256]{2,1,0:T(8,128)S(1)}, f32[4,8,256]{2,1,0:T(8,128)S(1)}, u32[]{:S(2)}, u32[]{:S(2)}) collective-permute-start(f32[4,8,256]{2,1,0:T(8,128)S(1)} %get-tuple-element.102), channel_id=1, source_target_pairs={{0,4},{1,5},{2,6},{3,7},{4,0},{5,1},{6,2},{7,3},{8,12},{9,13},{10,... | collective-permute-start | bytes 98312 | tf_op jit(solution)/shard_map/ppermute | solution.py:352
  55.8 2.0 %collective-permute-start.33 = (f32[4,8,256]{2,1,0:T(8,128)S(1)}, f32[4,8,256]{2,1,0:T(8,128)S(1)}, u32[]{:S(2)}, u32[]{:S(2)}) collective-permute-start(f32[4,8,256]{2,1,0:T(8,128)S(1)} %get-tuple-element.104), channel_id=1, source_target_pairs={{0,6},{1,7},{2,4},{3,5},{4,2},{5,3},{6,0},{7,1},{8,14},{9,15},{10,... | collective-permute-start | bytes 98312 | tf_op jit(solution)/shard_map/ppermute | solution.py:352
  59.1 1.5 %collective-permute-done.33.rest_5_ = f32[4,8,256]{2,1,0:T(8,128)S(1)} collective-permute-done((f32[4,8,256]{2,1,0:T(8,128)S(1)}, f32[4,8,256]{2,1,0:T(8,128)S(1)}, u32[]{:S(2)}, u32[]{:S(2)}) %collective-permute-start.33) | collective-permute-done | bytes 32800 | tf_op jit(solution)/shard_map/ppermute | solution.py:352
  60.6 1.5 %collective-permute-done.34.rest_6_ = f32[4,8,256]{2,1,0:T(8,128)S(1)} collective-permute-done((f32[4,8,256]{2,1,0:T(8,128)S(1)}, f32[4,8,256]{2,1,0:T(8,128)S(1)}, u32[]{:S(2)}, u32[]{:S(2)}) %collective-permute-start.34) | collective-permute-done | bytes 32800 | tf_op jit(solution)/shard_map/ppermute | solution.py:352
  62.2 2.7 %shard_map.110 = (f32[16,8,256]{2,1,0:T(8,128)S(1)}, f32[16,8,256]{2,1,0:T(8,128)S(1)}, f32[8,256]{1,0:T(8,128)S(1)}, f32[8,256]{1,0:T(8,128)S(1)}, f32[4,8,256]...) custom-call(s32[1,16]{1,0:T(1,128)S(1)} %copy-done.8, ...), custom_call_target="tpu_custom_call" | custom-call | flops 600000000 | bytes 37500000 | tf_op jit(solution)/shard_map/pallas_call | solution.py:311
  69.5 1.8 %collective-permute-start.41 = (f32[4,8,256]{2,1,0:T(8,128)S(1)}, f32[4,8,256]{2,1,0:T(8,128)S(1)}, u32[]{:S(2)}, u32[]{:S(2)}) collective-permute-start(f32[4,8,256]{2,1,0:T(8,128)S(1)} %get-tuple-element.118), channel_id=1, source_target_pairs={{0,7},{1,6},{2,5},{3,4},{4,3},{5,2},{6,1},{7,0},{8,15},{9,14},{10,... | collective-permute-start | bytes 98312 | tf_op jit(solution)/shard_map/ppermute | solution.py:352
  71.3 2.1 %collective-permute-done.40.rest_5_.rest_9_ = f32[4,8,256]{2,1,0:T(8,128)S(1)} collective-permute-done((f32[4,8,256]{2,1,0:T(8,128)S(1)}, f32[4,8,256]{2,1,0:T(8,128)S(1)}, u32[]{:S(2)}, u32[]{:S(2)}) %collective-permute-start.40) | collective-permute-done | bytes 32800 | tf_op jit(solution)/shard_map/ppermute | solution.py:352
  74.0 3.8 %collective-permute-start.44 = (f32[8,128]{1,0:T(8,128)S(1)}, f32[8,128]{1,0:T(8,128)S(1)}, u32[]{:S(2)}, u32[]{:S(2)}) collective-permute-start(f32[8,128]{1,0:T(8,128)S(1)} %shard_map.111.rest_0_), channel_id=1, source_target_pairs={{0,24},{8,0},{16,8},{24,16},{1,25},{9,1},{17,9},{25,17},{2,26},{10... | collective-permute-start | bytes 12296 | tf_op jit(solution)/shard_map/ppermute | solution.py:403
  77.8 1.2 %collective-permute-start.42 = (f32[8,128]{1,0:T(8,128)S(1)}, f32[8,128]{1,0:T(8,128)S(1)}, u32[]{:S(2)}, u32[]{:S(2)}) collective-permute-start(f32[8,128]{1,0:T(8,128)S(1)} %shard_map.111.rest_0_), channel_id=1, source_target_pairs={{0,8},{8,16},{16,24},{24,0},{1,9},{9,17},{17,25},{25,1},{2,10},{10... | collective-permute-start | bytes 12296 | tf_op jit(solution)/shard_map/ppermute | solution.py:403
  79.2 3.2 %collective-permute-done.43.rest_2_ = f32[8,128]{1,0:T(8,128)S(1)} collective-permute-done((f32[8,128]{1,0:T(8,128)S(1)}, f32[8,128]{1,0:T(8,128)S(1)}, u32[]{:S(2)}, u32[]{:S(2)}) %collective-permute-start.43) | collective-permute-done | bytes 4128 | tf_op jit(solution)/shard_map/ppermute | solution.py:403
  83.2 2.5 %shard_map.112 = (f32[8,16,256]{2,1,0:T(8,128)}, f32[8,16,256]{2,1,0:T(8,128)}) custom-call(s32[1,16]{1,0:T(1,128)S(1)} %copy-done.8, f32[8,128]{1,0:T(8,128)S(1)} %shard_map.111.rest_0_, f32[8,128]{1,0:T(8,128)S(1)} %collective-permute-done.42.rest_1_, f32[8,128]{1,0:T(8,128)S(1)} %collective-permute-done.43.rest_2_, ...), custom_call_target="tpu_custom_call" | custom-call | flops 4000000 | bytes 250000 | tf_op jit(solution)/shard_map/pallas_call | solution.py:311
  (93 shorter events, 21.5 us)
Async XLA Ops:
  2.9 4.9 %collective-permute-start.7 = (f32[3,8,256]{2,1,0:T(8,128)S(1)}, f32[3,8,256]{2,1,0:T(8,128)S(1)}, u32[]{:S(2)}, u32[]{:S(2)}) collective-permute-start(f32[3,8,256]{2,1,0:T(8,128)S(1)} %get-tuple-element.72), channel_id=1, source_target_pairs={{0,1},{1,0},{2,3},{3,2},{4,5},{5,4},{6,7},{7,6},{8,9},{9,8},{10,11... | collective-permute-start | bytes 73736 | tf_op jit(solution)/shard_map/ppermute | solution.py:352
  3.4 7.0 %collective-permute-start.8 = (f32[3,8,256]{2,1,0:T(8,128)S(1)}, f32[3,8,256]{2,1,0:T(8,128)S(1)}, u32[]{:S(2)}, u32[]{:S(2)}) collective-permute-start(f32[3,8,256]{2,1,0:T(8,128)S(1)} %get-tuple-element.73), channel_id=1, source_target_pairs={{0,2},{1,3},{2,0},{3,1},{4,6},{5,7},{6,4},{7,5},{8,10},{9,11},{10,... | collective-permute-start | bytes 73736 | tf_op jit(solution)/shard_map/ppermute | solution.py:352
  5.9 6.8 %collective-permute-start.9 = (f32[3,8,256]{2,1,0:T(8,128)S(1)}, f32[3,8,256]{2,1,0:T(8,128)S(1)}, u32[]{:S(2)}, u32[]{:S(2)}) collective-permute-start(f32[3,8,256]{2,1,0:T(8,128)S(1)} %get-tuple-element.74), channel_id=1, source_target_pairs={{0,3},{1,2},{2,1},{3,0},{4,7},{5,6},{6,5},{7,4},{8,11},{9,10},{10,... | collective-permute-start | bytes 73736 | tf_op jit(solution)/shard_map/ppermute | solution.py:352
  6.0 7.4 %collective-permute-start.10 = (f32[3,8,256]{2,1,0:T(8,128)S(1)}, f32[3,8,256]{2,1,0:T(8,128)S(1)}, u32[]{:S(2)}, u32[]{:S(2)}) collective-permute-start(f32[3,8,256]{2,1,0:T(8,128)S(1)} %get-tuple-element.75), channel_id=1, source_target_pairs={{0,4},{1,5},{2,6},{3,7},{4,0},{5,1},{6,2},{7,3},{8,12},{9,13},{10,... | collective-permute-start | bytes 73736 | tf_op jit(solution)/shard_map/ppermute | solution.py:352
  7.8 7.0 %collective-permute-start.11 = (f32[3,8,256]{2,1,0:T(8,128)S(1)}, f32[3,8,256]{2,1,0:T(8,128)S(1)}, u32[]{:S(2)}, u32[]{:S(2)}) collective-permute-start(f32[3,8,256]{2,1,0:T(8,128)S(1)} %get-tuple-element.76), channel_id=1, source_target_pairs={{0,5},{1,4},{2,7},{3,6},{4,1},{5,0},{6,3},{7,2},{8,13},{9,12},{10,... | collective-permute-start | bytes 73736 | tf_op jit(solution)/shard_map/ppermute | solution.py:352
  7.8 7.0 %collective-permute-start.12 = (f32[3,8,256]{2,1,0:T(8,128)S(1)}, f32[3,8,256]{2,1,0:T(8,128)S(1)}, u32[]{:S(2)}, u32[]{:S(2)}) collective-permute-start(f32[3,8,256]{2,1,0:T(8,128)S(1)} %get-tuple-element.77), channel_id=1, source_target_pairs={{0,6},{1,7},{2,4},{3,5},{4,2},{5,3},{6,0},{7,1},{8,14},{9,15},{10,... | collective-permute-start | bytes 73736 | tf_op jit(solution)/shard_map/ppermute | solution.py:352
  10.4 6.0 %collective-permute-start.13 = (f32[3,8,256]{2,1,0:T(8,128)S(1)}, f32[3,8,256]{2,1,0:T(8,128)S(1)}, u32[]{:S(2)}, u32[]{:S(2)}) collective-permute-start(f32[3,8,256]{2,1,0:T(8,128)S(1)} %get-tuple-element.78), channel_id=1, source_target_pairs={{0,7},{1,6},{2,5},{3,4},{4,3},{5,2},{6,1},{7,0},{8,15},{9,14},{10,... | collective-permute-start | bytes 73736 | tf_op jit(solution)/shard_map/ppermute | solution.py:352
  12.8 10.5 %collective-permute-start = (f32[3,8,256]{2,1,0:T(8,128)S(1)}, f32[3,8,256]{2,1,0:T(8,128)S(1)}, u32[]{:S(2)}, u32[]{:S(2)}) collective-permute-start(f32[3,8,256]{2,1,0:T(8,128)S(1)} %get-tuple-element.64), channel_id=1, source_target_pairs={{0,1},{1,0},{2,3},{3,2},{4,5},{5,4},{6,7},{7,6},{8,9},{9,8},{10,11... | collective-permute-start | bytes 73736 | tf_op jit(solution)/shard_map/ppermute | solution.py:352
  13.4 11.4 %collective-permute-start.1 = (f32[3,8,256]{2,1,0:T(8,128)S(1)}, f32[3,8,256]{2,1,0:T(8,128)S(1)}, u32[]{:S(2)}, u32[]{:S(2)}) collective-permute-start(f32[3,8,256]{2,1,0:T(8,128)S(1)} %get-tuple-element.65), channel_id=1, source_target_pairs={{0,2},{1,3},{2,0},{3,1},{4,6},{5,7},{6,4},{7,5},{8,10},{9,11},{10,... | collective-permute-start | bytes 73736 | tf_op jit(solution)/shard_map/ppermute | solution.py:352
  14.8 9.9 %collective-permute-start.2 = (f32[3,8,256]{2,1,0:T(8,128)S(1)}, f32[3,8,256]{2,1,0:T(8,128)S(1)}, u32[]{:S(2)}, u32[]{:S(2)}) collective-permute-start(f32[3,8,256]{2,1,0:T(8,128)S(1)} %get-tuple-element.66), channel_id=1, source_target_pairs={{0,3},{1,2},{2,1},{3,0},{4,7},{5,6},{6,5},{7,4},{8,11},{9,10},{10,... | collective-permute-start | bytes 73736 | tf_op jit(solution)/shard_map/ppermute | solution.py:352
  14.8 11.4 %collective-permute-start.3 = (f32[3,8,256]{2,1,0:T(8,128)S(1)}, f32[3,8,256]{2,1,0:T(8,128)S(1)}, u32[]{:S(2)}, u32[]{:S(2)}) collective-permute-start(f32[3,8,256]{2,1,0:T(8,128)S(1)} %get-tuple-element.67), channel_id=1, source_target_pairs={{0,4},{1,5},{2,6},{3,7},{4,0},{5,1},{6,2},{7,3},{8,12},{9,13},{10,... | collective-permute-start | bytes 73736 | tf_op jit(solution)/shard_map/ppermute | solution.py:352
  22.9 8.4 %collective-permute-start.14 = (f32[4,8,256]{2,1,0:T(8,128)S(1)}, f32[4,8,256]{2,1,0:T(8,128)S(1)}, u32[]{:S(2)}, u32[]{:S(2)}) collective-permute-start(f32[4,8,256]{2,1,0:T(8,128)S(1)} %get-tuple-element.80), channel_id=1, source_target_pairs={{0,1},{1,0},{2,3},{3,2},{4,5},{5,4},{6,7},{7,6},{8,9},{9,8},{10,11... | collective-permute-start | bytes 98312 | tf_op jit(solution)/shard_map/ppermute | solution.py:352
  23.2 10.3 %collective-permute-start.15 = (f32[4,8,256]{2,1,0:T(8,128)S(1)}, f32[4,8,256]{2,1,0:T(8,128)S(1)}, u32[]{:S(2)}, u32[]{:S(2)}) collective-permute-start(f32[4,8,256]{2,1,0:T(8,128)S(1)} %get-tuple-element.81), channel_id=1, source_target_pairs={{0,2},{1,3},{2,0},{3,1},{4,6},{5,7},{6,4},{7,5},{8,10},{9,11},{10,... | collective-permute-start | bytes 98312 | tf_op jit(solution)/shard_map/ppermute | solution.py:352
  24.8 4.8 %collective-permute-start.5 = (f32[3,8,256]{2,1,0:T(8,128)S(1)}, f32[3,8,256]{2,1,0:T(8,128)S(1)}, u32[]{:S(2)}, u32[]{:S(2)}) collective-permute-start(f32[3,8,256]{2,1,0:T(8,128)S(1)} %get-tuple-element.69), channel_id=1, source_target_pairs={{0,6},{1,7},{2,4},{3,5},{4,2},{5,3},{6,0},{7,1},{8,14},{9,15},{10,... | collective-permute-start | bytes 73736 | tf_op jit(solution)/shard_map/ppermute | solution.py:352
  26.3 5.0 %collective-permute-start.6 = (f32[3,8,256]{2,1,0:T(8,128)S(1)}, f32[3,8,256]{2,1,0:T(8,128)S(1)}, u32[]{:S(2)}, u32[]{:S(2)}) collective-permute-start(f32[3,8,256]{2,1,0:T(8,128)S(1)} %get-tuple-element.70), channel_id=1, source_target_pairs={{0,7},{1,6},{2,5},{3,4},{4,3},{5,2},{6,1},{7,0},{8,15},{9,14},{10,... | collective-permute-start | bytes 73736 | tf_op jit(solution)/shard_map/ppermute | solution.py:352
  28.2 7.7 %collective-permute-start.16 = (f32[4,8,256]{2,1,0:T(8,128)S(1)}, f32[4,8,256]{2,1,0:T(8,128)S(1)}, u32[]{:S(2)}, u32[]{:S(2)}) collective-permute-start(f32[4,8,256]{2,1,0:T(8,128)S(1)} %get-tuple-element.82), channel_id=1, source_target_pairs={{0,3},{1,2},{2,1},{3,0},{4,7},{5,6},{6,5},{7,4},{8,11},{9,10},{10,... | collective-permute-start | bytes 98312 | tf_op jit(solution)/shard_map/ppermute | solution.py:352
  29.5 6.3 %collective-permute-start.17 = (f32[4,8,256]{2,1,0:T(8,128)S(1)}, f32[4,8,256]{2,1,0:T(8,128)S(1)}, u32[]{:S(2)}, u32[]{:S(2)}) collective-permute-start(f32[4,8,256]{2,1,0:T(8,128)S(1)} %get-tuple-element.83), channel_id=1, source_target_pairs={{0,4},{1,5},{2,6},{3,7},{4,0},{5,1},{6,2},{7,3},{8,12},{9,13},{10,... | collective-permute-start | bytes 98312 | tf_op jit(solution)/shard_map/ppermute | solution.py:352
  31.2 4.7 %collective-permute-start.18 = (f32[4,8,256]{2,1,0:T(8,128)S(1)}, f32[4,8,256]{2,1,0:T(8,128)S(1)}, u32[]{:S(2)}, u32[]{:S(2)}) collective-permute-start(f32[4,8,256]{2,1,0:T(8,128)S(1)} %get-tuple-element.84), channel_id=1, source_target_pairs={{0,5},{1,4},{2,7},{3,6},{4,1},{5,0},{6,3},{7,2},{8,13},{9,12},{10,... | collective-permute-start | bytes 98312 | tf_op jit(solution)/shard_map/ppermute | solution.py:352
  31.2 4.9 %collective-permute-start.19 = (f32[4,8,256]{2,1,0:T(8,128)S(1)}, f32[4,8,256]{2,1,0:T(8,128)S(1)}, u32[]{:S(2)}, u32[]{:S(2)}) collective-permute-start(f32[4,8,256]{2,1,0:T(8,128)S(1)} %get-tuple-element.85), channel_id=1, source_target_pairs={{0,6},{1,7},{2,4},{3,5},{4,2},{5,3},{6,0},{7,1},{8,14},{9,15},{10,... | collective-permute-start | bytes 98312 | tf_op jit(solution)/shard_map/ppermute | solution.py:352
  40.7 4.5 %collective-permute-start.22 = (f32[4,8,256]{2,1,0:T(8,128)S(1)}, f32[4,8,256]{2,1,0:T(8,128)S(1)}, u32[]{:S(2)}, u32[]{:S(2)}) collective-permute-start(f32[4,8,256]{2,1,0:T(8,128)S(1)} %get-tuple-element.91), channel_id=1, source_target_pairs={{0,2},{1,3},{2,0},{3,1},{4,6},{5,7},{6,4},{7,5},{8,10},{9,11},{10,... | collective-permute-start | bytes 98312 | tf_op jit(solution)/shard_map/ppermute | solution.py:352
  41.6 5.4 %collective-permute-start.23 = (f32[4,8,256]{2,1,0:T(8,128)S(1)}, f32[4,8,256]{2,1,0:T(8,128)S(1)}, u32[]{:S(2)}, u32[]{:S(2)}) collective-permute-start(f32[4,8,256]{2,1,0:T(8,128)S(1)} %get-tuple-element.92), channel_id=1, source_target_pairs={{0,3},{1,2},{2,1},{3,0},{4,7},{5,6},{6,5},{7,4},{8,11},{9,10},{10,... | collective-permute-start | bytes 98312 | tf_op jit(solution)/shard_map/ppermute | solution.py:352
  44.3 4.8 %collective-permute-start.26 = (f32[4,8,256]{2,1,0:T(8,128)S(1)}, f32[4,8,256]{2,1,0:T(8,128)S(1)}, u32[]{:S(2)}, u32[]{:S(2)}) collective-permute-start(f32[4,8,256]{2,1,0:T(8,128)S(1)} %get-tuple-element.95), channel_id=1, source_target_pairs={{0,6},{1,7},{2,4},{3,5},{4,2},{5,3},{6,0},{7,1},{8,14},{9,15},{10,... | collective-permute-start | bytes 98312 | tf_op jit(solution)/shard_map/ppermute | solution.py:352
  52.3 5.5 %collective-permute-start.29 = (f32[4,8,256]{2,1,0:T(8,128)S(1)}, f32[4,8,256]{2,1,0:T(8,128)S(1)}, u32[]{:S(2)}, u32[]{:S(2)}) collective-permute-start(f32[4,8,256]{2,1,0:T(8,128)S(1)} %get-tuple-element.100), channel_id=1, source_target_pairs={{0,2},{1,3},{2,0},{3,1},{4,6},{5,7},{6,4},{7,5},{8,10},{9,11},{10,... | collective-permute-start | bytes 98312 | tf_op jit(solution)/shard_map/ppermute | solution.py:352
  53.2 5.2 %collective-permute-start.30 = (f32[4,8,256]{2,1,0:T(8,128)S(1)}, f32[4,8,256]{2,1,0:T(8,128)S(1)}, u32[]{:S(2)}, u32[]{:S(2)}) collective-permute-start(f32[4,8,256]{2,1,0:T(8,128)S(1)} %get-tuple-element.101), channel_id=1, source_target_pairs={{0,3},{1,2},{2,1},{3,0},{4,7},{5,6},{6,5},{7,4},{8,11},{9,10},{10,... | collective-permute-start | bytes 98312 | tf_op jit(solution)/shard_map/ppermute | solution.py:352
  55.8 4.8 %collective-permute-start.33 = (f32[4,8,256]{2,1,0:T(8,128)S(1)}, f32[4,8,256]{2,1,0:T(8,128)S(1)}, u32[]{:S(2)}, u32[]{:S(2)}) collective-permute-start(f32[4,8,256]{2,1,0:T(8,128)S(1)} %get-tuple-element.104), channel_id=1, source_target_pairs={{0,6},{1,7},{2,4},{3,5},{4,2},{5,3},{6,0},{7,1},{8,14},{9,15},{10,... | collective-permute-start | bytes 98312 | tf_op jit(solution)/shard_map/ppermute | solution.py:352
  65.1 4.4 %collective-permute-start.36 = (f32[4,8,256]{2,1,0:T(8,128)S(1)}, f32[4,8,256]{2,1,0:T(8,128)S(1)}, u32[]{:S(2)}, u32[]{:S(2)}) collective-permute-start(f32[4,8,256]{2,1,0:T(8,128)S(1)} %get-tuple-element.113), channel_id=1, source_target_pairs={{0,2},{1,3},{2,0},{3,1},{4,6},{5,7},{6,4},{7,5},{8,10},{9,11},{10,... | collective-permute-start | bytes 98312 | tf_op jit(solution)/shard_map/ppermute | solution.py:352
  66.0 5.2 %collective-permute-start.37 = (f32[4,8,256]{2,1,0:T(8,128)S(1)}, f32[4,8,256]{2,1,0:T(8,128)S(1)}, u32[]{:S(2)}, u32[]{:S(2)}) collective-permute-start(f32[4,8,256]{2,1,0:T(8,128)S(1)} %get-tuple-element.114), channel_id=1, source_target_pairs={{0,3},{1,2},{2,1},{3,0},{4,7},{5,6},{6,5},{7,4},{8,11},{9,10},{10,... | collective-permute-start | bytes 98312 | tf_op jit(solution)/shard_map/ppermute | solution.py:352
  66.8 4.4 %collective-permute-start.38 = (f32[4,8,256]{2,1,0:T(8,128)S(1)}, f32[4,8,256]{2,1,0:T(8,128)S(1)}, u32[]{:S(2)}, u32[]{:S(2)}) collective-permute-start(f32[4,8,256]{2,1,0:T(8,128)S(1)} %get-tuple-element.115), channel_id=1, source_target_pairs={{0,4},{1,5},{2,6},{3,7},{4,0},{5,1},{6,2},{7,3},{8,12},{9,13},{10,... | collective-permute-start | bytes 98312 | tf_op jit(solution)/shard_map/ppermute | solution.py:352
  68.6 4.8 %collective-permute-start.40 = (f32[4,8,256]{2,1,0:T(8,128)S(1)}, f32[4,8,256]{2,1,0:T(8,128)S(1)}, u32[]{:S(2)}, u32[]{:S(2)}) collective-permute-start(f32[4,8,256]{2,1,0:T(8,128)S(1)} %get-tuple-element.117), channel_id=1, source_target_pairs={{0,6},{1,7},{2,4},{3,5},{4,2},{5,3},{6,0},{7,1},{8,14},{9,15},{10,... | collective-permute-start | bytes 98312 | tf_op jit(solution)/shard_map/ppermute | solution.py:352
  74.0 5.1 %collective-permute-start.44 = (f32[8,128]{1,0:T(8,128)S(1)}, f32[8,128]{1,0:T(8,128)S(1)}, u32[]{:S(2)}, u32[]{:S(2)}) collective-permute-start(f32[8,128]{1,0:T(8,128)S(1)} %shard_map.111.rest_0_), channel_id=1, source_target_pairs={{0,24},{8,0},{16,8},{24,16},{1,25},{9,1},{17,9},{25,17},{2,26},{10... | collective-permute-start | bytes 12296 | tf_op jit(solution)/shard_map/ppermute | solution.py:403
  77.8 4.5 %collective-permute-start.43 = (f32[8,128]{1,0:T(8,128)S(1)}, f32[8,128]{1,0:T(8,128)S(1)}, u32[]{:S(2)}, u32[]{:S(2)}) collective-permute-start(f32[8,128]{1,0:T(8,128)S(1)} %shard_map.111.rest_0_), channel_id=1, source_target_pairs={{0,16},{8,24},{16,0},{24,8},{1,17},{9,25},{17,1},{25,9},{2,18},{10... | collective-permute-start | bytes 12296 | tf_op jit(solution)/shard_map/ppermute | solution.py:403
  77.8 5.4 %collective-permute-start.42 = (f32[8,128]{1,0:T(8,128)S(1)}, f32[8,128]{1,0:T(8,128)S(1)}, u32[]{:S(2)}, u32[]{:S(2)}) collective-permute-start(f32[8,128]{1,0:T(8,128)S(1)} %shard_map.111.rest_0_), channel_id=1, source_target_pairs={{0,8},{8,16},{16,24},{24,0},{1,9},{9,17},{17,25},{25,1},{2,10},{10... | collective-permute-start | bytes 12296 | tf_op jit(solution)/shard_map/ppermute | solution.py:403
  (26 other events, 146.7 us)

commit v2 on v1

v2 whole, which is shorter than its diff:
```python
import functools

import jax
import jax.numpy as jnp
from jax import lax
from jax.experimental import pallas as pl
from jax.experimental.pallas import tpu as pltpu
from jax.sharding import PartitionSpec as P

ITERS = 4
HIGH = lax.Precision.HIGHEST
F32 = jnp.float32
BF16 = jnp.bfloat16
VMEM = pl.BlockSpec(memory_space=pltpu.VMEM)
SMEM = pl.BlockSpec(memory_space=pltpu.SMEM)
HBM = pl.BlockSpec(memory_space=pltpu.HBM)
LIMIT = 24 * 1024 * 1024
PAIRS = [(i, j) for j in range(ITERS) for i in range(j + 1)]
ENTRIES = len(PAIRS) + ITERS
NN = (((1,), (0,)), ((), ()))
NT = (((1,), (1,)), ((), ()))
TN = (((0,), (0,)), ((), ()))


def dot(a, b, dims):
    return lax.dot_general(a, b, dims, preferred_element_type=F32)


def dot_high(a, b, dims):
    return lax.dot_general(a, b, dims, precision=HIGH, preferred_element_type=F32)


def split(a):
    high = a.astype(BF16).astype(F32)
    return jnp.concatenate([high, a - high], axis=0).astype(BF16)


def fold(a):
    half = a.shape[0] // 2
    return a[:half] + a[half:]


def lane_ids(shape):
    return lax.broadcasted_iota(jnp.int32, shape, 1)


class Sizes:
    def __init__(self, load, corner_coupling, coarse_inverse, mesh):
        self.columns = load.shape[0]
        self.blocks = load.shape[1]
        self.width = load.shape[2]
        self.corners = corner_coupling.shape[0]
        assert self.corners == self.columns
        self.coarse = coarse_inverse.shape[1]
        self.peers = mesh["sub"]
        self.groups = mesh["group"]
        self.capacity = (self.blocks + self.peers - 2) // (self.peers - 1)
        self.all_corners = self.peers * self.corners
        self.max_lane = self.all_corners
        self.gram_lane = self.max_lane + self.peers
        self.extra_chunks = -(-(self.gram_lane + ENTRIES) // self.width)
        self.extra = self.extra_chunks * self.width
        self.far = range(2, self.peers, 2)
        self.odd = range(1, self.peers, 2)
        self.slots = self.peers * self.capacity
        self.inverse = self.slots
        self.pattern = self.inverse + self.blocks
        self.partner = self.pattern + self.blocks
        self.table = self.partner + self.blocks

    def near_rows(self, kinds):
        return len(self.odd) * kinds * self.capacity

    def far_rows(self, kinds):
        return 2 * kinds * self.capacity


def fill_table(z, partner, pattern, table, counts):
    me = lax.axis_index("sub")
    for entry in range(z.slots):
        table[entry] = z.blocks
    for m in range(z.peers):
        counts[m] = 0
    for i in range(z.blocks):
        mate = partner[0, i]
        source = pattern[0, i]
        m = mate ^ me
        rank = counts[m]
        table[m * z.capacity + rank] = i
        counts[m] = rank + 1
        table[z.inverse + source] = i
        table[z.pattern + i] = source
        table[z.partner + i] = mate


def block_of(z, table, m, r):
    return jnp.minimum(table[m * z.capacity + r], z.blocks - 1)


def fill_near(z, table, sources, near):
    row = 0
    for m in z.odd:
        for source in sources:
            for r in range(z.capacity):
                near[row] = source[block_of(z, table, m, r)]
                row += 1


def place(z, table, near, fars, kind, kinds, target):
    for r in range(z.capacity):
        target[table[z.capacity + r]] = near[kind * z.capacity + r]
    for m, far in zip(z.far, fars):
        for r in range(z.capacity):
            row = 2 * kind * z.capacity + r
            target[table[m * z.capacity + r]] = far[row]
            target[table[(m + 1) * z.capacity + r]] = far[row + z.capacity]


def begin(z, partner, pattern, load, scale, coupling, table, field, lift, scale_out, coupling_out, near, *scratch):
    here, partner_here, pattern_here, counts, sems = scratch
    copies = [
        pltpu.make_async_copy(a, b, sems.at[k])
        for k, (a, b) in enumerate(
            [
                (partner, partner_here),
                (pattern, pattern_here),
                (load, here),
                (scale, scale_out),
                (coupling, coupling_out),
            ]
        )
    ]
    for copy in copies:
        copy.start()
    copies[0].wait()
    copies[1].wait()
    fill_table(z, partner_here, pattern_here, table, counts)
    for copy in copies[2:]:
        copy.wait()
    for i in range(z.blocks):
        field[i] = here[:, i, :]
        part = coupling_out[:, i * z.width : (i + 1) * z.width].astype(F32)
        lift[i] = scale_out[i : i + 1, :] * part
    fill_near(z, table, [field, lift], near)


def relay(z, kinds, table, *rest):
    sources, rest = rest[:kinds], rest[kinds:]
    extras = z.extra_chunks if kinds == 1 else 0
    if extras:
        own_extra, rest = rest[0], rest[1:]
    near, fars = rest[0], rest[1:]
    for m, far in zip(z.far, fars):
        for kind, source in enumerate(sources):
            row = 2 * kind * z.capacity
            base = (m // 2 * kinds + kind) * z.capacity
            for r in range(z.capacity):
                far[row + r] = source[block_of(z, table, m, r)]
                far[row + z.capacity + r] = near[base + r]
    for j in range(extras):
        chunk = own_extra[:, j * z.width : (j + 1) * z.width] + near[z.near_rows(1) + j]
        for far in fars:
            far[z.far_rows(1) + j] = chunk


def split3(a):
    high = a.astype(BF16).astype(F32)
    middle = (a - high).astype(BF16).astype(F32)
    return [high, middle, a - high - middle]


def build_operator(z, index, inverse, operator):
    rows = lax.broadcasted_iota(jnp.int32, (z.coarse, z.all_corners), 0)
    select = (rows == index[...]).astype(BF16)
    parts = jnp.concatenate(split3(inverse[...]), axis=0).astype(BF16)
    half = dot(parts, select, NN)
    half = sum(half[k * z.coarse : (k + 1) * z.coarse] for k in range(3))
    parts = jnp.concatenate(split3(half), axis=1).astype(BF16)
    full = dot(select, parts, TN)
    operator[...] = sum(full[:, k * z.all_corners : (k + 1) * z.all_corners] for k in range(3))


def build_lift(z, table, operator, lift, near, *rest):
    fars, (jump_lift, other) = rest[:-2], rest[-2:]
    place(z, table, near, fars, 1, 2, other)
    me = lax.axis_index("sub")
    own = operator[pl.ds(pl.multiple_of(me * z.corners, z.corners), z.corners), :]
    for i in range(z.blocks):
        at = pl.multiple_of(table[z.partner + i] * z.corners, z.corners)
        left = split(jnp.concatenate([own, -operator[pl.ds(at, z.corners), :]], axis=0))
        right = split(jnp.concatenate([lift[i], other[i]], axis=0))
        count = 2 * z.corners
        left = jnp.concatenate([left, left[:count]], axis=0)
        right = jnp.concatenate([right[:count], right[:count], right[count:]], axis=0)
        jump_lift[i] = split(dot(left, right, TN))


def extra_sum(z, own, near, fars):
    def read(ref, row):
        return jnp.concatenate([ref[row + j] for j in range(z.extra_chunks)], axis=1)

    total = own[...] + read(near, z.near_rows(1))
    for far in fars:
        total = total + read(far, z.far_rows(1))
    return total


def cluster_max(z, total):
    lanes = lane_ids(total.shape)
    own = (lanes >= z.max_lane) & (lanes < z.gram_lane)
    return jnp.max(jnp.where(own, total, 0.0), axis=1, keepdims=True)


def corner_rows(z, total):
    rows = split(total[:, : z.all_corners])
    return jnp.concatenate([rows, rows], axis=1)


def lane_sum(a):
    return jnp.sum(a, axis=1, keepdims=True)


def apply_round(z, step, table, *rest):
    count = len(z.far)
    first, last = step == 1, step == ITERS
    rest = list(rest)
    take = lambda n: [rest.pop(0) for _ in range(n)]
    near, *fars = take(1 + count)
    (before,) = take(1)
    if not first:
        own_extra, jump_lift = take(2)
    scale, diag, off, coupling = take(4)
    older = take(ITERS - 1) if last else []
    field, image = take(2)
    if first:
        sources, (diag, off) = (diag, off), take(2)
    else:
        (total_out,) = take(1)
    extra, near_out = take(2)
    other, parts = take(2)
    if first:
        (sems,) = rest
        copies = [
            [
                pltpu.make_async_copy(a.at[i], b.at[i], sems.at[k, i])
                for k, (a, b) in enumerate(zip(sources, (diag, off)))
            ]
            for i in range(z.blocks)
        ]
        for pair in copies:
            for copy in pair:
                copy.start()
    place(z, table, near, fars, 0, 2 if first else 1, other)
    if not first:
        total = extra_sum(z, own_extra, near, fars)
        total_out[...] = total
        rows = corner_rows(z, total)
        shrink = 1.0 / cluster_max(z, total)
    for i in range(z.blocks):
        value = before[i] - other[i]
        if not first:
            value = (value + fold(dot(rows, jump_lift[i], NN))) * shrink
        field[i] = value
        parts[i] = split(scale[i : i + 1, :] * value)
    if first:
        for pair in copies:
            for copy in pair:
                copy.wait()
    partial = jnp.zeros((2 * z.columns, z.corners), F32)
    top = jnp.zeros((z.columns, z.width), F32)
    for i in range(z.blocks):
        mine = parts[i]
        partial = partial + dot(mine, coupling[:, i * z.width : (i + 1) * z.width], NT)
        source = table[z.inverse + i]
        coupled = dot(mine, diag[i], NT) + dot(mine, diag[i], NN)
        coupled = coupled + dot(parts[table[z.pattern + i]], off[i], NT)
        coupled = coupled + dot(parts[source], off[source], NN)
        row = scale[i : i + 1, :]
        result = row * (row * field[i] + fold(coupled))
        image[i] = result
        top = jnp.maximum(top, jnp.abs(result))
    fill_near(z, table, [image], near_out)
    me = lax.axis_index("sub")
    lanes = lane_ids((z.columns, z.extra))
    sums = fold(partial)
    padded = jnp.concatenate(
        [sums, jnp.zeros((z.columns, z.extra - z.corners), F32)], axis=1
    )
    tile = pltpu.roll(padded, me * z.corners, 1)
    tile = jnp.where(lanes == z.max_lane + me, jnp.max(top, axis=1, keepdims=True), tile)
    if last:
        fields = older + [field]
        products = [(fields[i], fields[j]) for i, j in PAIRS] + [(f, image) for f in fields]
        for entry, (a, b) in enumerate(products):
            acc = a[0] * b[0]
            for i in range(1, z.blocks):
                acc = acc + a[i] * b[i]
            tile = jnp.where(lanes == z.gram_lane + entry, lane_sum(acc), tile)
    extra[...] = tile
    for j in range(z.extra_chunks):
        near_out[z.near_rows(1) + j] = tile[:, j * z.width : (j + 1) * z.width]


def cluster_gram(z, operator, own_extra, near, *rest):
    count = len(z.far)
    fars, totals, (gram,) = rest[:count], rest[count:-1], rest[-1:]
    total = extra_sum(z, own_extra, near, fars)
    totals = [t[...] for t in totals]
    partials = [t[:, : z.all_corners] for t in totals + [total]]
    lifted = dot_high(partials[-1], operator[...], NT)
    lanes = lane_ids(gram.shape)
    tile = jnp.zeros(gram.shape, F32)
    for entry in range(ENTRIES):
        lane = z.gram_lane + entry
        value = total[:, lane : lane + 1]
        if entry >= len(PAIRS):
            value = 2.0 * (value + lane_sum(partials[entry - len(PAIRS)] * lifted))
        tile = jnp.where(lanes == entry, value, tile)
    for step, t in enumerate(totals):
        tile = jnp.where(lanes == ENTRIES + step, cluster_max(z, t), tile)
    gram[...] = tile


def last_vector(z, table, before, own_extra, jump_lift, near, *rest):
    fars, (field, other) = rest[:-2], rest[-2:]
    place(z, table, near, fars, 0, 1, other)
    rows = corner_rows(z, extra_sum(z, own_extra, near, fars))
    for i in range(z.blocks):
        field[i] = before[i] - other[i] + fold(dot(rows, jump_lift[i], NN))


def finish(z, *rest):
    grams, rest = rest[: z.groups], rest[z.groups :]
    fields, (multipliers, residual) = rest[:-2], rest[-2:]
    tables = [gram[...] for gram in grams]
    mine = tables[0]
    one = jnp.ones((z.columns, 1), F32)
    ratio = [[one] * z.groups]
    own_ratio = [one]
    growth = [None]
    for step in range(1, ITERS + 1):
        if step < ITERS:
            lane = ENTRIES + step - 1
            grown = [q * t[:, lane : lane + 1] for q, t in zip(ratio[-1], tables)]
            own = own_ratio[-1] * mine[:, lane : lane + 1]
        else:
            grown, own = ratio[-1], own_ratio[-1]
        top = functools.reduce(jnp.maximum, grown)
        ratio.append([q / top for q in grown])
        own_ratio.append(own / top)
        growth.append(top)
    gram = {}
    pairs = PAIRS + [(i, ITERS) for i in range(ITERS)]
    for entry, (i, j) in enumerate(pairs):
        value = 0.0
        for g in range(z.groups):
            value = value + ratio[i][g] * ratio[j][g] * tables[g][:, entry : entry + 1]
        gram[i, j] = gram[j, i] = value

    def inner(a, b):
        return sum(a[i] * sum(gram[i, j] * b[j] for j in b) for i in a)

    def add(a, weight, b):
        out = dict(a)
        for i, value in b.items():
            out[i] = out[i] + weight * value if i in out else weight * value
        return out

    rest_of, way, found = {0: one}, {0: one}, {}
    norm = gram[0, 0]
    for step in range(ITERS):
        product = {i + 1: growth[i + 1] * value for i, value in way.items()}
        alpha = norm / inner(way, product)
        found = add(found, alpha, way)
        rest_of = add(rest_of, -alpha, product)
        if step < ITERS - 1:
            following = inner(rest_of, rest_of)
            way = add(rest_of, following / norm, way)
            norm = following
    found = {i: value * own_ratio[i] for i, value in found.items()}
    rest_of = {i: value * own_ratio[i] for i, value in rest_of.items()}
    for i in range(z.blocks):
        values = [f[i] for f in fields]
        multipliers[:, i, :] = sum(c * values[j] for j, c in found.items())
        residual[:, i, :] = sum(c * values[j] for j, c in rest_of.items())


def call(body, outs, scratch, cost, args, table=True, away=(), table_out=False):
    specs = [HBM if k in away else VMEM for k in range(len(args))]
    if table:
        specs[0] = SMEM
    out_specs = [VMEM] * len(outs)
    if table_out:
        out_specs[0] = SMEM
    return pl.pallas_call(
        body,
        out_shape=[jax.ShapeDtypeStruct(s, t) for s, t in outs],
        in_specs=specs,
        out_specs=out_specs,
        scratch_shapes=scratch,
        compiler_params=pltpu.CompilerParams(vmem_limit_bytes=LIMIT),
        cost_estimate=pl.CostEstimate(flops=cost, bytes_accessed=cost // 16, transcendentals=0),
    )(*args)


def on_device(
    load,
    row_scale,
    diag_blocks,
    off_blocks,
    off_pattern,
    partner,
    corner_coupling,
    corner_index,
    coarse_inverse,
    *,
    mesh,
):
    z = Sizes(load, corner_coupling, coarse_inverse, mesh)
    cols, blocks, width = z.columns, z.blocks, z.width
    field = ((blocks, cols, width), F32)
    other = pltpu.VMEM((blocks + 1, cols, width), F32)
    parts = pltpu.VMEM((blocks, 2 * cols, width), BF16)
    extra = ((cols, z.extra), F32)
    gram = ((cols, 128), F32)
    light, heavy = 4_000_000, 600_000_000

    def near_shape(kinds):
        return ((z.near_rows(kinds) + (z.extra_chunks if kinds == 1 else 0), cols, width), F32)

    def far_shape(kinds):
        return ((z.far_rows(kinds) + (z.extra_chunks if kinds == 1 else 0), cols, width), F32)

    def kernel(body, *extra_args):
        return functools.partial(body, z, *extra_args)

    def across(piece, m):
        return lax.ppermute(piece, "sub", [(t, t ^ m) for t in range(z.peers)])

    def exchange(near, sources):
        kinds = 1 if len(sources) == 1 else 2
        near = across(near, 1)
        own = [own_extra] if kinds == 1 else []
        pieces = call(
            kernel(relay, kinds), [far_shape(kinds)] * len(z.far), [], light,
            [table, *sources, *own, near],
        )
        return [near] + [across(piece, m) for m, piece in zip(z.far, pieces)]

    table, loaded, lift, scale, coupling, near = call(
        kernel(begin),
        [
            ((z.table,), jnp.int32),
            field,
            field,
            (row_scale.shape, F32),
            (corner_coupling.shape, BF16),
            near_shape(2),
        ],
        [
            pltpu.VMEM(load.shape, F32),
            pltpu.SMEM(partner.shape, jnp.int32),
            pltpu.SMEM(off_pattern.shape, jnp.int32),
            pltpu.SMEM((z.peers,), jnp.int32),
            pltpu.SemaphoreType.DMA((5,)),
        ],
        light,
        [partner, off_pattern, load, row_scale, corner_coupling],
        False, range(5), True,
    )
    arrived = exchange(near, [loaded, lift])
    (operator,) = call(
        kernel(build_operator), [((z.all_corners, z.all_corners), F32)], [], light,
        [corner_index, coarse_inverse], False,
    )
    weight = (diag_blocks.shape, BF16)
    newest, image, diag, off, own_extra, near = call(
        kernel(apply_round, 1),
        [field, field, weight, weight, extra, near_shape(1)],
        [other, parts, pltpu.SemaphoreType.DMA((2, blocks))], heavy,
        [table, *arrived, loaded, scale, diag_blocks, off_blocks, coupling],
        True, (len(arrived) + 3, len(arrived) + 4),
    )
    (jump_lift,) = call(
        kernel(build_lift), [((blocks, 2 * z.all_corners, width), BF16)], [other], heavy,
        [table, operator, lift, *arrived],
    )
    arrived = exchange(near, [image])
    fields, totals = [newest], []
    for step in range(2, ITERS + 1):
        older = fields if step == ITERS else []
        newest, image, total, own_extra, near = call(
            kernel(apply_round, step),
            [field, field, extra, extra, near_shape(1)], [other, parts], heavy,
            [table, *arrived, image, own_extra, jump_lift, scale, diag, off, coupling, *older],
        )
        fields.append(newest)
        totals.append(total)
        arrived = exchange(near, [image])
    (own_gram,) = call(
        kernel(cluster_gram), [gram], [], light, [operator, own_extra, *arrived, *totals], False
    )
    power = z.groups & (z.groups - 1) == 0
    grams = [own_gram] + [
        lax.ppermute(
            own_gram, "group",
            [(a, a ^ k if power else (a + k) % z.groups) for a in range(z.groups)],
        )
        for k in range(1, z.groups)
    ]
    (newest,) = call(
        kernel(last_vector), [field], [other], light,
        [table, image, own_extra, jump_lift, *arrived],
    )
    multipliers, residual = call(
        kernel(finish), [(load.shape, F32)] * 2, [], light, [*grams, *fields, newest], False
    )
    return multipliers, residual


def solution(mesh):
    return jax.shard_map(
        functools.partial(on_device, mesh=dict(mesh.shape)),
        mesh=mesh,
        in_specs=(
            P(None, ("group", "sub"), None),
            P(("group", "sub"), None),
            P(("group", "sub"), None, None),
            P(("group", "sub"), None, None),
            P(("group", "sub"), None),
            P(("group", "sub"), None),
            P(("group", "sub"), None),
            P("group", None),
            P("group", None),
        ),
        out_specs=(P(None, ("group", "sub"), None), P(None, ("group", "sub"), None)),
        check_vma=False,
    )
```

time: 86 us -> 84.4 us (0.981)
  starting transfers between devices: 44.5 us -> 23.8 us
  waiting for transfers between devices: 16.8 us -> 27.8 us
  Pallas kernels: 16.7 us -> 24.8 us
    ppermute x45 -> x23, starting transfers between devices: 44.5 us -> 23.8 us  [the longest x20 19.4 us: across(): return lax.ppermute(piece, 'sub', [(t, t ^ m) for t in range(z.peers)])]
    ppermute x45 -> x23, waiting for transfers between devices: 16.8 us -> 27.8 us  [the longest x20 24.9 us: across(): return lax.ppermute(piece, 'sub', [(t, t ^ m) for t in range(z.peers)])]
    pallas_call x9 -> x15, Pallas kernels: 16.7 us -> 24.8 us  [call(): pl.pallas_call(body, out_shape=[jax.ShapeDtypeStruct(s, t) for s, t in ou...]
    unnamed x26 -> x18, local copies, waits for them, and re-layouts: 6.98 us -> 6.95 us
  transfers between devices with their start and end apart: 45 -> 23, of which waited for: 14 -> 21; matrix products, arithmetic and copies ran while one was open for 0% -> 0% of each run, Pallas kernels for 6% -> 3%
where the time goes in v2:
time: 84.4 us; the launch traced here: 84.1 us
  waiting for transfers between devices  27.8 us (33%)
  Pallas kernels  24.8 us (29%)
  starting transfers between devices  23.8 us (28%)
  local copies, waits for them, and re-layouts  6.95 us (8%)
    ppermute x20, waiting for transfers between devices, across(): return lax.ppermute(piece, 'sub', [(t, t ^ m) for t in range(z.peers)])  24.9 us
    pallas_call x15, Pallas kernels, call(): pl.pallas_call(body, out_shape=[jax.ShapeDtypeStruct(s, t) for s, t in ou...  24.8 us
    ppermute x20, starting transfers between devices, across(): return lax.ppermute(piece, 'sub', [(t, t ^ m) for t in range(z.peers)])  19.4 us
    unnamed x18, local copies, waits for them, and re-layouts  6.95 us
    ppermute x3, starting transfers between devices, on_device(): lax.ppermute(own_gram, 'group', [(a, a ^ k if power else (a + k) % z.grou...  4.43 us
    ppermute x3, waiting for transfers between devices, on_device(): lax.ppermute(own_gram, 'group', [(a, a ^ k if power else (a + k) % z.grou...  2.87 us
  transfers between devices with their start and end apart: 23, of which 21 were waited for; matrix products, arithmetic and copies ran while one was open for 0% of the time, Pallas kernels for 3%

profile of v2, /device:TPU:0, one launch (start us, length us, event | category | flops | bytes accessed | tf_op | source)
XLA Modules:
  0.0 84.1 jit_solution(2622350021630587389)
XLA Ops:
  4.4 1.4 %shard_map.105 = (s32[72]{0:T(128)S(1)}, f32[16,8,256]{2,1,0:T(8,128)S(1)}, f32[16,8,256]{2,1,0:T(8,128)S(1)}, f32[16,256]{1,0:T(8,128)S(1)}, bf16[8,4096]{1,0:T(8,128)(2,1)S(1)}, /*index=5*/f32[24,8,256]{2,1,0:T(8,128)S(1)}) custom-call(s32[1,16]{1,0:T(1,128)S(1)} %copy-done.6, s32[1,16]{1,0:T(1,128)S(1)} %copy-done.7, f32[8,16,256]{2,1,0:T(8,128)S(1)} %copy-done.2, ...), custom_call_target="tpu_custom_call" | custom-call | flops 4000000 | bytes 250000 | tf_op jit(solution)/shard_map/pallas_call | solution.py:395
  7.9 2.9 %collective-permute-start.1 = (f32[12,8,256]{2,1,0:T(8,128)S(1)}, f32[12,8,256]{2,1,0:T(8,128)S(1)}, u32[]{:S(2)}, u32[]{:S(2)}) collective-permute-start(f32[12,8,256]{2,1,0:T(8,128)S(1)} %get-tuple-element.48), channel_id=1, source_target_pairs={{0,2},{1,3},{2,0},{3,1},{4,6},{5,7},{6,4},{7,5},{8,10},{9,11},{10,... | collective-permute-start | bytes 294920 | tf_op jit(solution)/shard_map/ppermute | solution.py:438
  10.8 1.5 %collective-permute-start.2 = (f32[12,8,256]{2,1,0:T(8,128)S(1)}, f32[12,8,256]{2,1,0:T(8,128)S(1)}, u32[]{:S(2)}, u32[]{:S(2)}) collective-permute-start(f32[12,8,256]{2,1,0:T(8,128)S(1)} %get-tuple-element.49), channel_id=1, source_target_pairs={{0,4},{1,5},{2,6},{3,7},{4,0},{5,1},{6,2},{7,3},{8,12},{9,13},{10,... | collective-permute-start | bytes 294920 | tf_op jit(solution)/shard_map/ppermute | solution.py:438
  12.4 1.6 %collective-permute-done.1.rest_1_.rest_0_ = f32[12,8,256]{2,1,0:T(8,128)S(1)} collective-permute-done((f32[12,8,256]{2,1,0:T(8,128)S(1)}, f32[12,8,256]{2,1,0:T(8,128)S(1)}, u32[]{:S(2)}, u32[]{:S(2)}) %collective-permute-start.1) | collective-permute-done | bytes 98336 | tf_op jit(solution)/shard_map/ppermute | solution.py:438
  14.0 2.6 %collective-permute-done.2.rest_2_.rest_1_ = f32[12,8,256]{2,1,0:T(8,128)S(1)} collective-permute-done((f32[12,8,256]{2,1,0:T(8,128)S(1)}, f32[12,8,256]{2,1,0:T(8,128)S(1)}, u32[]{:S(2)}, u32[]{:S(2)}) %collective-permute-start.2) | collective-permute-done | bytes 98336 | tf_op jit(solution)/shard_map/ppermute | solution.py:438
  16.6 1.3 %collective-permute-done.3.rest_3_.rest_2_ = f32[12,8,256]{2,1,0:T(8,128)S(1)} collective-permute-done((f32[12,8,256]{2,1,0:T(8,128)S(1)}, f32[12,8,256]{2,1,0:T(8,128)S(1)}, u32[]{:S(2)}, u32[]{:S(2)}) %collective-permute-start.3) | collective-permute-done | bytes 98336 | tf_op jit(solution)/shard_map/ppermute | solution.py:438
  17.9 1.6 %copy-done = bf16[16,256,256]{2,1,0:T(8,128)(2,1)S(1)} copy-done((bf16[16,256,256]{2,1,0:T(8,128)(2,1)S(1)}, bf16[16,256,256]{2,1,0:T(8,128)(2,1)}, u32[]{:S(2)}) %copy-start) | copy-done | bytes 2097176
  19.5 1.6 %copy-done.1 = bf16[16,256,256]{2,1,0:T(8,128)(2,1)S(1)} copy-done((bf16[16,256,256]{2,1,0:T(8,128)(2,1)S(1)}, bf16[16,256,256]{2,1,0:T(8,128)(2,1)}, u32[]{:S(2)}) %copy-start.1) | copy-done | bytes 2097176
  21.1 8.3 %shard_map.107 = (f32[16,8,256]{2,1,0:T(8,128)S(1)}, f32[16,8,256]{2,1,0:T(8,128)S(1)}, bf16[16,256,256]{2,1,0:T(8,128)(2,1)S(1)}, bf16[16,256,256]{2,1,0:T(8,12...) custom-call(s32[72]{0:T(128)S(1)} %get-tuple-element.44.table, ...), custom_call_target="tpu_custom_call" | custom-call | flops 600000000 | bytes 37500000 | tf_op jit(solution)/shard_map/pallas_call | solution.py:395
  29.4 1.3 %collective-permute-done.4.rest_2_.rest_0_ = f32[13,8,256]{2,1,0:T(8,128)S(1)} collective-permute-done((f32[13,8,256]{2,1,0:T(8,128)S(1)}, f32[13,8,256]{2,1,0:T(8,128)S(1)}, u32[]{:S(2)}, u32[]{:S(2)}) %collective-permute-start.4) | collective-permute-done | bytes 106528 | tf_op jit(solution)/shard_map/ppermute | solution.py:438
  33.0 1.8 %collective-permute-start.7 = (f32[7,8,256]{2,1,0:T(8,128)S(1)}, f32[7,8,256]{2,1,0:T(8,128)S(1)}, u32[]{:S(2)}, u32[]{:S(2)}) collective-permute-start(f32[7,8,256]{2,1,0:T(8,128)S(1)} %get-tuple-element.58), channel_id=1, source_target_pairs={{0,6},{1,7},{2,4},{3,5},{4,2},{5,3},{6,0},{7,1},{8,14},{9,15},{10,... | collective-permute-start | bytes 172040 | tf_op jit(solution)/shard_map/ppermute | solution.py:438
  37.0 1.1 %collective-permute-done.7.rest_3_ = f32[7,8,256]{2,1,0:T(8,128)S(1)} collective-permute-done((f32[7,8,256]{2,1,0:T(8,128)S(1)}, f32[7,8,256]{2,1,0:T(8,128)S(1)}, u32[]{:S(2)}, u32[]{:S(2)}) %collective-permute-start.7) | collective-permute-done | bytes 57376 | tf_op jit(solution)/shard_map/ppermute | solution.py:438
  38.1 2.7 %shard_map.110 = (f32[16,8,256]{2,1,0:T(8,128)S(1)}, f32[16,8,256]{2,1,0:T(8,128)S(1)}, f32[8,256]{1,0:T(8,128)S(1)}, f32[8,256]{1,0:T(8,128)S(1)}, f32[13,8,256]{2,1,0:T(8,128)S(1)}) custom-call(s32[72]{0:T(128)S(1)} %get-tuple-element.44.table, f32[13,8,256]{2,1,0:T(8,128)S(1)} %collective-permute-done.4.rest_2_.rest_0_, ...), custom_call_target="tpu_custom_call" | custom-call | flops 600000000 | bytes 37500000 | tf_op jit(solution)/shard_map/pallas_call | solution.py:395
  40.8 1.3 %collective-permute-done.8.rest_2_.rest_0_ = f32[13,8,256]{2,1,0:T(8,128)S(1)} collective-permute-done((f32[13,8,256]{2,1,0:T(8,128)S(1)}, f32[13,8,256]{2,1,0:T(8,128)S(1)}, u32[]{:S(2)}, u32[]{:S(2)}) %collective-permute-start.8) | collective-permute-done | bytes 106528 | tf_op jit(solution)/shard_map/ppermute | solution.py:438
  42.7 1.6 %collective-permute-start.9 = (f32[7,8,256]{2,1,0:T(8,128)S(1)}, f32[7,8,256]{2,1,0:T(8,128)S(1)}, u32[]{:S(2)}, u32[]{:S(2)}) collective-permute-start(f32[7,8,256]{2,1,0:T(8,128)S(1)} %get-tuple-element.64), channel_id=1, source_target_pairs={{0,2},{1,3},{2,0},{3,1},{4,6},{5,7},{6,4},{7,5},{8,10},{9,11},{10,... | collective-permute-start | bytes 172040 | tf_op jit(solution)/shard_map/ppermute | solution.py:438
  45.1 1.1 %collective-permute-start.11 = (f32[7,8,256]{2,1,0:T(8,128)S(1)}, f32[7,8,256]{2,1,0:T(8,128)S(1)}, u32[]{:S(2)}, u32[]{:S(2)}) collective-permute-start(f32[7,8,256]{2,1,0:T(8,128)S(1)} %get-tuple-element.66), channel_id=1, source_target_pairs={{0,6},{1,7},{2,4},{3,5},{4,2},{5,3},{6,0},{7,1},{8,14},{9,15},{10,... | collective-permute-start | bytes 172040 | tf_op jit(solution)/shard_map/ppermute | solution.py:438
  46.9 2.2 %collective-permute-done.10.rest_2_ = f32[7,8,256]{2,1,0:T(8,128)S(1)} collective-permute-done((f32[7,8,256]{2,1,0:T(8,128)S(1)}, f32[7,8,256]{2,1,0:T(8,128)S(1)}, u32[]{:S(2)}, u32[]{:S(2)}) %collective-permute-start.10) | collective-permute-done | bytes 57376 | tf_op jit(solution)/shard_map/ppermute | solution.py:438
  49.1 1.1 %collective-permute-done.11.rest_3_ = f32[7,8,256]{2,1,0:T(8,128)S(1)} collective-permute-done((f32[7,8,256]{2,1,0:T(8,128)S(1)}, f32[7,8,256]{2,1,0:T(8,128)S(1)}, u32[]{:S(2)}, u32[]{:S(2)}) %collective-permute-start.11) | collective-permute-done | bytes 57376 | tf_op jit(solution)/shard_map/ppermute | solution.py:438
  50.2 2.7 %shard_map.112 = (f32[16,8,256]{2,1,0:T(8,128)S(1)}, f32[16,8,256]{2,1,0:T(8,128)S(1)}, f32[8,256]{1,0:T(8,128)S(1)}, f32[8,256]{1,0:T(8,128)S(1)}, f32[13,8,256]{2,1,0:T(8,128)S(1)}) custom-call(s32[72]{0:T(128)S(1)} %get-tuple-element.44.table, f32[13,8,256]{2,1,0:T(8,128)S(1)} %collective-permute-done.8.rest_2_.rest_0_, ...), custom_call_target="tpu_custom_call" | custom-call | flops 600000000 | bytes 37500000 | tf_op jit(solution)/shard_map/pallas_call | solution.py:395
  52.9 1.3 %collective-permute-done.12.rest_2_.rest_0_ = f32[13,8,256]{2,1,0:T(8,128)S(1)} collective-permute-done((f32[13,8,256]{2,1,0:T(8,128)S(1)}, f32[13,8,256]{2,1,0:T(8,128)S(1)}, u32[]{:S(2)}, u32[]{:S(2)}) %collective-permute-start.12) | collective-permute-done | bytes 106528 | tf_op jit(solution)/shard_map/ppermute | solution.py:438
  56.5 1.8 %collective-permute-start.15 = (f32[7,8,256]{2,1,0:T(8,128)S(1)}, f32[7,8,256]{2,1,0:T(8,128)S(1)}, u32[]{:S(2)}, u32[]{:S(2)}) collective-permute-start(f32[7,8,256]{2,1,0:T(8,128)S(1)} %get-tuple-element.72), channel_id=1, source_target_pairs={{0,6},{1,7},{2,4},{3,5},{4,2},{5,3},{6,0},{7,1},{8,14},{9,15},{10,... | collective-permute-start | bytes 172040 | tf_op jit(solution)/shard_map/ppermute | solution.py:438
  59.0 1.5 %collective-permute-done.14.rest_2_ = f32[7,8,256]{2,1,0:T(8,128)S(1)} collective-permute-done((f32[7,8,256]{2,1,0:T(8,128)S(1)}, f32[7,8,256]{2,1,0:T(8,128)S(1)}, u32[]{:S(2)}, u32[]{:S(2)}) %collective-permute-start.14) | collective-permute-done | bytes 57376 | tf_op jit(solution)/shard_map/ppermute | solution.py:438
  60.5 1.1 %collective-permute-done.15.rest_3_ = f32[7,8,256]{2,1,0:T(8,128)S(1)} collective-permute-done((f32[7,8,256]{2,1,0:T(8,128)S(1)}, f32[7,8,256]{2,1,0:T(8,128)S(1)}, u32[]{:S(2)}, u32[]{:S(2)}) %collective-permute-start.15) | collective-permute-done | bytes 57376 | tf_op jit(solution)/shard_map/ppermute | solution.py:438
  61.6 2.7 %shard_map.114 = (f32[16,8,256]{2,1,0:T(8,128)S(1)}, f32[16,8,256]{2,1,0:T(8,128)S(1)}, f32[8,256]{1,0:T(8,128)S(1)}, f32[8,256]{1,0:T(8,128)S(1)}, f32[13,8,256]{2,1,0:T(8,128)S(1)}) custom-call(s32[72]{0:T(128)S(1)} %get-tuple-element.44.table, f32[13,8,256]{2,1,0:T(8,128)S(1)} %collective-permute-done.12.rest_2_.rest_0_, ...), custom_call_target="tpu_custom_call" | custom-call | flops 600000000 | bytes 37500000 | tf_op jit(solution)/shard_map/pallas_call | solution.py:395
  64.4 1.3 %collective-permute-done.16.rest_2_.near = f32[13,8,256]{2,1,0:T(8,128)S(1)} collective-permute-done((f32[13,8,256]{2,1,0:T(8,128)S(1)}, f32[13,8,256]{2,1,0:T(8,128)S(1)}, u32[]{:S(2)}, u32[]{:S(2)}) %collective-permute-start.16) | collective-permute-done | bytes 106528 | tf_op jit(solution)/shard_map/ppermute | solution.py:438
  66.2 1.6 %collective-permute-start.17 = (f32[7,8,256]{2,1,0:T(8,128)S(1)}, f32[7,8,256]{2,1,0:T(8,128)S(1)}, u32[]{:S(2)}, u32[]{:S(2)}) collective-permute-start(f32[7,8,256]{2,1,0:T(8,128)S(1)} %get-tuple-element.79), channel_id=1, source_target_pairs={{0,2},{1,3},{2,0},{3,1},{4,6},{5,7},{6,4},{7,5},{8,10},{9,11},{10,... | collective-permute-start | bytes 172040 | tf_op jit(solution)/shard_map/ppermute | solution.py:438
  68.7 1.1 %collective-permute-start.19 = (f32[7,8,256]{2,1,0:T(8,128)S(1)}, f32[7,8,256]{2,1,0:T(8,128)S(1)}, u32[]{:S(2)}, u32[]{:S(2)}) collective-permute-start(f32[7,8,256]{2,1,0:T(8,128)S(1)} %get-tuple-element.81), channel_id=1, source_target_pairs={{0,6},{1,7},{2,4},{3,5},{4,2},{5,3},{6,0},{7,1},{8,14},{9,15},{10,... | collective-permute-start | bytes 172040 | tf_op jit(solution)/shard_map/ppermute | solution.py:438
  70.5 2.2 %collective-permute-done.18.rest_1_ = f32[7,8,256]{2,1,0:T(8,128)S(1)} collective-permute-done((f32[7,8,256]{2,1,0:T(8,128)S(1)}, f32[7,8,256]{2,1,0:T(8,128)S(1)}, u32[]{:S(2)}, u32[]{:S(2)}) %collective-permute-start.18) | collective-permute-done | bytes 57376 | tf_op jit(solution)/shard_map/ppermute | solution.py:438
  72.6 1.1 %collective-permute-done.19.rest_2_ = f32[7,8,256]{2,1,0:T(8,128)S(1)} collective-permute-done((f32[7,8,256]{2,1,0:T(8,128)S(1)}, f32[7,8,256]{2,1,0:T(8,128)S(1)}, u32[]{:S(2)}, u32[]{:S(2)}) %collective-permute-start.19) | collective-permute-done | bytes 57376 | tf_op jit(solution)/shard_map/ppermute | solution.py:438
  74.0 3.6 %collective-permute-start.22 = (f32[8,128]{1,0:T(8,128)S(1)}, f32[8,128]{1,0:T(8,128)S(1)}, u32[]{:S(2)}, u32[]{:S(2)}) collective-permute-start(f32[8,128]{1,0:T(8,128)S(1)} %shard_map.116.rest_0_), channel_id=1, source_target_pairs={{0,24},{8,16},{16,8},{24,0},{1,25},{9,17},{17,9},{25,1},{2,26},{10... | collective-permute-start | bytes 12296 | tf_op jit(solution)/shard_map/ppermute | solution.py:505
  79.5 2.7 %collective-permute-done.21.rest_2_ = f32[8,128]{1,0:T(8,128)S(1)} collective-permute-done((f32[8,128]{1,0:T(8,128)S(1)}, f32[8,128]{1,0:T(8,128)S(1)}, u32[]{:S(2)}, u32[]{:S(2)}) %collective-permute-start.21) | collective-permute-done | bytes 4128 | tf_op jit(solution)/shard_map/ppermute | solution.py:505
  82.2 1.9 %shard_map.118 = (f32[8,16,256]{2,1,0:T(8,128)}, f32[8,16,256]{2,1,0:T(8,128)}) custom-call(f32[8,128]{1,0:T(8,128)S(1)} %shard_map.116.rest_0_, f32[8,128]{1,0:T(8,128)S(1)} %collective-permute-done.20.rest_1_, f32[8,128]{1,0:T(8,128)S(1)} %collective-permute-done.21.rest_2_, f32[8,128]{1,0:T(8,128)S(1)} %collective-permute-done.22.rest_3_, ...), custom_call_target="tpu_custom_call" | custom-call | flops 4000000 | bytes 250000 | tf_op jit(solution)/shard_map/pallas_call | solution.py:395
  (47 shorter events, 19.8 us)
Async XLA Ops:
  0.6 0.9 %copy-start.2 = (f32[8,16,256]{2,1,0:T(8,128)S(1)}, f32[8,16,256]{2,1,0:T(8,128)}, u32[]{:S(2)}) copy-start(f32[8,16,256]{2,1,0:T(8,128)} %load.1) | copy-start | bytes 393220
  1.5 0.8 copy-start.3
  2.4 0.7 copy-start.5
  3.1 0.7 copy-start.6
  3.8 0.7 copy-start.7
  5.8 1.6 %collective-permute-start = (f32[24,8,256]{2,1,0:T(8,128)S(1)}, f32[24,8,256]{2,1,0:T(8,128)S(1)}, u32[]{:S(2)}, u32[]{:S(2)}) collective-permute-start(f32[24,8,256]{2,1,0:T(8,128)S(1)} %get-tuple-element.45), channel_id=1, source_target_pairs={{0,1},{1,0},{2,3},{3,2},{4,5},{5,4},{6,7},{7,6},{8,9},{9,8},{10,11... | collective-permute-start | bytes 589832 | tf_op jit(solution)/shard_map/ppermute | solution.py:438
  7.9 6.1 %collective-permute-start.1 = (f32[12,8,256]{2,1,0:T(8,128)S(1)}, f32[12,8,256]{2,1,0:T(8,128)S(1)}, u32[]{:S(2)}, u32[]{:S(2)}) collective-permute-start(f32[12,8,256]{2,1,0:T(8,128)S(1)} %get-tuple-element.48), channel_id=1, source_target_pairs={{0,2},{1,3},{2,0},{3,1},{4,6},{5,7},{6,4},{7,5},{8,10},{9,11},{10,... | collective-permute-start | bytes 294920 | tf_op jit(solution)/shard_map/ppermute | solution.py:438
  10.8 5.8 %collective-permute-start.2 = (f32[12,8,256]{2,1,0:T(8,128)S(1)}, f32[12,8,256]{2,1,0:T(8,128)S(1)}, u32[]{:S(2)}, u32[]{:S(2)}) collective-permute-start(f32[12,8,256]{2,1,0:T(8,128)S(1)} %get-tuple-element.49), channel_id=1, source_target_pairs={{0,4},{1,5},{2,6},{3,7},{4,0},{5,1},{6,2},{7,3},{8,12},{9,13},{10,... | collective-permute-start | bytes 294920 | tf_op jit(solution)/shard_map/ppermute | solution.py:438
  12.4 5.5 %collective-permute-start.3 = (f32[12,8,256]{2,1,0:T(8,128)S(1)}, f32[12,8,256]{2,1,0:T(8,128)S(1)}, u32[]{:S(2)}, u32[]{:S(2)}) collective-permute-start(f32[12,8,256]{2,1,0:T(8,128)S(1)} %get-tuple-element.50), channel_id=1, source_target_pairs={{0,6},{1,7},{2,4},{3,5},{4,2},{5,3},{6,0},{7,1},{8,14},{9,15},{10,... | collective-permute-start | bytes 294920 | tf_op jit(solution)/shard_map/ppermute | solution.py:438
  17.9 1.6 %copy-start = (bf16[16,256,256]{2,1,0:T(8,128)(2,1)S(1)}, bf16[16,256,256]{2,1,0:T(8,128)(2,1)}, u32[]{:S(2)}) copy-start(bf16[16,256,256]{2,1,0:T(8,128)(2,1)} %rest_6_.1) | copy-start | bytes 6291460
  19.5 1.6 %copy-start.1 = (bf16[16,256,256]{2,1,0:T(8,128)(2,1)S(1)}, bf16[16,256,256]{2,1,0:T(8,128)(2,1)}, u32[]{:S(2)}) copy-start(bf16[16,256,256]{2,1,0:T(8,128)(2,1)} %rest_7_.1) | copy-start | bytes 6291460
  21.1 13.8 %copy-start.4 = (f32[32,32]{1,0:T(8,128)S(1)}, f32[32,32]{1,0:T(8,128)}, u32[]{:S(2)}) copy-start(f32[32,32]{1,0:T(8,128)} %inverse.1) | copy-start | bytes 12292
  21.1 13.8 %copy-start.8 = (s32[1,64]{1,0:T(1,128)S(1)}, s32[1,64]{1,0:T(1,128)}, u32[]{:S(2)}) copy-start(s32[1,64]{1,0:T(1,128)} %index.1) | copy-start | bytes 772
  29.3 1.4 %collective-permute-start.4 = (f32[13,8,256]{2,1,0:T(8,128)S(1)}, f32[13,8,256]{2,1,0:T(8,128)S(1)}, u32[]{:S(2)}, u32[]{:S(2)}) collective-permute-start(f32[13,8,256]{2,1,0:T(8,128)S(1)} %get-tuple-element.53), channel_id=1, source_target_pairs={{0,1},{1,0},{2,3},{3,2},{4,5},{5,4},{6,7},{7,6},{8,9},{9,8},{10,11... | collective-permute-start | bytes 319496 | tf_op jit(solution)/shard_map/ppermute | solution.py:438
  31.3 4.9 %collective-permute-start.5 = (f32[7,8,256]{2,1,0:T(8,128)S(1)}, f32[7,8,256]{2,1,0:T(8,128)S(1)}, u32[]{:S(2)}, u32[]{:S(2)}) collective-permute-start(f32[7,8,256]{2,1,0:T(8,128)S(1)} %get-tuple-element.56), channel_id=1, source_target_pairs={{0,2},{1,3},{2,0},{3,1},{4,6},{5,7},{6,4},{7,5},{8,10},{9,11},{10,... | collective-permute-start | bytes 172040 | tf_op jit(solution)/shard_map/ppermute | solution.py:438
  32.2 4.8 %collective-permute-start.6 = (f32[7,8,256]{2,1,0:T(8,128)S(1)}, f32[7,8,256]{2,1,0:T(8,128)S(1)}, u32[]{:S(2)}, u32[]{:S(2)}) collective-permute-start(f32[7,8,256]{2,1,0:T(8,128)S(1)} %get-tuple-element.57), channel_id=1, source_target_pairs={{0,4},{1,5},{2,6},{3,7},{4,0},{5,1},{6,2},{7,3},{8,12},{9,13},{10,... | collective-permute-start | bytes 172040 | tf_op jit(solution)/shard_map/ppermute | solution.py:438
  33.0 5.1 %collective-permute-start.7 = (f32[7,8,256]{2,1,0:T(8,128)S(1)}, f32[7,8,256]{2,1,0:T(8,128)S(1)}, u32[]{:S(2)}, u32[]{:S(2)}) collective-permute-start(f32[7,8,256]{2,1,0:T(8,128)S(1)} %get-tuple-element.58), channel_id=1, source_target_pairs={{0,6},{1,7},{2,4},{3,5},{4,2},{5,3},{6,0},{7,1},{8,14},{9,15},{10,... | collective-permute-start | bytes 172040 | tf_op jit(solution)/shard_map/ppermute | solution.py:438
  40.8 1.3 %collective-permute-start.8 = (f32[13,8,256]{2,1,0:T(8,128)S(1)}, f32[13,8,256]{2,1,0:T(8,128)S(1)}, u32[]{:S(2)}, u32[]{:S(2)}) collective-permute-start(f32[13,8,256]{2,1,0:T(8,128)S(1)} %get-tuple-element.61), channel_id=1, source_target_pairs={{0,1},{1,0},{2,3},{3,2},{4,5},{5,4},{6,7},{7,6},{8,9},{9,8},{10,11... | collective-permute-start | bytes 319496 | tf_op jit(solution)/shard_map/ppermute | solution.py:438
  42.7 4.2 %collective-permute-start.9 = (f32[7,8,256]{2,1,0:T(8,128)S(1)}, f32[7,8,256]{2,1,0:T(8,128)S(1)}, u32[]{:S(2)}, u32[]{:S(2)}) collective-permute-start(f32[7,8,256]{2,1,0:T(8,128)S(1)} %get-tuple-element.64), channel_id=1, source_target_pairs={{0,2},{1,3},{2,0},{3,1},{4,6},{5,7},{6,4},{7,5},{8,10},{9,11},{10,... | collective-permute-start | bytes 172040 | tf_op jit(solution)/shard_map/ppermute | solution.py:438
  44.3 4.8 %collective-permute-start.10 = (f32[7,8,256]{2,1,0:T(8,128)S(1)}, f32[7,8,256]{2,1,0:T(8,128)S(1)}, u32[]{:S(2)}, u32[]{:S(2)}) collective-permute-start(f32[7,8,256]{2,1,0:T(8,128)S(1)} %get-tuple-element.65), channel_id=1, source_target_pairs={{0,4},{1,5},{2,6},{3,7},{4,0},{5,1},{6,2},{7,3},{8,12},{9,13},{10,... | collective-permute-start | bytes 172040 | tf_op jit(solution)/shard_map/ppermute | solution.py:438
  45.1 5.1 %collective-permute-start.11 = (f32[7,8,256]{2,1,0:T(8,128)S(1)}, f32[7,8,256]{2,1,0:T(8,128)S(1)}, u32[]{:S(2)}, u32[]{:S(2)}) collective-permute-start(f32[7,8,256]{2,1,0:T(8,128)S(1)} %get-tuple-element.66), channel_id=1, source_target_pairs={{0,6},{1,7},{2,4},{3,5},{4,2},{5,3},{6,0},{7,1},{8,14},{9,15},{10,... | collective-permute-start | bytes 172040 | tf_op jit(solution)/shard_map/ppermute | solution.py:438
  52.9 1.3 %collective-permute-start.12 = (f32[13,8,256]{2,1,0:T(8,128)S(1)}, f32[13,8,256]{2,1,0:T(8,128)S(1)}, u32[]{:S(2)}, u32[]{:S(2)}) collective-permute-start(f32[13,8,256]{2,1,0:T(8,128)S(1)} %get-tuple-element.67), channel_id=1, source_target_pairs={{0,1},{1,0},{2,3},{3,2},{4,5},{5,4},{6,7},{7,6},{8,9},{9,8},{10,11... | collective-permute-start | bytes 319496 | tf_op jit(solution)/shard_map/ppermute | solution.py:438
  54.7 4.2 %collective-permute-start.13 = (f32[7,8,256]{2,1,0:T(8,128)S(1)}, f32[7,8,256]{2,1,0:T(8,128)S(1)}, u32[]{:S(2)}, u32[]{:S(2)}) collective-permute-start(f32[7,8,256]{2,1,0:T(8,128)S(1)} %get-tuple-element.70), channel_id=1, source_target_pairs={{0,2},{1,3},{2,0},{3,1},{4,6},{5,7},{6,4},{7,5},{8,10},{9,11},{10,... | collective-permute-start | bytes 172040 | tf_op jit(solution)/shard_map/ppermute | solution.py:438
  55.7 4.8 %collective-permute-start.14 = (f32[7,8,256]{2,1,0:T(8,128)S(1)}, f32[7,8,256]{2,1,0:T(8,128)S(1)}, u32[]{:S(2)}, u32[]{:S(2)}) collective-permute-start(f32[7,8,256]{2,1,0:T(8,128)S(1)} %get-tuple-element.71), channel_id=1, source_target_pairs={{0,4},{1,5},{2,6},{3,7},{4,0},{5,1},{6,2},{7,3},{8,12},{9,13},{10,... | collective-permute-start | bytes 172040 | tf_op jit(solution)/shard_map/ppermute | solution.py:438
  56.5 5.1 %collective-permute-start.15 = (f32[7,8,256]{2,1,0:T(8,128)S(1)}, f32[7,8,256]{2,1,0:T(8,128)S(1)}, u32[]{:S(2)}, u32[]{:S(2)}) collective-permute-start(f32[7,8,256]{2,1,0:T(8,128)S(1)} %get-tuple-element.72), channel_id=1, source_target_pairs={{0,6},{1,7},{2,4},{3,5},{4,2},{5,3},{6,0},{7,1},{8,14},{9,15},{10,... | collective-permute-start | bytes 172040 | tf_op jit(solution)/shard_map/ppermute | solution.py:438
  64.3 1.4 %collective-permute-start.16 = (f32[13,8,256]{2,1,0:T(8,128)S(1)}, f32[13,8,256]{2,1,0:T(8,128)S(1)}, u32[]{:S(2)}, u32[]{:S(2)}) collective-permute-start(f32[13,8,256]{2,1,0:T(8,128)S(1)} %get-tuple-element.77), channel_id=1, source_target_pairs={{0,1},{1,0},{2,3},{3,2},{4,5},{5,4},{6,7},{7,6},{8,9},{9,8},{10,11... | collective-permute-start | bytes 319496 | tf_op jit(solution)/shard_map/ppermute | solution.py:438
  66.2 4.2 %collective-permute-start.17 = (f32[7,8,256]{2,1,0:T(8,128)S(1)}, f32[7,8,256]{2,1,0:T(8,128)S(1)}, u32[]{:S(2)}, u32[]{:S(2)}) collective-permute-start(f32[7,8,256]{2,1,0:T(8,128)S(1)} %get-tuple-element.79), channel_id=1, source_target_pairs={{0,2},{1,3},{2,0},{3,1},{4,6},{5,7},{6,4},{7,5},{8,10},{9,11},{10,... | collective-permute-start | bytes 172040 | tf_op jit(solution)/shard_map/ppermute | solution.py:438
  67.8 4.8 %collective-permute-start.18 = (f32[7,8,256]{2,1,0:T(8,128)S(1)}, f32[7,8,256]{2,1,0:T(8,128)S(1)}, u32[]{:S(2)}, u32[]{:S(2)}) collective-permute-start(f32[7,8,256]{2,1,0:T(8,128)S(1)} %get-tuple-element.80), channel_id=1, source_target_pairs={{0,4},{1,5},{2,6},{3,7},{4,0},{5,1},{6,2},{7,3},{8,12},{9,13},{10,... | collective-permute-start | bytes 172040 | tf_op jit(solution)/shard_map/ppermute | solution.py:438
  68.7 5.1 %collective-permute-start.19 = (f32[7,8,256]{2,1,0:T(8,128)S(1)}, f32[7,8,256]{2,1,0:T(8,128)S(1)}, u32[]{:S(2)}, u32[]{:S(2)}) collective-permute-start(f32[7,8,256]{2,1,0:T(8,128)S(1)} %get-tuple-element.81), channel_id=1, source_target_pairs={{0,6},{1,7},{2,4},{3,5},{4,2},{5,3},{6,0},{7,1},{8,14},{9,15},{10,... | collective-permute-start | bytes 172040 | tf_op jit(solution)/shard_map/ppermute | solution.py:438
  74.0 5.5 %collective-permute-start.22 = (f32[8,128]{1,0:T(8,128)S(1)}, f32[8,128]{1,0:T(8,128)S(1)}, u32[]{:S(2)}, u32[]{:S(2)}) collective-permute-start(f32[8,128]{1,0:T(8,128)S(1)} %shard_map.116.rest_0_), channel_id=1, source_target_pairs={{0,24},{8,16},{16,8},{24,0},{1,25},{9,17},{17,9},{25,1},{2,26},{10... | collective-permute-start | bytes 12296 | tf_op jit(solution)/shard_map/ppermute | solution.py:505
  77.7 4.5 %collective-permute-start.21 = (f32[8,128]{1,0:T(8,128)S(1)}, f32[8,128]{1,0:T(8,128)S(1)}, u32[]{:S(2)}, u32[]{:S(2)}) collective-permute-start(f32[8,128]{1,0:T(8,128)S(1)} %shard_map.116.rest_0_), channel_id=1, source_target_pairs={{0,16},{8,24},{16,0},{24,8},{1,17},{9,25},{17,1},{25,9},{2,18},{10... | collective-permute-start | bytes 12296 | tf_op jit(solution)/shard_map/ppermute | solution.py:505
  77.7 4.5 %collective-permute-start.20 = (f32[8,128]{1,0:T(8,128)S(1)}, f32[8,128]{1,0:T(8,128)S(1)}, u32[]{:S(2)}, u32[]{:S(2)}) collective-permute-start(f32[8,128]{1,0:T(8,128)S(1)} %shard_map.116.rest_0_), channel_id=1, source_target_pairs={{0,8},{8,0},{16,24},{24,16},{1,9},{9,1},{17,25},{25,17},{2,10},{10... | collective-permute-start | bytes 12296 | tf_op jit(solution)/shard_map/ppermute | solution.py:505

commit v3 on v2

--- a/solution.py
+++ b/solution.py
@@ -15,6 +15,7 @@
 SMEM = pl.BlockSpec(memory_space=pltpu.SMEM)
 HBM = pl.BlockSpec(memory_space=pltpu.HBM)
 LIMIT = 24 * 1024 * 1024
+LANES = 128
 PAIRS = [(i, j) for j in range(ITERS) for i in range(j + 1)]
 ENTRIES = len(PAIRS) + ITERS
 NN = (((1,), (0,)), ((), ()))
@@ -58,21 +59,18 @@
         self.all_corners = self.peers * self.corners
         self.max_lane = self.all_corners
         self.gram_lane = self.max_lane + self.peers
-        self.extra_chunks = -(-(self.gram_lane + ENTRIES) // self.width)
-        self.extra = self.extra_chunks * self.width
-        self.far = range(2, self.peers, 2)
-        self.odd = range(1, self.peers, 2)
+        self.extra_chunks = -(-(self.gram_lane + ENTRIES) // LANES)
+        self.extra = self.extra_chunks * LANES
+        self.halves = self.width // LANES
+        self.masks = range(self.peers - 1, 0, -1)
         self.slots = self.peers * self.capacity
         self.inverse = self.slots
         self.pattern = self.inverse + self.blocks
         self.partner = self.pattern + self.blocks
         self.table = self.partner + self.blocks
 
-    def near_rows(self, kinds):
-        return len(self.odd) * kinds * self.capacity
-
-    def far_rows(self, kinds):
-        return 2 * kinds * self.capacity
+    def rows(self, kinds):
+        return kinds * self.capacity * self.halves
 
 
 def fill_table(z, partner, pattern, table, counts):
@@ -93,31 +91,30 @@
         table[z.partner + i] = mate
 
 
-def block_of(z, table, m, r):
-    return jnp.minimum(table[m * z.capacity + r], z.blocks - 1)
-
-
-def fill_near(z, table, sources, near):
-    row = 0
-    for m in z.odd:
+def fill_pieces(z, table, sources, pieces):
+    for m, piece in zip(z.masks, pieces):
+        row = 0
         for source in sources:
             for r in range(z.capacity):
-                near[row] = source[block_of(z, table, m, r)]
+                block = jnp.minimum(table[m * z.capacity + r], z.blocks - 1)
+                value = source[block]
+                for h in range(z.halves):
+                    piece[row] = value[:, h * LANES : (h + 1) * LANES]
+                    row += 1
+
+
+def place(z, table, pieces, kind, target):
+    for m, piece in zip(z.masks, pieces):
+        row = z.rows(kind)
+        for r in range(z.capacity):
+            block = table[m * z.capacity + r]
+            for h in range(z.halves):
+                target[block, :, h * LANES : (h + 1) * LANES] = piece[row]
                 row += 1
 
 
-def place(z, table, near, fars, kind, kinds, target):
-    for r in range(z.capacity):
-        target[table[z.capacity + r]] = near[kind * z.capacity + r]
-    for m, far in zip(z.far, fars):
-        for r in range(z.capacity):
-            row = 2 * kind * z.capacity + r
-            target[table[m * z.capacity + r]] = far[row]
-            target[table[(m + 1) * z.capacity + r]] = far[row + z.capacity]
-
-
-def begin(z, partner, pattern, load, scale, coupling, table, field, lift, scale_out, coupling_out, near, *scratch):
-    here, partner_here, pattern_here, counts, sems = scratch
+def begin(z, partner, pattern, load, scale, coupling, table, field, lift, scale_out, coupling_out, *rest):
+    pieces, (here, partner_here, pattern_here, counts, sems) = rest[:-5], rest[-5:]
     copies = [
         pltpu.make_async_copy(a, b, sems.at[k])
         for k, (a, b) in enumerate(
@@ -141,26 +138,7 @@
         field[i] = here[:, i, :]
         part = coupling_out[:, i * z.width : (i + 1) * z.width].astype(F32)
         lift[i] = scale_out[i : i + 1, :] * part
-    fill_near(z, table, [field, lift], near)
-
-
-def relay(z, kinds, table, *rest):
-    sources, rest = rest[:kinds], rest[kinds:]
-    extras = z.extra_chunks if kinds == 1 else 0
-    if extras:
-        own_extra, rest = rest[0], rest[1:]
-    near, fars = rest[0], rest[1:]
-    for m, far in zip(z.far, fars):
-        for kind, source in enumerate(sources):
-            row = 2 * kind * z.capacity
-            base = (m // 2 * kinds + kind) * z.capacity
-            for r in range(z.capacity):
-                far[row + r] = source[block_of(z, table, m, r)]
-                far[row + z.capacity + r] = near[base + r]
-    for j in range(extras):
-        chunk = own_extra[:, j * z.width : (j + 1) * z.width] + near[z.near_rows(1) + j]
-        for far in fars:
-            far[z.far_rows(1) + j] = chunk
+    fill_pieces(z, table, [field, lift], pieces)
 
 
 def split3(a):
@@ -180,9 +158,9 @@
     operator[...] = sum(full[:, k * z.all_corners : (k + 1) * z.all_corners] for k in range(3))
 
 
-def build_lift(z, table, operator, lift, near, *rest):
-    fars, (jump_lift, other) = rest[:-2], rest[-2:]
-    place(z, table, near, fars, 1, 2, other)
+def build_lift(z, table, operator, lift, *rest):
+    pieces, (jump_lift, other) = rest[:-2], rest[-2:]
+    place(z, table, pieces, 1, other)
     me = lax.axis_index("sub")
     own = operator[pl.ds(pl.multiple_of(me * z.corners, z.corners), z.corners), :]
     for i in range(z.blocks):
@@ -195,13 +173,12 @@
         jump_lift[i] = split(dot(left, right, TN))
 
 
-def extra_sum(z, own, near, fars):
-    def read(ref, row):
-        return jnp.concatenate([ref[row + j] for j in range(z.extra_chunks)], axis=1)
-
-    total = own[...] + read(near, z.near_rows(1))
-    for far in fars:
-        total = total + read(far, z.far_rows(1))
+def extra_sum(z, own, pieces):
+    total = own[...]
+    for piece in pieces:
+        total = total + jnp.concatenate(
+            [piece[z.rows(1) + j] for j in range(z.extra_chunks)], axis=1
+        )
     return total
 
 
@@ -221,22 +198,25 @@
 
 
 def apply_round(z, step, table, *rest):
-    count = len(z.far)
+    count = len(z.masks)
     first, last = step == 1, step == ITERS
     rest = list(rest)
     take = lambda n: [rest.pop(0) for _ in range(n)]
-    near, *fars = take(1 + count)
+    arrived = take(count)
     (before,) = take(1)
     if not first:
         own_extra, jump_lift = take(2)
     scale, diag, off, coupling = take(4)
     older = take(ITERS - 1) if last else []
+    if first:
+        take(1)
     field, image = take(2)
     if first:
         sources, (diag, off) = (diag, off), take(2)
     else:
         (total_out,) = take(1)
-    extra, near_out = take(2)
+    (extra,) = take(1)
+    pieces = take(count)
     other, parts = take(2)
     if first:
         (sems,) = rest
@@ -250,9 +230,9 @@
         for pair in copies:
             for copy in pair:
                 copy.start()
-    place(z, table, near, fars, 0, 2 if first else 1, other)
+    place(z, table, arrived, 0, other)
     if not first:
-        total = extra_sum(z, own_extra, near, fars)
+        total = extra_sum(z, own_extra, arrived)
         total_out[...] = total
         rows = corner_rows(z, total)
         shrink = 1.0 / cluster_max(z, total)
@@ -279,7 +259,7 @@
         result = row * (row * field[i] + fold(coupled))
         image[i] = result
         top = jnp.maximum(top, jnp.abs(result))
-    fill_near(z, table, [image], near_out)
+    fill_pieces(z, table, [image], pieces)
     me = lax.axis_index("sub")
     lanes = lane_ids((z.columns, z.extra))
     sums = fold(partial)
@@ -297,14 +277,15 @@
                 acc = acc + a[i] * b[i]
             tile = jnp.where(lanes == z.gram_lane + entry, lane_sum(acc), tile)
     extra[...] = tile
-    for j in range(z.extra_chunks):
-        near_out[z.near_rows(1) + j] = tile[:, j * z.width : (j + 1) * z.width]
-
-
-def cluster_gram(z, operator, own_extra, near, *rest):
-    count = len(z.far)
-    fars, totals, (gram,) = rest[:count], rest[count:-1], rest[-1:]
-    total = extra_sum(z, own_extra, near, fars)
+    for piece in pieces:
+        for j in range(z.extra_chunks):
+            piece[z.rows(1) + j] = tile[:, j * LANES : (j + 1) * LANES]
+
+
+def cluster_gram(z, operator, own_extra, *rest):
+    count = len(z.masks)
+    arrived, totals, (gram,) = rest[:count], rest[count:-1], rest[-1:]
+    total = extra_sum(z, own_extra, arrived)
     totals = [t[...] for t in totals]
     partials = [t[:, : z.all_corners] for t in totals + [total]]
     lifted = dot_high(partials[-1], operator[...], NT)
@@ -321,10 +302,10 @@
     gram[...] = tile
 
 
-def last_vector(z, table, before, own_extra, jump_lift, near, *rest):
-    fars, (field, other) = rest[:-2], rest[-2:]
-    place(z, table, near, fars, 0, 1, other)
-    rows = corner_rows(z, extra_sum(z, own_extra, near, fars))
+def last_vector(z, table, before, own_extra, jump_lift, *rest):
+    arrived, (field, other) = rest[:-2], rest[-2:]
+    place(z, table, arrived, 0, other)
+    rows = corner_rows(z, extra_sum(z, own_extra, arrived))
     for i in range(z.blocks):
         field[i] = before[i] - other[i] + fold(dot(rows, jump_lift[i], NN))
 
@@ -385,18 +366,22 @@
         residual[:, i, :] = sum(c * values[j] for j, c in rest_of.items())
 
 
-def call(body, outs, scratch, cost, args, table=True, away=(), table_out=False):
+def call(body, outs, scratch, cost, args, table=True, away=()):
+    args = [
+        pltpu.with_memory_space_constraint(a, pltpu.HBM) if k in away else a
+        for k, a in enumerate(args)
+    ]
     specs = [HBM if k in away else VMEM for k in range(len(args))]
     if table:
         specs[0] = SMEM
-    out_specs = [VMEM] * len(outs)
-    if table_out:
-        out_specs[0] = SMEM
+    shapes = [
+        pltpu.SMEM(s, t) if t == jnp.int32 else jax.ShapeDtypeStruct(s, t) for s, t in outs
+    ]
     return pl.pallas_call(
         body,
-        out_shape=[jax.ShapeDtypeStruct(s, t) for s, t in outs],
+        out_shape=shapes,
         in_specs=specs,
-        out_specs=out_specs,
+        out_specs=[SMEM if t == jnp.int32 else VMEM for _, t in outs],
         scratch_shapes=scratch,
         compiler_params=pltpu.CompilerParams(vmem_limit_bytes=LIMIT),
         cost_estimate=pl.CostEstimate(flops=cost, bytes_accessed=cost // 16, transcendentals=0),
@@ -425,29 +410,20 @@
     gram = ((cols, 128), F32)
     light, heavy = 4_000_000, 600_000_000
 
-    def near_shape(kinds):
-        return ((z.near_rows(kinds) + (z.extra_chunks if kinds == 1 else 0), cols, width), F32)
-
-    def far_shape(kinds):
-        return ((z.far_rows(kinds) + (z.extra_chunks if kinds == 1 else 0), cols, width), F32)
+    def piece_shapes(kinds):
+        rows = z.rows(kinds) + (z.extra_chunks if kinds == 1 else 0)
+        return [((rows, cols, LANES), F32)] * len(z.masks)
 
     def kernel(body, *extra_args):
         return functools.partial(body, z, *extra_args)
 
-    def across(piece, m):
-        return lax.ppermute(piece, "sub", [(t, t ^ m) for t in range(z.peers)])
-
-    def exchange(near, sources):
-        kinds = 1 if len(sources) == 1 else 2
-        near = across(near, 1)
-        own = [own_extra] if kinds == 1 else []
-        pieces = call(
-            kernel(relay, kinds), [far_shape(kinds)] * len(z.far), [], light,
-            [table, *sources, *own, near],
-        )
-        return [near] + [across(piece, m) for m, piece in zip(z.far, pieces)]
-
-    table, loaded, lift, scale, coupling, near = call(
+    def exchange(pieces):
+        return [
+            lax.ppermute(piece, "sub", [(t, t ^ m) for t in range(z.peers)])
+            for m, piece in zip(z.masks, pieces)
+        ]
+
+    table, loaded, lift, scale, coupling, *pieces = call(
         kernel(begin),
         [
             ((z.table,), jnp.int32),
@@ -455,8 +431,8 @@
             field,
             (row_scale.shape, F32),
             (corner_coupling.shape, BF16),
-            near_shape(2),
-        ],
+        ]
+        + piece_shapes(2),
         [
             pltpu.VMEM(load.shape, F32),
             pltpu.SMEM(partner.shape, jnp.int32),
@@ -466,37 +442,37 @@
         ],
         light,
         [partner, off_pattern, load, row_scale, corner_coupling],
-        False, range(5), True,
-    )
-    arrived = exchange(near, [loaded, lift])
+        False, range(5),
+    )
+    arrived = exchange(pieces)
     (operator,) = call(
         kernel(build_operator), [((z.all_corners, z.all_corners), F32)], [], light,
         [corner_index, coarse_inverse], False,
     )
     weight = (diag_blocks.shape, BF16)
-    newest, image, diag, off, own_extra, near = call(
+    newest, image, diag, off, own_extra, *pieces = call(
         kernel(apply_round, 1),
-        [field, field, weight, weight, extra, near_shape(1)],
+        [field, field, weight, weight, extra] + piece_shapes(1),
         [other, parts, pltpu.SemaphoreType.DMA((2, blocks))], heavy,
-        [table, *arrived, loaded, scale, diag_blocks, off_blocks, coupling],
+        [table, *arrived, loaded, scale, diag_blocks, off_blocks, coupling, operator],
         True, (len(arrived) + 3, len(arrived) + 4),
     )
     (jump_lift,) = call(
         kernel(build_lift), [((blocks, 2 * z.all_corners, width), BF16)], [other], heavy,
         [table, operator, lift, *arrived],
     )
-    arrived = exchange(near, [image])
+    arrived = exchange(pieces)
     fields, totals = [newest], []
     for step in range(2, ITERS + 1):
         older = fields if step == ITERS else []
-        newest, image, total, own_extra, near = call(
+        newest, image, total, own_extra, *pieces = call(
             kernel(apply_round, step),
-            [field, field, extra, extra, near_shape(1)], [other, parts], heavy,
+            [field, field, extra, extra] + piece_shapes(1), [other, parts], heavy,
             [table, *arrived, image, own_extra, jump_lift, scale, diag, off, coupling, *older],
         )
         fields.append(newest)
         totals.append(total)
-        arrived = exchange(near, [image])
+        arrived = exchange(pieces)
     (own_gram,) = call(
         kernel(cluster_gram), [gram], [], light, [operator, own_extra, *arrived, *totals], False
     )

time: 84.4 us -> 70.1 us (0.83)
  starting transfers between devices: 23.8 us -> 35.9 us
  waiting for transfers between devices: 27.8 us -> 16.6 us
  Pallas kernels: 24.8 us -> 15.3 us
  local copies, waits for them, and re-layouts: 6.95 us -> 1.37 us
    ppermute x20 -> x35, starting transfers between devices: 19.4 us -> 31.4 us  [exchange(): lax.ppermute(piece, 'sub', [(t, t ^ m) for t in range(z.peers)])]
    ppermute x20 -> x35, waiting for transfers between devices: 24.9 us -> 13.2 us  [exchange(): lax.ppermute(piece, 'sub', [(t, t ^ m) for t in range(z.peers)])]
    pallas_call x15 -> x10, Pallas kernels: 24.8 us -> 15.3 us  [call(): pl.pallas_call(body, out_shape=shapes, in_specs=specs, out_specs=[SMEM if...]
    unnamed x18 -> x4, local copies, waits for them, and re-layouts: 6.95 us -> 1.37 us
  transfers between devices with their start and end apart: 23 -> 38, of which waited for: 21 -> 20; matrix products, arithmetic and copies ran while one was open for 0% -> 0% of each run, Pallas kernels for 3% -> 1%
where the time goes in v3:
time: 70.1 us; the launch traced here: 69.9 us
  starting transfers between devices  35.9 us (51%)
  waiting for transfers between devices  16.6 us (24%)
  Pallas kernels  15.3 us (22%)
  local copies, waits for them, and re-layouts  1.37 us (2%)
  between operations  0.75 us (1%)
    ppermute x35, starting transfers between devices, exchange(): lax.ppermute(piece, 'sub', [(t, t ^ m) for t in range(z.peers)])  31.4 us
    pallas_call x10, Pallas kernels, call(): pl.pallas_call(body, out_shape=shapes, in_specs=specs, out_specs=[SMEM if...  15.3 us
    ppermute x35, waiting for transfers between devices, exchange(): lax.ppermute(piece, 'sub', [(t, t ^ m) for t in range(z.peers)])  13.2 us
    ppermute x3, starting transfers between devices, on_device(): lax.ppermute(own_gram, 'group', [(a, a ^ k if power else (a + k) % z.grou...  4.44 us
    ppermute x3, waiting for transfers between devices, on_device(): lax.ppermute(own_gram, 'group', [(a, a ^ k if power else (a + k) % z.grou...  3.42 us
  transfers between devices with their start and end apart: 38, of which 20 were waited for; matrix products, arithmetic and copies ran while one was open for 0% of the time, Pallas kernels for 1%

profile of v3, /device:TPU:0, one launch (start us, length us, event | category | flops | bytes accessed | tf_op | source)
XLA Modules:
  0.0 69.9 jit_solution(221908056051214879)
XLA Ops:
  0.6 1.1 %shard_map.105 = (s32[72]{0:T(128)S(4)}, f32[16,8,256]{2,1,0:T(8,128)S(1)}, f32[16,8,256]{2,1,0:T(8,128)S(1)}, f32[16,256]{1,0:T(8,128)S(1)}, bf16[8,4096]{1,0:T...) custom-call(s32[1,16]{1,0:T(1,128)} %partner.1, ...), custom_call_target="tpu_custom_call" | custom-call | flops 4000000 | bytes 250000 | tf_op jit(solution)/shard_map/pallas_call | solution.py:380
  1.7 3.4 %collective-permute-start = (f32[12,8,128]{2,1,0:T(8,128)S(1)}, f32[12,8,128]{2,1,0:T(8,128)S(1)}, u32[]{:S(2)}, u32[]{:S(2)}) collective-permute-start(f32[12,8,128]{2,1,0:T(8,128)S(1)} %get-tuple-element.60), channel_id=1, source_target_pairs={{0,7},{1,6},{2,5},{3,4},{4,3},{5,2},{6,1},{7,0},{8,15},{9,14},{10,... | collective-permute-start | bytes 147464 | tf_op jit(solution)/shard_map/ppermute | solution.py:422
  5.8 1.4 %collective-permute-start.2 = (f32[12,8,128]{2,1,0:T(8,128)S(1)}, f32[12,8,128]{2,1,0:T(8,128)S(1)}, u32[]{:S(2)}, u32[]{:S(2)}) collective-permute-start(f32[12,8,128]{2,1,0:T(8,128)S(1)} %get-tuple-element.62), channel_id=1, source_target_pairs={{0,5},{1,4},{2,7},{3,6},{4,1},{5,0},{6,3},{7,2},{8,13},{9,12},{10,... | collective-permute-start | bytes 147464 | tf_op jit(solution)/shard_map/ppermute | solution.py:422
  7.4 1.1 %collective-permute-start.4 = (f32[12,8,128]{2,1,0:T(8,128)S(1)}, f32[12,8,128]{2,1,0:T(8,128)S(1)}, u32[]{:S(2)}, u32[]{:S(2)}) collective-permute-start(f32[12,8,128]{2,1,0:T(8,128)S(1)} %get-tuple-element.64), channel_id=1, source_target_pairs={{0,3},{1,2},{2,1},{3,0},{4,7},{5,6},{6,5},{7,4},{8,11},{9,10},{10,... | collective-permute-start | bytes 147464 | tf_op jit(solution)/shard_map/ppermute | solution.py:422
  8.6 1.1 %collective-permute-start.5 = (f32[12,8,128]{2,1,0:T(8,128)S(1)}, f32[12,8,128]{2,1,0:T(8,128)S(1)}, u32[]{:S(2)}, u32[]{:S(2)}) collective-permute-start(f32[12,8,128]{2,1,0:T(8,128)S(1)} %get-tuple-element.65), channel_id=1, source_target_pairs={{0,2},{1,3},{2,0},{3,1},{4,6},{5,7},{6,4},{7,5},{8,10},{9,11},{10,... | collective-permute-start | bytes 147464 | tf_op jit(solution)/shard_map/ppermute | solution.py:422
  12.9 4.5 %shard_map.106 = (f32[16,8,256]{2,1,0:T(8,128)S(1)}, f32[16,8,256]{2,1,0:T(8,128)S(1)}, bf16[16,256,256]{2,1,0:T(8,128)(2,1)S(1)}, bf16[16,256,256]{2,1,0:T(8,12...) custom-call(s32[72]{0:T(128)S(4)} %get-tuple-element.59.table, ...), custom_call_target="tpu_custom_call" | custom-call | flops 600000000 | bytes 37500000 | tf_op jit(solution)/shard_map/pallas_call | solution.py:380
  17.4 2.0 %collective-permute-start.7 = (f32[7,8,128]{2,1,0:T(8,128)S(1)}, f32[7,8,128]{2,1,0:T(8,128)S(1)}, u32[]{:S(2)}, u32[]{:S(2)}) collective-permute-start(f32[7,8,128]{2,1,0:T(8,128)S(1)} %get-tuple-element.70), channel_id=1, source_target_pairs={{0,7},{1,6},{2,5},{3,4},{4,3},{5,2},{6,1},{7,0},{8,15},{9,14},{10,... | collective-permute-start | bytes 86024 | tf_op jit(solution)/shard_map/ppermute | solution.py:422
  19.9 1.5 %collective-permute-start.9 = (f32[7,8,128]{2,1,0:T(8,128)S(1)}, f32[7,8,128]{2,1,0:T(8,128)S(1)}, u32[]{:S(2)}, u32[]{:S(2)}) collective-permute-start(f32[7,8,128]{2,1,0:T(8,128)S(1)} %get-tuple-element.72), channel_id=1, source_target_pairs={{0,5},{1,4},{2,7},{3,6},{4,1},{5,0},{6,3},{7,2},{8,13},{9,12},{10,... | collective-permute-start | bytes 86024 | tf_op jit(solution)/shard_map/ppermute | solution.py:422
  21.8 1.0 %collective-permute-start.11 = (f32[7,8,128]{2,1,0:T(8,128)S(1)}, f32[7,8,128]{2,1,0:T(8,128)S(1)}, u32[]{:S(2)}, u32[]{:S(2)}) collective-permute-start(f32[7,8,128]{2,1,0:T(8,128)S(1)} %get-tuple-element.74), channel_id=1, source_target_pairs={{0,3},{1,2},{2,1},{3,0},{4,7},{5,6},{6,5},{7,4},{8,11},{9,10},{10,... | collective-permute-start | bytes 86024 | tf_op jit(solution)/shard_map/ppermute | solution.py:422
  23.4 0.8 %collective-permute-done.8.rest_1_ = f32[7,8,128]{2,1,0:T(8,128)S(1)} collective-permute-done((f32[7,8,128]{2,1,0:T(8,128)S(1)}, f32[7,8,128]{2,1,0:T(8,128)S(1)}, u32[]{:S(2)}, u32[]{:S(2)}) %collective-permute-start.8) | collective-permute-done | bytes 28704 | tf_op jit(solution)/shard_map/ppermute | solution.py:422
  25.4 1.3 %collective-permute-done.12.rest_5_ = f32[7,8,128]{2,1,0:T(8,128)S(1)} collective-permute-done((f32[7,8,128]{2,1,0:T(8,128)S(1)}, f32[7,8,128]{2,1,0:T(8,128)S(1)}, u32[]{:S(2)}, u32[]{:S(2)}) %collective-permute-start.12) | collective-permute-done | bytes 28704 | tf_op jit(solution)/shard_map/ppermute | solution.py:422
  26.7 2.1 %shard_map.108 = (f32[16,8,256]{2,1,0:T(8,128)S(1)}, f32[16,8,256]{2,1,0:T(8,128)S(1)}, f32[8,128]{1,0:T(8,128)S(1)}, f32[8,128]{1,0:T(8,128)S(1)}, f32[7,8,128]...) custom-call(s32[72]{0:T(128)S(4)} %get-tuple-element.59.table, ...), custom_call_target="tpu_custom_call" | custom-call | flops 600000000 | bytes 37500000 | tf_op jit(solution)/shard_map/pallas_call | solution.py:380
  28.8 1.2 %collective-permute-start.14 = (f32[7,8,128]{2,1,0:T(8,128)S(1)}, f32[7,8,128]{2,1,0:T(8,128)S(1)}, u32[]{:S(2)}, u32[]{:S(2)}) collective-permute-start(f32[7,8,128]{2,1,0:T(8,128)S(1)} %get-tuple-element.82), channel_id=1, source_target_pairs={{0,7},{1,6},{2,5},{3,4},{4,3},{5,2},{6,1},{7,0},{8,15},{9,14},{10,... | collective-permute-start | bytes 86024 | tf_op jit(solution)/shard_map/ppermute | solution.py:422
  30.7 2.1 %collective-permute-start.16 = (f32[7,8,128]{2,1,0:T(8,128)S(1)}, f32[7,8,128]{2,1,0:T(8,128)S(1)}, u32[]{:S(2)}, u32[]{:S(2)}) collective-permute-start(f32[7,8,128]{2,1,0:T(8,128)S(1)} %get-tuple-element.84), channel_id=1, source_target_pairs={{0,5},{1,4},{2,7},{3,6},{4,1},{5,0},{6,3},{7,2},{8,13},{9,12},{10,... | collective-permute-start | bytes 86024 | tf_op jit(solution)/shard_map/ppermute | solution.py:422
  33.5 1.1 %collective-permute-start.19 = (f32[7,8,128]{2,1,0:T(8,128)S(1)}, f32[7,8,128]{2,1,0:T(8,128)S(1)}, u32[]{:S(2)}, u32[]{:S(2)}) collective-permute-start(f32[7,8,128]{2,1,0:T(8,128)S(1)} %get-tuple-element.87), channel_id=1, source_target_pairs={{0,2},{1,3},{2,0},{3,1},{4,6},{5,7},{6,4},{7,5},{8,10},{9,11},{10,... | collective-permute-start | bytes 86024 | tf_op jit(solution)/shard_map/ppermute | solution.py:422
  35.1 1.5 %collective-permute-done.17.rest_3_ = f32[7,8,128]{2,1,0:T(8,128)S(1)} collective-permute-done((f32[7,8,128]{2,1,0:T(8,128)S(1)}, f32[7,8,128]{2,1,0:T(8,128)S(1)}, u32[]{:S(2)}, u32[]{:S(2)}) %collective-permute-start.17) | collective-permute-done | bytes 28704 | tf_op jit(solution)/shard_map/ppermute | solution.py:422
  37.3 2.1 %shard_map.109 = (f32[16,8,256]{2,1,0:T(8,128)S(1)}, f32[16,8,256]{2,1,0:T(8,128)S(1)}, f32[8,128]{1,0:T(8,128)S(1)}, f32[8,128]{1,0:T(8,128)S(1)}, f32[7,8,128]...) custom-call(s32[72]{0:T(128)S(4)} %get-tuple-element.59.table, ...), custom_call_target="tpu_custom_call" | custom-call | flops 600000000 | bytes 37500000 | tf_op jit(solution)/shard_map/pallas_call | solution.py:380
  39.5 1.5 %collective-permute-start.21 = (f32[7,8,128]{2,1,0:T(8,128)S(1)}, f32[7,8,128]{2,1,0:T(8,128)S(1)}, u32[]{:S(2)}, u32[]{:S(2)}) collective-permute-start(f32[7,8,128]{2,1,0:T(8,128)S(1)} %get-tuple-element.91), channel_id=1, source_target_pairs={{0,7},{1,6},{2,5},{3,4},{4,3},{5,2},{6,1},{7,0},{8,15},{9,14},{10,... | collective-permute-start | bytes 86024 | tf_op jit(solution)/shard_map/ppermute | solution.py:422
  41.5 1.9 %collective-permute-start.23 = (f32[7,8,128]{2,1,0:T(8,128)S(1)}, f32[7,8,128]{2,1,0:T(8,128)S(1)}, u32[]{:S(2)}, u32[]{:S(2)}) collective-permute-start(f32[7,8,128]{2,1,0:T(8,128)S(1)} %get-tuple-element.93), channel_id=1, source_target_pairs={{0,5},{1,4},{2,7},{3,6},{4,1},{5,0},{6,3},{7,2},{8,13},{9,12},{10,... | collective-permute-start | bytes 86024 | tf_op jit(solution)/shard_map/ppermute | solution.py:422
  43.9 0.9 %collective-permute-start.25 = (f32[7,8,128]{2,1,0:T(8,128)S(1)}, f32[7,8,128]{2,1,0:T(8,128)S(1)}, u32[]{:S(2)}, u32[]{:S(2)}) collective-permute-start(f32[7,8,128]{2,1,0:T(8,128)S(1)} %get-tuple-element.95), channel_id=1, source_target_pairs={{0,3},{1,2},{2,1},{3,0},{4,7},{5,6},{6,5},{7,4},{8,11},{9,10},{10,... | collective-permute-start | bytes 86024 | tf_op jit(solution)/shard_map/ppermute | solution.py:422
  45.8 1.5 %collective-permute-done.24.rest_3_ = f32[7,8,128]{2,1,0:T(8,128)S(1)} collective-permute-done((f32[7,8,128]{2,1,0:T(8,128)S(1)}, f32[7,8,128]{2,1,0:T(8,128)S(1)}, u32[]{:S(2)}, u32[]{:S(2)}) %collective-permute-start.24) | collective-permute-done | bytes 28704 | tf_op jit(solution)/shard_map/ppermute | solution.py:422
  47.3 1.3 %collective-permute-done.26.rest_5_ = f32[7,8,128]{2,1,0:T(8,128)S(1)} collective-permute-done((f32[7,8,128]{2,1,0:T(8,128)S(1)}, f32[7,8,128]{2,1,0:T(8,128)S(1)}, u32[]{:S(2)}, u32[]{:S(2)}) %collective-permute-start.26) | collective-permute-done | bytes 28704 | tf_op jit(solution)/shard_map/ppermute | solution.py:422
  48.7 2.2 %shard_map.110 = (f32[16,8,256]{2,1,0:T(8,128)S(1)}, f32[16,8,256]{2,1,0:T(8,128)S(1)}, f32[8,128]{1,0:T(8,128)S(1)}, f32[8,128]{1,0:T(8,128)S(1)}, f32[7,8,128]...) custom-call(s32[72]{0:T(128)S(4)} %get-tuple-element.59.table, ...), custom_call_target="tpu_custom_call" | custom-call | flops 600000000 | bytes 37500000 | tf_op jit(solution)/shard_map/pallas_call | solution.py:380
  50.8 1.1 %collective-permute-start.28 = (f32[7,8,128]{2,1,0:T(8,128)S(1)}, f32[7,8,128]{2,1,0:T(8,128)S(1)}, u32[]{:S(2)}, u32[]{:S(2)}) collective-permute-start(f32[7,8,128]{2,1,0:T(8,128)S(1)} %get-tuple-element.104), channel_id=1, source_target_pairs={{0,7},{1,6},{2,5},{3,4},{4,3},{5,2},{6,1},{7,0},{8,15},{9,14},{10,... | collective-permute-start | bytes 86024 | tf_op jit(solution)/shard_map/ppermute | solution.py:422
  51.9 0.8 %collective-permute-start.29 = (f32[7,8,128]{2,1,0:T(8,128)S(1)}, f32[7,8,128]{2,1,0:T(8,128)S(1)}, u32[]{:S(2)}, u32[]{:S(2)}) collective-permute-start(f32[7,8,128]{2,1,0:T(8,128)S(1)} %get-tuple-element.105), channel_id=1, source_target_pairs={{0,6},{1,7},{2,4},{3,5},{4,2},{5,3},{6,0},{7,1},{8,14},{9,15},{10,... | collective-permute-start | bytes 86024 | tf_op jit(solution)/shard_map/ppermute | solution.py:422
  52.8 1.6 %collective-permute-start.30 = (f32[7,8,128]{2,1,0:T(8,128)S(1)}, f32[7,8,128]{2,1,0:T(8,128)S(1)}, u32[]{:S(2)}, u32[]{:S(2)}) collective-permute-start(f32[7,8,128]{2,1,0:T(8,128)S(1)} %get-tuple-element.106), channel_id=1, source_target_pairs={{0,5},{1,4},{2,7},{3,6},{4,1},{5,0},{6,3},{7,2},{8,13},{9,12},{10,... | collective-permute-start | bytes 86024 | tf_op jit(solution)/shard_map/ppermute | solution.py:422
  54.4 0.9 %collective-permute-start.31 = (f32[7,8,128]{2,1,0:T(8,128)S(1)}, f32[7,8,128]{2,1,0:T(8,128)S(1)}, u32[]{:S(2)}, u32[]{:S(2)}) collective-permute-start(f32[7,8,128]{2,1,0:T(8,128)S(1)} %get-tuple-element.107), channel_id=1, source_target_pairs={{0,4},{1,5},{2,6},{3,7},{4,0},{5,1},{6,2},{7,3},{8,12},{9,13},{10,... | collective-permute-start | bytes 86024 | tf_op jit(solution)/shard_map/ppermute | solution.py:422
  57.2 1.1 %collective-permute-done.31.rest_3_ = f32[7,8,128]{2,1,0:T(8,128)S(1)} collective-permute-done((f32[7,8,128]{2,1,0:T(8,128)S(1)}, f32[7,8,128]{2,1,0:T(8,128)S(1)}, u32[]{:S(2)}, u32[]{:S(2)}) %collective-permute-start.31) | collective-permute-done | bytes 28704 | tf_op jit(solution)/shard_map/ppermute | solution.py:422
  58.6 0.9 %collective-permute-done.33.rest_5_ = f32[7,8,128]{2,1,0:T(8,128)S(1)} collective-permute-done((f32[7,8,128]{2,1,0:T(8,128)S(1)}, f32[7,8,128]{2,1,0:T(8,128)S(1)}, u32[]{:S(2)}, u32[]{:S(2)}) %collective-permute-start.33) | collective-permute-done | bytes 28704 | tf_op jit(solution)/shard_map/ppermute | solution.py:422
  59.8 3.7 %collective-permute-start.37 = (f32[8,128]{1,0:T(8,128)S(1)}, f32[8,128]{1,0:T(8,128)S(1)}, u32[]{:S(2)}, u32[]{:S(2)}) collective-permute-start(f32[8,128]{1,0:T(8,128)S(1)} %shard_map.111.rest_0_), channel_id=1, source_target_pairs={{0,24},{8,16},{16,8},{24,0},{1,25},{9,17},{17,9},{25,1},{2,26},{10... | collective-permute-start | bytes 12296 | tf_op jit(solution)/shard_map/ppermute | solution.py:481
  65.2 2.7 %collective-permute-done.36.rest_2_ = f32[8,128]{1,0:T(8,128)S(1)} collective-permute-done((f32[8,128]{1,0:T(8,128)S(1)}, f32[8,128]{1,0:T(8,128)S(1)}, u32[]{:S(2)}, u32[]{:S(2)}) %collective-permute-start.36) | collective-permute-done | bytes 4128 | tf_op jit(solution)/shard_map/ppermute | solution.py:481
  68.0 1.9 %shard_map.113 = (f32[8,16,256]{2,1,0:T(8,128)}, f32[8,16,256]{2,1,0:T(8,128)}) custom-call(f32[8,128]{1,0:T(8,128)S(1)} %shard_map.111.rest_0_, f32[8,128]{1,0:T(8,128)S(1)} %collective-permute-done.35.rest_1_, f32[8,128]{1,0:T(8,128)S(1)} %collective-permute-done.36.rest_2_, f32[8,128]{1,0:T(8,128)S(1)} %collective-permute-done.37.rest_3_, ...), custom_call_target="tpu_custom_call" | custom-call | flops 4000000 | bytes 250000 | tf_op jit(solution)/shard_map/pallas_call | solution.py:380
  (58 shorter events, 15.9 us)
Async XLA Ops:
  1.7 6.8 %collective-permute-start = (f32[12,8,128]{2,1,0:T(8,128)S(1)}, f32[12,8,128]{2,1,0:T(8,128)S(1)}, u32[]{:S(2)}, u32[]{:S(2)}) collective-permute-start(f32[12,8,128]{2,1,0:T(8,128)S(1)} %get-tuple-element.60), channel_id=1, source_target_pairs={{0,7},{1,6},{2,5},{3,4},{4,3},{5,2},{6,1},{7,0},{8,15},{9,14},{10,... | collective-permute-start | bytes 147464 | tf_op jit(solution)/shard_map/ppermute | solution.py:422
  5.1 5.3 %collective-permute-start.1 = (f32[12,8,128]{2,1,0:T(8,128)S(1)}, f32[12,8,128]{2,1,0:T(8,128)S(1)}, u32[]{:S(2)}, u32[]{:S(2)}) collective-permute-start(f32[12,8,128]{2,1,0:T(8,128)S(1)} %get-tuple-element.61), channel_id=1, source_target_pairs={{0,6},{1,7},{2,4},{3,5},{4,2},{5,3},{6,0},{7,1},{8,14},{9,15},{10,... | collective-permute-start | bytes 147464 | tf_op jit(solution)/shard_map/ppermute | solution.py:422
  5.8 6.5 %collective-permute-start.2 = (f32[12,8,128]{2,1,0:T(8,128)S(1)}, f32[12,8,128]{2,1,0:T(8,128)S(1)}, u32[]{:S(2)}, u32[]{:S(2)}) collective-permute-start(f32[12,8,128]{2,1,0:T(8,128)S(1)} %get-tuple-element.62), channel_id=1, source_target_pairs={{0,5},{1,4},{2,7},{3,6},{4,1},{5,0},{6,3},{7,2},{8,13},{9,12},{10,... | collective-permute-start | bytes 147464 | tf_op jit(solution)/shard_map/ppermute | solution.py:422
  7.2 5.1 %collective-permute-start.3 = (f32[12,8,128]{2,1,0:T(8,128)S(1)}, f32[12,8,128]{2,1,0:T(8,128)S(1)}, u32[]{:S(2)}, u32[]{:S(2)}) collective-permute-start(f32[12,8,128]{2,1,0:T(8,128)S(1)} %get-tuple-element.63), channel_id=1, source_target_pairs={{0,4},{1,5},{2,6},{3,7},{4,0},{5,1},{6,2},{7,3},{8,12},{9,13},{10,... | collective-permute-start | bytes 147464 | tf_op jit(solution)/shard_map/ppermute | solution.py:422
  7.4 4.8 %collective-permute-start.4 = (f32[12,8,128]{2,1,0:T(8,128)S(1)}, f32[12,8,128]{2,1,0:T(8,128)S(1)}, u32[]{:S(2)}, u32[]{:S(2)}) collective-permute-start(f32[12,8,128]{2,1,0:T(8,128)S(1)} %get-tuple-element.64), channel_id=1, source_target_pairs={{0,3},{1,2},{2,1},{3,0},{4,7},{5,6},{6,5},{7,4},{8,11},{9,10},{10,... | collective-permute-start | bytes 147464 | tf_op jit(solution)/shard_map/ppermute | solution.py:422
  8.6 4.4 %collective-permute-start.5 = (f32[12,8,128]{2,1,0:T(8,128)S(1)}, f32[12,8,128]{2,1,0:T(8,128)S(1)}, u32[]{:S(2)}, u32[]{:S(2)}) collective-permute-start(f32[12,8,128]{2,1,0:T(8,128)S(1)} %get-tuple-element.65), channel_id=1, source_target_pairs={{0,2},{1,3},{2,0},{3,1},{4,6},{5,7},{6,4},{7,5},{8,10},{9,11},{10,... | collective-permute-start | bytes 147464 | tf_op jit(solution)/shard_map/ppermute | solution.py:422
  17.4 5.4 %collective-permute-start.7 = (f32[7,8,128]{2,1,0:T(8,128)S(1)}, f32[7,8,128]{2,1,0:T(8,128)S(1)}, u32[]{:S(2)}, u32[]{:S(2)}) collective-permute-start(f32[7,8,128]{2,1,0:T(8,128)S(1)} %get-tuple-element.70), channel_id=1, source_target_pairs={{0,7},{1,6},{2,5},{3,4},{4,3},{5,2},{6,1},{7,0},{8,15},{9,14},{10,... | collective-permute-start | bytes 86024 | tf_op jit(solution)/shard_map/ppermute | solution.py:422
  19.4 4.8 %collective-permute-start.8 = (f32[7,8,128]{2,1,0:T(8,128)S(1)}, f32[7,8,128]{2,1,0:T(8,128)S(1)}, u32[]{:S(2)}, u32[]{:S(2)}) collective-permute-start(f32[7,8,128]{2,1,0:T(8,128)S(1)} %get-tuple-element.71), channel_id=1, source_target_pairs={{0,6},{1,7},{2,4},{3,5},{4,2},{5,3},{6,0},{7,1},{8,14},{9,15},{10,... | collective-permute-start | bytes 86024 | tf_op jit(solution)/shard_map/ppermute | solution.py:422
  19.9 4.7 %collective-permute-start.9 = (f32[7,8,128]{2,1,0:T(8,128)S(1)}, f32[7,8,128]{2,1,0:T(8,128)S(1)}, u32[]{:S(2)}, u32[]{:S(2)}) collective-permute-start(f32[7,8,128]{2,1,0:T(8,128)S(1)} %get-tuple-element.72), channel_id=1, source_target_pairs={{0,5},{1,4},{2,7},{3,6},{4,1},{5,0},{6,3},{7,2},{8,13},{9,12},{10,... | collective-permute-start | bytes 86024 | tf_op jit(solution)/shard_map/ppermute | solution.py:422
  21.3 3.9 %collective-permute-start.10 = (f32[7,8,128]{2,1,0:T(8,128)S(1)}, f32[7,8,128]{2,1,0:T(8,128)S(1)}, u32[]{:S(2)}, u32[]{:S(2)}) collective-permute-start(f32[7,8,128]{2,1,0:T(8,128)S(1)} %get-tuple-element.73), channel_id=1, source_target_pairs={{0,4},{1,5},{2,6},{3,7},{4,0},{5,1},{6,2},{7,3},{8,12},{9,13},{10,... | collective-permute-start | bytes 86024 | tf_op jit(solution)/shard_map/ppermute | solution.py:422
  21.8 3.5 %collective-permute-start.11 = (f32[7,8,128]{2,1,0:T(8,128)S(1)}, f32[7,8,128]{2,1,0:T(8,128)S(1)}, u32[]{:S(2)}, u32[]{:S(2)}) collective-permute-start(f32[7,8,128]{2,1,0:T(8,128)S(1)} %get-tuple-element.74), channel_id=1, source_target_pairs={{0,3},{1,2},{2,1},{3,0},{4,7},{5,6},{6,5},{7,4},{8,11},{9,10},{10,... | collective-permute-start | bytes 86024 | tf_op jit(solution)/shard_map/ppermute | solution.py:422
  22.8 3.9 %collective-permute-start.12 = (f32[7,8,128]{2,1,0:T(8,128)S(1)}, f32[7,8,128]{2,1,0:T(8,128)S(1)}, u32[]{:S(2)}, u32[]{:S(2)}) collective-permute-start(f32[7,8,128]{2,1,0:T(8,128)S(1)} %get-tuple-element.75), channel_id=1, source_target_pairs={{0,2},{1,3},{2,0},{3,1},{4,6},{5,7},{6,4},{7,5},{8,10},{9,11},{10,... | collective-permute-start | bytes 86024 | tf_op jit(solution)/shard_map/ppermute | solution.py:422
  28.8 4.6 %collective-permute-start.14 = (f32[7,8,128]{2,1,0:T(8,128)S(1)}, f32[7,8,128]{2,1,0:T(8,128)S(1)}, u32[]{:S(2)}, u32[]{:S(2)}) collective-permute-start(f32[7,8,128]{2,1,0:T(8,128)S(1)} %get-tuple-element.82), channel_id=1, source_target_pairs={{0,7},{1,6},{2,5},{3,4},{4,3},{5,2},{6,1},{7,0},{8,15},{9,14},{10,... | collective-permute-start | bytes 86024 | tf_op jit(solution)/shard_map/ppermute | solution.py:422
  30.0 4.8 %collective-permute-start.15 = (f32[7,8,128]{2,1,0:T(8,128)S(1)}, f32[7,8,128]{2,1,0:T(8,128)S(1)}, u32[]{:S(2)}, u32[]{:S(2)}) collective-permute-start(f32[7,8,128]{2,1,0:T(8,128)S(1)} %get-tuple-element.83), channel_id=1, source_target_pairs={{0,6},{1,7},{2,4},{3,5},{4,2},{5,3},{6,0},{7,1},{8,14},{9,15},{10,... | collective-permute-start | bytes 86024 | tf_op jit(solution)/shard_map/ppermute | solution.py:422
  30.7 4.4 %collective-permute-start.16 = (f32[7,8,128]{2,1,0:T(8,128)S(1)}, f32[7,8,128]{2,1,0:T(8,128)S(1)}, u32[]{:S(2)}, u32[]{:S(2)}) collective-permute-start(f32[7,8,128]{2,1,0:T(8,128)S(1)} %get-tuple-element.84), channel_id=1, source_target_pairs={{0,5},{1,4},{2,7},{3,6},{4,1},{5,0},{6,3},{7,2},{8,13},{9,12},{10,... | collective-permute-start | bytes 86024 | tf_op jit(solution)/shard_map/ppermute | solution.py:422
  32.7 3.9 %collective-permute-start.17 = (f32[7,8,128]{2,1,0:T(8,128)S(1)}, f32[7,8,128]{2,1,0:T(8,128)S(1)}, u32[]{:S(2)}, u32[]{:S(2)}) collective-permute-start(f32[7,8,128]{2,1,0:T(8,128)S(1)} %get-tuple-element.85), channel_id=1, source_target_pairs={{0,4},{1,5},{2,6},{3,7},{4,0},{5,1},{6,2},{7,3},{8,12},{9,13},{10,... | collective-permute-start | bytes 86024 | tf_op jit(solution)/shard_map/ppermute | solution.py:422
  33.3 3.4 %collective-permute-start.18 = (f32[7,8,128]{2,1,0:T(8,128)S(1)}, f32[7,8,128]{2,1,0:T(8,128)S(1)}, u32[]{:S(2)}, u32[]{:S(2)}) collective-permute-start(f32[7,8,128]{2,1,0:T(8,128)S(1)} %get-tuple-element.86), channel_id=1, source_target_pairs={{0,3},{1,2},{2,1},{3,0},{4,7},{5,6},{6,5},{7,4},{8,11},{9,10},{10,... | collective-permute-start | bytes 86024 | tf_op jit(solution)/shard_map/ppermute | solution.py:422
  33.5 3.9 %collective-permute-start.19 = (f32[7,8,128]{2,1,0:T(8,128)S(1)}, f32[7,8,128]{2,1,0:T(8,128)S(1)}, u32[]{:S(2)}, u32[]{:S(2)}) collective-permute-start(f32[7,8,128]{2,1,0:T(8,128)S(1)} %get-tuple-element.87), channel_id=1, source_target_pairs={{0,2},{1,3},{2,0},{3,1},{4,6},{5,7},{6,4},{7,5},{8,10},{9,11},{10,... | collective-permute-start | bytes 86024 | tf_op jit(solution)/shard_map/ppermute | solution.py:422
  39.5 5.3 %collective-permute-start.21 = (f32[7,8,128]{2,1,0:T(8,128)S(1)}, f32[7,8,128]{2,1,0:T(8,128)S(1)}, u32[]{:S(2)}, u32[]{:S(2)}) collective-permute-start(f32[7,8,128]{2,1,0:T(8,128)S(1)} %get-tuple-element.91), channel_id=1, source_target_pairs={{0,7},{1,6},{2,5},{3,4},{4,3},{5,2},{6,1},{7,0},{8,15},{9,14},{10,... | collective-permute-start | bytes 86024 | tf_op jit(solution)/shard_map/ppermute | solution.py:422
  41.0 4.8 %collective-permute-start.22 = (f32[7,8,128]{2,1,0:T(8,128)S(1)}, f32[7,8,128]{2,1,0:T(8,128)S(1)}, u32[]{:S(2)}, u32[]{:S(2)}) collective-permute-start(f32[7,8,128]{2,1,0:T(8,128)S(1)} %get-tuple-element.92), channel_id=1, source_target_pairs={{0,6},{1,7},{2,4},{3,5},{4,2},{5,3},{6,0},{7,1},{8,14},{9,15},{10,... | collective-permute-start | bytes 86024 | tf_op jit(solution)/shard_map/ppermute | solution.py:422
  41.5 4.3 %collective-permute-start.23 = (f32[7,8,128]{2,1,0:T(8,128)S(1)}, f32[7,8,128]{2,1,0:T(8,128)S(1)}, u32[]{:S(2)}, u32[]{:S(2)}) collective-permute-start(f32[7,8,128]{2,1,0:T(8,128)S(1)} %get-tuple-element.93), channel_id=1, source_target_pairs={{0,5},{1,4},{2,7},{3,6},{4,1},{5,0},{6,3},{7,2},{8,13},{9,12},{10,... | collective-permute-start | bytes 86024 | tf_op jit(solution)/shard_map/ppermute | solution.py:422
  43.4 3.9 %collective-permute-start.24 = (f32[7,8,128]{2,1,0:T(8,128)S(1)}, f32[7,8,128]{2,1,0:T(8,128)S(1)}, u32[]{:S(2)}, u32[]{:S(2)}) collective-permute-start(f32[7,8,128]{2,1,0:T(8,128)S(1)} %get-tuple-element.94), channel_id=1, source_target_pairs={{0,4},{1,5},{2,6},{3,7},{4,0},{5,1},{6,2},{7,3},{8,12},{9,13},{10,... | collective-permute-start | bytes 86024 | tf_op jit(solution)/shard_map/ppermute | solution.py:422
  43.9 3.4 %collective-permute-start.25 = (f32[7,8,128]{2,1,0:T(8,128)S(1)}, f32[7,8,128]{2,1,0:T(8,128)S(1)}, u32[]{:S(2)}, u32[]{:S(2)}) collective-permute-start(f32[7,8,128]{2,1,0:T(8,128)S(1)} %get-tuple-element.95), channel_id=1, source_target_pairs={{0,3},{1,2},{2,1},{3,0},{4,7},{5,6},{6,5},{7,4},{8,11},{9,10},{10,... | collective-permute-start | bytes 86024 | tf_op jit(solution)/shard_map/ppermute | solution.py:422
  44.8 3.9 %collective-permute-start.26 = (f32[7,8,128]{2,1,0:T(8,128)S(1)}, f32[7,8,128]{2,1,0:T(8,128)S(1)}, u32[]{:S(2)}, u32[]{:S(2)}) collective-permute-start(f32[7,8,128]{2,1,0:T(8,128)S(1)} %get-tuple-element.96), channel_id=1, source_target_pairs={{0,2},{1,3},{2,0},{3,1},{4,6},{5,7},{6,4},{7,5},{8,10},{9,11},{10,... | collective-permute-start | bytes 86024 | tf_op jit(solution)/shard_map/ppermute | solution.py:422
  50.8 4.8 %collective-permute-start.28 = (f32[7,8,128]{2,1,0:T(8,128)S(1)}, f32[7,8,128]{2,1,0:T(8,128)S(1)}, u32[]{:S(2)}, u32[]{:S(2)}) collective-permute-start(f32[7,8,128]{2,1,0:T(8,128)S(1)} %get-tuple-element.104), channel_id=1, source_target_pairs={{0,7},{1,6},{2,5},{3,4},{4,3},{5,2},{6,1},{7,0},{8,15},{9,14},{10,... | collective-permute-start | bytes 86024 | tf_op jit(solution)/shard_map/ppermute | solution.py:422
  51.9 4.8 %collective-permute-start.29 = (f32[7,8,128]{2,1,0:T(8,128)S(1)}, f32[7,8,128]{2,1,0:T(8,128)S(1)}, u32[]{:S(2)}, u32[]{:S(2)}) collective-permute-start(f32[7,8,128]{2,1,0:T(8,128)S(1)} %get-tuple-element.105), channel_id=1, source_target_pairs={{0,6},{1,7},{2,4},{3,5},{4,2},{5,3},{6,0},{7,1},{8,14},{9,15},{10,... | collective-permute-start | bytes 86024 | tf_op jit(solution)/shard_map/ppermute | solution.py:422
  52.8 4.4 %collective-permute-start.30 = (f32[7,8,128]{2,1,0:T(8,128)S(1)}, f32[7,8,128]{2,1,0:T(8,128)S(1)}, u32[]{:S(2)}, u32[]{:S(2)}) collective-permute-start(f32[7,8,128]{2,1,0:T(8,128)S(1)} %get-tuple-element.106), channel_id=1, source_target_pairs={{0,5},{1,4},{2,7},{3,6},{4,1},{5,0},{6,3},{7,2},{8,13},{9,12},{10,... | collective-permute-start | bytes 86024 | tf_op jit(solution)/shard_map/ppermute | solution.py:422
  54.4 3.9 %collective-permute-start.31 = (f32[7,8,128]{2,1,0:T(8,128)S(1)}, f32[7,8,128]{2,1,0:T(8,128)S(1)}, u32[]{:S(2)}, u32[]{:S(2)}) collective-permute-start(f32[7,8,128]{2,1,0:T(8,128)S(1)} %get-tuple-element.107), channel_id=1, source_target_pairs={{0,4},{1,5},{2,6},{3,7},{4,0},{5,1},{6,2},{7,3},{8,12},{9,13},{10,... | collective-permute-start | bytes 86024 | tf_op jit(solution)/shard_map/ppermute | solution.py:422
  55.6 3.9 %collective-permute-start.33 = (f32[7,8,128]{2,1,0:T(8,128)S(1)}, f32[7,8,128]{2,1,0:T(8,128)S(1)}, u32[]{:S(2)}, u32[]{:S(2)}) collective-permute-start(f32[7,8,128]{2,1,0:T(8,128)S(1)} %get-tuple-element.109), channel_id=1, source_target_pairs={{0,2},{1,3},{2,0},{3,1},{4,6},{5,7},{6,4},{7,5},{8,10},{9,11},{10,... | collective-permute-start | bytes 86024 | tf_op jit(solution)/shard_map/ppermute | solution.py:422
  59.8 5.5 %collective-permute-start.37 = (f32[8,128]{1,0:T(8,128)S(1)}, f32[8,128]{1,0:T(8,128)S(1)}, u32[]{:S(2)}, u32[]{:S(2)}) collective-permute-start(f32[8,128]{1,0:T(8,128)S(1)} %shard_map.111.rest_0_), channel_id=1, source_target_pairs={{0,24},{8,16},{16,8},{24,0},{1,25},{9,17},{17,9},{25,1},{2,26},{10... | collective-permute-start | bytes 12296 | tf_op jit(solution)/shard_map/ppermute | solution.py:481
  63.4 4.5 %collective-permute-start.36 = (f32[8,128]{1,0:T(8,128)S(1)}, f32[8,128]{1,0:T(8,128)S(1)}, u32[]{:S(2)}, u32[]{:S(2)}) collective-permute-start(f32[8,128]{1,0:T(8,128)S(1)} %shard_map.111.rest_0_), channel_id=1, source_target_pairs={{0,16},{8,24},{16,0},{24,8},{1,17},{9,25},{17,1},{25,9},{2,18},{10... | collective-permute-start | bytes 12296 | tf_op jit(solution)/shard_map/ppermute | solution.py:481
  63.4 4.5 %collective-permute-start.35 = (f32[8,128]{1,0:T(8,128)S(1)}, f32[8,128]{1,0:T(8,128)S(1)}, u32[]{:S(2)}, u32[]{:S(2)}) collective-permute-start(f32[8,128]{1,0:T(8,128)S(1)} %shard_map.111.rest_0_), channel_id=1, source_target_pairs={{0,8},{8,0},{16,24},{24,16},{1,9},{9,1},{17,25},{25,17},{2,10},{10... | collective-permute-start | bytes 12296 | tf_op jit(solution)/shard_map/ppermute | solution.py:481
  (8 other events, 17.8 us)

commit v4 on v3

--- a/solution.py
+++ b/solution.py
@@ -62,7 +62,8 @@
         self.extra_chunks = -(-(self.gram_lane + ENTRIES) // LANES)
         self.extra = self.extra_chunks * LANES
         self.halves = self.width // LANES
-        self.masks = range(self.peers - 1, 0, -1)
+        self.pairs = self.peers // 2
+        self.masks = range(1, self.peers)
         self.slots = self.peers * self.capacity
         self.inverse = self.slots
         self.pattern = self.inverse + self.blocks
@@ -91,30 +92,36 @@
         table[z.partner + i] = mate
 
 
+def pair_of(m):
+    return (lax.axis_index("sub") ^ m) >> 1
+
+
 def fill_pieces(z, table, sources, pieces):
-    for m, piece in zip(z.masks, pieces):
+    for m in z.masks:
+        pair = pair_of(m)
         row = 0
         for source in sources:
             for r in range(z.capacity):
                 block = jnp.minimum(table[m * z.capacity + r], z.blocks - 1)
                 value = source[block]
                 for h in range(z.halves):
-                    piece[row] = value[:, h * LANES : (h + 1) * LANES]
+                    pieces[pair, m % 2, row] = value[:, h * LANES : (h + 1) * LANES]
                     row += 1
 
 
-def place(z, table, pieces, kind, target):
-    for m, piece in zip(z.masks, pieces):
+def place(z, table, arrived, kind, target):
+    for m in z.masks:
+        pair = pair_of(m)
         row = z.rows(kind)
         for r in range(z.capacity):
             block = table[m * z.capacity + r]
             for h in range(z.halves):
-                target[block, :, h * LANES : (h + 1) * LANES] = piece[row]
+                target[block, :, h * LANES : (h + 1) * LANES] = arrived[m % 2][pair, m % 2, row]
                 row += 1
 
 
-def begin(z, partner, pattern, load, scale, coupling, table, field, lift, scale_out, coupling_out, *rest):
-    pieces, (here, partner_here, pattern_here, counts, sems) = rest[:-5], rest[-5:]
+def begin(z, partner, pattern, load, scale, coupling, table, field, lift, scale_out, coupling_out, pieces, *scratch):
+    here, partner_here, pattern_here, counts, sems = scratch
     copies = [
         pltpu.make_async_copy(a, b, sems.at[k])
         for k, (a, b) in enumerate(
@@ -147,7 +154,17 @@
     return [high, middle, a - high - middle]
 
 
-def build_operator(z, index, inverse, operator):
+def prepare(z, index_in, inverse_in, diag, off, operator, diag_out, off_out, index, inverse, sems):
+    copies = [
+        pltpu.make_async_copy(a, b, sems.at[k])
+        for k, (a, b) in enumerate(
+            [(index_in, index), (inverse_in, inverse), (diag, diag_out), (off, off_out)]
+        )
+    ]
+    for copy in copies:
+        copy.start()
+    copies[0].wait()
+    copies[1].wait()
     rows = lax.broadcasted_iota(jnp.int32, (z.coarse, z.all_corners), 0)
     select = (rows == index[...]).astype(BF16)
     parts = jnp.concatenate(split3(inverse[...]), axis=0).astype(BF16)
@@ -156,11 +173,12 @@
     parts = jnp.concatenate(split3(half), axis=1).astype(BF16)
     full = dot(select, parts, TN)
     operator[...] = sum(full[:, k * z.all_corners : (k + 1) * z.all_corners] for k in range(3))
-
-
-def build_lift(z, table, operator, lift, *rest):
-    pieces, (jump_lift, other) = rest[:-2], rest[-2:]
-    place(z, table, pieces, 1, other)
+    copies[2].wait()
+    copies[3].wait()
+
+
+def build_lift(z, table, operator, lift, same, across, jump_lift, other):
+    place(z, table, (same, across), 1, other)
     me = lax.axis_index("sub")
     own = operator[pl.ds(pl.multiple_of(me * z.corners, z.corners), z.corners), :]
     for i in range(z.blocks):
@@ -173,11 +191,12 @@
         jump_lift[i] = split(dot(left, right, TN))
 
 
-def extra_sum(z, own, pieces):
+def extra_sum(z, own, arrived):
     total = own[...]
-    for piece in pieces:
+    for m in z.masks:
+        pair = pair_of(m)
         total = total + jnp.concatenate(
-            [piece[z.rows(1) + j] for j in range(z.extra_chunks)], axis=1
+            [arrived[m % 2][pair, m % 2, z.rows(1) + j] for j in range(z.extra_chunks)], axis=1
         )
     return total
 
@@ -198,38 +217,19 @@
 
 
 def apply_round(z, step, table, *rest):
-    count = len(z.masks)
     first, last = step == 1, step == ITERS
     rest = list(rest)
     take = lambda n: [rest.pop(0) for _ in range(n)]
-    arrived = take(count)
+    arrived = take(2)
     (before,) = take(1)
     if not first:
         own_extra, jump_lift = take(2)
     scale, diag, off, coupling = take(4)
     older = take(ITERS - 1) if last else []
-    if first:
-        take(1)
     field, image = take(2)
-    if first:
-        sources, (diag, off) = (diag, off), take(2)
-    else:
+    if not first:
         (total_out,) = take(1)
-    (extra,) = take(1)
-    pieces = take(count)
-    other, parts = take(2)
-    if first:
-        (sems,) = rest
-        copies = [
-            [
-                pltpu.make_async_copy(a.at[i], b.at[i], sems.at[k, i])
-                for k, (a, b) in enumerate(zip(sources, (diag, off)))
-            ]
-            for i in range(z.blocks)
-        ]
-        for pair in copies:
-            for copy in pair:
-                copy.start()
+    extra, pieces, other, parts = rest
     place(z, table, arrived, 0, other)
     if not first:
         total = extra_sum(z, own_extra, arrived)
@@ -242,10 +242,6 @@
             value = (value + fold(dot(rows, jump_lift[i], NN))) * shrink
         field[i] = value
         parts[i] = split(scale[i : i + 1, :] * value)
-    if first:
-        for pair in copies:
-            for copy in pair:
-                copy.wait()
     partial = jnp.zeros((2 * z.columns, z.corners), F32)
     top = jnp.zeros((z.columns, z.width), F32)
     for i in range(z.blocks):
@@ -277,14 +273,14 @@
                 acc = acc + a[i] * b[i]
             tile = jnp.where(lanes == z.gram_lane + entry, lane_sum(acc), tile)
     extra[...] = tile
-    for piece in pieces:
+    for m in z.masks:
+        pair = pair_of(m)
         for j in range(z.extra_chunks):
-            piece[z.rows(1) + j] = tile[:, j * LANES : (j + 1) * LANES]
+            pieces[pair, m % 2, z.rows(1) + j] = tile[:, j * LANES : (j + 1) * LANES]
 
 
 def cluster_gram(z, operator, own_extra, *rest):
-    count = len(z.masks)
-    arrived, totals, (gram,) = rest[:count], rest[count:-1], rest[-1:]
+    arrived, totals, (gram,) = rest[:2], rest[2:-1], rest[-1:]
     total = extra_sum(z, own_extra, arrived)
     totals = [t[...] for t in totals]
     partials = [t[:, : z.all_corners] for t in totals + [total]]
@@ -410,20 +406,19 @@
     gram = ((cols, 128), F32)
     light, heavy = 4_000_000, 600_000_000
 
-    def piece_shapes(kinds):
+    def piece_shape(kinds):
         rows = z.rows(kinds) + (z.extra_chunks if kinds == 1 else 0)
-        return [((rows, cols, LANES), F32)] * len(z.masks)
+        return ((z.pairs, 2, rows, cols, LANES), F32)
 
     def kernel(body, *extra_args):
         return functools.partial(body, z, *extra_args)
 
     def exchange(pieces):
-        return [
-            lax.ppermute(piece, "sub", [(t, t ^ m) for t in range(z.peers)])
-            for m, piece in zip(z.masks, pieces)
-        ]
-
-    table, loaded, lift, scale, coupling, *pieces = call(
+        sides = [list(range(side, z.peers, 2)) for side in range(2)]
+        same = lax.all_to_all(pieces, "sub", 0, 0, axis_index_groups=sides, tiled=True)
+        return same, lax.ppermute(same, "sub", [(t, t ^ 1) for t in range(z.peers)])
+
+    table, loaded, lift, scale, coupling, pieces = call(
         kernel(begin),
         [
             ((z.table,), jnp.int32),
@@ -431,8 +426,8 @@
             field,
             (row_scale.shape, F32),
             (corner_coupling.shape, BF16),
-        ]
-        + piece_shapes(2),
+            piece_shape(2),
+        ],
         [
             pltpu.VMEM(load.shape, F32),
             pltpu.SMEM(partner.shape, jnp.int32),
@@ -445,17 +440,20 @@
         False, range(5),
     )
     arrived = exchange(pieces)
-    (operator,) = call(
-        kernel(build_operator), [((z.all_corners, z.all_corners), F32)], [], light,
-        [corner_index, coarse_inverse], False,
-    )
     weight = (diag_blocks.shape, BF16)
-    newest, image, diag, off, own_extra, *pieces = call(
+    operator, diag, off = call(
+        kernel(prepare), [((z.all_corners, z.all_corners), F32), weight, weight],
+        [
+            pltpu.VMEM(corner_index.shape, jnp.int32),
+            pltpu.VMEM(coarse_inverse.shape, F32),
+            pltpu.SemaphoreType.DMA((4,)),
+        ],
+        heavy, [corner_index, coarse_inverse, diag_blocks, off_blocks], False, range(4),
+    )
+    newest, image, own_extra, pieces = call(
         kernel(apply_round, 1),
-        [field, field, weight, weight, extra] + piece_shapes(1),
-        [other, parts, pltpu.SemaphoreType.DMA((2, blocks))], heavy,
-        [table, *arrived, loaded, scale, diag_blocks, off_blocks, coupling, operator],
-        True, (len(arrived) + 3, len(arrived) + 4),
+        [field, field, extra, piece_shape(1)], [other, parts], heavy,
+        [table, *arrived, loaded, scale, diag, off, coupling],
     )
     (jump_lift,) = call(
         kernel(build_lift), [((blocks, 2 * z.all_corners, width), BF16)], [other], heavy,
@@ -465,9 +463,9 @@
     fields, totals = [newest], []
     for step in range(2, ITERS + 1):
         older = fields if step == ITERS else []
-        newest, image, total, own_extra, *pieces = call(
+        newest, image, total, own_extra, pieces = call(
             kernel(apply_round, step),
-            [field, field, extra, extra] + piece_shapes(1), [other, parts], heavy,
+            [field, field, extra, extra, piece_shape(1)], [other, parts], heavy,
             [table, *arrived, image, own_extra, jump_lift, scale, diag, off, coupling, *older],
         )
         fields.append(newest)

time: 70.1 us -> 75.2 us (1.073)
  blocking collectives: 0 us -> 46.1 us
  starting transfers between devices: 35.9 us -> 4.44 us
  waiting for transfers between devices: 16.6 us -> 9.01 us
  local copies, waits for them, and re-layouts: 1.37 us -> 0 us
    all_to_all x0 -> x5, blocking collectives: none -> 46.1 us  [exchange(): lax.all_to_all(pieces, 'sub', 0, 0, axis_index_groups=sides, tiled=True)]
    ppermute x35 -> x5, starting transfers between devices: 31.4 us -> 0.01 us  [exchange(): lax.ppermute(same, 'sub', [(t, t ^ 1) for t in range(z.peers)])]
    ppermute x35 -> x5, waiting for transfers between devices: 13.2 us -> 5.61 us  [exchange(): lax.ppermute(same, 'sub', [(t, t ^ 1) for t in range(z.peers)])]
    unnamed x4 -> x0, local copies, waits for them, and re-layouts: 1.37 us -> none
  transfers between devices with their start and end apart: 38 -> 8, of which waited for: 20 -> 6; matrix products, arithmetic and copies ran while one was open for 0% -> 0% of each run, Pallas kernels for 1% -> 4%
where the time goes in v4:
time: 75.2 us; the launch traced here: 74.9 us
  blocking collectives  46.1 us (61%)
  Pallas kernels  14.7 us (20%)
  waiting for transfers between devices  9.01 us (12%)
  starting transfers between devices  4.44 us (6%)
    all_to_all x5, blocking collectives, exchange(): lax.all_to_all(pieces, 'sub', 0, 0, axis_index_groups=sides, tiled=True)  46.1 us
    pallas_call x10, Pallas kernels, call(): pl.pallas_call(body, out_shape=shapes, in_specs=specs, out_specs=[SMEM if...  14.7 us
    ppermute x5, waiting for transfers between devices, exchange(): lax.ppermute(same, 'sub', [(t, t ^ 1) for t in range(z.peers)])  5.61 us
    ppermute x3, starting transfers between devices, on_device(): lax.ppermute(own_gram, 'group', [(a, a ^ k if power else (a + k) % z.grou...  4.43 us
    ppermute x3, waiting for transfers between devices, on_device(): lax.ppermute(own_gram, 'group', [(a, a ^ k if power else (a + k) % z.grou...  3.41 us
  transfers between devices with their start and end apart: 8, of which 6 were waited for; matrix products, arithmetic and copies ran while one was open for 0% of the time, Pallas kernels for 4%

profile of v4, /device:TPU:0, one launch (start us, length us, event | category | flops | bytes accessed | tf_op | source)
XLA Modules:
  0.0 74.9 jit_solution(10155996977382687708)
XLA Ops:
  0.6 1.1 %shard_map.105 = (s32[72]{0:T(128)S(4)}, f32[16,8,256]{2,1,0:T(8,128)S(1)}, f32[16,8,256]{2,1,0:T(8,128)S(1)}, f32[16,256]{1,0:T(8,128)S(1)}, bf16[8,4096]{1,0:T...) custom-call(s32[1,16]{1,0:T(1,128)} %partner.1, s32[1,16]{1,0:T(1,128)} %pattern.1, f32[8,16,256]{2,1,0:T(8,128)} %load.1, ...), custom_call_target="tpu_custom_call" | custom-call | flops 4000000 | bytes 250000 | tf_op jit(solution)/shard_map/pallas_call | solution.py:376
  1.7 12.1 %all_to_all.25.rest_0_.same = f32[4,2,12,8,128]{4,3,2,1,0:T(8,128)S(1)} all-to-all(f32[4,2,12,8,128]{4,3,2,1,0:T(8,128)S(1)} %get-tuple-element.32), channel_id=1, replica_groups={{0,2,4,6},{1,3,5,7},{8,10,12,14},{9,11,13,15},{16,18,20,22},{17,19,21,2..., dimensions={0} | all-to-all | bytes 786432 | tf_op jit(solution)/shard_map/all_to_all | solution.py:418
  13.8 0.0 collective-permute-start
  13.8 2.3 %shard_map.104 = (f32[64,64]{1,0:T(8,128)S(1)}, bf16[16,256,256]{2,1,0:T(8,128)(2,1)S(1)}, bf16[16,256,256]{2,1,0:T(8,128)(2,1)S(1)}) custom-call(s32[1,64]{1,0:T(1,128)} %index_in.1, f32[32,32]{1,0:T(8,128)} %inverse_in.1, bf16[16,256,256]{2,1,0:T(8,128)(2,1)} %diag.1, bf16[16,256,256]{2,1,0:T(8,128)(2,1)} %off.1), custom_call_target="tpu_custom_call" | custom-call | flops 600000000 | bytes 37500000 | tf_op jit(solution)/shard_map/pallas_call | solution.py:376
  16.1 0.0 collective-permute-done.rest_1_.across
  16.1 2.0 %shard_map.106 = (f32[16,8,256]{2,1,0:T(8,128)S(1)}, f32[16,8,256]{2,1,0:T(8,128)S(1)}, f32[8,128]{1,0:T(8,128)S(1)}, f32[4,2,7,8,128]{4,3,2,1,0:T(8,128)S(1)}) custom-call(s32[72]{0:T(128)S(4)} %get-tuple-element.31.table, f32[4,2,12,8,128]{4,3,2,1,0:T(8,128)S(1)} %all_to_all.25.rest_0_.same, f32[4,2,12,8,128]{4,3,2,1,0:T(8,128)S(1)} %collective-permute-done.rest_1_.across, ...), custom_call_target="tpu_custom_call" | custom-call | flops 600000000 | bytes 37500000 | tf_op jit(solution)/shard_map/pallas_call | solution.py:376
  18.1 8.8 %all_to_all.26.rest_0_ = f32[4,2,7,8,128]{4,3,2,1,0:T(8,128)S(1)} all-to-all(f32[4,2,7,8,128]{4,3,2,1,0:T(8,128)S(1)} %get-tuple-element.38), channel_id=1, replica_groups={{0,2,4,6},{1,3,5,7},{8,10,12,14},{9,11,13,15},{16,18,20,22},{17,19,21,2..., dimensions={0} | all-to-all | bytes 458752 | tf_op jit(solution)/shard_map/all_to_all | solution.py:418
  26.9 0.0 collective-permute-start.1
  26.9 0.3 shard_map.107.rest_4_.jump_lift
  27.2 1.1 %collective-permute-done.1.rest_1_ = f32[4,2,7,8,128]{4,3,2,1,0:T(8,128)S(1)} collective-permute-done((f32[4,2,7,8,128]{4,3,2,1,0:T(8,128)S(1)}, f32[4,2,7,8,128]{4,3,2,1,0:T(8,128)S(1)}, u32[]{:S(2)}, u32[]{:S(2)}) %collective-permute-start.1) | collective-permute-done | bytes 229408 | tf_op jit(solution)/shard_map/ppermute | solution.py:419
  28.4 2.1 %shard_map.108 = (f32[16,8,256]{2,1,0:T(8,128)S(1)}, f32[16,8,256]{2,1,0:T(8,128)S(1)}, f32[8,128]{1,0:T(8,128)S(1)}, f32[8,128]{1,0:T(8,128)S(1)}, f32[4,2,7,8,128]{4,3,2,1,0:T(8,128)S(1)}) custom-call(s32[72]{0:T(128)S(4)} %get-tuple-element.31.table, f32[4,2,7,8,128]{4,3,2,1,0:T(8,128)S(1)} %all_to_all.26.rest_0_, ...), custom_call_target="tpu_custom_call" | custom-call | flops 600000000 | bytes 37500000 | tf_op jit(solution)/shard_map/pallas_call | solution.py:376
  30.5 8.4 %all_to_all.27.rest_0_ = f32[4,2,7,8,128]{4,3,2,1,0:T(8,128)S(1)} all-to-all(f32[4,2,7,8,128]{4,3,2,1,0:T(8,128)S(1)} %get-tuple-element.42), channel_id=1, replica_groups={{0,2,4,6},{1,3,5,7},{8,10,12,14},{9,11,13,15},{16,18,20,22},{17,19,21,2..., dimensions={0} | all-to-all | bytes 458752 | tf_op jit(solution)/shard_map/all_to_all | solution.py:418
  38.9 0.0 collective-permute-start.2
  38.9 1.5 %collective-permute-done.2.rest_1_ = f32[4,2,7,8,128]{4,3,2,1,0:T(8,128)S(1)} collective-permute-done((f32[4,2,7,8,128]{4,3,2,1,0:T(8,128)S(1)}, f32[4,2,7,8,128]{4,3,2,1,0:T(8,128)S(1)}, u32[]{:S(2)}, u32[]{:S(2)}) %collective-permute-start.2) | collective-permute-done | bytes 229408 | tf_op jit(solution)/shard_map/ppermute | solution.py:419
  40.4 2.2 %shard_map.109 = (f32[16,8,256]{2,1,0:T(8,128)S(1)}, f32[16,8,256]{2,1,0:T(8,128)S(1)}, f32[8,128]{1,0:T(8,128)S(1)}, f32[8,128]{1,0:T(8,128)S(1)}, f32[4,2,7,8,128]{4,3,2,1,0:T(8,128)S(1)}) custom-call(s32[72]{0:T(128)S(4)} %get-tuple-element.31.table, f32[4,2,7,8,128]{4,3,2,1,0:T(8,128)S(1)} %all_to_all.27.rest_0_, ...), custom_call_target="tpu_custom_call" | custom-call | flops 600000000 | bytes 37500000 | tf_op jit(solution)/shard_map/pallas_call | solution.py:376
  42.5 8.4 %all_to_all.28.rest_0_ = f32[4,2,7,8,128]{4,3,2,1,0:T(8,128)S(1)} all-to-all(f32[4,2,7,8,128]{4,3,2,1,0:T(8,128)S(1)} %get-tuple-element.45), channel_id=1, replica_groups={{0,2,4,6},{1,3,5,7},{8,10,12,14},{9,11,13,15},{16,18,20,22},{17,19,21,2..., dimensions={0} | all-to-all | bytes 458752 | tf_op jit(solution)/shard_map/all_to_all | solution.py:418
  51.0 0.0 collective-permute-start.3
  51.0 1.5 %collective-permute-done.3.rest_1_ = f32[4,2,7,8,128]{4,3,2,1,0:T(8,128)S(1)} collective-permute-done((f32[4,2,7,8,128]{4,3,2,1,0:T(8,128)S(1)}, f32[4,2,7,8,128]{4,3,2,1,0:T(8,128)S(1)}, u32[]{:S(2)}, u32[]{:S(2)}) %collective-permute-start.3) | collective-permute-done | bytes 229408 | tf_op jit(solution)/shard_map/ppermute | solution.py:419
  52.4 2.2 %shard_map.110 = (f32[16,8,256]{2,1,0:T(8,128)S(1)}, f32[16,8,256]{2,1,0:T(8,128)S(1)}, f32[8,128]{1,0:T(8,128)S(1)}, f32[8,128]{1,0:T(8,128)S(1)}, f32[4,2,7,8,128]{4,3,2,1,0:T(8,128)S(1)}) custom-call(s32[72]{0:T(128)S(4)} %get-tuple-element.31.table, f32[4,2,7,8,128]{4,3,2,1,0:T(8,128)S(1)} %all_to_all.28.rest_0_, ...), custom_call_target="tpu_custom_call" | custom-call | flops 600000000 | bytes 37500000 | tf_op jit(solution)/shard_map/pallas_call | solution.py:376
  54.6 8.4 %all_to_all.29.rest_0_ = f32[4,2,7,8,128]{4,3,2,1,0:T(8,128)S(1)} all-to-all(f32[4,2,7,8,128]{4,3,2,1,0:T(8,128)S(1)} %get-tuple-element.52), channel_id=1, replica_groups={{0,2,4,6},{1,3,5,7},{8,10,12,14},{9,11,13,15},{16,18,20,22},{17,19,21,2..., dimensions={0} | all-to-all | bytes 458752 | tf_op jit(solution)/shard_map/all_to_all | solution.py:418
  63.0 0.0 collective-permute-start.4
  63.1 1.5 %collective-permute-done.4.rest_1_ = f32[4,2,7,8,128]{4,3,2,1,0:T(8,128)S(1)} collective-permute-done((f32[4,2,7,8,128]{4,3,2,1,0:T(8,128)S(1)}, f32[4,2,7,8,128]{4,3,2,1,0:T(8,128)S(1)}, u32[]{:S(2)}, u32[]{:S(2)}) %collective-permute-start.4) | collective-permute-done | bytes 229408 | tf_op jit(solution)/shard_map/ppermute | solution.py:419
  64.5 0.3 shard_map.111.rest_0_
  64.8 3.6 %collective-permute-start.7 = (f32[8,128]{1,0:T(8,128)S(1)}, f32[8,128]{1,0:T(8,128)S(1)}, u32[]{:S(2)}, u32[]{:S(2)}) collective-permute-start(f32[8,128]{1,0:T(8,128)S(1)} %shard_map.111.rest_0_), channel_id=1, source_target_pairs={{0,24},{8,16},{16,8},{24,0},{1,25},{9,17},{17,9},{25,1},{2,26},{10... | collective-permute-start | bytes 12296 | tf_op jit(solution)/shard_map/ppermute | solution.py:479
  68.5 0.0 collective-permute-start.6
  68.5 0.8 %collective-permute-start.5 = (f32[8,128]{1,0:T(8,128)S(1)}, f32[8,128]{1,0:T(8,128)S(1)}, u32[]{:S(2)}, u32[]{:S(2)}) collective-permute-start(f32[8,128]{1,0:T(8,128)S(1)} %shard_map.111.rest_0_), channel_id=1, source_target_pairs={{0,8},{8,0},{16,24},{24,16},{1,9},{9,1},{17,25},{25,17},{2,10},{10... | collective-permute-start | bytes 12296 | tf_op jit(solution)/shard_map/ppermute | solution.py:479
  69.3 0.3 shard_map.112.rest_8_
  69.6 0.7 collective-permute-done.7.rest_3_
  70.3 2.7 %collective-permute-done.6.rest_2_ = f32[8,128]{1,0:T(8,128)S(1)} collective-permute-done((f32[8,128]{1,0:T(8,128)S(1)}, f32[8,128]{1,0:T(8,128)S(1)}, u32[]{:S(2)}, u32[]{:S(2)}) %collective-permute-start.6) | collective-permute-done | bytes 4128 | tf_op jit(solution)/shard_map/ppermute | solution.py:479
  73.0 0.0 collective-permute-done.5.rest_1_
  73.0 1.9 %shard_map.113 = (f32[8,16,256]{2,1,0:T(8,128)}, f32[8,16,256]{2,1,0:T(8,128)}) custom-call(f32[8,128]{1,0:T(8,128)S(1)} %shard_map.111.rest_0_, f32[8,128]{1,0:T(8,128)S(1)} %collective-permute-done.5.rest_1_, f32[8,128]{1,0:T(8,128)S(1)} %collective-permute-done.6.rest_2_, f32[8,128]{1,0:T(8,128)S(1)} %collective-permute-done.7.rest_3_, ...), custom_call_target="tpu_custom_call" | custom-call | flops 4000000 | bytes 250000 | tf_op jit(solution)/shard_map/pallas_call | solution.py:376
Async XLA Ops:
  13.8 2.3 %collective-permute-start = (f32[4,2,12,8,128]{4,3,2,1,0:T(8,128)S(1)}, f32[4,2,12,8,128]{4,3,2,1,0:T(8,128)S(1)}, u32[]{:S(2)}, u32[]{:S(2)}) collective-permute-start(f32[4,2,12,8,128]{4,3,2,1,0:T(8,128)S(1)} %all_to_all.25.rest_0_.same), channel_id=1, source_target_pairs={{0,1},{1,0},{2,3},{3,2},{4,5},{5,4},{6,7},{7,6},{8,9},{9,8},{10,11... | collective-permute-start | bytes 1179656 | tf_op jit(solution)/shard_map/ppermute | solution.py:419
  26.9 1.5 %collective-permute-start.1 = (f32[4,2,7,8,128]{4,3,2,1,0:T(8,128)S(1)}, f32[4,2,7,8,128]{4,3,2,1,0:T(8,128)S(1)}, u32[]{:S(2)}, u32[]{:S(2)}) collective-permute-start(f32[4,2,7,8,128]{4,3,2,1,0:T(8,128)S(1)} %all_to_all.26.rest_0_), channel_id=1, source_target_pairs={{0,1},{1,0},{2,3},{3,2},{4,5},{5,4},{6,7},{7,6},{8,9},{9,8},{10,11... | collective-permute-start | bytes 688136 | tf_op jit(solution)/shard_map/ppermute | solution.py:419
  38.9 1.5 %collective-permute-start.2 = (f32[4,2,7,8,128]{4,3,2,1,0:T(8,128)S(1)}, f32[4,2,7,8,128]{4,3,2,1,0:T(8,128)S(1)}, u32[]{:S(2)}, u32[]{:S(2)}) collective-permute-start(f32[4,2,7,8,128]{4,3,2,1,0:T(8,128)S(1)} %all_to_all.27.rest_0_), channel_id=1, source_target_pairs={{0,1},{1,0},{2,3},{3,2},{4,5},{5,4},{6,7},{7,6},{8,9},{9,8},{10,11... | collective-permute-start | bytes 688136 | tf_op jit(solution)/shard_map/ppermute | solution.py:419
  51.0 1.5 %collective-permute-start.3 = (f32[4,2,7,8,128]{4,3,2,1,0:T(8,128)S(1)}, f32[4,2,7,8,128]{4,3,2,1,0:T(8,128)S(1)}, u32[]{:S(2)}, u32[]{:S(2)}) collective-permute-start(f32[4,2,7,8,128]{4,3,2,1,0:T(8,128)S(1)} %all_to_all.28.rest_0_), channel_id=1, source_target_pairs={{0,1},{1,0},{2,3},{3,2},{4,5},{5,4},{6,7},{7,6},{8,9},{9,8},{10,11... | collective-permute-start | bytes 688136 | tf_op jit(solution)/shard_map/ppermute | solution.py:419
  63.0 1.5 %collective-permute-start.4 = (f32[4,2,7,8,128]{4,3,2,1,0:T(8,128)S(1)}, f32[4,2,7,8,128]{4,3,2,1,0:T(8,128)S(1)}, u32[]{:S(2)}, u32[]{:S(2)}) collective-permute-start(f32[4,2,7,8,128]{4,3,2,1,0:T(8,128)S(1)} %all_to_all.29.rest_0_), channel_id=1, source_target_pairs={{0,1},{1,0},{2,3},{3,2},{4,5},{5,4},{6,7},{7,6},{8,9},{9,8},{10,11... | collective-permute-start | bytes 688136 | tf_op jit(solution)/shard_map/ppermute | solution.py:419
  64.8 5.4 %collective-permute-start.7 = (f32[8,128]{1,0:T(8,128)S(1)}, f32[8,128]{1,0:T(8,128)S(1)}, u32[]{:S(2)}, u32[]{:S(2)}) collective-permute-start(f32[8,128]{1,0:T(8,128)S(1)} %shard_map.111.rest_0_), channel_id=1, source_target_pairs={{0,24},{8,16},{16,8},{24,0},{1,25},{9,17},{17,9},{25,1},{2,26},{10... | collective-permute-start | bytes 12296 | tf_op jit(solution)/shard_map/ppermute | solution.py:479
  68.5 4.5 %collective-permute-start.6 = (f32[8,128]{1,0:T(8,128)S(1)}, f32[8,128]{1,0:T(8,128)S(1)}, u32[]{:S(2)}, u32[]{:S(2)}) collective-permute-start(f32[8,128]{1,0:T(8,128)S(1)} %shard_map.111.rest_0_), channel_id=1, source_target_pairs={{0,16},{8,24},{16,0},{24,8},{1,17},{9,25},{17,1},{25,9},{2,18},{10... | collective-permute-start | bytes 12296 | tf_op jit(solution)/shard_map/ppermute | solution.py:479
  68.5 4.5 %collective-permute-start.5 = (f32[8,128]{1,0:T(8,128)S(1)}, f32[8,128]{1,0:T(8,128)S(1)}, u32[]{:S(2)}, u32[]{:S(2)}) collective-permute-start(f32[8,128]{1,0:T(8,128)S(1)} %shard_map.111.rest_0_), channel_id=1, source_target_pairs={{0,8},{8,0},{16,24},{24,16},{1,9},{9,1},{17,25},{25,17},{2,10},{10... | collective-permute-start | bytes 12296 | tf_op jit(solution)/shard_map/ppermute | solution.py:479

commit v5 on v4

--- a/solution.py
+++ b/solution.py
@@ -62,8 +62,10 @@
         self.extra_chunks = -(-(self.gram_lane + ENTRIES) // LANES)
         self.extra = self.extra_chunks * LANES
         self.halves = self.width // LANES
-        self.pairs = self.peers // 2
-        self.masks = range(1, self.peers)
+        distances = range(2, self.peers, 2)
+        self.paired = [m for m in distances if m & (m - 1) == 0]
+        self.direct = [n for m in distances if m & (m - 1) for n in (m + 1, m)]
+        self.handed = [1] + [m + 1 for m in self.paired]
         self.slots = self.peers * self.capacity
         self.inverse = self.slots
         self.pattern = self.inverse + self.blocks
@@ -72,6 +74,21 @@
 
     def rows(self, kinds):
         return kinds * self.capacity * self.halves
+
+    def sent(self, kinds):
+        rows = self.rows(kinds)
+        near = len(self.handed) * rows
+        return [near] + [rows] * len(self.direct) + [2 * rows] * len(self.paired)
+
+    def first(self):
+        return 1 + len(self.direct)
+
+    def sources(self):
+        found = [(1, 0, 0)]
+        found += [(m, 1 + k, 0) for k, m in enumerate(self.direct)]
+        for k, m in enumerate(self.paired):
+            found += [(m + side, self.first() + k, side) for side in range(2)]
+        return found
 
 
 def fill_table(z, partner, pattern, table, counts):
@@ -92,36 +109,51 @@
         table[z.partner + i] = mate
 
 
-def pair_of(m):
-    return (lax.axis_index("sub") ^ m) >> 1
-
-
-def fill_pieces(z, table, sources, pieces):
-    for m in z.masks:
-        pair = pair_of(m)
-        row = 0
-        for source in sources:
-            for r in range(z.capacity):
-                block = jnp.minimum(table[m * z.capacity + r], z.blocks - 1)
-                value = source[block]
-                for h in range(z.halves):
-                    pieces[pair, m % 2, row] = value[:, h * LANES : (h + 1) * LANES]
-                    row += 1
-
-
-def place(z, table, arrived, kind, target):
-    for m in z.masks:
-        pair = pair_of(m)
-        row = z.rows(kind)
+def fill_piece(z, table, sources, m, piece, row):
+    for source in sources:
+        for r in range(z.capacity):
+            value = source[jnp.minimum(table[m * z.capacity + r], z.blocks - 1)]
+            for h in range(z.halves):
+                piece[row] = value[:, h * LANES : (h + 1) * LANES]
+                row += 1
+
+
+def fill_first(z, table, sources, pieces):
+    rows = z.rows(len(sources))
+    for k, m in enumerate(z.handed):
+        fill_piece(z, table, sources, m, pieces[0], k * rows)
+    for m, piece in zip(z.direct, pieces[1:]):
+        fill_piece(z, table, sources, m, piece, 0)
+
+
+def relay(z, kinds, table, *rest):
+    sources, rest = rest[:kinds], rest[kinds:]
+    chunks = z.extra_chunks if kinds == 1 else 0
+    if chunks:
+        own_extra, rest = rest[0], rest[1:]
+    near, pieces = rest[0], rest[1:]
+    rows = z.rows(kinds)
+    for k, (m, piece) in enumerate(zip(z.paired, pieces)):
+        fill_piece(z, table, sources, m, piece, 0)
+        for row in range(rows):
+            piece[rows + row] = near[(k + 1) * rows + row]
+        for j in range(chunks):
+            mine = own_extra[:, j * LANES : (j + 1) * LANES]
+            piece[2 * rows + j] = mine + near[z.sent(1)[0] + j]
+
+
+def place(z, table, arrived, kind, kinds, target):
+    for m, transfer, piece in z.sources():
+        row = piece * z.rows(kinds) + z.rows(kind)
         for r in range(z.capacity):
             block = table[m * z.capacity + r]
             for h in range(z.halves):
-                target[block, :, h * LANES : (h + 1) * LANES] = arrived[m % 2][pair, m % 2, row]
+                target[block, :, h * LANES : (h + 1) * LANES] = arrived[transfer][row]
                 row += 1
 
 
-def begin(z, partner, pattern, load, scale, coupling, table, field, lift, scale_out, coupling_out, pieces, *scratch):
-    here, partner_here, pattern_here, counts, sems = scratch
+def begin(z, partner, pattern, load, scale, coupling, table, field, lift, scale_out, coupling_out, *rest):
+    pieces, (here, partner_here, pattern_here, counts, sems) = rest[:-5], rest[-5:]
     copies = [
         pltpu.make_async_copy(a, b, sems.at[k])
         for k, (a, b) in enumerate(
@@ -145,7 +177,7 @@
         field[i] = here[:, i, :]
         part = coupling_out[:, i * z.width : (i + 1) * z.width].astype(F32)
         lift[i] = scale_out[i : i + 1, :] * part
-    fill_pieces(z, table, [field, lift], pieces)
+    fill_first(z, table, [field, lift], pieces)
 
 
 def split3(a):
@@ -177,8 +209,9 @@
     copies[3].wait()
 
 
-def build_lift(z, table, operator, lift, same, across, jump_lift, other):
-    place(z, table, (same, across), 1, other)
+def build_lift(z, table, operator, lift, *rest):
+    pieces, (jump_lift, other) = rest[:-2], rest[-2:]
+    place(z, table, pieces, 1, 2, other)
     me = lax.axis_index("sub")
     own = operator[pl.ds(pl.multiple_of(me * z.corners, z.corners), z.corners), :]
     for i in range(z.blocks):
@@ -193,11 +226,8 @@
 
 def extra_sum(z, own, arrived):
     total = own[...]
-    for m in z.masks:
-        pair = pair_of(m)
-        total = total + jnp.concatenate(
-            [arrived[m % 2][pair, m % 2, z.rows(1) + j] for j in range(z.extra_chunks)], axis=1
-        )
+    for rows, piece in zip(z.sent(1), arrived):
+        total = total + jnp.concatenate([piece[rows + j] for j in range(z.extra_chunks)], axis=1)
     return total
 
 
@@ -217,10 +247,11 @@
 
 
 def apply_round(z, step, table, *rest):
+    count = len(z.sent(1))
     first, last = step == 1, step == ITERS
     rest = list(rest)
     take = lambda n: [rest.pop(0) for _ in range(n)]
-    arrived = take(2)
+    arrived = take(count)
     (before,) = take(1)
     if not first:
         own_extra, jump_lift = take(2)
@@ -229,8 +260,10 @@
     field, image = take(2)
     if not first:
         (total_out,) = take(1)
-    extra, pieces, other, parts = rest
-    place(z, table, arrived, 0, other)
+    (extra,) = take(1)
+    pieces = take(z.first())
+    other, parts = rest
+    place(z, table, arrived, 0, 2 if first else 1, other)
     if not first:
         total = extra_sum(z, own_extra, arrived)
         total_out[...] = total
@@ -255,7 +288,7 @@
         result = row * (row * field[i] + fold(coupled))
         image[i] = result
         top = jnp.maximum(top, jnp.abs(result))
-    fill_pieces(z, table, [image], pieces)
+    fill_first(z, table, [image], pieces)
     me = lax.axis_index("sub")
     lanes = lane_ids((z.columns, z.extra))
     sums = fold(partial)
@@ -273,14 +306,14 @@
                 acc = acc + a[i] * b[i]
             tile = jnp.where(lanes == z.gram_lane + entry, lane_sum(acc), tile)
     extra[...] = tile
-    for m in z.masks:
-        pair = pair_of(m)
+    for rows, piece in zip(z.sent(1), pieces):
         for j in range(z.extra_chunks):
-            pieces[pair, m % 2, z.rows(1) + j] = tile[:, j * LANES : (j + 1) * LANES]
+            piece[rows + j] = tile[:, j * LANES : (j + 1) * LANES]
 
 
 def cluster_gram(z, operator, own_extra, *rest):
-    arrived, totals, (gram,) = rest[:2], rest[2:-1], rest[-1:]
+    count = len(z.sent(1))
+    arrived, totals, (gram,) = rest[:count], rest[count:-1], rest[-1:]
     total = extra_sum(z, own_extra, arrived)
     totals = [t[...] for t in totals]
     partials = [t[:, : z.all_corners] for t in totals + [total]]
@@ -300,7 +333,7 @@
 
 def last_vector(z, table, before, own_extra, jump_lift, *rest):
     arrived, (field, other) = rest[:-2], rest[-2:]
-    place(z, table, arrived, 0, other)
+    place(z, table, arrived, 0, 1, other)
     rows = corner_rows(z, extra_sum(z, own_extra, arrived))
     for i in range(z.blocks):
         field[i] = before[i] - other[i] + fold(dot(rows, jump_lift[i], NN))
@@ -310,29 +343,41 @@
     grams, rest = rest[: z.groups], rest[z.groups :]
     fields, (multipliers, residual) = rest[:-2], rest[-2:]
     tables = [gram[...] for gram in grams]
-    mine = tables[0]
-    one = jnp.ones((z.columns, 1), F32)
+    shape = (z.columns, LANES)
+    lanes = lane_ids(shape)
+
+    def column(table, lane):
+        return jnp.broadcast_to(table[:, lane : lane + 1], shape)
+
+    one = jnp.ones(shape, F32)
     ratio = [[one] * z.groups]
-    own_ratio = [one]
     growth = [None]
     for step in range(1, ITERS + 1):
+        grown = ratio[-1]
         if step < ITERS:
-            lane = ENTRIES + step - 1
-            grown = [q * t[:, lane : lane + 1] for q, t in zip(ratio[-1], tables)]
-            own = own_ratio[-1] * mine[:, lane : lane + 1]
-        else:
-            grown, own = ratio[-1], own_ratio[-1]
+            grown = [q * column(t, ENTRIES + step - 1) for q, t in zip(grown, tables)]
         top = functools.reduce(jnp.maximum, grown)
-        ratio.append([q / top for q in grown])
-        own_ratio.append(own / top)
+        inverse = 1.0 / top
+        ratio.append([q * inverse for q in grown])
         growth.append(top)
+    pairs = PAIRS + [(i, ITERS) for i in range(ITERS)]
+
+    def lanes_of(side, level):
+        chosen = [e for e, pair in enumerate(pairs) if pair[side] == level]
+        return functools.reduce(jnp.logical_or, [lanes == e for e in chosen])
+
+    where = [[lanes_of(side, level) for level in range(side, ITERS + side)] for side in range(2)]
+    total = jnp.zeros(shape, F32)
+    for g, table in enumerate(tables):
+        for side in range(2):
+            weight = one
+            for level in range(1, ITERS + side):
+                weight = jnp.where(where[side][level - side], ratio[level][g], weight)
+            table = table * weight
+        total = total + table
     gram = {}
-    pairs = PAIRS + [(i, ITERS) for i in range(ITERS)]
     for entry, (i, j) in enumerate(pairs):
-        value = 0.0
-        for g in range(z.groups):
-            value = value + ratio[i][g] * ratio[j][g] * tables[g][:, entry : entry + 1]
-        gram[i, j] = gram[j, i] = value
+        gram[i, j] = gram[j, i] = column(total, entry)
 
     def inner(a, b):
         return sum(a[i] * sum(gram[i, j] * b[j] for j in b) for i in a)
@@ -354,12 +399,14 @@
             following = inner(rest_of, rest_of)
             way = add(rest_of, following / norm, way)
             norm = following
-    found = {i: value * own_ratio[i] for i, value in found.items()}
-    rest_of = {i: value * own_ratio[i] for i, value in rest_of.items()}
-    for i in range(z.blocks):
-        values = [f[i] for f in fields]
-        multipliers[:, i, :] = sum(c * values[j] for j, c in found.items())
-        residual[:, i, :] = sum(c * values[j] for j, c in rest_of.items())
+    found = {i: value * ratio[i][0] for i, value in found.items()}
+    rest_of = {i: value * ratio[i][0] for i, value in rest_of.items()}
+    for i in range(z.blocks):
+        for h in range(z.halves):
+            part = slice(h * LANES, (h + 1) * LANES)
+            values = [f[i, :, part] for f in fields]
+            multipliers[:, i, part] = sum(c * values[j] for j, c in found.items())
+            residual[:, i, part] = sum(c * values[j] for j, c in rest_of.items())
 
 
 def call(body, outs, scratch, cost, args, table=True, away=()):
@@ -406,19 +453,25 @@
     gram = ((cols, 128), F32)
     light, heavy = 4_000_000, 600_000_000
 
-    def piece_shape(kinds):
-        rows = z.rows(kinds) + (z.extra_chunks if kinds == 1 else 0)
-        return ((z.pairs, 2, rows, cols, LANES), F32)
+    def piece_shapes(kinds):
+        chunks = z.extra_chunks if kinds == 1 else 0
+        return [((rows + chunks, cols, LANES), F32) for rows in z.sent(kinds)]
 
     def kernel(body, *extra_args):
         return functools.partial(body, z, *extra_args)
 
-    def exchange(pieces):
-        sides = [list(range(side, z.peers, 2)) for side in range(2)]
-        same = lax.all_to_all(pieces, "sub", 0, 0, axis_index_groups=sides, tiled=True)
-        return same, lax.ppermute(same, "sub", [(t, t ^ 1) for t in range(z.peers)])
-
-    table, loaded, lift, scale, coupling, pieces = call(
+    def across(piece, m):
+        return lax.ppermute(piece, "sub", [(t, t ^ m) for t in range(z.peers)])
+
+    def exchange(kinds, pieces, *sources):
+        arrived = [across(piece, m) for m, piece in zip([1] + z.direct, pieces)]
+        more = call(
+            kernel(relay, kinds), piece_shapes(kinds)[z.first() :], [], light,
+            [table, *sources, arrived[0]],
+        )
+        return arrived + [across(piece, m) for m, piece in zip(z.paired, more)]
+
+    table, loaded, lift, scale, coupling, *pieces = call(
         kernel(begin),
         [
             ((z.table,), jnp.int32),
@@ -426,8 +479,8 @@
             field,
             (row_scale.shape, F32),
             (corner_coupling.shape, BF16),
-            piece_shape(2),
-        ],
+        ]
+        + piece_shapes(2)[: z.first()],
         [
             pltpu.VMEM(load.shape, F32),
             pltpu.SMEM(partner.shape, jnp.int32),
@@ -439,7 +492,7 @@
         [partner, off_pattern, load, row_scale, corner_coupling],
         False, range(5),
     )
-    arrived = exchange(pieces)
+    arrived = exchange(2, pieces, loaded, lift)
     weight = (diag_blocks.shape, BF16)
     operator, diag, off = call(
         kernel(prepare), [((z.all_corners, z.all_corners), F32), weight, weight],
@@ -450,27 +503,27 @@
         ],
         heavy, [corner_index, coarse_inverse, diag_blocks, off_blocks], False, range(4),
     )
-    newest, image, own_extra, pieces = call(
+    newest, image, own_extra, *pieces = call(
         kernel(apply_round, 1),
-        [field, field, extra, piece_shape(1)], [other, parts], heavy,
+        [field, field, extra] + piece_shapes(1)[: z.first()], [other, parts], heavy,
         [table, *arrived, loaded, scale, diag, off, coupling],
     )
     (jump_lift,) = call(
         kernel(build_lift), [((blocks, 2 * z.all_corners, width), BF16)], [other], heavy,
         [table, operator, lift, *arrived],
     )
-    arrived = exchange(pieces)
+    arrived = exchange(1, pieces, image, own_extra)
     fields, totals = [newest], []
     for step in range(2, ITERS + 1):
         older = fields if step == ITERS else []
-        newest, image, total, own_extra, pieces = call(
+        newest, image, total, own_extra, *pieces = call(
             kernel(apply_round, step),
-            [field, field, extra, extra, piece_shape(1)], [other, parts], heavy,
+            [field, field, extra, extra] + piece_shapes(1)[: z.first()], [other, parts], heavy,
             [table, *arrived, image, own_extra, jump_lift, scale, diag, off, coupling, *older],
         )
         fields.append(newest)
         totals.append(total)
-        arrived = exchange(pieces)
+        arrived = exchange(1, pieces, image, own_extra)
     (own_gram,) = call(
         kernel(cluster_gram), [gram], [], light, [operator, own_extra, *arrived, *totals], False
     )

time: 75.2 us -> 67.1 us (0.89)
  blocking collectives: 46.1 us -> 0 us
  starting transfers between devices: 4.44 us -> 30.4 us
  waiting for transfers between devices: 9.01 us -> 21.9 us
    all_to_all x5 -> x0, blocking collectives: 46.1 us -> none  [exchange(): lax.all_to_all(pieces, 'sub', 0, 0, axis_index_groups=sides, tiled=True)]
    ppermute x5 -> x25, starting transfers between devices: 0.01 us -> 25.9 us  [across(): return lax.ppermute(piece, 'sub', [(t, t ^ m) for t in range(z.peers)])]
    ppermute x5 -> x25, waiting for transfers between devices: 5.61 us -> 18.5 us  [across(): return lax.ppermute(piece, 'sub', [(t, t ^ m) for t in range(z.peers)])]
    pallas_call x10 -> x15, Pallas kernels: 14.7 us -> 14 us  [call(): pl.pallas_call(body, out_shape=shapes, in_specs=specs, out_specs=[SMEM if...]
  transfers between devices with their start and end apart: 8 -> 28, of which waited for: 6 -> 17; matrix products, arithmetic and copies ran while one was open for 0% -> 0% of each run, Pallas kernels for 4% -> 4%
where the time goes in v5:
time: 67.1 us; the launch traced here: 67 us
  starting transfers between devices  30.4 us (45%)
  waiting for transfers between devices  21.9 us (33%)
  Pallas kernels  14 us (21%)
  between operations  0.74 us (1%)
    ppermute x25, starting transfers between devices, across(): return lax.ppermute(piece, 'sub', [(t, t ^ m) for t in range(z.peers)])  25.9 us
    ppermute x25, waiting for transfers between devices, across(): return lax.ppermute(piece, 'sub', [(t, t ^ m) for t in range(z.peers)])  18.5 us
    pallas_call x15, Pallas kernels, call(): pl.pallas_call(body, out_shape=shapes, in_specs=specs, out_specs=[SMEM if...  14 us
    ppermute x3, starting transfers between devices, on_device(): lax.ppermute(own_gram, 'group', [(a, a ^ k if power else (a + k) % z.grou...  4.44 us
    ppermute x3, waiting for transfers between devices, on_device(): lax.ppermute(own_gram, 'group', [(a, a ^ k if power else (a + k) % z.grou...  3.42 us
  transfers between devices with their start and end apart: 28, of which 17 were waited for; matrix products, arithmetic and copies ran while one was open for 0% of the time, Pallas kernels for 4%

profile of v5, /device:TPU:0, one launch (start us, length us, event | category | flops | bytes accessed | tf_op | source)
XLA Modules:
  0.0 67.0 jit_solution(6416309063449696557)
XLA Ops:
  0.6 1.1 %shard_map.105 = (s32[72]{0:T(128)S(4)}, f32[16,8,256]{2,1,0:T(8,128)S(1)}, f32[16,8,256]{2,1,0:T(8,128)S(1)}, f32[16,256]{1,0:T(8,128)S(1)}, bf16[8,4096]{1,0:T...) custom-call(s32[1,16]{1,0:T(1,128)} %partner.1, ...), custom_call_target="tpu_custom_call" | custom-call | flops 4000000 | bytes 250000 | tf_op jit(solution)/shard_map/pallas_call | solution.py:423
  2.2 1.0 %collective-permute-done.rest_2_.rest_0_ = f32[36,8,128]{2,1,0:T(8,128)S(1)} collective-permute-done((f32[36,8,128]{2,1,0:T(8,128)S(1)}, f32[36,8,128]{2,1,0:T(8,128)S(1)}, u32[]{:S(2)}, u32[]{:S(2)}) %collective-permute-start) | collective-permute-done | bytes 147488 | tf_op jit(solution)/shard_map/ppermute | solution.py:464
  3.2 2.9 %collective-permute-start.3 = (f32[24,8,128]{2,1,0:T(8,128)S(1)}, f32[24,8,128]{2,1,0:T(8,128)S(1)}, u32[]{:S(2)}, u32[]{:S(2)}) collective-permute-start(f32[24,8,128]{2,1,0:T(8,128)S(1)} %get-tuple-element.57), channel_id=1, source_target_pairs={{0,2},{1,3},{2,0},{3,1},{4,6},{5,7},{6,4},{7,5},{8,10},{9,11},{10,... | collective-permute-start | bytes 294920 | tf_op jit(solution)/shard_map/ppermute | solution.py:464
  6.2 1.5 %collective-permute-start.4 = (f32[24,8,128]{2,1,0:T(8,128)S(1)}, f32[24,8,128]{2,1,0:T(8,128)S(1)}, u32[]{:S(2)}, u32[]{:S(2)}) collective-permute-start(f32[24,8,128]{2,1,0:T(8,128)S(1)} %get-tuple-element.58), channel_id=1, source_target_pairs={{0,4},{1,5},{2,6},{3,7},{4,0},{5,1},{6,2},{7,3},{8,12},{9,13},{10,... | collective-permute-start | bytes 294920 | tf_op jit(solution)/shard_map/ppermute | solution.py:464
  7.7 2.1 %collective-permute-start.2 = (f32[12,8,128]{2,1,0:T(8,128)S(1)}, f32[12,8,128]{2,1,0:T(8,128)S(1)}, u32[]{:S(2)}, u32[]{:S(2)}) collective-permute-start(f32[12,8,128]{2,1,0:T(8,128)S(1)} %get-tuple-element.54), channel_id=1, source_target_pairs={{0,6},{1,7},{2,4},{3,5},{4,2},{5,3},{6,0},{7,1},{8,14},{9,15},{10,... | collective-permute-start | bytes 147464 | tf_op jit(solution)/shard_map/ppermute | solution.py:464
  9.8 2.3 %shard_map.104 = (f32[64,64]{1,0:T(8,128)S(1)}, bf16[16,256,256]{2,1,0:T(8,128)(2,1)S(1)}, bf16[16,256,256]{2,1,0:T(8,128)(2,1)S(1)}) custom-call(s32[1,64]{1,0:T(1,128)} %index_in.1, f32[32,32]{1,0:T(8,128)} %inverse_in.1, bf16[16,256,256]{2,1,0:T(8,128)(2,1)} %diag.1, bf16[16,256,256]{2,1,0:T(8,128)(2,1)} %off.1), custom_call_target="tpu_custom_call" | custom-call | flops 600000000 | bytes 37500000 | tf_op jit(solution)/shard_map/pallas_call | solution.py:423
  13.2 2.0 %shard_map.107 = (f32[16,8,256]{2,1,0:T(8,128)S(1)}, f32[16,8,256]{2,1,0:T(8,128)S(1)}, f32[8,128]{1,0:T(8,128)S(1)}, f32[19,8,128]{2,1,0:T(8,128)S(1)}, f32[7,8...) custom-call(s32[72]{0:T(128)S(4)} %get-tuple-element.51.table, f32[36,8,128]{2,1,0:T(8,128)S(1)} %collective-permute-done.rest_2_.rest_0_, ...), custom_call_target="tpu_custom_call" | custom-call | flops 600000000 | bytes 37500000 | tf_op jit(solution)/shard_map/pallas_call | solution.py:423
  15.3 2.1 %collective-permute-start.6 = (f32[7,8,128]{2,1,0:T(8,128)S(1)}, f32[7,8,128]{2,1,0:T(8,128)S(1)}, u32[]{:S(2)}, u32[]{:S(2)}) collective-permute-start(f32[7,8,128]{2,1,0:T(8,128)S(1)} %get-tuple-element.64), channel_id=1, source_target_pairs={{0,7},{1,6},{2,5},{3,4},{4,3},{5,2},{6,1},{7,0},{8,15},{9,14},{10,... | collective-permute-start | bytes 86024 | tf_op jit(solution)/shard_map/ppermute | solution.py:464
  18.3 1.2 %collective-permute-start.8 = (f32[13,8,128]{2,1,0:T(8,128)S(1)}, f32[13,8,128]{2,1,0:T(8,128)S(1)}, u32[]{:S(2)}, u32[]{:S(2)}) collective-permute-start(f32[13,8,128]{2,1,0:T(8,128)S(1)} %get-tuple-element.68), channel_id=1, source_target_pairs={{0,2},{1,3},{2,0},{3,1},{4,6},{5,7},{6,4},{7,5},{8,10},{9,11},{10,... | collective-permute-start | bytes 159752 | tf_op jit(solution)/shard_map/ppermute | solution.py:464
  19.4 1.5 %collective-permute-start.9 = (f32[13,8,128]{2,1,0:T(8,128)S(1)}, f32[13,8,128]{2,1,0:T(8,128)S(1)}, u32[]{:S(2)}, u32[]{:S(2)}) collective-permute-start(f32[13,8,128]{2,1,0:T(8,128)S(1)} %get-tuple-element.69), channel_id=1, source_target_pairs={{0,4},{1,5},{2,6},{3,7},{4,0},{5,1},{6,2},{7,3},{8,12},{9,13},{10,... | collective-permute-start | bytes 159752 | tf_op jit(solution)/shard_map/ppermute | solution.py:464
  22.5 1.1 %collective-permute-done.9.rest_4_ = f32[13,8,128]{2,1,0:T(8,128)S(1)} collective-permute-done((f32[13,8,128]{2,1,0:T(8,128)S(1)}, f32[13,8,128]{2,1,0:T(8,128)S(1)}, u32[]{:S(2)}, u32[]{:S(2)}) %collective-permute-start.9) | collective-permute-done | bytes 53280 | tf_op jit(solution)/shard_map/ppermute | solution.py:464
  23.6 2.1 %shard_map.110 = (f32[16,8,256]{2,1,0:T(8,128)S(1)}, f32[16,8,256]{2,1,0:T(8,128)S(1)}, f32[8,128]{1,0:T(8,128)S(1)}, f32[8,128]{1,0:T(8,128)S(1)}, f32[19,8,128...) custom-call(s32[72]{0:T(128)S(4)} %get-tuple-element.51.table, ...), custom_call_target="tpu_custom_call" | custom-call | flops 600000000 | bytes 37500000 | tf_op jit(solution)/shard_map/pallas_call | solution.py:423
  25.7 1.3 %collective-permute-done.10.rest_2_.rest_0_ = f32[19,8,128]{2,1,0:T(8,128)S(1)} collective-permute-done((f32[19,8,128]{2,1,0:T(8,128)S(1)}, f32[19,8,128]{2,1,0:T(8,128)S(1)}, u32[]{:S(2)}, u32[]{:S(2)}) %collective-permute-start.10) | collective-permute-done | bytes 77856 | tf_op jit(solution)/shard_map/ppermute | solution.py:464
  28.0 1.2 %collective-permute-start.14 = (f32[13,8,128]{2,1,0:T(8,128)S(1)}, f32[13,8,128]{2,1,0:T(8,128)S(1)}, u32[]{:S(2)}, u32[]{:S(2)}) collective-permute-start(f32[13,8,128]{2,1,0:T(8,128)S(1)} %get-tuple-element.76), channel_id=1, source_target_pairs={{0,4},{1,5},{2,6},{3,7},{4,0},{5,1},{6,2},{7,3},{8,12},{9,13},{10,... | collective-permute-start | bytes 159752 | tf_op jit(solution)/shard_map/ppermute | solution.py:464
  29.8 1.5 %collective-permute-start.12 = (f32[7,8,128]{2,1,0:T(8,128)S(1)}, f32[7,8,128]{2,1,0:T(8,128)S(1)}, u32[]{:S(2)}, u32[]{:S(2)}) collective-permute-start(f32[7,8,128]{2,1,0:T(8,128)S(1)} %get-tuple-element.72), channel_id=1, source_target_pairs={{0,6},{1,7},{2,4},{3,5},{4,2},{5,3},{6,0},{7,1},{8,14},{9,15},{10,... | collective-permute-start | bytes 86024 | tf_op jit(solution)/shard_map/ppermute | solution.py:464
  31.3 2.2 %collective-permute-done.11.rest_1_ = f32[7,8,128]{2,1,0:T(8,128)S(1)} collective-permute-done((f32[7,8,128]{2,1,0:T(8,128)S(1)}, f32[7,8,128]{2,1,0:T(8,128)S(1)}, u32[]{:S(2)}, u32[]{:S(2)}) %collective-permute-start.11) | collective-permute-done | bytes 28704 | tf_op jit(solution)/shard_map/ppermute | solution.py:464
  33.5 1.3 %collective-permute-done.12.rest_2_ = f32[7,8,128]{2,1,0:T(8,128)S(1)} collective-permute-done((f32[7,8,128]{2,1,0:T(8,128)S(1)}, f32[7,8,128]{2,1,0:T(8,128)S(1)}, u32[]{:S(2)}, u32[]{:S(2)}) %collective-permute-start.12) | collective-permute-done | bytes 28704 | tf_op jit(solution)/shard_map/ppermute | solution.py:464
  34.8 2.1 %shard_map.112 = (f32[16,8,256]{2,1,0:T(8,128)S(1)}, f32[16,8,256]{2,1,0:T(8,128)S(1)}, f32[8,128]{1,0:T(8,128)S(1)}, f32[8,128]{1,0:T(8,128)S(1)}, f32[19,8,128...) custom-call(s32[72]{0:T(128)S(4)} %get-tuple-element.51.table, ...), custom_call_target="tpu_custom_call" | custom-call | flops 600000000 | bytes 37500000 | tf_op jit(solution)/shard_map/pallas_call | solution.py:423
  37.0 1.2 %collective-permute-done.15.rest_2_.rest_0_ = f32[19,8,128]{2,1,0:T(8,128)S(1)} collective-permute-done((f32[19,8,128]{2,1,0:T(8,128)S(1)}, f32[19,8,128]{2,1,0:T(8,128)S(1)}, u32[]{:S(2)}, u32[]{:S(2)}) %collective-permute-start.15) | collective-permute-done | bytes 77856 | tf_op jit(solution)/shard_map/ppermute | solution.py:464
  39.2 1.2 %collective-permute-start.19 = (f32[13,8,128]{2,1,0:T(8,128)S(1)}, f32[13,8,128]{2,1,0:T(8,128)S(1)}, u32[]{:S(2)}, u32[]{:S(2)}) collective-permute-start(f32[13,8,128]{2,1,0:T(8,128)S(1)} %get-tuple-element.83), channel_id=1, source_target_pairs={{0,4},{1,5},{2,6},{3,7},{4,0},{5,1},{6,2},{7,3},{8,12},{9,13},{10,... | collective-permute-start | bytes 159752 | tf_op jit(solution)/shard_map/ppermute | solution.py:464
  41.0 1.6 %collective-permute-start.17 = (f32[7,8,128]{2,1,0:T(8,128)S(1)}, f32[7,8,128]{2,1,0:T(8,128)S(1)}, u32[]{:S(2)}, u32[]{:S(2)}) collective-permute-start(f32[7,8,128]{2,1,0:T(8,128)S(1)} %get-tuple-element.79), channel_id=1, source_target_pairs={{0,6},{1,7},{2,4},{3,5},{4,2},{5,3},{6,0},{7,1},{8,14},{9,15},{10,... | collective-permute-start | bytes 86024 | tf_op jit(solution)/shard_map/ppermute | solution.py:464
  42.6 2.2 %collective-permute-done.16.rest_1_ = f32[7,8,128]{2,1,0:T(8,128)S(1)} collective-permute-done((f32[7,8,128]{2,1,0:T(8,128)S(1)}, f32[7,8,128]{2,1,0:T(8,128)S(1)}, u32[]{:S(2)}, u32[]{:S(2)}) %collective-permute-start.16) | collective-permute-done | bytes 28704 | tf_op jit(solution)/shard_map/ppermute | solution.py:464
  44.7 1.3 %collective-permute-done.17.rest_2_ = f32[7,8,128]{2,1,0:T(8,128)S(1)} collective-permute-done((f32[7,8,128]{2,1,0:T(8,128)S(1)}, f32[7,8,128]{2,1,0:T(8,128)S(1)}, u32[]{:S(2)}, u32[]{:S(2)}) %collective-permute-start.17) | collective-permute-done | bytes 28704 | tf_op jit(solution)/shard_map/ppermute | solution.py:464
  46.0 2.2 %shard_map.114 = (f32[16,8,256]{2,1,0:T(8,128)S(1)}, f32[16,8,256]{2,1,0:T(8,128)S(1)}, f32[8,128]{1,0:T(8,128)S(1)}, f32[8,128]{1,0:T(8,128)S(1)}, f32[19,8,128...) custom-call(s32[72]{0:T(128)S(4)} %get-tuple-element.51.table, ...), custom_call_target="tpu_custom_call" | custom-call | flops 600000000 | bytes 37500000 | tf_op jit(solution)/shard_map/pallas_call | solution.py:423
  48.3 1.2 %collective-permute-done.20.rest_2_.rest_0_ = f32[19,8,128]{2,1,0:T(8,128)S(1)} collective-permute-done((f32[19,8,128]{2,1,0:T(8,128)S(1)}, f32[19,8,128]{2,1,0:T(8,128)S(1)}, u32[]{:S(2)}, u32[]{:S(2)}) %collective-permute-start.20) | collective-permute-done | bytes 77856 | tf_op jit(solution)/shard_map/ppermute | solution.py:464
  50.5 1.2 %collective-permute-start.24 = (f32[13,8,128]{2,1,0:T(8,128)S(1)}, f32[13,8,128]{2,1,0:T(8,128)S(1)}, u32[]{:S(2)}, u32[]{:S(2)}) collective-permute-start(f32[13,8,128]{2,1,0:T(8,128)S(1)} %get-tuple-element.93), channel_id=1, source_target_pairs={{0,4},{1,5},{2,6},{3,7},{4,0},{5,1},{6,2},{7,3},{8,12},{9,13},{10,... | collective-permute-start | bytes 159752 | tf_op jit(solution)/shard_map/ppermute | solution.py:464
  52.3 1.6 %collective-permute-start.22 = (f32[7,8,128]{2,1,0:T(8,128)S(1)}, f32[7,8,128]{2,1,0:T(8,128)S(1)}, u32[]{:S(2)}, u32[]{:S(2)}) collective-permute-start(f32[7,8,128]{2,1,0:T(8,128)S(1)} %get-tuple-element.90), channel_id=1, source_target_pairs={{0,6},{1,7},{2,4},{3,5},{4,2},{5,3},{6,0},{7,1},{8,14},{9,15},{10,... | collective-permute-start | bytes 86024 | tf_op jit(solution)/shard_map/ppermute | solution.py:464
  53.9 2.2 %collective-permute-done.21.rest_1_ = f32[7,8,128]{2,1,0:T(8,128)S(1)} collective-permute-done((f32[7,8,128]{2,1,0:T(8,128)S(1)}, f32[7,8,128]{2,1,0:T(8,128)S(1)}, u32[]{:S(2)}, u32[]{:S(2)}) %collective-permute-start.21) | collective-permute-done | bytes 28704 | tf_op jit(solution)/shard_map/ppermute | solution.py:464
  56.0 1.3 %collective-permute-done.22.rest_2_ = f32[7,8,128]{2,1,0:T(8,128)S(1)} collective-permute-done((f32[7,8,128]{2,1,0:T(8,128)S(1)}, f32[7,8,128]{2,1,0:T(8,128)S(1)}, u32[]{:S(2)}, u32[]{:S(2)}) %collective-permute-start.22) | collective-permute-done | bytes 28704 | tf_op jit(solution)/shard_map/ppermute | solution.py:464
  57.6 3.6 %collective-permute-start.27 = (f32[8,128]{1,0:T(8,128)S(1)}, f32[8,128]{1,0:T(8,128)S(1)}, u32[]{:S(2)}, u32[]{:S(2)}) collective-permute-start(f32[8,128]{1,0:T(8,128)S(1)} %shard_map.116.rest_0_), channel_id=1, source_target_pairs={{0,24},{8,16},{16,8},{24,0},{1,25},{9,17},{17,9},{25,1},{2,26},{10... | collective-permute-start | bytes 12296 | tf_op jit(solution)/shard_map/ppermute | solution.py:532
  63.1 2.7 %collective-permute-done.26.rest_2_ = f32[8,128]{1,0:T(8,128)S(1)} collective-permute-done((f32[8,128]{1,0:T(8,128)S(1)}, f32[8,128]{1,0:T(8,128)S(1)}, u32[]{:S(2)}, u32[]{:S(2)}) %collective-permute-start.26) | collective-permute-done | bytes 4128 | tf_op jit(solution)/shard_map/ppermute | solution.py:532
  65.8 1.2 %shard_map.118 = (f32[8,16,256]{2,1,0:T(8,128)}, f32[8,16,256]{2,1,0:T(8,128)}) custom-call(f32[8,128]{1,0:T(8,128)S(1)} %shard_map.116.rest_0_, f32[8,128]{1,0:T(8,128)S(1)} %collective-permute-done.25.rest_1_, f32[8,128]{1,0:T(8,128)S(1)} %collective-permute-done.26.rest_2_, f32[8,128]{1,0:T(8,128)S(1)} %collective-permute-done.27.rest_3_, ...), custom_call_target="tpu_custom_call" | custom-call | flops 4000000 | bytes 250000 | tf_op jit(solution)/shard_map/pallas_call | solution.py:423
  (39 shorter events, 11.2 us)
Async XLA Ops:
  1.7 1.5 %collective-permute-start = (f32[36,8,128]{2,1,0:T(8,128)S(1)}, f32[36,8,128]{2,1,0:T(8,128)S(1)}, u32[]{:S(2)}, u32[]{:S(2)}) collective-permute-start(f32[36,8,128]{2,1,0:T(8,128)S(1)} %get-tuple-element.52), channel_id=1, source_target_pairs={{0,1},{1,0},{2,3},{3,2},{4,5},{5,4},{6,7},{7,6},{8,9},{9,8},{10,11... | collective-permute-start | bytes 442376 | tf_op jit(solution)/shard_map/ppermute | solution.py:464
  3.2 10.0 %collective-permute-start.3 = (f32[24,8,128]{2,1,0:T(8,128)S(1)}, f32[24,8,128]{2,1,0:T(8,128)S(1)}, u32[]{:S(2)}, u32[]{:S(2)}) collective-permute-start(f32[24,8,128]{2,1,0:T(8,128)S(1)} %get-tuple-element.57), channel_id=1, source_target_pairs={{0,2},{1,3},{2,0},{3,1},{4,6},{5,7},{6,4},{7,5},{8,10},{9,11},{10,... | collective-permute-start | bytes 294920 | tf_op jit(solution)/shard_map/ppermute | solution.py:464
  6.2 7.1 %collective-permute-start.4 = (f32[24,8,128]{2,1,0:T(8,128)S(1)}, f32[24,8,128]{2,1,0:T(8,128)S(1)}, u32[]{:S(2)}, u32[]{:S(2)}) collective-permute-start(f32[24,8,128]{2,1,0:T(8,128)S(1)} %get-tuple-element.58), channel_id=1, source_target_pairs={{0,4},{1,5},{2,6},{3,7},{4,0},{5,1},{6,2},{7,3},{8,12},{9,13},{10,... | collective-permute-start | bytes 294920 | tf_op jit(solution)/shard_map/ppermute | solution.py:464
  7.7 4.9 %collective-permute-start.1 = (f32[12,8,128]{2,1,0:T(8,128)S(1)}, f32[12,8,128]{2,1,0:T(8,128)S(1)}, u32[]{:S(2)}, u32[]{:S(2)}) collective-permute-start(f32[12,8,128]{2,1,0:T(8,128)S(1)} %get-tuple-element.53), channel_id=1, source_target_pairs={{0,7},{1,6},{2,5},{3,4},{4,3},{5,2},{6,1},{7,0},{8,15},{9,14},{10,... | collective-permute-start | bytes 147464 | tf_op jit(solution)/shard_map/ppermute | solution.py:464
  7.7 5.5 %collective-permute-start.2 = (f32[12,8,128]{2,1,0:T(8,128)S(1)}, f32[12,8,128]{2,1,0:T(8,128)S(1)}, u32[]{:S(2)}, u32[]{:S(2)}) collective-permute-start(f32[12,8,128]{2,1,0:T(8,128)S(1)} %get-tuple-element.54), channel_id=1, source_target_pairs={{0,6},{1,7},{2,4},{3,5},{4,2},{5,3},{6,0},{7,1},{8,14},{9,15},{10,... | collective-permute-start | bytes 147464 | tf_op jit(solution)/shard_map/ppermute | solution.py:464
  15.2 3.1 %collective-permute-start.5 = (f32[19,8,128]{2,1,0:T(8,128)S(1)}, f32[19,8,128]{2,1,0:T(8,128)S(1)}, u32[]{:S(2)}, u32[]{:S(2)}) collective-permute-start(f32[19,8,128]{2,1,0:T(8,128)S(1)} %get-tuple-element.63), channel_id=1, source_target_pairs={{0,1},{1,0},{2,3},{3,2},{4,5},{5,4},{6,7},{7,6},{8,9},{9,8},{10,11... | collective-permute-start | bytes 233480 | tf_op jit(solution)/shard_map/ppermute | solution.py:464
  15.3 6.0 %collective-permute-start.6 = (f32[7,8,128]{2,1,0:T(8,128)S(1)}, f32[7,8,128]{2,1,0:T(8,128)S(1)}, u32[]{:S(2)}, u32[]{:S(2)}) collective-permute-start(f32[7,8,128]{2,1,0:T(8,128)S(1)} %get-tuple-element.64), channel_id=1, source_target_pairs={{0,7},{1,6},{2,5},{3,4},{4,3},{5,2},{6,1},{7,0},{8,15},{9,14},{10,... | collective-permute-start | bytes 86024 | tf_op jit(solution)/shard_map/ppermute | solution.py:464
  17.4 4.9 %collective-permute-start.7 = (f32[7,8,128]{2,1,0:T(8,128)S(1)}, f32[7,8,128]{2,1,0:T(8,128)S(1)}, u32[]{:S(2)}, u32[]{:S(2)}) collective-permute-start(f32[7,8,128]{2,1,0:T(8,128)S(1)} %get-tuple-element.65), channel_id=1, source_target_pairs={{0,6},{1,7},{2,4},{3,5},{4,2},{5,3},{6,0},{7,1},{8,14},{9,15},{10,... | collective-permute-start | bytes 86024 | tf_op jit(solution)/shard_map/ppermute | solution.py:464
  18.3 4.2 %collective-permute-start.8 = (f32[13,8,128]{2,1,0:T(8,128)S(1)}, f32[13,8,128]{2,1,0:T(8,128)S(1)}, u32[]{:S(2)}, u32[]{:S(2)}) collective-permute-start(f32[13,8,128]{2,1,0:T(8,128)S(1)} %get-tuple-element.68), channel_id=1, source_target_pairs={{0,2},{1,3},{2,0},{3,1},{4,6},{5,7},{6,4},{7,5},{8,10},{9,11},{10,... | collective-permute-start | bytes 159752 | tf_op jit(solution)/shard_map/ppermute | solution.py:464
  19.4 4.1 %collective-permute-start.9 = (f32[13,8,128]{2,1,0:T(8,128)S(1)}, f32[13,8,128]{2,1,0:T(8,128)S(1)}, u32[]{:S(2)}, u32[]{:S(2)}) collective-permute-start(f32[13,8,128]{2,1,0:T(8,128)S(1)} %get-tuple-element.69), channel_id=1, source_target_pairs={{0,4},{1,5},{2,6},{3,7},{4,0},{5,1},{6,2},{7,3},{8,12},{9,13},{10,... | collective-permute-start | bytes 159752 | tf_op jit(solution)/shard_map/ppermute | solution.py:464
  25.7 1.3 %collective-permute-start.10 = (f32[19,8,128]{2,1,0:T(8,128)S(1)}, f32[19,8,128]{2,1,0:T(8,128)S(1)}, u32[]{:S(2)}, u32[]{:S(2)}) collective-permute-start(f32[19,8,128]{2,1,0:T(8,128)S(1)} %get-tuple-element.70), channel_id=1, source_target_pairs={{0,1},{1,0},{2,3},{3,2},{4,5},{5,4},{6,7},{7,6},{8,9},{9,8},{10,11... | collective-permute-start | bytes 233480 | tf_op jit(solution)/shard_map/ppermute | solution.py:464
  27.0 7.8 %collective-permute-start.13 = (f32[13,8,128]{2,1,0:T(8,128)S(1)}, f32[13,8,128]{2,1,0:T(8,128)S(1)}, u32[]{:S(2)}, u32[]{:S(2)}) collective-permute-start(f32[13,8,128]{2,1,0:T(8,128)S(1)} %get-tuple-element.75), channel_id=1, source_target_pairs={{0,2},{1,3},{2,0},{3,1},{4,6},{5,7},{6,4},{7,5},{8,10},{9,11},{10,... | collective-permute-start | bytes 159752 | tf_op jit(solution)/shard_map/ppermute | solution.py:464
  28.0 6.8 %collective-permute-start.14 = (f32[13,8,128]{2,1,0:T(8,128)S(1)}, f32[13,8,128]{2,1,0:T(8,128)S(1)}, u32[]{:S(2)}, u32[]{:S(2)}) collective-permute-start(f32[13,8,128]{2,1,0:T(8,128)S(1)} %get-tuple-element.76), channel_id=1, source_target_pairs={{0,4},{1,5},{2,6},{3,7},{4,0},{5,1},{6,2},{7,3},{8,12},{9,13},{10,... | collective-permute-start | bytes 159752 | tf_op jit(solution)/shard_map/ppermute | solution.py:464
  29.2 4.3 %collective-permute-start.11 = (f32[7,8,128]{2,1,0:T(8,128)S(1)}, f32[7,8,128]{2,1,0:T(8,128)S(1)}, u32[]{:S(2)}, u32[]{:S(2)}) collective-permute-start(f32[7,8,128]{2,1,0:T(8,128)S(1)} %get-tuple-element.71), channel_id=1, source_target_pairs={{0,7},{1,6},{2,5},{3,4},{4,3},{5,2},{6,1},{7,0},{8,15},{9,14},{10,... | collective-permute-start | bytes 86024 | tf_op jit(solution)/shard_map/ppermute | solution.py:464
  29.8 5.0 %collective-permute-start.12 = (f32[7,8,128]{2,1,0:T(8,128)S(1)}, f32[7,8,128]{2,1,0:T(8,128)S(1)}, u32[]{:S(2)}, u32[]{:S(2)}) collective-permute-start(f32[7,8,128]{2,1,0:T(8,128)S(1)} %get-tuple-element.72), channel_id=1, source_target_pairs={{0,6},{1,7},{2,4},{3,5},{4,2},{5,3},{6,0},{7,1},{8,14},{9,15},{10,... | collective-permute-start | bytes 86024 | tf_op jit(solution)/shard_map/ppermute | solution.py:464
  36.9 1.3 %collective-permute-start.15 = (f32[19,8,128]{2,1,0:T(8,128)S(1)}, f32[19,8,128]{2,1,0:T(8,128)S(1)}, u32[]{:S(2)}, u32[]{:S(2)}) collective-permute-start(f32[19,8,128]{2,1,0:T(8,128)S(1)} %get-tuple-element.77), channel_id=1, source_target_pairs={{0,1},{1,0},{2,3},{3,2},{4,5},{5,4},{6,7},{7,6},{8,9},{9,8},{10,11... | collective-permute-start | bytes 233480 | tf_op jit(solution)/shard_map/ppermute | solution.py:464
  38.2 7.8 %collective-permute-start.18 = (f32[13,8,128]{2,1,0:T(8,128)S(1)}, f32[13,8,128]{2,1,0:T(8,128)S(1)}, u32[]{:S(2)}, u32[]{:S(2)}) collective-permute-start(f32[13,8,128]{2,1,0:T(8,128)S(1)} %get-tuple-element.82), channel_id=1, source_target_pairs={{0,2},{1,3},{2,0},{3,1},{4,6},{5,7},{6,4},{7,5},{8,10},{9,11},{10,... | collective-permute-start | bytes 159752 | tf_op jit(solution)/shard_map/ppermute | solution.py:464
  39.2 6.8 %collective-permute-start.19 = (f32[13,8,128]{2,1,0:T(8,128)S(1)}, f32[13,8,128]{2,1,0:T(8,128)S(1)}, u32[]{:S(2)}, u32[]{:S(2)}) collective-permute-start(f32[13,8,128]{2,1,0:T(8,128)S(1)} %get-tuple-element.83), channel_id=1, source_target_pairs={{0,4},{1,5},{2,6},{3,7},{4,0},{5,1},{6,2},{7,3},{8,12},{9,13},{10,... | collective-permute-start | bytes 159752 | tf_op jit(solution)/shard_map/ppermute | solution.py:464
  40.4 4.3 %collective-permute-start.16 = (f32[7,8,128]{2,1,0:T(8,128)S(1)}, f32[7,8,128]{2,1,0:T(8,128)S(1)}, u32[]{:S(2)}, u32[]{:S(2)}) collective-permute-start(f32[7,8,128]{2,1,0:T(8,128)S(1)} %get-tuple-element.78), channel_id=1, source_target_pairs={{0,7},{1,6},{2,5},{3,4},{4,3},{5,2},{6,1},{7,0},{8,15},{9,14},{10,... | collective-permute-start | bytes 86024 | tf_op jit(solution)/shard_map/ppermute | solution.py:464
  41.0 5.0 %collective-permute-start.17 = (f32[7,8,128]{2,1,0:T(8,128)S(1)}, f32[7,8,128]{2,1,0:T(8,128)S(1)}, u32[]{:S(2)}, u32[]{:S(2)}) collective-permute-start(f32[7,8,128]{2,1,0:T(8,128)S(1)} %get-tuple-element.79), channel_id=1, source_target_pairs={{0,6},{1,7},{2,4},{3,5},{4,2},{5,3},{6,0},{7,1},{8,14},{9,15},{10,... | collective-permute-start | bytes 86024 | tf_op jit(solution)/shard_map/ppermute | solution.py:464
  48.2 1.3 %collective-permute-start.20 = (f32[19,8,128]{2,1,0:T(8,128)S(1)}, f32[19,8,128]{2,1,0:T(8,128)S(1)}, u32[]{:S(2)}, u32[]{:S(2)}) collective-permute-start(f32[19,8,128]{2,1,0:T(8,128)S(1)} %get-tuple-element.88), channel_id=1, source_target_pairs={{0,1},{1,0},{2,3},{3,2},{4,5},{5,4},{6,7},{7,6},{8,9},{9,8},{10,11... | collective-permute-start | bytes 233480 | tf_op jit(solution)/shard_map/ppermute | solution.py:464
  49.5 7.8 %collective-permute-start.23 = (f32[13,8,128]{2,1,0:T(8,128)S(1)}, f32[13,8,128]{2,1,0:T(8,128)S(1)}, u32[]{:S(2)}, u32[]{:S(2)}) collective-permute-start(f32[13,8,128]{2,1,0:T(8,128)S(1)} %get-tuple-element.92), channel_id=1, source_target_pairs={{0,2},{1,3},{2,0},{3,1},{4,6},{5,7},{6,4},{7,5},{8,10},{9,11},{10,... | collective-permute-start | bytes 159752 | tf_op jit(solution)/shard_map/ppermute | solution.py:464
  50.5 6.8 %collective-permute-start.24 = (f32[13,8,128]{2,1,0:T(8,128)S(1)}, f32[13,8,128]{2,1,0:T(8,128)S(1)}, u32[]{:S(2)}, u32[]{:S(2)}) collective-permute-start(f32[13,8,128]{2,1,0:T(8,128)S(1)} %get-tuple-element.93), channel_id=1, source_target_pairs={{0,4},{1,5},{2,6},{3,7},{4,0},{5,1},{6,2},{7,3},{8,12},{9,13},{10,... | collective-permute-start | bytes 159752 | tf_op jit(solution)/shard_map/ppermute | solution.py:464
  51.7 4.3 %collective-permute-start.21 = (f32[7,8,128]{2,1,0:T(8,128)S(1)}, f32[7,8,128]{2,1,0:T(8,128)S(1)}, u32[]{:S(2)}, u32[]{:S(2)}) collective-permute-start(f32[7,8,128]{2,1,0:T(8,128)S(1)} %get-tuple-element.89), channel_id=1, source_target_pairs={{0,7},{1,6},{2,5},{3,4},{4,3},{5,2},{6,1},{7,0},{8,15},{9,14},{10,... | collective-permute-start | bytes 86024 | tf_op jit(solution)/shard_map/ppermute | solution.py:464
  52.3 5.0 %collective-permute-start.22 = (f32[7,8,128]{2,1,0:T(8,128)S(1)}, f32[7,8,128]{2,1,0:T(8,128)S(1)}, u32[]{:S(2)}, u32[]{:S(2)}) collective-permute-start(f32[7,8,128]{2,1,0:T(8,128)S(1)} %get-tuple-element.90), channel_id=1, source_target_pairs={{0,6},{1,7},{2,4},{3,5},{4,2},{5,3},{6,0},{7,1},{8,14},{9,15},{10,... | collective-permute-start | bytes 86024 | tf_op jit(solution)/shard_map/ppermute | solution.py:464
  57.6 5.5 %collective-permute-start.27 = (f32[8,128]{1,0:T(8,128)S(1)}, f32[8,128]{1,0:T(8,128)S(1)}, u32[]{:S(2)}, u32[]{:S(2)}) collective-permute-start(f32[8,128]{1,0:T(8,128)S(1)} %shard_map.116.rest_0_), channel_id=1, source_target_pairs={{0,24},{8,16},{16,8},{24,0},{1,25},{9,17},{17,9},{25,1},{2,26},{10... | collective-permute-start | bytes 12296 | tf_op jit(solution)/shard_map/ppermute | solution.py:532
  61.3 4.5 %collective-permute-start.26 = (f32[8,128]{1,0:T(8,128)S(1)}, f32[8,128]{1,0:T(8,128)S(1)}, u32[]{:S(2)}, u32[]{:S(2)}) collective-permute-start(f32[8,128]{1,0:T(8,128)S(1)} %shard_map.116.rest_0_), channel_id=1, source_target_pairs={{0,16},{8,24},{16,0},{24,8},{1,17},{9,25},{17,1},{25,9},{2,18},{10... | collective-permute-start | bytes 12296 | tf_op jit(solution)/shard_map/ppermute | solution.py:532
  61.3 4.5 %collective-permute-start.25 = (f32[8,128]{1,0:T(8,128)S(1)}, f32[8,128]{1,0:T(8,128)S(1)}, u32[]{:S(2)}, u32[]{:S(2)}) collective-permute-start(f32[8,128]{1,0:T(8,128)S(1)} %shard_map.116.rest_0_), channel_id=1, source_target_pairs={{0,8},{8,0},{16,24},{24,16},{1,9},{9,1},{17,25},{25,17},{2,10},{10... | collective-permute-start | bytes 12296 | tf_op jit(solution)/shard_map/ppermute | solution.py:532

commit v6 on v5

--- a/solution.py
+++ b/solution.py
@@ -62,32 +62,30 @@
         self.extra_chunks = -(-(self.gram_lane + ENTRIES) // LANES)
         self.extra = self.extra_chunks * LANES
         self.halves = self.width // LANES
-        distances = range(2, self.peers, 2)
-        self.paired = [m for m in distances if m & (m - 1) == 0]
-        self.direct = [n for m in distances if m & (m - 1) for n in (m + 1, m)]
-        self.handed = [1] + [m + 1 for m in self.paired]
+        evens = range(2, self.peers, 2)
+        self.far = sorted(evens, key=lambda m: -m.bit_count())
+        self.handed = [m + 1 for m in self.far]
         self.slots = self.peers * self.capacity
         self.inverse = self.slots
         self.pattern = self.inverse + self.blocks
         self.partner = self.pattern + self.blocks
-        self.table = self.partner + self.blocks
+        self.order = self.partner + self.blocks
+        self.count = self.order + self.blocks + 1
+        self.table = self.count + 1
+        most = len(self.far) * self.capacity
+        self.early = min(-(-most * 3 // 4), self.blocks)
+        self.middle = max(self.early, min(most, self.blocks))
 
     def rows(self, kinds):
         return kinds * self.capacity * self.halves
 
-    def sent(self, kinds):
-        rows = self.rows(kinds)
-        near = len(self.handed) * rows
-        return [near] + [rows] * len(self.direct) + [2 * rows] * len(self.paired)
-
-    def first(self):
-        return 1 + len(self.direct)
+    def near_rows(self, kinds):
+        return len(self.handed) * self.rows(kinds)
 
     def sources(self):
         found = [(1, 0, 0)]
-        found += [(m, 1 + k, 0) for k, m in enumerate(self.direct)]
-        for k, m in enumerate(self.paired):
-            found += [(m + side, self.first() + k, side) for side in range(2)]
+        for k, m in enumerate(self.far):
+            found += [(m + side, 1 + k, side) for side in range(2)]
         return found
 
 
@@ -107,6 +105,14 @@
         table[z.inverse + source] = i
         table[z.pattern + i] = source
         table[z.partner + i] = mate
+    place = jnp.int32(0)
+    for m in z.handed + z.far + [1]:
+        for r in range(z.capacity):
+            block = table[m * z.capacity + r]
+            table[z.order + place] = block
+            place = place + (block < z.blocks).astype(jnp.int32)
+        if m == z.handed[-1]:
+            table[z.count] = place
 
 
 def fill_piece(z, table, sources, m, piece, row):
@@ -118,28 +124,38 @@
                 row += 1
 
 
-def fill_first(z, table, sources, pieces):
-    rows = z.rows(len(sources))
+def fill_near(z, table, sources, near):
     for k, m in enumerate(z.handed):
-        fill_piece(z, table, sources, m, pieces[0], k * rows)
-    for m, piece in zip(z.direct, pieces[1:]):
-        fill_piece(z, table, sources, m, piece, 0)
-
-
-def relay(z, kinds, table, *rest):
+        fill_piece(z, table, sources, m, near, k * z.rows(len(sources)))
+
+
+def store_extra(z, tile, piece, row):
+    for j in range(z.extra_chunks):
+        piece[row + j] = tile[:, j * LANES : (j + 1) * LANES]
+
+
+def load_extra(z, piece, row):
+    return jnp.concatenate([piece[row + j] for j in range(z.extra_chunks)], axis=1)
+
+
+def relay(z, kinds, late, table, *rest):
     sources, rest = rest[:kinds], rest[kinds:]
-    chunks = z.extra_chunks if kinds == 1 else 0
-    if chunks:
-        own_extra, rest = rest[0], rest[1:]
-    near, pieces = rest[0], rest[1:]
+    if kinds == 1:
+        extra, rest = rest[0], rest[1:]
+    near, rest = rest[0], rest[1:]
+    if late:
+        beside, rest = rest[0], rest[1:]
     rows = z.rows(kinds)
-    for k, (m, piece) in enumerate(zip(z.paired, pieces)):
+    if kinds == 1:
+        tile = extra[...] + load_extra(z, near, z.near_rows(1))
+        if late:
+            tile = tile + load_extra(z, beside, rows)
+    for k, (m, piece) in enumerate(zip(z.far, rest)):
         fill_piece(z, table, sources, m, piece, 0)
         for row in range(rows):
-            piece[rows + row] = near[(k + 1) * rows + row]
-        for j in range(chunks):
-            mine = own_extra[:, j * LANES : (j + 1) * LANES]
-            piece[2 * rows + j] = mine + near[z.sent(1)[0] + j]
+            piece[rows + row] = near[k * rows + row]
+        if kinds == 1:
+            store_extra(z, tile, piece, 2 * rows)
 
 
 def place(z, table, arrived, kind, kinds, target):
@@ -152,8 +168,8 @@
                 row += 1
 
 
-def begin(z, partner, pattern, load, scale, coupling, table, field, lift, scale_out, coupling_out, *rest):
-    pieces, (here, partner_here, pattern_here, counts, sems) = rest[:-5], rest[-5:]
+def begin(z, partner, pattern, load, scale, coupling, table, field, lift, wide, coupling_out, near, beside, *scratch):
+    here, scale_here, partner_here, pattern_here, counts, sems = scratch
     copies = [
         pltpu.make_async_copy(a, b, sems.at[k])
         for k, (a, b) in enumerate(
@@ -161,7 +177,7 @@
                 (partner, partner_here),
                 (pattern, pattern_here),
                 (load, here),
-                (scale, scale_out),
+                (scale, scale_here),
                 (coupling, coupling_out),
             ]
         )
@@ -175,9 +191,11 @@
         copy.wait()
     for i in range(z.blocks):
         field[i] = here[:, i, :]
-        part = coupling_out[:, i * z.width : (i + 1) * z.width].astype(F32)
-        lift[i] = scale_out[i : i + 1, :] * part
-    fill_first(z, table, [field, lift], pieces)
+        row = jnp.broadcast_to(scale_here[i : i + 1, :], (z.columns, z.width))
+        wide[i] = row
+        lift[i] = row * coupling_out[:, i * z.width : (i + 1) * z.width].astype(F32)
+    fill_near(z, table, [field, lift], near)
+    fill_piece(z, table, [field, lift], 1, beside, 0)
 
 
 def split3(a):
@@ -224,10 +242,12 @@
         jump_lift[i] = split(dot(left, right, TN))
 
 
-def extra_sum(z, own, arrived):
-    total = own[...]
-    for rows, piece in zip(z.sent(1), arrived):
-        total = total + jnp.concatenate([piece[rows + j] for j in range(z.extra_chunks)], axis=1)
+def extra_sum(z, own, near, beside, *far):
+    total = own[...] + load_extra(z, near, z.near_rows(1))
+    if beside is not None:
+        total = total + load_extra(z, beside, z.rows(1))
+    for piece in far:
+        total = total + load_extra(z, piece, 2 * z.rows(1))
     return total
 
 
@@ -246,49 +266,58 @@
     return jnp.sum(a, axis=1, keepdims=True)
 
 
-def apply_round(z, step, table, *rest):
-    count = len(z.sent(1))
-    first, last = step == 1, step == ITERS
+def couple(z, table, position, wide, diag, off, parts, field, image):
+    i = table[z.order + position]
+    source = table[z.inverse + i]
+    mine = parts[i]
+    coupled = dot(mine, diag[i], NT) + dot(mine, diag[i], NN)
+    coupled = coupled + dot(parts[table[z.pattern + i]], off[i], NT)
+    coupled = coupled + dot(parts[source], off[source], NN)
+    row = wide[i]
+    image[i] = row * (row * field[i] + fold(coupled))
+
+
+def first_half(z, step, table, *rest):
     rest = list(rest)
     take = lambda n: [rest.pop(0) for _ in range(n)]
-    arrived = take(count)
+    beside, *far = take(1 + len(z.far))
     (before,) = take(1)
-    if not first:
-        own_extra, jump_lift = take(2)
-    scale, diag, off, coupling = take(4)
-    older = take(ITERS - 1) if last else []
-    field, image = take(2)
-    if not first:
+    if step > 1:
+        near, own_extra, jump_lift = take(3)
+    wide, diag, off, coupling = take(4)
+    field, image, parts = take(3)
+    if step > 1:
         (total_out,) = take(1)
-    (extra,) = take(1)
-    pieces = take(z.first())
-    other, parts = rest
-    place(z, table, arrived, 0, 2 if first else 1, other)
-    if not first:
-        total = extra_sum(z, own_extra, arrived)
+    extra, near_out, other = rest
+    place(z, table, [beside, *far], 0, 2 if step == 1 else 1, other)
+    if step > 1:
+        total = extra_sum(z, own_extra, near, None, *far)
         total_out[...] = total
         rows = corner_rows(z, total)
         shrink = 1.0 / cluster_max(z, total)
-    for i in range(z.blocks):
-        value = before[i] - other[i]
-        if not first:
-            value = (value + fold(dot(rows, jump_lift[i], NN))) * shrink
-        field[i] = value
-        parts[i] = split(scale[i : i + 1, :] * value)
     partial = jnp.zeros((2 * z.columns, z.corners), F32)
     top = jnp.zeros((z.columns, z.width), F32)
     for i in range(z.blocks):
-        mine = parts[i]
+        value = before[i] - other[i]
+        if step > 1:
+            value = (value + fold(dot(rows, jump_lift[i], NN))) * shrink
+        field[i] = value
+        scaled = wide[i] * value
+        top = jnp.maximum(top, jnp.abs(wide[i] * scaled))
+        mine = split(scaled)
+        parts[i] = mine
         partial = partial + dot(mine, coupling[:, i * z.width : (i + 1) * z.width], NT)
-        source = table[z.inverse + i]
-        coupled = dot(mine, diag[i], NT) + dot(mine, diag[i], NN)
-        coupled = coupled + dot(parts[table[z.pattern + i]], off[i], NT)
-        coupled = coupled + dot(parts[source], off[source], NN)
-        row = scale[i : i + 1, :]
-        result = row * (row * field[i] + fold(coupled))
-        image[i] = result
-        top = jnp.maximum(top, jnp.abs(result))
-    fill_first(z, table, [image], pieces)
+    work = functools.partial(couple, z, table)
+    refs = (wide, diag, off, parts, field, image)
+    for position in range(z.early):
+        work(position, *refs)
+
+    @pl.when(table[z.count] > z.early)
+    def _():
+        for position in range(z.early, z.middle):
+            work(position, *refs)
+
+    fill_near(z, table, [image], near_out)
     me = lax.axis_index("sub")
     lanes = lane_ids((z.columns, z.extra))
     sums = fold(partial)
@@ -297,7 +326,32 @@
     )
     tile = pltpu.roll(padded, me * z.corners, 1)
     tile = jnp.where(lanes == z.max_lane + me, jnp.max(top, axis=1, keepdims=True), tile)
+    extra[...] = tile
+    store_extra(z, tile, near_out, z.near_rows(1))
+
+
+def second_half(z, last, table, wide, diag, off, parts, field, image_in, *rest):
+    rest = list(rest)
+    take = lambda n: [rest.pop(0) for _ in range(n)]
+    extra, *older = take(ITERS) if last else (None,)
+    image, beside = take(2)
+    work = functools.partial(couple, z, table)
+    refs = (wide, diag, off, parts, field, image)
+    for i in range(z.blocks):
+        image[i] = image_in[i]
+
+    @pl.when(table[z.count] <= z.early)
+    def _():
+        for position in range(z.early, z.middle):
+            work(position, *refs)
+
+    for position in range(z.middle, z.blocks):
+        work(position, *refs)
+    fill_piece(z, table, [image], 1, beside, 0)
     if last:
+        (extra_out,) = rest
+        lanes = lane_ids((z.columns, z.extra))
+        tile = jnp.zeros((z.columns, z.extra), F32)
         fields = older + [field]
         products = [(fields[i], fields[j]) for i, j in PAIRS] + [(f, image) for f in fields]
         for entry, (a, b) in enumerate(products):
@@ -305,16 +359,14 @@
             for i in range(1, z.blocks):
                 acc = acc + a[i] * b[i]
             tile = jnp.where(lanes == z.gram_lane + entry, lane_sum(acc), tile)
-    extra[...] = tile
-    for rows, piece in zip(z.sent(1), pieces):
-        for j in range(z.extra_chunks):
-            piece[rows + j] = tile[:, j * LANES : (j + 1) * LANES]
-
-
-def cluster_gram(z, operator, own_extra, *rest):
-    count = len(z.sent(1))
-    arrived, totals, (gram,) = rest[:count], rest[count:-1], rest[-1:]
-    total = extra_sum(z, own_extra, arrived)
+        extra_out[...] = extra[...] + tile
+        store_extra(z, tile, beside, z.rows(1))
+
+
+def cluster_gram(z, operator, own_extra, near, beside, *rest):
+    count = len(z.far)
+    far, totals, (gram,) = rest[:count], rest[count:-1], rest[-1:]
+    total = extra_sum(z, own_extra, near, beside, *far)
     totals = [t[...] for t in totals]
     partials = [t[:, : z.all_corners] for t in totals + [total]]
     lifted = dot_high(partials[-1], operator[...], NT)
@@ -331,10 +383,10 @@
     gram[...] = tile
 
 
-def last_vector(z, table, before, own_extra, jump_lift, *rest):
-    arrived, (field, other) = rest[:-2], rest[-2:]
-    place(z, table, arrived, 0, 1, other)
-    rows = corner_rows(z, extra_sum(z, own_extra, arrived))
+def last_vector(z, table, before, own_extra, jump_lift, near, beside, *rest):
+    far, (field, other) = rest[:-2], rest[-2:]
+    place(z, table, [beside, *far], 0, 1, other)
+    rows = corner_rows(z, extra_sum(z, own_extra, near, beside, *far))
     for i in range(z.blocks):
         field[i] = before[i] - other[i] + fold(dot(rows, jump_lift[i], NN))
 
@@ -448,14 +500,15 @@
     cols, blocks, width = z.columns, z.blocks, z.width
     field = ((blocks, cols, width), F32)
     other = pltpu.VMEM((blocks + 1, cols, width), F32)
-    parts = pltpu.VMEM((blocks, 2 * cols, width), BF16)
     extra = ((cols, z.extra), F32)
     gram = ((cols, 128), F32)
     light, heavy = 4_000_000, 600_000_000
 
-    def piece_shapes(kinds):
-        chunks = z.extra_chunks if kinds == 1 else 0
-        return [((rows + chunks, cols, LANES), F32) for rows in z.sent(kinds)]
+    def shape(rows, kinds):
+        return ((rows + (z.extra_chunks if kinds == 1 else 0), cols, LANES), F32)
+
+    def near_shapes(kinds):
+        return [shape(z.near_rows(kinds), kinds), shape(z.rows(kinds), kinds)]
 
     def kernel(body, *extra_args):
         return functools.partial(body, z, *extra_args)
@@ -463,26 +516,21 @@
     def across(piece, m):
         return lax.ppermute(piece, "sub", [(t, t ^ m) for t in range(z.peers)])
 
-    def exchange(kinds, pieces, *sources):
-        arrived = [across(piece, m) for m, piece in zip([1] + z.direct, pieces)]
-        more = call(
-            kernel(relay, kinds), piece_shapes(kinds)[z.first() :], [], light,
-            [table, *sources, arrived[0]],
+    def far_exchange(kinds, sources, near, late=()):
+        pieces = call(
+            kernel(relay, kinds, len(late) > 0),
+            [shape(2 * z.rows(kinds), kinds)] * len(z.far), [], light,
+            [table, *sources, near, *late],
         )
-        return arrived + [across(piece, m) for m, piece in zip(z.paired, more)]
-
-    table, loaded, lift, scale, coupling, *pieces = call(
+        return [across(piece, m) for m, piece in zip(z.far, pieces)]
+
+    table, loaded, lift, wide, coupling, near, beside = call(
         kernel(begin),
-        [
-            ((z.table,), jnp.int32),
-            field,
-            field,
-            (row_scale.shape, F32),
-            (corner_coupling.shape, BF16),
-        ]
-        + piece_shapes(2)[: z.first()],
+        [((z.table,), jnp.int32), field, field, field, (corner_coupling.shape, BF16)]
+        + near_shapes(2),
         [
             pltpu.VMEM(load.shape, F32),
+            pltpu.VMEM(row_scale.shape, F32),
             pltpu.SMEM(partner.shape, jnp.int32),
             pltpu.SMEM(off_pattern.shape, jnp.int32),
             pltpu.SMEM((z.peers,), jnp.int32),
@@ -492,7 +540,9 @@
         [partner, off_pattern, load, row_scale, corner_coupling],
         False, range(5),
     )
-    arrived = exchange(2, pieces, loaded, lift)
+    near = across(near, 1)
+    beside = across(beside, 1)
+    arrived = [beside, *far_exchange(2, [loaded, lift], near)]
     weight = (diag_blocks.shape, BF16)
     operator, diag, off = call(
         kernel(prepare), [((z.all_corners, z.all_corners), F32), weight, weight],
@@ -503,29 +553,39 @@
         ],
         heavy, [corner_index, coarse_inverse, diag_blocks, off_blocks], False, range(4),
     )
-    newest, image, own_extra, *pieces = call(
-        kernel(apply_round, 1),
-        [field, field, extra] + piece_shapes(1)[: z.first()], [other, parts], heavy,
-        [table, *arrived, loaded, scale, diag, off, coupling],
-    )
-    (jump_lift,) = call(
-        kernel(build_lift), [((blocks, 2 * z.all_corners, width), BF16)], [other], heavy,
-        [table, operator, lift, *arrived],
-    )
-    arrived = exchange(1, pieces, image, own_extra)
-    fields, totals = [newest], []
-    for step in range(2, ITERS + 1):
-        older = fields if step == ITERS else []
-        newest, image, total, own_extra, *pieces = call(
-            kernel(apply_round, step),
-            [field, field, extra, extra] + piece_shapes(1)[: z.first()], [other, parts], heavy,
-            [table, *arrived, image, own_extra, jump_lift, scale, diag, off, coupling, *older],
+    half = ((blocks, 2 * cols, width), BF16)
+    fields, totals = [], []
+    image, own_extra, jump_lift = loaded, None, None
+    for step in range(1, ITERS + 1):
+        last = step == ITERS
+        more = [near, own_extra, jump_lift] if step > 1 else []
+        newest, part, parts, *total, own_extra, near = call(
+            kernel(first_half, step),
+            [field, field, half] + [extra] * (step > 1) + [extra, near_shapes(1)[0]],
+            [other], heavy, [table, *arrived, image, *more, wide, diag, off, coupling],
         )
+        near = across(near, 1)
+        older = [own_extra, *fields] if last else []
+        image, beside, *finished = call(
+            kernel(second_half, last),
+            [field, near_shapes(1)[1]] + [extra] * last, [], heavy,
+            [table, wide, diag, off, parts, newest, part, *older],
+        )
+        beside = across(beside, 1)
         fields.append(newest)
-        totals.append(total)
-        arrived = exchange(1, pieces, image, own_extra)
+        totals += total
+        if step == 1:
+            (jump_lift,) = call(
+                kernel(build_lift), [((blocks, 2 * z.all_corners, width), BF16)], [other], heavy,
+                [table, operator, lift, *arrived],
+            )
+        if last:
+            (own_extra,) = finished
+        late = [beside] if last else []
+        arrived = [beside, *far_exchange(1, [image, own_extra], near, late)]
     (own_gram,) = call(
-        kernel(cluster_gram), [gram], [], light, [operator, own_extra, *arrived, *totals], False
+        kernel(cluster_gram), [gram], [], light,
+        [operator, own_extra, near, *arrived, *totals], False,
     )
     power = z.groups & (z.groups - 1) == 0
     grams = [own_gram] + [
@@ -537,7 +597,7 @@
     ]
     (newest,) = call(
         kernel(last_vector), [field], [other], light,
-        [table, image, own_extra, jump_lift, *arrived],
+        [table, image, own_extra, jump_lift, near, *arrived],
     )
     multipliers, residual = call(
         kernel(finish), [(load.shape, F32)] * 2, [], light, [*grams, *fields, newest], False

time: 67.1 us -> 63 us (0.939)
  starting transfers between devices: 30.4 us -> 24.9 us
  Pallas kernels: 14 us -> 17.1 us
  waiting for transfers between devices: 21.9 us -> 20.1 us
    ppermute x25, starting transfers between devices: 25.9 us -> 20.4 us  [across(): return lax.ppermute(piece, 'sub', [(t, t ^ m) for t in range(z.peers)])]
    pallas_call x15 -> x19, Pallas kernels: 14 us -> 17.1 us  [call(): pl.pallas_call(body, out_shape=shapes, in_specs=specs, out_specs=[SMEM if...]
    ppermute x25, waiting for transfers between devices: 18.5 us -> 16.7 us  [across(): return lax.ppermute(piece, 'sub', [(t, t ^ m) for t in range(z.peers)])]
  transfers between devices with their start and end apart: 28 -> 28, of which waited for: 17 -> 22; matrix products, arithmetic and copies ran while one was open for 0% -> 0% of each run, Pallas kernels for 4% -> 12%
where the time goes in v6:
time: 63 us; the launch traced here: 62.9 us
  starting transfers between devices  24.9 us (40%)
  waiting for transfers between devices  20.1 us (32%)
  Pallas kernels  17.1 us (27%)
  between operations  0.8 us (1%)
    ppermute x25, starting transfers between devices, across(): return lax.ppermute(piece, 'sub', [(t, t ^ m) for t in range(z.peers)])  20.4 us
    pallas_call x19, Pallas kernels, call(): pl.pallas_call(body, out_shape=shapes, in_specs=specs, out_specs=[SMEM if...  17.1 us
    ppermute x25, waiting for transfers between devices, across(): return lax.ppermute(piece, 'sub', [(t, t ^ m) for t in range(z.peers)])  16.7 us
    ppermute x3, starting transfers between devices, on_device(): lax.ppermute(own_gram, 'group', [(a, a ^ k if power else (a + k) % z.grou...  4.44 us
    ppermute x3, waiting for transfers between devices, on_device(): lax.ppermute(own_gram, 'group', [(a, a ^ k if power else (a + k) % z.grou...  3.43 us
  transfers between devices with their start and end apart: 28, of which 22 were waited for; matrix products, arithmetic and copies ran while one was open for 0% of the time, Pallas kernels for 12%

profile of v6, /device:TPU:0, one launch (start us, length us, event | category | flops | bytes accessed | tf_op | source)
XLA Modules:
  0.0 62.9 jit_solution(16362201874514869761)
XLA Ops:
  0.6 1.0 %shard_map.105 = (s32[90]{0:T(128)S(4)}, f32[16,8,256]{2,1,0:T(8,128)S(1)}, f32[16,8,256]{2,1,0:T(8,128)S(1)}, f32[16,8,256]{2,1,0:T(8,128)S(1)}, bf16[8,4096]{1...) custom-call(s32[1,16]{1,0:T(1,128)} %partner.1, s32[1,16]{1,0:T(1,128)} %pattern.1, ...), custom_call_target="tpu_custom_call" | custom-call | flops 4000000 | bytes 250000 | tf_op jit(solution)/shard_map/pallas_call | solution.py:475
  2.2 1.0 %collective-permute-done.1.rest_2_ = f32[36,8,128]{2,1,0:T(8,128)S(1)} collective-permute-done((f32[36,8,128]{2,1,0:T(8,128)S(1)}, f32[36,8,128]{2,1,0:T(8,128)S(1)}, u32[]{:S(2)}, u32[]{:S(2)}) %collective-permute-start.1) | collective-permute-done | bytes 147488 | tf_op jit(solution)/shard_map/ppermute | solution.py:517
  3.2 3.9 %collective-permute-start.2 = (f32[24,8,128]{2,1,0:T(8,128)S(1)}, f32[24,8,128]{2,1,0:T(8,128)S(1)}, u32[]{:S(2)}, u32[]{:S(2)}) collective-permute-start(f32[24,8,128]{2,1,0:T(8,128)S(1)} %get-tuple-element.68), channel_id=1, source_target_pairs={{0,6},{1,7},{2,4},{3,5},{4,2},{5,3},{6,0},{7,1},{8,14},{9,15},{10,... | collective-permute-start | bytes 294920 | tf_op jit(solution)/shard_map/ppermute | solution.py:517
  7.8 2.3 %shard_map.104 = (f32[64,64]{1,0:T(8,128)S(1)}, bf16[16,256,256]{2,1,0:T(8,128)(2,1)S(1)}, bf16[16,256,256]{2,1,0:T(8,128)(2,1)S(1)}) custom-call(s32[1,64]{1,0:T(1,128)} %index_in.1, f32[32,32]{1,0:T(8,128)} %inverse_in.1, bf16[16,256,256]{2,1,0:T(8,128)(2,1)} %diag.1, bf16[16,256,256]{2,1,0:T(8,128)(2,1)} %off.1), custom_call_target="tpu_custom_call" | custom-call | flops 600000000 | bytes 37500000 | tf_op jit(solution)/shard_map/pallas_call | solution.py:475
  10.1 0.6 %collective-permute-done.2.rest_1_ = f32[24,8,128]{2,1,0:T(8,128)S(1)} collective-permute-done((f32[24,8,128]{2,1,0:T(8,128)S(1)}, f32[24,8,128]{2,1,0:T(8,128)S(1)}, u32[]{:S(2)}, u32[]{:S(2)}) %collective-permute-start.2) | collective-permute-done | bytes 98336 | tf_op jit(solution)/shard_map/ppermute | solution.py:517
  10.7 1.9 %collective-permute-done.3.rest_2_ = f32[24,8,128]{2,1,0:T(8,128)S(1)} collective-permute-done((f32[24,8,128]{2,1,0:T(8,128)S(1)}, f32[24,8,128]{2,1,0:T(8,128)S(1)}, u32[]{:S(2)}, u32[]{:S(2)}) %collective-permute-start.3) | collective-permute-done | bytes 98336 | tf_op jit(solution)/shard_map/ppermute | solution.py:517
  12.6 1.0 %shard_map.107 = (f32[16,8,256]{2,1,0:T(8,128)S(1)}, f32[16,8,256]{2,1,0:T(8,128)S(1)}, bf16[16,16,256]{2,1,0:T(8,128)(2,1)S(1)}, f32[8,128]{1,0:T(8,128)S(1)}, f32[19,8,128]{2,1,0:T(8,128)S(1)}) custom-call(s32[90]{0:T(128)S(4)} %get-tuple-element.60.table, f32[12,8,128]{2,1,0:T(8,128)S(1)} %collective-permute-done.rest_0_, ...), custom_call_target="tpu_custom_call" | custom-call | flops 600000000 | bytes 37500000 | tf_op jit(solution)/shard_map/pallas_call | solution.py:475
  13.6 1.2 %shard_map.108 = (f32[16,8,256]{2,1,0:T(8,128)S(1)}, f32[7,8,128]{2,1,0:T(8,128)S(1)}) custom-call(s32[90]{0:T(128)S(4)} %get-tuple-element.60.table, f32[16,8,256]{2,1,0:T(8,128)S(1)} %get-tuple-element.61.rest_5_.wide.rest_8_, bf16[16,256,256]{2,1,0:T(8,128)(2,1)S(1)} %get-tuple-element.62.rest_6_.diag.rest_9_, ...), custom_call_target="tpu_custom_call" | custom-call | flops 600000000 | bytes 37500000 | tf_op jit(solution)/shard_map/pallas_call | solution.py:475
  15.4 2.5 %collective-permute-start.7 = (f32[13,8,128]{2,1,0:T(8,128)S(1)}, f32[13,8,128]{2,1,0:T(8,128)S(1)}, u32[]{:S(2)}, u32[]{:S(2)}) collective-permute-start(f32[13,8,128]{2,1,0:T(8,128)S(1)} %get-tuple-element.79), channel_id=1, source_target_pairs={{0,6},{1,7},{2,4},{3,5},{4,2},{5,3},{6,0},{7,1},{8,14},{9,15},{10,... | collective-permute-start | bytes 159752 | tf_op jit(solution)/shard_map/ppermute | solution.py:517
  19.3 1.4 %collective-permute-done.7.rest_1_ = f32[13,8,128]{2,1,0:T(8,128)S(1)} collective-permute-done((f32[13,8,128]{2,1,0:T(8,128)S(1)}, f32[13,8,128]{2,1,0:T(8,128)S(1)}, u32[]{:S(2)}, u32[]{:S(2)}) %collective-permute-start.7) | collective-permute-done | bytes 53280 | tf_op jit(solution)/shard_map/ppermute | solution.py:517
  20.8 1.2 %collective-permute-done.8.rest_2_ = f32[13,8,128]{2,1,0:T(8,128)S(1)} collective-permute-done((f32[13,8,128]{2,1,0:T(8,128)S(1)}, f32[13,8,128]{2,1,0:T(8,128)S(1)}, u32[]{:S(2)}, u32[]{:S(2)}) %collective-permute-start.8) | collective-permute-done | bytes 53280 | tf_op jit(solution)/shard_map/ppermute | solution.py:517
  22.5 1.9 %shard_map.111 = (f32[16,8,256]{2,1,0:T(8,128)S(1)}, f32[16,8,256]{2,1,0:T(8,128)S(1)}, bf16[16,16,256]{2,1,0:T(8,128)(2,1)S(1)}, f32[8,128]{1,0:T(8,128)S(1)}, ...) custom-call(s32[90]{0:T(128)S(4)} %get-tuple-element.60.table, f32[7,8,128]{2,1,0:T(8,128)S(1)} %collective-permute-done.5.rest_0_, ...), custom_call_target="tpu_custom_call" | custom-call | flops 600000000 | bytes 37500000 | tf_op jit(solution)/shard_map/pallas_call | solution.py:475
  24.5 1.2 %shard_map.112 = (f32[16,8,256]{2,1,0:T(8,128)S(1)}, f32[7,8,128]{2,1,0:T(8,128)S(1)}) custom-call(s32[90]{0:T(128)S(4)} %get-tuple-element.60.table, f32[16,8,256]{2,1,0:T(8,128)S(1)} %get-tuple-element.61.rest_5_.wide.rest_8_, bf16[16,256,256]{2,1,0:T(8,128)(2,1)S(1)} %get-tuple-element.62.rest_6_.diag.rest_9_, ...), custom_call_target="tpu_custom_call" | custom-call | flops 600000000 | bytes 37500000 | tf_op jit(solution)/shard_map/pallas_call | solution.py:475
  25.7 1.6 %collective-permute-start.12 = (f32[13,8,128]{2,1,0:T(8,128)S(1)}, f32[13,8,128]{2,1,0:T(8,128)S(1)}, u32[]{:S(2)}, u32[]{:S(2)}) collective-permute-start(f32[13,8,128]{2,1,0:T(8,128)S(1)} %get-tuple-element.89), channel_id=1, source_target_pairs={{0,6},{1,7},{2,4},{3,5},{4,2},{5,3},{6,0},{7,1},{8,14},{9,15},{10,... | collective-permute-start | bytes 159752 | tf_op jit(solution)/shard_map/ppermute | solution.py:517
  27.8 1.5 %collective-permute-start.14 = (f32[13,8,128]{2,1,0:T(8,128)S(1)}, f32[13,8,128]{2,1,0:T(8,128)S(1)}, u32[]{:S(2)}, u32[]{:S(2)}) collective-permute-start(f32[13,8,128]{2,1,0:T(8,128)S(1)} %get-tuple-element.91), channel_id=1, source_target_pairs={{0,4},{1,5},{2,6},{3,7},{4,0},{5,1},{6,2},{7,3},{8,12},{9,13},{10,... | collective-permute-start | bytes 159752 | tf_op jit(solution)/shard_map/ppermute | solution.py:517
  29.3 1.2 %collective-permute-done.10.rest_0_ = f32[7,8,128]{2,1,0:T(8,128)S(1)} collective-permute-done((f32[7,8,128]{2,1,0:T(8,128)S(1)}, f32[7,8,128]{2,1,0:T(8,128)S(1)}, u32[]{:S(2)}, u32[]{:S(2)}) %collective-permute-start.10) | collective-permute-done | bytes 28704 | tf_op jit(solution)/shard_map/ppermute | solution.py:517
  32.0 1.9 %shard_map.114 = (f32[16,8,256]{2,1,0:T(8,128)S(1)}, f32[16,8,256]{2,1,0:T(8,128)S(1)}, bf16[16,16,256]{2,1,0:T(8,128)(2,1)S(1)}, f32[8,128]{1,0:T(8,128)S(1)}, ...) custom-call(s32[90]{0:T(128)S(4)} %get-tuple-element.60.table, f32[7,8,128]{2,1,0:T(8,128)S(1)} %collective-permute-done.10.rest_0_, ...), custom_call_target="tpu_custom_call" | custom-call | flops 600000000 | bytes 37500000 | tf_op jit(solution)/shard_map/pallas_call | solution.py:475
  33.9 1.2 %shard_map.115 = (f32[16,8,256]{2,1,0:T(8,128)S(1)}, f32[7,8,128]{2,1,0:T(8,128)S(1)}) custom-call(s32[90]{0:T(128)S(4)} %get-tuple-element.60.table, f32[16,8,256]{2,1,0:T(8,128)S(1)} %get-tuple-element.61.rest_5_.wide.rest_8_, bf16[16,256,256]{2,1,0:T(8,128)(2,1)S(1)} %get-tuple-element.62.rest_6_.diag.rest_9_, ...), custom_call_target="tpu_custom_call" | custom-call | flops 600000000 | bytes 37500000 | tf_op jit(solution)/shard_map/pallas_call | solution.py:475
  35.2 2.4 %collective-permute-start.17 = (f32[13,8,128]{2,1,0:T(8,128)S(1)}, f32[13,8,128]{2,1,0:T(8,128)S(1)}, u32[]{:S(2)}, u32[]{:S(2)}) collective-permute-start(f32[13,8,128]{2,1,0:T(8,128)S(1)} %get-tuple-element.99), channel_id=1, source_target_pairs={{0,6},{1,7},{2,4},{3,5},{4,2},{5,3},{6,0},{7,1},{8,14},{9,15},{10,... | collective-permute-start | bytes 159752 | tf_op jit(solution)/shard_map/ppermute | solution.py:517
  38.8 1.2 %collective-permute-done.15.rest_0_ = f32[7,8,128]{2,1,0:T(8,128)S(1)} collective-permute-done((f32[7,8,128]{2,1,0:T(8,128)S(1)}, f32[7,8,128]{2,1,0:T(8,128)S(1)}, u32[]{:S(2)}, u32[]{:S(2)}) %collective-permute-start.15) | collective-permute-done | bytes 28704 | tf_op jit(solution)/shard_map/ppermute | solution.py:517
  40.4 1.4 %collective-permute-done.18.rest_2_ = f32[13,8,128]{2,1,0:T(8,128)S(1)} collective-permute-done((f32[13,8,128]{2,1,0:T(8,128)S(1)}, f32[13,8,128]{2,1,0:T(8,128)S(1)}, u32[]{:S(2)}, u32[]{:S(2)}) %collective-permute-start.18) | collective-permute-done | bytes 53280 | tf_op jit(solution)/shard_map/ppermute | solution.py:517
  42.3 1.9 %shard_map.117 = (f32[16,8,256]{2,1,0:T(8,128)S(1)}, f32[16,8,256]{2,1,0:T(8,128)S(1)}, bf16[16,16,256]{2,1,0:T(8,128)(2,1)S(1)}, f32[8,128]{1,0:T(8,128)S(1)}, ...) custom-call(s32[90]{0:T(128)S(4)} %get-tuple-element.60.table, f32[7,8,128]{2,1,0:T(8,128)S(1)} %collective-permute-done.15.rest_0_, ...), custom_call_target="tpu_custom_call" | custom-call | flops 600000000 | bytes 37500000 | tf_op jit(solution)/shard_map/pallas_call | solution.py:475
  44.2 1.3 %shard_map.118 = (f32[16,8,256]{2,1,0:T(8,128)S(1)}, f32[7,8,128]{2,1,0:T(8,128)S(1)}, f32[8,128]{1,0:T(8,128)S(1)}) custom-call(s32[90]{0:T(128)S(4)} %get-tuple-element.60.table, f32[16,8,256]{2,1,0:T(8,128)S(1)} %get-tuple-element.61.rest_5_.wide.rest_8_, bf16[16,256,256]{2,1,0:T(8,128)(2,1)S(1)} %get-tuple-element.62.rest_6_.diag.rest_9_, ...), custom_call_target="tpu_custom_call" | custom-call | flops 600000000 | bytes 37500000 | tf_op jit(solution)/shard_map/pallas_call | solution.py:475
  46.0 0.9 %collective-permute-done.21.rest_3_.beside = f32[7,8,128]{2,1,0:T(8,128)S(1)} collective-permute-done((f32[7,8,128]{2,1,0:T(8,128)S(1)}, f32[7,8,128]{2,1,0:T(8,128)S(1)}, u32[]{:S(2)}, u32[]{:S(2)}) %collective-permute-start.21) | collective-permute-done | bytes 28704 | tf_op jit(solution)/shard_map/ppermute | solution.py:517
  46.9 1.6 %collective-permute-start.22 = (f32[13,8,128]{2,1,0:T(8,128)S(1)}, f32[13,8,128]{2,1,0:T(8,128)S(1)}, u32[]{:S(2)}, u32[]{:S(2)}) collective-permute-start(f32[13,8,128]{2,1,0:T(8,128)S(1)} %get-tuple-element.110), channel_id=1, source_target_pairs={{0,6},{1,7},{2,4},{3,5},{4,2},{5,3},{6,0},{7,1},{8,14},{9,15},{10,... | collective-permute-start | bytes 159752 | tf_op jit(solution)/shard_map/ppermute | solution.py:517
  49.0 1.4 %collective-permute-start.24 = (f32[13,8,128]{2,1,0:T(8,128)S(1)}, f32[13,8,128]{2,1,0:T(8,128)S(1)}, u32[]{:S(2)}, u32[]{:S(2)}) collective-permute-start(f32[13,8,128]{2,1,0:T(8,128)S(1)} %get-tuple-element.112), channel_id=1, source_target_pairs={{0,4},{1,5},{2,6},{3,7},{4,0},{5,1},{6,2},{7,3},{8,12},{9,13},{10,... | collective-permute-start | bytes 159752 | tf_op jit(solution)/shard_map/ppermute | solution.py:517
  50.5 1.6 %collective-permute-done.22.rest_0_ = f32[13,8,128]{2,1,0:T(8,128)S(1)} collective-permute-done((f32[13,8,128]{2,1,0:T(8,128)S(1)}, f32[13,8,128]{2,1,0:T(8,128)S(1)}, u32[]{:S(2)}, u32[]{:S(2)}) %collective-permute-start.22) | collective-permute-done | bytes 53280 | tf_op jit(solution)/shard_map/ppermute | solution.py:517
  53.5 3.7 %collective-permute-start.27 = (f32[8,128]{1,0:T(8,128)S(1)}, f32[8,128]{1,0:T(8,128)S(1)}, u32[]{:S(2)}, u32[]{:S(2)}) collective-permute-start(f32[8,128]{1,0:T(8,128)S(1)} %shard_map.120.rest_0_), channel_id=1, source_target_pairs={{0,24},{8,16},{16,8},{24,0},{1,25},{9,17},{17,9},{25,1},{2,26},{10... | collective-permute-start | bytes 12296 | tf_op jit(solution)/shard_map/ppermute | solution.py:592
  57.1 0.8 %collective-permute-start.25 = (f32[8,128]{1,0:T(8,128)S(1)}, f32[8,128]{1,0:T(8,128)S(1)}, u32[]{:S(2)}, u32[]{:S(2)}) collective-permute-start(f32[8,128]{1,0:T(8,128)S(1)} %shard_map.120.rest_0_), channel_id=1, source_target_pairs={{0,8},{8,0},{16,24},{24,16},{1,9},{9,1},{17,25},{25,17},{2,10},{10... | collective-permute-start | bytes 12296 | tf_op jit(solution)/shard_map/ppermute | solution.py:592
  58.2 0.7 %collective-permute-done.27.rest_3_ = f32[8,128]{1,0:T(8,128)S(1)} collective-permute-done((f32[8,128]{1,0:T(8,128)S(1)}, f32[8,128]{1,0:T(8,128)S(1)}, u32[]{:S(2)}, u32[]{:S(2)}) %collective-permute-start.27) | collective-permute-done | bytes 4128 | tf_op jit(solution)/shard_map/ppermute | solution.py:592
  58.9 2.7 %collective-permute-done.26.rest_2_ = f32[8,128]{1,0:T(8,128)S(1)} collective-permute-done((f32[8,128]{1,0:T(8,128)S(1)}, f32[8,128]{1,0:T(8,128)S(1)}, u32[]{:S(2)}, u32[]{:S(2)}) %collective-permute-start.26) | collective-permute-done | bytes 4128 | tf_op jit(solution)/shard_map/ppermute | solution.py:592
  61.6 1.2 %shard_map.122 = (f32[8,16,256]{2,1,0:T(8,128)}, f32[8,16,256]{2,1,0:T(8,128)}) custom-call(f32[8,128]{1,0:T(8,128)S(1)} %shard_map.120.rest_0_, f32[8,128]{1,0:T(8,128)S(1)} %collective-permute-done.25.rest_1_, f32[8,128]{1,0:T(8,128)S(1)} %collective-permute-done.26.rest_2_, f32[8,128]{1,0:T(8,128)S(1)} %collective-permute-done.27.rest_3_, ...), custom_call_target="tpu_custom_call" | custom-call | flops 4000000 | bytes 250000 | tf_op jit(solution)/shard_map/pallas_call | solution.py:475
  (43 shorter events, 10.8 us)
Async XLA Ops:
  1.7 1.5 %collective-permute-start.1 = (f32[36,8,128]{2,1,0:T(8,128)S(1)}, f32[36,8,128]{2,1,0:T(8,128)S(1)}, u32[]{:S(2)}, u32[]{:S(2)}) collective-permute-start(f32[36,8,128]{2,1,0:T(8,128)S(1)} %get-tuple-element.67), channel_id=1, source_target_pairs={{0,1},{1,0},{2,3},{3,2},{4,5},{5,4},{6,7},{7,6},{8,9},{9,8},{10,11... | collective-permute-start | bytes 442376 | tf_op jit(solution)/shard_map/ppermute | solution.py:517
  3.2 7.5 %collective-permute-start.2 = (f32[24,8,128]{2,1,0:T(8,128)S(1)}, f32[24,8,128]{2,1,0:T(8,128)S(1)}, u32[]{:S(2)}, u32[]{:S(2)}) collective-permute-start(f32[24,8,128]{2,1,0:T(8,128)S(1)} %get-tuple-element.68), channel_id=1, source_target_pairs={{0,6},{1,7},{2,4},{3,5},{4,2},{5,3},{6,0},{7,1},{8,14},{9,15},{10,... | collective-permute-start | bytes 294920 | tf_op jit(solution)/shard_map/ppermute | solution.py:517
  7.1 5.5 %collective-permute-start.3 = (f32[24,8,128]{2,1,0:T(8,128)S(1)}, f32[24,8,128]{2,1,0:T(8,128)S(1)}, u32[]{:S(2)}, u32[]{:S(2)}) collective-permute-start(f32[24,8,128]{2,1,0:T(8,128)S(1)} %get-tuple-element.69), channel_id=1, source_target_pairs={{0,2},{1,3},{2,0},{3,1},{4,6},{5,7},{6,4},{7,5},{8,10},{9,11},{10,... | collective-permute-start | bytes 294920 | tf_op jit(solution)/shard_map/ppermute | solution.py:517
  7.7 4.9 %collective-permute-start.4 = (f32[24,8,128]{2,1,0:T(8,128)S(1)}, f32[24,8,128]{2,1,0:T(8,128)S(1)}, u32[]{:S(2)}, u32[]{:S(2)}) collective-permute-start(f32[24,8,128]{2,1,0:T(8,128)S(1)} %get-tuple-element.70), channel_id=1, source_target_pairs={{0,4},{1,5},{2,6},{3,7},{4,0},{5,1},{6,2},{7,3},{8,12},{9,13},{10,... | collective-permute-start | bytes 294920 | tf_op jit(solution)/shard_map/ppermute | solution.py:517
  7.8 2.3 %collective-permute-start = (f32[12,8,128]{2,1,0:T(8,128)S(1)}, f32[12,8,128]{2,1,0:T(8,128)S(1)}, u32[]{:S(2)}, u32[]{:S(2)}) collective-permute-start(f32[12,8,128]{2,1,0:T(8,128)S(1)} %get-tuple-element.64), channel_id=1, source_target_pairs={{0,1},{1,0},{2,3},{3,2},{4,5},{5,4},{6,7},{7,6},{8,9},{9,8},{10,11... | collective-permute-start | bytes 147464 | tf_op jit(solution)/shard_map/ppermute | solution.py:517
  13.6 1.8 %collective-permute-start.6 = (f32[19,8,128]{2,1,0:T(8,128)S(1)}, f32[19,8,128]{2,1,0:T(8,128)S(1)}, u32[]{:S(2)}, u32[]{:S(2)}) collective-permute-start(f32[19,8,128]{2,1,0:T(8,128)S(1)} %get-tuple-element.78), channel_id=1, source_target_pairs={{0,1},{1,0},{2,3},{3,2},{4,5},{5,4},{6,7},{7,6},{8,9},{9,8},{10,11... | collective-permute-start | bytes 233480 | tf_op jit(solution)/shard_map/ppermute | solution.py:517
  14.8 4.5 %collective-permute-start.5 = (f32[7,8,128]{2,1,0:T(8,128)S(1)}, f32[7,8,128]{2,1,0:T(8,128)S(1)}, u32[]{:S(2)}, u32[]{:S(2)}) collective-permute-start(f32[7,8,128]{2,1,0:T(8,128)S(1)} %get-tuple-element.75), channel_id=1, source_target_pairs={{0,1},{1,0},{2,3},{3,2},{4,5},{5,4},{6,7},{7,6},{8,9},{9,8},{10,11... | collective-permute-start | bytes 86024 | tf_op jit(solution)/shard_map/ppermute | solution.py:517
  15.4 5.4 %collective-permute-start.7 = (f32[13,8,128]{2,1,0:T(8,128)S(1)}, f32[13,8,128]{2,1,0:T(8,128)S(1)}, u32[]{:S(2)}, u32[]{:S(2)}) collective-permute-start(f32[13,8,128]{2,1,0:T(8,128)S(1)} %get-tuple-element.79), channel_id=1, source_target_pairs={{0,6},{1,7},{2,4},{3,5},{4,2},{5,3},{6,0},{7,1},{8,14},{9,15},{10,... | collective-permute-start | bytes 159752 | tf_op jit(solution)/shard_map/ppermute | solution.py:517
  17.9 4.1 %collective-permute-start.8 = (f32[13,8,128]{2,1,0:T(8,128)S(1)}, f32[13,8,128]{2,1,0:T(8,128)S(1)}, u32[]{:S(2)}, u32[]{:S(2)}) collective-permute-start(f32[13,8,128]{2,1,0:T(8,128)S(1)} %get-tuple-element.80), channel_id=1, source_target_pairs={{0,2},{1,3},{2,0},{3,1},{4,6},{5,7},{6,4},{7,5},{8,10},{9,11},{10,... | collective-permute-start | bytes 159752 | tf_op jit(solution)/shard_map/ppermute | solution.py:517
  18.4 4.1 %collective-permute-start.9 = (f32[13,8,128]{2,1,0:T(8,128)S(1)}, f32[13,8,128]{2,1,0:T(8,128)S(1)}, u32[]{:S(2)}, u32[]{:S(2)}) collective-permute-start(f32[13,8,128]{2,1,0:T(8,128)S(1)} %get-tuple-element.81), channel_id=1, source_target_pairs={{0,4},{1,5},{2,6},{3,7},{4,0},{5,1},{6,2},{7,3},{8,12},{9,13},{10,... | collective-permute-start | bytes 159752 | tf_op jit(solution)/shard_map/ppermute | solution.py:517
  24.4 1.3 %collective-permute-start.11 = (f32[19,8,128]{2,1,0:T(8,128)S(1)}, f32[19,8,128]{2,1,0:T(8,128)S(1)}, u32[]{:S(2)}, u32[]{:S(2)}) collective-permute-start(f32[19,8,128]{2,1,0:T(8,128)S(1)} %get-tuple-element.88), channel_id=1, source_target_pairs={{0,1},{1,0},{2,3},{3,2},{4,5},{5,4},{6,7},{7,6},{8,9},{9,8},{10,11... | collective-permute-start | bytes 233480 | tf_op jit(solution)/shard_map/ppermute | solution.py:517
  25.7 5.2 %collective-permute-start.12 = (f32[13,8,128]{2,1,0:T(8,128)S(1)}, f32[13,8,128]{2,1,0:T(8,128)S(1)}, u32[]{:S(2)}, u32[]{:S(2)}) collective-permute-start(f32[13,8,128]{2,1,0:T(8,128)S(1)} %get-tuple-element.89), channel_id=1, source_target_pairs={{0,6},{1,7},{2,4},{3,5},{4,2},{5,3},{6,0},{7,1},{8,14},{9,15},{10,... | collective-permute-start | bytes 159752 | tf_op jit(solution)/shard_map/ppermute | solution.py:517
  27.3 4.1 %collective-permute-start.13 = (f32[13,8,128]{2,1,0:T(8,128)S(1)}, f32[13,8,128]{2,1,0:T(8,128)S(1)}, u32[]{:S(2)}, u32[]{:S(2)}) collective-permute-start(f32[13,8,128]{2,1,0:T(8,128)S(1)} %get-tuple-element.90), channel_id=1, source_target_pairs={{0,2},{1,3},{2,0},{3,1},{4,6},{5,7},{6,4},{7,5},{8,10},{9,11},{10,... | collective-permute-start | bytes 159752 | tf_op jit(solution)/shard_map/ppermute | solution.py:517
  27.8 4.2 %collective-permute-start.14 = (f32[13,8,128]{2,1,0:T(8,128)S(1)}, f32[13,8,128]{2,1,0:T(8,128)S(1)}, u32[]{:S(2)}, u32[]{:S(2)}) collective-permute-start(f32[13,8,128]{2,1,0:T(8,128)S(1)} %get-tuple-element.91), channel_id=1, source_target_pairs={{0,4},{1,5},{2,6},{3,7},{4,0},{5,1},{6,2},{7,3},{8,12},{9,13},{10,... | collective-permute-start | bytes 159752 | tf_op jit(solution)/shard_map/ppermute | solution.py:517
  29.3 1.2 %collective-permute-start.10 = (f32[7,8,128]{2,1,0:T(8,128)S(1)}, f32[7,8,128]{2,1,0:T(8,128)S(1)}, u32[]{:S(2)}, u32[]{:S(2)}) collective-permute-start(f32[7,8,128]{2,1,0:T(8,128)S(1)} %get-tuple-element.85), channel_id=1, source_target_pairs={{0,1},{1,0},{2,3},{3,2},{4,5},{5,4},{6,7},{7,6},{8,9},{9,8},{10,11... | collective-permute-start | bytes 86024 | tf_op jit(solution)/shard_map/ppermute | solution.py:517
  33.9 1.3 %collective-permute-start.16 = (f32[19,8,128]{2,1,0:T(8,128)S(1)}, f32[19,8,128]{2,1,0:T(8,128)S(1)}, u32[]{:S(2)}, u32[]{:S(2)}) collective-permute-start(f32[19,8,128]{2,1,0:T(8,128)S(1)} %get-tuple-element.98), channel_id=1, source_target_pairs={{0,1},{1,0},{2,3},{3,2},{4,5},{5,4},{6,7},{7,6},{8,9},{9,8},{10,11... | collective-permute-start | bytes 233480 | tf_op jit(solution)/shard_map/ppermute | solution.py:517
  35.2 5.1 %collective-permute-start.17 = (f32[13,8,128]{2,1,0:T(8,128)S(1)}, f32[13,8,128]{2,1,0:T(8,128)S(1)}, u32[]{:S(2)}, u32[]{:S(2)}) collective-permute-start(f32[13,8,128]{2,1,0:T(8,128)S(1)} %get-tuple-element.99), channel_id=1, source_target_pairs={{0,6},{1,7},{2,4},{3,5},{4,2},{5,3},{6,0},{7,1},{8,14},{9,15},{10,... | collective-permute-start | bytes 159752 | tf_op jit(solution)/shard_map/ppermute | solution.py:517
  37.6 4.1 %collective-permute-start.18 = (f32[13,8,128]{2,1,0:T(8,128)S(1)}, f32[13,8,128]{2,1,0:T(8,128)S(1)}, u32[]{:S(2)}, u32[]{:S(2)}) collective-permute-start(f32[13,8,128]{2,1,0:T(8,128)S(1)} %get-tuple-element.100), channel_id=1, source_target_pairs={{0,2},{1,3},{2,0},{3,1},{4,6},{5,7},{6,4},{7,5},{8,10},{9,11},{10,... | collective-permute-start | bytes 159752 | tf_op jit(solution)/shard_map/ppermute | solution.py:517
  38.2 4.1 %collective-permute-start.19 = (f32[13,8,128]{2,1,0:T(8,128)S(1)}, f32[13,8,128]{2,1,0:T(8,128)S(1)}, u32[]{:S(2)}, u32[]{:S(2)}) collective-permute-start(f32[13,8,128]{2,1,0:T(8,128)S(1)} %get-tuple-element.101), channel_id=1, source_target_pairs={{0,4},{1,5},{2,6},{3,7},{4,0},{5,1},{6,2},{7,3},{8,12},{9,13},{10,... | collective-permute-start | bytes 159752 | tf_op jit(solution)/shard_map/ppermute | solution.py:517
  38.8 1.2 %collective-permute-start.15 = (f32[7,8,128]{2,1,0:T(8,128)S(1)}, f32[7,8,128]{2,1,0:T(8,128)S(1)}, u32[]{:S(2)}, u32[]{:S(2)}) collective-permute-start(f32[7,8,128]{2,1,0:T(8,128)S(1)} %get-tuple-element.95), channel_id=1, source_target_pairs={{0,1},{1,0},{2,3},{3,2},{4,5},{5,4},{6,7},{7,6},{8,9},{9,8},{10,11... | collective-permute-start | bytes 86024 | tf_op jit(solution)/shard_map/ppermute | solution.py:517
  44.2 2.7 %collective-permute-start.20 = (f32[19,8,128]{2,1,0:T(8,128)S(1)}, f32[19,8,128]{2,1,0:T(8,128)S(1)}, u32[]{:S(2)}, u32[]{:S(2)}) collective-permute-start(f32[19,8,128]{2,1,0:T(8,128)S(1)} %get-tuple-element.107), channel_id=1, source_target_pairs={{0,1},{1,0},{2,3},{3,2},{4,5},{5,4},{6,7},{7,6},{8,9},{9,8},{10,11... | collective-permute-start | bytes 233480 | tf_op jit(solution)/shard_map/ppermute | solution.py:517
  45.5 1.4 %collective-permute-start.21 = (f32[7,8,128]{2,1,0:T(8,128)S(1)}, f32[7,8,128]{2,1,0:T(8,128)S(1)}, u32[]{:S(2)}, u32[]{:S(2)}) collective-permute-start(f32[7,8,128]{2,1,0:T(8,128)S(1)} %get-tuple-element.108), channel_id=1, source_target_pairs={{0,1},{1,0},{2,3},{3,2},{4,5},{5,4},{6,7},{7,6},{8,9},{9,8},{10,11... | collective-permute-start | bytes 86024 | tf_op jit(solution)/shard_map/ppermute | solution.py:517
  46.9 5.2 %collective-permute-start.22 = (f32[13,8,128]{2,1,0:T(8,128)S(1)}, f32[13,8,128]{2,1,0:T(8,128)S(1)}, u32[]{:S(2)}, u32[]{:S(2)}) collective-permute-start(f32[13,8,128]{2,1,0:T(8,128)S(1)} %get-tuple-element.110), channel_id=1, source_target_pairs={{0,6},{1,7},{2,4},{3,5},{4,2},{5,3},{6,0},{7,1},{8,14},{9,15},{10,... | collective-permute-start | bytes 159752 | tf_op jit(solution)/shard_map/ppermute | solution.py:517
  48.5 4.1 %collective-permute-start.23 = (f32[13,8,128]{2,1,0:T(8,128)S(1)}, f32[13,8,128]{2,1,0:T(8,128)S(1)}, u32[]{:S(2)}, u32[]{:S(2)}) collective-permute-start(f32[13,8,128]{2,1,0:T(8,128)S(1)} %get-tuple-element.111), channel_id=1, source_target_pairs={{0,2},{1,3},{2,0},{3,1},{4,6},{5,7},{6,4},{7,5},{8,10},{9,11},{10,... | collective-permute-start | bytes 159752 | tf_op jit(solution)/shard_map/ppermute | solution.py:517
  49.0 4.1 %collective-permute-start.24 = (f32[13,8,128]{2,1,0:T(8,128)S(1)}, f32[13,8,128]{2,1,0:T(8,128)S(1)}, u32[]{:S(2)}, u32[]{:S(2)}) collective-permute-start(f32[13,8,128]{2,1,0:T(8,128)S(1)} %get-tuple-element.112), channel_id=1, source_target_pairs={{0,4},{1,5},{2,6},{3,7},{4,0},{5,1},{6,2},{7,3},{8,12},{9,13},{10,... | collective-permute-start | bytes 159752 | tf_op jit(solution)/shard_map/ppermute | solution.py:517
  53.5 5.5 %collective-permute-start.27 = (f32[8,128]{1,0:T(8,128)S(1)}, f32[8,128]{1,0:T(8,128)S(1)}, u32[]{:S(2)}, u32[]{:S(2)}) collective-permute-start(f32[8,128]{1,0:T(8,128)S(1)} %shard_map.120.rest_0_), channel_id=1, source_target_pairs={{0,24},{8,16},{16,8},{24,0},{1,25},{9,17},{17,9},{25,1},{2,26},{10... | collective-permute-start | bytes 12296 | tf_op jit(solution)/shard_map/ppermute | solution.py:592
  57.1 4.5 %collective-permute-start.26 = (f32[8,128]{1,0:T(8,128)S(1)}, f32[8,128]{1,0:T(8,128)S(1)}, u32[]{:S(2)}, u32[]{:S(2)}) collective-permute-start(f32[8,128]{1,0:T(8,128)S(1)} %shard_map.120.rest_0_), channel_id=1, source_target_pairs={{0,16},{8,24},{16,0},{24,8},{1,17},{9,25},{17,1},{25,9},{2,18},{10... | collective-permute-start | bytes 12296 | tf_op jit(solution)/shard_map/ppermute | solution.py:592
  57.1 4.5 %collective-permute-start.25 = (f32[8,128]{1,0:T(8,128)S(1)}, f32[8,128]{1,0:T(8,128)S(1)}, u32[]{:S(2)}, u32[]{:S(2)}) collective-permute-start(f32[8,128]{1,0:T(8,128)S(1)} %shard_map.120.rest_0_), channel_id=1, source_target_pairs={{0,8},{8,0},{16,24},{24,16},{1,9},{9,1},{17,25},{25,17},{2,10},{10... | collective-permute-start | bytes 12296 | tf_op jit(solution)/shard_map/ppermute | solution.py:592

commit v7 on v6

--- a/solution.py
+++ b/solution.py
@@ -63,7 +63,9 @@
         self.extra = self.extra_chunks * LANES
         self.halves = self.width // LANES
         evens = range(2, self.peers, 2)
-        self.far = sorted(evens, key=lambda m: -m.bit_count())
+        self.beyond = [m for m in evens if m & (m - 1)]
+        self.beside = [m for m in evens if m & (m - 1) == 0]
+        self.far = self.beyond + self.beside
         self.handed = [m + 1 for m in self.far]
         self.slots = self.peers * self.capacity
         self.inverse = self.slots
@@ -82,9 +84,22 @@
     def near_rows(self, kinds):
         return len(self.handed) * self.rows(kinds)
 
+    def at(self, k, core):
+        first = len(self.beyond)
+        return k if k < first else first + (k - first + core) % len(self.beside)
+
+    def mine(self, k):
+        core = lax.axis_index("sub") & 1
+        at = [self.at(k, c) for c in range(2)]
+        return tuple(
+            jnp.where(core == 0, jnp.int32(a), jnp.int32(b))
+            for a, b in [at, [self.far[n] for n in at]]
+        )
+
     def sources(self):
         found = [(1, 0, 0)]
-        for k, m in enumerate(self.far):
+        for k in range(len(self.far)):
+            _, m = self.mine(k)
             found += [(m + side, 1 + k, side) for side in range(2)]
         return found
 
@@ -138,22 +153,19 @@
     return jnp.concatenate([piece[row + j] for j in range(z.extra_chunks)], axis=1)
 
 
-def relay(z, kinds, late, table, *rest):
+def relay(z, kinds, table, *rest):
     sources, rest = rest[:kinds], rest[kinds:]
     if kinds == 1:
         extra, rest = rest[0], rest[1:]
-    near, rest = rest[0], rest[1:]
-    if late:
-        beside, rest = rest[0], rest[1:]
+    near, pieces = rest[0], rest[1:]
     rows = z.rows(kinds)
     if kinds == 1:
         tile = extra[...] + load_extra(z, near, z.near_rows(1))
-        if late:
-            tile = tile + load_extra(z, beside, rows)
-    for k, (m, piece) in enumerate(zip(z.far, rest)):
+    for k, piece in enumerate(pieces):
+        which, m = z.mine(k)
         fill_piece(z, table, sources, m, piece, 0)
         for row in range(rows):
-            piece[rows + row] = near[k * rows + row]
+            piece[rows + row] = near[which * rows + row]
         if kinds == 1:
             store_extra(z, tile, piece, 2 * rows)
 
@@ -168,8 +180,8 @@
                 row += 1
 
 
-def begin(z, partner, pattern, load, scale, coupling, table, field, lift, wide, coupling_out, near, beside, *scratch):
-    here, scale_here, partner_here, pattern_here, counts, sems = scratch
+def begin(z, partner, pattern, load, scale, coupling, table, field, lift, wide, corners, near, beside, *scratch):
+    here, scale_here, coupling_here, partner_here, pattern_here, counts, sems = scratch
     copies = [
         pltpu.make_async_copy(a, b, sems.at[k])
         for k, (a, b) in enumerate(
@@ -178,7 +190,7 @@
                 (pattern, pattern_here),
                 (load, here),
                 (scale, scale_here),
-                (coupling, coupling_out),
+                (coupling, coupling_here),
             ]
         )
     ]
@@ -193,7 +205,9 @@
         field[i] = here[:, i, :]
         row = jnp.broadcast_to(scale_here[i : i + 1, :], (z.columns, z.width))
         wide[i] = row
-        lift[i] = row * coupling_out[:, i * z.width : (i + 1) * z.width].astype(F32)
+        part = coupling_here[:, i * z.width : (i + 1) * z.width].astype(F32)
+        lift[i] = row * part
+        corners[i] = jnp.concatenate([part, jnp.zeros_like(part)], axis=0).astype(BF16)
     fill_near(z, table, [field, lift], near)
     fill_piece(z, table, [field, lift], 1, beside, 0)
 
@@ -227,25 +241,38 @@
     copies[3].wait()
 
 
-def build_lift(z, table, operator, lift, *rest):
-    pieces, (jump_lift, other) = rest[:-2], rest[-2:]
-    place(z, table, pieces, 1, 2, other)
+def build_lift(z, table, operator, lift, wide, diag, off, corners, *rest):
+    count = 1 + len(z.far)
+    arrived, (jump_lift, image_lift, corner_lift, other, scaled, half) = rest[:count], rest[count:]
+    place(z, table, arrived, 1, 2, other)
     me = lax.axis_index("sub")
     own = operator[pl.ds(pl.multiple_of(me * z.corners, z.corners), z.corners), :]
+    size = 2 * z.corners
+    to_corners = jnp.zeros((2 * z.all_corners, size), F32)
     for i in range(z.blocks):
         at = pl.multiple_of(table[z.partner + i] * z.corners, z.corners)
         left = split(jnp.concatenate([own, -operator[pl.ds(at, z.corners), :]], axis=0))
         right = split(jnp.concatenate([lift[i], other[i]], axis=0))
-        count = 2 * z.corners
-        left = jnp.concatenate([left, left[:count]], axis=0)
-        right = jnp.concatenate([right[:count], right[:count], right[count:]], axis=0)
-        jump_lift[i] = split(dot(left, right, TN))
-
-
-def extra_sum(z, own, near, beside, *far):
+        left = jnp.concatenate([left, left[:size]], axis=0)
+        right = jnp.concatenate([right[:size], right[:size], right[size:]], axis=0)
+        jump = dot(left, right, TN)
+        jump_lift[i] = split(jump)
+        jump = wide[i, 0:1, :] * jump
+        scaled[i] = jump
+        half[i] = jump.astype(BF16)
+        to_corners = to_corners + dot(split(jump), corners[i], NT)
+    corner_lift[...] = split(fold(to_corners))
+    for i in range(z.blocks):
+        source = table[z.inverse + i]
+        mine = half[i]
+        coupled = dot(mine, diag[i], NT) + dot(mine, diag[i], NN)
+        coupled = coupled + dot(half[table[z.pattern + i]], off[i], NT)
+        coupled = coupled + dot(half[source], off[source], NN)
+        image_lift[i] = split(wide[i, 0:1, :] * (scaled[i] + coupled))
+
+
+def extra_sum(z, own, near, *far):
     total = own[...] + load_extra(z, near, z.near_rows(1))
-    if beside is not None:
-        total = total + load_extra(z, beside, z.rows(1))
     for piece in far:
         total = total + load_extra(z, piece, 2 * z.rows(1))
     return total
@@ -266,92 +293,98 @@
     return jnp.sum(a, axis=1, keepdims=True)
 
 
-def couple(z, table, position, wide, diag, off, parts, field, image):
-    i = table[z.order + position]
+def couple(z, i, table, wide, diag, off, parts, diff, rows, image_lift, shrink):
     source = table[z.inverse + i]
     mine = parts[i]
     coupled = dot(mine, diag[i], NT) + dot(mine, diag[i], NN)
     coupled = coupled + dot(parts[table[z.pattern + i]], off[i], NT)
     coupled = coupled + dot(parts[source], off[source], NN)
     row = wide[i]
-    image[i] = row * (row * field[i] + fold(coupled))
+    value = row * (row * diff[i] + fold(coupled))
+    if rows is not None:
+        value = (value + fold(dot(rows, image_lift[i], NN))) * shrink
+    return value
+
+
+def corner_data(z, total):
+    return corner_rows(z, total), 1.0 / cluster_max(z, total)
 
 
 def first_half(z, step, table, *rest):
+    first, last = step == 1, step == ITERS
     rest = list(rest)
     take = lambda n: [rest.pop(0) for _ in range(n)]
     beside, *far = take(1 + len(z.far))
     (before,) = take(1)
-    if step > 1:
-        near, own_extra, jump_lift = take(3)
-    wide, diag, off, coupling = take(4)
-    field, image, parts = take(3)
-    if step > 1:
+    if not first:
+        near, own_extra, image_lift, corner_lift = take(4)
+    wide, diag, off, corners = take(4)
+    if last:
+        jump_lift, *older = take(ITERS)
+    elif not first:
+        take(step - 2)
+    diff, image = take(2)
+    if not last:
+        (parts,) = take(1)
+    if not first:
         (total_out,) = take(1)
-    extra, near_out, other = rest
-    place(z, table, [beside, *far], 0, 2 if step == 1 else 1, other)
-    if step > 1:
-        total = extra_sum(z, own_extra, near, None, *far)
-        total_out[...] = total
-        rows = corner_rows(z, total)
-        shrink = 1.0 / cluster_max(z, total)
-    partial = jnp.zeros((2 * z.columns, z.corners), F32)
+    if last:
+        field, beside_out = take(2)
+    extra, near_out, other = take(3)
+    if last:
+        (parts,) = rest
+    place(z, table, [beside, *far], 0, 2 if first else 1, other)
+    partial = jnp.zeros((2 * z.columns, 2 * z.corners), F32)
     top = jnp.zeros((z.columns, z.width), F32)
     for i in range(z.blocks):
         value = before[i] - other[i]
-        if step > 1:
-            value = (value + fold(dot(rows, jump_lift[i], NN))) * shrink
-        field[i] = value
+        diff[i] = value
         scaled = wide[i] * value
         top = jnp.maximum(top, jnp.abs(wide[i] * scaled))
         mine = split(scaled)
         parts[i] = mine
-        partial = partial + dot(mine, coupling[:, i * z.width : (i + 1) * z.width], NT)
-    work = functools.partial(couple, z, table)
-    refs = (wide, diag, off, parts, field, image)
-    for position in range(z.early):
-        work(position, *refs)
-
-    @pl.when(table[z.count] > z.early)
-    def _():
-        for position in range(z.early, z.middle):
-            work(position, *refs)
+        partial = partial + dot(mine, corners[i], NT)
+    sums = fold(partial)
+    if first:
+        more = (None, None, None)
+    else:
+        total = extra_sum(z, own_extra, near, *far)
+        total_out[...] = total
+        rows, shrink = corner_data(z, total)
+        sums = (sums + fold(dot(rows, corner_lift[...], NN))) * shrink
+        top = top * shrink
+        more = (rows, image_lift, shrink)
+    refs = (table, wide, diag, off, parts, diff, *more)
+    if last:
+        for i in range(z.blocks):
+            value = couple(z, i, *refs)
+            image[i] = value
+            top = jnp.maximum(top, jnp.abs(value))
+        fill_piece(z, table, [image], 1, beside_out, 0)
+    else:
+        for position in range(z.early):
+            i = table[z.order + position]
+            value = couple(z, i, *refs)
+            image[i] = value
+            top = jnp.maximum(top, jnp.abs(value))
+
+        @pl.when(table[z.count] > z.early)
+        def _():
+            for position in range(z.early, z.middle):
+                i = table[z.order + position]
+                image[i] = couple(z, i, *refs)
 
     fill_near(z, table, [image], near_out)
     me = lax.axis_index("sub")
     lanes = lane_ids((z.columns, z.extra))
-    sums = fold(partial)
     padded = jnp.concatenate(
-        [sums, jnp.zeros((z.columns, z.extra - z.corners), F32)], axis=1
+        [sums, jnp.zeros((z.columns, z.extra - sums.shape[1]), F32)], axis=1
     )
     tile = pltpu.roll(padded, me * z.corners, 1)
     tile = jnp.where(lanes == z.max_lane + me, jnp.max(top, axis=1, keepdims=True), tile)
-    extra[...] = tile
-    store_extra(z, tile, near_out, z.near_rows(1))
-
-
-def second_half(z, last, table, wide, diag, off, parts, field, image_in, *rest):
-    rest = list(rest)
-    take = lambda n: [rest.pop(0) for _ in range(n)]
-    extra, *older = take(ITERS) if last else (None,)
-    image, beside = take(2)
-    work = functools.partial(couple, z, table)
-    refs = (wide, diag, off, parts, field, image)
-    for i in range(z.blocks):
-        image[i] = image_in[i]
-
-    @pl.when(table[z.count] <= z.early)
-    def _():
-        for position in range(z.early, z.middle):
-            work(position, *refs)
-
-    for position in range(z.middle, z.blocks):
-        work(position, *refs)
-    fill_piece(z, table, [image], 1, beside, 0)
     if last:
-        (extra_out,) = rest
-        lanes = lane_ids((z.columns, z.extra))
-        tile = jnp.zeros((z.columns, z.extra), F32)
+        for i in range(z.blocks):
+            field[i] = (diff[i] + fold(dot(rows, jump_lift[i], NN))) * shrink
         fields = older + [field]
         products = [(fields[i], fields[j]) for i, j in PAIRS] + [(f, image) for f in fields]
         for entry, (a, b) in enumerate(products):
@@ -359,14 +392,44 @@
             for i in range(1, z.blocks):
                 acc = acc + a[i] * b[i]
             tile = jnp.where(lanes == z.gram_lane + entry, lane_sum(acc), tile)
-        extra_out[...] = extra[...] + tile
-        store_extra(z, tile, beside, z.rows(1))
-
-
-def cluster_gram(z, operator, own_extra, near, beside, *rest):
+    extra[...] = tile
+    store_extra(z, tile, near_out, z.near_rows(1))
+
+
+def second_half(z, first, table, wide, diag, off, parts, diff, image_in, *rest):
+    if first:
+        image, beside = rest
+        more = (None, None, None)
+    else:
+        total, image_lift, image, beside = rest
+        rows, shrink = corner_data(z, total[...])
+        more = (rows, image_lift, shrink)
+    refs = (table, wide, diag, off, parts, diff, *more)
+    for i in range(z.blocks):
+        image[i] = image_in[i]
+
+    @pl.when(table[z.count] <= z.early)
+    def _():
+        for position in range(z.early, z.middle):
+            i = table[z.order + position]
+            image[i] = couple(z, i, *refs)
+
+    for position in range(z.middle, z.blocks):
+        i = table[z.order + position]
+        image[i] = couple(z, i, *refs)
+    fill_piece(z, table, [image], 1, beside, 0)
+
+
+def vector(z, total, diff, jump_lift, field):
+    rows, shrink = corner_data(z, total[...])
+    for i in range(z.blocks):
+        field[i] = (diff[i] + fold(dot(rows, jump_lift[i], NN))) * shrink
+
+
+def cluster_gram(z, operator, own_extra, near, *rest):
     count = len(z.far)
     far, totals, (gram,) = rest[:count], rest[count:-1], rest[-1:]
-    total = extra_sum(z, own_extra, near, beside, *far)
+    total = extra_sum(z, own_extra, near, *far)
     totals = [t[...] for t in totals]
     partials = [t[:, : z.all_corners] for t in totals + [total]]
     lifted = dot_high(partials[-1], operator[...], NT)
@@ -386,7 +449,7 @@
 def last_vector(z, table, before, own_extra, jump_lift, near, beside, *rest):
     far, (field, other) = rest[:-2], rest[-2:]
     place(z, table, [beside, *far], 0, 1, other)
-    rows = corner_rows(z, extra_sum(z, own_extra, near, beside, *far))
+    rows = corner_rows(z, extra_sum(z, own_extra, near, *far))
     for i in range(z.blocks):
         field[i] = before[i] - other[i] + fold(dot(rows, jump_lift[i], NN))
 
@@ -508,29 +571,35 @@
         return ((rows + (z.extra_chunks if kinds == 1 else 0), cols, LANES), F32)
 
     def near_shapes(kinds):
-        return [shape(z.near_rows(kinds), kinds), shape(z.rows(kinds), kinds)]
+        return [shape(z.near_rows(kinds), kinds), ((z.rows(kinds), cols, LANES), F32)]
 
     def kernel(body, *extra_args):
         return functools.partial(body, z, *extra_args)
 
-    def across(piece, m):
-        return lax.ppermute(piece, "sub", [(t, t ^ m) for t in range(z.peers)])
-
-    def far_exchange(kinds, sources, near, late=()):
+    def across(piece, mask_of):
+        pairs = [(t, t ^ mask_of(t & 1)) for t in range(z.peers)]
+        return lax.ppermute(piece, "sub", pairs)
+
+    def to_near(piece):
+        return across(piece, lambda core: 1)
+
+    def far_exchange(kinds, sources, near):
         pieces = call(
-            kernel(relay, kinds, len(late) > 0),
-            [shape(2 * z.rows(kinds), kinds)] * len(z.far), [], light,
-            [table, *sources, near, *late],
+            kernel(relay, kinds), [shape(2 * z.rows(kinds), kinds)] * len(z.far), [], light,
+            [table, *sources, near],
         )
-        return [across(piece, m) for m, piece in zip(z.far, pieces)]
-
-    table, loaded, lift, wide, coupling, near, beside = call(
+        return [
+            across(piece, lambda core: z.far[z.at(k, core)]) for k, piece in enumerate(pieces)
+        ]
+
+    table, loaded, lift, wide, corners, near, beside = call(
         kernel(begin),
-        [((z.table,), jnp.int32), field, field, field, (corner_coupling.shape, BF16)]
+        [((z.table,), jnp.int32), field, field, field, ((blocks, 2 * z.corners, width), BF16)]
         + near_shapes(2),
         [
             pltpu.VMEM(load.shape, F32),
             pltpu.VMEM(row_scale.shape, F32),
+            pltpu.VMEM(corner_coupling.shape, BF16),
             pltpu.SMEM(partner.shape, jnp.int32),
             pltpu.SMEM(off_pattern.shape, jnp.int32),
             pltpu.SMEM((z.peers,), jnp.int32),
@@ -540,8 +609,8 @@
         [partner, off_pattern, load, row_scale, corner_coupling],
         False, range(5),
     )
-    near = across(near, 1)
-    beside = across(beside, 1)
+    near = to_near(near)
+    beside = to_near(beside)
     arrived = [beside, *far_exchange(2, [loaded, lift], near)]
     weight = (diag_blocks.shape, BF16)
     operator, diag, off = call(
@@ -554,38 +623,57 @@
         heavy, [corner_index, coarse_inverse, diag_blocks, off_blocks], False, range(4),
     )
     half = ((blocks, 2 * cols, width), BF16)
+    coarse = (2 * z.all_corners, width)
+    fixed = [wide, diag, off, corners]
     fields, totals = [], []
-    image, own_extra, jump_lift = loaded, None, None
+    image = loaded
     for step in range(1, ITERS + 1):
-        last = step == ITERS
-        more = [near, own_extra, jump_lift] if step > 1 else []
-        newest, part, parts, *total, own_extra, near = call(
+        first, last = step == 1, step == ITERS
+        more = [] if first else [near, own_extra, image_lift, corner_lift]
+        older = [jump_lift, *fields] if last else fields[1:]
+        near_shape, beside_shape = near_shapes(1)
+        diff, part, *rest = call(
             kernel(first_half, step),
-            [field, field, half] + [extra] * (step > 1) + [extra, near_shapes(1)[0]],
-            [other], heavy, [table, *arrived, image, *more, wide, diag, off, coupling],
+            [field, field] + [half] * (not last) + [extra] * (not first)
+            + [field, beside_shape] * last + [extra, near_shape],
+            [other] + [pltpu.VMEM(*half)] * last, heavy,
+            [table, *arrived, image, *more, *fixed, *older],
         )
-        near = across(near, 1)
-        older = [own_extra, *fields] if last else []
-        image, beside, *finished = call(
-            kernel(second_half, last),
-            [field, near_shapes(1)[1]] + [extra] * last, [], heavy,
-            [table, wide, diag, off, parts, newest, part, *older],
-        )
-        beside = across(beside, 1)
-        fields.append(newest)
-        totals += total
-        if step == 1:
-            (jump_lift,) = call(
-                kernel(build_lift), [((blocks, 2 * z.all_corners, width), BF16)], [other], heavy,
-                [table, operator, lift, *arrived],
+        parts = None if last else rest.pop(0)
+        if not first:
+            totals.append(rest.pop(0))
+        if last:
+            fields.append(rest.pop(0))
+            image, beside = part, rest.pop(0)
+        own_extra, near = rest
+        near = to_near(near)
+        if not last:
+            more = [] if first else [totals[-1], image_lift]
+            image, beside = call(
+                kernel(second_half, first), [field, beside_shape], [], heavy,
+                [table, wide, diag, off, parts, diff, part, *more],
             )
-        if last:
-            (own_extra,) = finished
-        late = [beside] if last else []
-        arrived = [beside, *far_exchange(1, [image, own_extra], near, late)]
+        beside = to_near(beside)
+        if first:
+            fields.append(diff)
+            jump_lift, image_lift, corner_lift = call(
+                kernel(build_lift),
+                [((blocks, *coarse), BF16)] * 2 + [((coarse[0], 2 * z.corners), BF16)],
+                [
+                    other,
+                    pltpu.VMEM((blocks, z.all_corners, width), F32),
+                    pltpu.VMEM((blocks, z.all_corners, width), BF16),
+                ],
+                heavy, [table, operator, lift, *fixed, *arrived],
+            )
+        elif not last:
+            fields += call(
+                kernel(vector), [field], [], heavy, [totals[-1], diff, jump_lift], False
+            )
+        arrived = [beside, *far_exchange(1, [image, own_extra], near)]
     (own_gram,) = call(
         kernel(cluster_gram), [gram], [], light,
-        [operator, own_extra, near, *arrived, *totals], False,
+        [operator, own_extra, near, *arrived[1:], *totals], False,
     )
     power = z.groups & (z.groups - 1) == 0
     grams = [own_gram] + [

time: 63 us -> 62.2 us (0.987)
  waiting for transfers between devices: 20.1 us -> 17.5 us
  Pallas kernels: 17.1 us -> 18.3 us
    ppermute x25, waiting for transfers between devices: 16.7 us -> 14.1 us  [across(): return lax.ppermute(piece, 'sub', pairs)]
    pallas_call x19 -> x20, Pallas kernels: 17.1 us -> 18.3 us  [call(): pl.pallas_call(body, out_shape=shapes, in_specs=specs, out_specs=[SMEM if...]
  transfers between devices with their start and end apart: 28 -> 28, of which waited for: 22 -> 17; matrix products, arithmetic and copies ran while one was open for 0% -> 0% of each run, Pallas kernels for 12% -> 16%
where the time goes in v7:
time: 62.2 us; the launch traced here: 62.1 us
  starting transfers between devices  25.4 us (41%)
  Pallas kernels  18.3 us (29%)
  waiting for transfers between devices  17.5 us (28%)
  between operations  0.81 us (1%)
    ppermute x25, starting transfers between devices, across(): return lax.ppermute(piece, 'sub', pairs)  21 us
    pallas_call x20, Pallas kernels, call(): pl.pallas_call(body, out_shape=shapes, in_specs=specs, out_specs=[SMEM if...  18.3 us
    ppermute x25, waiting for transfers between devices, across(): return lax.ppermute(piece, 'sub', pairs)  14.1 us
    ppermute x3, starting transfers between devices, on_device(): lax.ppermute(own_gram, 'group', [(a, a ^ k if power else (a + k) % z.grou...  4.44 us
    ppermute x3, waiting for transfers between devices, on_device(): lax.ppermute(own_gram, 'group', [(a, a ^ k if power else (a + k) % z.grou...  3.42 us
  transfers between devices with their start and end apart: 28, of which 17 were waited for; matrix products, arithmetic and copies ran while one was open for 0% of the time, Pallas kernels for 16%

profile of v7, /device:TPU:0, one launch (start us, length us, event | category | flops | bytes accessed | tf_op | source)
XLA Modules:
  0.0 62.1 jit_solution(2010634583630397219)
XLA Ops:
  0.6 1.0 %shard_map.105 = (s32[90]{0:T(128)S(4)}, f32[16,8,256]{2,1,0:T(8,128)S(1)}, f32[16,8,256]{2,1,0:T(8,128)S(1)}, f32[16,8,256]{2,1,0:T(8,128)S(1)}, bf16[16,16,256...) custom-call(s32[1,16]{1,0:T(1,128)} %partner.1, s32[1,16]{1,0:T(1,128)} %pattern.1, ...), custom_call_target="tpu_custom_call" | custom-call | flops 4000000 | bytes 250000 | tf_op jit(solution)/shard_map/pallas_call | solution.py:538
  2.2 1.0 %collective-permute-done.1.rest_2_ = f32[36,8,128]{2,1,0:T(8,128)S(1)} collective-permute-done((f32[36,8,128]{2,1,0:T(8,128)S(1)}, f32[36,8,128]{2,1,0:T(8,128)S(1)}, u32[]{:S(2)}, u32[]{:S(2)}) %collective-permute-start.1) | collective-permute-done | bytes 147488 | tf_op jit(solution)/shard_map/ppermute | solution.py:581
  3.2 3.9 %collective-permute-start.2 = (f32[24,8,128]{2,1,0:T(8,128)S(1)}, f32[24,8,128]{2,1,0:T(8,128)S(1)}, u32[]{:S(2)}, u32[]{:S(2)}) collective-permute-start(f32[24,8,128]{2,1,0:T(8,128)S(1)} %get-tuple-element.68), channel_id=1, source_target_pairs={{0,6},{1,7},{2,4},{3,5},{4,2},{5,3},{6,0},{7,1},{8,14},{9,15},{10,... | collective-permute-start | bytes 294920 | tf_op jit(solution)/shard_map/ppermute | solution.py:581
  7.8 2.3 %shard_map.104 = (f32[64,64]{1,0:T(8,128)S(1)}, bf16[16,256,256]{2,1,0:T(8,128)(2,1)S(1)}, bf16[16,256,256]{2,1,0:T(8,128)(2,1)S(1)}) custom-call(s32[1,64]{1,0:T(1,128)} %index_in.1, f32[32,32]{1,0:T(8,128)} %inverse_in.1, bf16[16,256,256]{2,1,0:T(8,128)(2,1)} %diag.1, bf16[16,256,256]{2,1,0:T(8,128)(2,1)} %off.1), custom_call_target="tpu_custom_call" | custom-call | flops 600000000 | bytes 37500000 | tf_op jit(solution)/shard_map/pallas_call | solution.py:538
  10.3 2.3 %collective-permute-done.3.rest_2_ = f32[24,8,128]{2,1,0:T(8,128)S(1)} collective-permute-done((f32[24,8,128]{2,1,0:T(8,128)S(1)}, f32[24,8,128]{2,1,0:T(8,128)S(1)}, u32[]{:S(2)}, u32[]{:S(2)}) %collective-permute-start.3) | collective-permute-done | bytes 98336 | tf_op jit(solution)/shard_map/ppermute | solution.py:581
  12.6 1.1 %shard_map.107 = (f32[16,8,256]{2,1,0:T(8,128)S(1)}, f32[16,8,256]{2,1,0:T(8,128)S(1)}, bf16[16,16,256]{2,1,0:T(8,128)(2,1)S(1)}, f32[8,128]{1,0:T(8,128)S(1)}, f32[19,8,128]{2,1,0:T(8,128)S(1)}) custom-call(s32[90]{0:T(128)S(4)} %get-tuple-element.60.table, f32[12,8,128]{2,1,0:T(8,128)S(1)} %collective-permute-done.rest_0_, ...), custom_call_target="tpu_custom_call" | custom-call | flops 600000000 | bytes 37500000 | tf_op jit(solution)/shard_map/pallas_call | solution.py:538
  13.7 1.2 %shard_map.108 = (f32[16,8,256]{2,1,0:T(8,128)S(1)}, f32[6,8,128]{2,1,0:T(8,128)S(1)}) custom-call(s32[90]{0:T(128)S(4)} %get-tuple-element.60.table, f32[16,8,256]{2,1,0:T(8,128)S(1)} %get-tuple-element.61.rest_5_.wide.rest_9_, bf16[16,256,256]{2,1,0:T(8,128)(2,1)S(1)} %get-tuple-element.62.rest_6_.diag.rest_10_, ...), custom_call_target="tpu_custom_call" | custom-call | flops 600000000 | bytes 37500000 | tf_op jit(solution)/shard_map/pallas_call | solution.py:538
  15.4 1.7 %collective-permute-start.7 = (f32[13,8,128]{2,1,0:T(8,128)S(1)}, f32[13,8,128]{2,1,0:T(8,128)S(1)}, u32[]{:S(2)}, u32[]{:S(2)}) collective-permute-start(f32[13,8,128]{2,1,0:T(8,128)S(1)} %get-tuple-element.79), channel_id=1, source_target_pairs={{0,6},{1,7},{2,4},{3,5},{4,2},{5,3},{6,0},{7,1},{8,14},{9,15},{10,... | collective-permute-start | bytes 159752 | tf_op jit(solution)/shard_map/ppermute | solution.py:581
  17.2 1.3 %collective-permute-start.8 = (f32[13,8,128]{2,1,0:T(8,128)S(1)}, f32[13,8,128]{2,1,0:T(8,128)S(1)}, u32[]{:S(2)}, u32[]{:S(2)}) collective-permute-start(f32[13,8,128]{2,1,0:T(8,128)S(1)} %get-tuple-element.80), channel_id=1, source_target_pairs={{0,2},{1,5},{2,0},{3,7},{4,6},{5,1},{6,4},{7,3},{8,10},{9,13},{10,... | collective-permute-start | bytes 159752 | tf_op jit(solution)/shard_map/ppermute | solution.py:581
  19.0 2.5 %shard_map.110 = (bf16[16,128,256]{2,1,0:T(8,128)(2,1)S(1)}, bf16[16,128,256]{2,1,0:T(8,128)(2,1)S(1)}, bf16[128,16]{1,0:T(8,128)(2,1)S(1)}) custom-call(s32[90]{0:T(128)S(4)} %get-tuple-element.60.table, f32[64,64]{1,0:T(8,128)S(1)} %get-tuple-element.59.operator, f32[16,8,256]{2,1,0:T(8,128)S(1)} %get-tuple-element.66.rest_1_.lift, ...), custom_call_target="tpu_custom_call" | custom-call | flops 600000000 | bytes 37500000 | tf_op jit(solution)/shard_map/pallas_call | solution.py:538
  21.7 0.8 %collective-permute-done.9.rest_3_ = f32[13,8,128]{2,1,0:T(8,128)S(1)} collective-permute-done((f32[13,8,128]{2,1,0:T(8,128)S(1)}, f32[13,8,128]{2,1,0:T(8,128)S(1)}, u32[]{:S(2)}, u32[]{:S(2)}) %collective-permute-start.9) | collective-permute-done | bytes 53280 | tf_op jit(solution)/shard_map/ppermute | solution.py:581
  22.6 1.1 %shard_map.111 = (f32[16,8,256]{2,1,0:T(8,128)S(1)}, f32[16,8,256]{2,1,0:T(8,128)S(1)}, bf16[16,16,256]{2,1,0:T(8,128)(2,1)S(1)}, f32[8,128]{1,0:T(8,128)S(1)}, ...) custom-call(s32[90]{0:T(128)S(4)} %get-tuple-element.60.table, f32[6,8,128]{2,1,0:T(8,128)S(1)} %collective-permute-done.5.rest_0_, ...), custom_call_target="tpu_custom_call" | custom-call | flops 600000000 | bytes 37500000 | tf_op jit(solution)/shard_map/pallas_call | solution.py:538
  23.7 1.3 %shard_map.112 = (f32[16,8,256]{2,1,0:T(8,128)S(1)}, f32[6,8,128]{2,1,0:T(8,128)S(1)}) custom-call(s32[90]{0:T(128)S(4)} %get-tuple-element.60.table, f32[16,8,256]{2,1,0:T(8,128)S(1)} %get-tuple-element.61.rest_5_.wide.rest_9_, bf16[16,256,256]{2,1,0:T(8,128)(2,1)S(1)} %get-tuple-element.62.rest_6_.diag.rest_10_, ...), custom_call_target="tpu_custom_call" | custom-call | flops 600000000 | bytes 37500000 | tf_op jit(solution)/shard_map/pallas_call | solution.py:538
  25.6 1.6 %collective-permute-start.12 = (f32[13,8,128]{2,1,0:T(8,128)S(1)}, f32[13,8,128]{2,1,0:T(8,128)S(1)}, u32[]{:S(2)}, u32[]{:S(2)}) collective-permute-start(f32[13,8,128]{2,1,0:T(8,128)S(1)} %get-tuple-element.92), channel_id=1, source_target_pairs={{0,6},{1,7},{2,4},{3,5},{4,2},{5,3},{6,0},{7,1},{8,14},{9,15},{10,... | collective-permute-start | bytes 159752 | tf_op jit(solution)/shard_map/ppermute | solution.py:581
  27.7 1.5 %collective-permute-start.14 = (f32[13,8,128]{2,1,0:T(8,128)S(1)}, f32[13,8,128]{2,1,0:T(8,128)S(1)}, u32[]{:S(2)}, u32[]{:S(2)}) collective-permute-start(f32[13,8,128]{2,1,0:T(8,128)S(1)} %get-tuple-element.94), channel_id=1, source_target_pairs={{0,4},{1,3},{2,6},{3,1},{4,0},{5,7},{6,2},{7,5},{8,12},{9,11},{10,... | collective-permute-start | bytes 159752 | tf_op jit(solution)/shard_map/ppermute | solution.py:581
  29.5 1.3 %collective-permute-done.12.rest_1_ = f32[13,8,128]{2,1,0:T(8,128)S(1)} collective-permute-done((f32[13,8,128]{2,1,0:T(8,128)S(1)}, f32[13,8,128]{2,1,0:T(8,128)S(1)}, u32[]{:S(2)}, u32[]{:S(2)}) %collective-permute-start.12) | collective-permute-done | bytes 53280 | tf_op jit(solution)/shard_map/ppermute | solution.py:581
  31.9 1.1 %shard_map.115 = (f32[16,8,256]{2,1,0:T(8,128)S(1)}, f32[16,8,256]{2,1,0:T(8,128)S(1)}, bf16[16,16,256]{2,1,0:T(8,128)(2,1)S(1)}, f32[8,128]{1,0:T(8,128)S(1)}, ...) custom-call(s32[90]{0:T(128)S(4)} %get-tuple-element.60.table, f32[6,8,128]{2,1,0:T(8,128)S(1)} %collective-permute-done.10.rest_0_, ...), custom_call_target="tpu_custom_call" | custom-call | flops 600000000 | bytes 37500000 | tf_op jit(solution)/shard_map/pallas_call | solution.py:538
  33.0 1.3 %shard_map.116 = (f32[16,8,256]{2,1,0:T(8,128)S(1)}, f32[6,8,128]{2,1,0:T(8,128)S(1)}) custom-call(s32[90]{0:T(128)S(4)} %get-tuple-element.60.table, f32[16,8,256]{2,1,0:T(8,128)S(1)} %get-tuple-element.61.rest_5_.wide.rest_9_, bf16[16,256,256]{2,1,0:T(8,128)(2,1)S(1)} %get-tuple-element.62.rest_6_.diag.rest_10_, ...), custom_call_target="tpu_custom_call" | custom-call | flops 600000000 | bytes 37500000 | tf_op jit(solution)/shard_map/pallas_call | solution.py:538
  34.9 1.7 %collective-permute-start.17 = (f32[13,8,128]{2,1,0:T(8,128)S(1)}, f32[13,8,128]{2,1,0:T(8,128)S(1)}, u32[]{:S(2)}, u32[]{:S(2)}) collective-permute-start(f32[13,8,128]{2,1,0:T(8,128)S(1)} %get-tuple-element.104), channel_id=1, source_target_pairs={{0,6},{1,7},{2,4},{3,5},{4,2},{5,3},{6,0},{7,1},{8,14},{9,15},{10,... | collective-permute-start | bytes 159752 | tf_op jit(solution)/shard_map/ppermute | solution.py:581
  36.6 1.3 %collective-permute-start.18 = (f32[13,8,128]{2,1,0:T(8,128)S(1)}, f32[13,8,128]{2,1,0:T(8,128)S(1)}, u32[]{:S(2)}, u32[]{:S(2)}) collective-permute-start(f32[13,8,128]{2,1,0:T(8,128)S(1)} %get-tuple-element.105), channel_id=1, source_target_pairs={{0,2},{1,5},{2,0},{3,7},{4,6},{5,1},{6,4},{7,3},{8,10},{9,13},{10,... | collective-permute-start | bytes 159752 | tf_op jit(solution)/shard_map/ppermute | solution.py:581
  38.8 1.3 %collective-permute-done.17.rest_1_ = f32[13,8,128]{2,1,0:T(8,128)S(1)} collective-permute-done((f32[13,8,128]{2,1,0:T(8,128)S(1)}, f32[13,8,128]{2,1,0:T(8,128)S(1)}, u32[]{:S(2)}, u32[]{:S(2)}) %collective-permute-start.17) | collective-permute-done | bytes 53280 | tf_op jit(solution)/shard_map/ppermute | solution.py:581
  40.1 1.1 %collective-permute-done.18.rest_2_ = f32[13,8,128]{2,1,0:T(8,128)S(1)} collective-permute-done((f32[13,8,128]{2,1,0:T(8,128)S(1)}, f32[13,8,128]{2,1,0:T(8,128)S(1)}, u32[]{:S(2)}, u32[]{:S(2)}) %collective-permute-start.18) | collective-permute-done | bytes 53280 | tf_op jit(solution)/shard_map/ppermute | solution.py:581
  41.2 0.8 %collective-permute-done.19.rest_3_ = f32[13,8,128]{2,1,0:T(8,128)S(1)} collective-permute-done((f32[13,8,128]{2,1,0:T(8,128)S(1)}, f32[13,8,128]{2,1,0:T(8,128)S(1)}, u32[]{:S(2)}, u32[]{:S(2)}) %collective-permute-start.19) | collective-permute-done | bytes 53280 | tf_op jit(solution)/shard_map/ppermute | solution.py:581
  42.0 2.9 %shard_map.119 = (f32[16,8,256]{2,1,0:T(8,128)}, f32[16,8,256]{2,1,0:T(8,128)S(1)}, f32[8,128]{1,0:T(8,128)S(1)}, f32[16,8,256]{2,1,0:T(8,128)S(1)}, f32[6,8,128...) custom-call(s32[90]{0:T(128)S(4)} %get-tuple-element.60.table, ...), custom_call_target="tpu_custom_call" | custom-call | flops 600000000 | bytes 37500000 | tf_op jit(solution)/shard_map/pallas_call | solution.py:538
  44.9 1.3 %collective-permute-done.20.rest_2_.near = f32[19,8,128]{2,1,0:T(8,128)S(1)} collective-permute-done((f32[19,8,128]{2,1,0:T(8,128)S(1)}, f32[19,8,128]{2,1,0:T(8,128)S(1)}, u32[]{:S(2)}, u32[]{:S(2)}) %collective-permute-start.20) | collective-permute-done | bytes 77856 | tf_op jit(solution)/shard_map/ppermute | solution.py:581
  46.2 1.6 %collective-permute-start.21 = (f32[13,8,128]{2,1,0:T(8,128)S(1)}, f32[13,8,128]{2,1,0:T(8,128)S(1)}, u32[]{:S(2)}, u32[]{:S(2)}) collective-permute-start(f32[13,8,128]{2,1,0:T(8,128)S(1)} %get-tuple-element.110), channel_id=1, source_target_pairs={{0,6},{1,7},{2,4},{3,5},{4,2},{5,3},{6,0},{7,1},{8,14},{9,15},{10,... | collective-permute-start | bytes 159752 | tf_op jit(solution)/shard_map/ppermute | solution.py:581
  48.3 1.5 %collective-permute-start.23 = (f32[13,8,128]{2,1,0:T(8,128)S(1)}, f32[13,8,128]{2,1,0:T(8,128)S(1)}, u32[]{:S(2)}, u32[]{:S(2)}) collective-permute-start(f32[13,8,128]{2,1,0:T(8,128)S(1)} %get-tuple-element.112), channel_id=1, source_target_pairs={{0,4},{1,3},{2,6},{3,1},{4,0},{5,7},{6,2},{7,5},{8,12},{9,11},{10,... | collective-permute-start | bytes 159752 | tf_op jit(solution)/shard_map/ppermute | solution.py:581
  49.7 1.6 %collective-permute-done.21.rest_0_ = f32[13,8,128]{2,1,0:T(8,128)S(1)} collective-permute-done((f32[13,8,128]{2,1,0:T(8,128)S(1)}, f32[13,8,128]{2,1,0:T(8,128)S(1)}, u32[]{:S(2)}, u32[]{:S(2)}) %collective-permute-start.21) | collective-permute-done | bytes 53280 | tf_op jit(solution)/shard_map/ppermute | solution.py:581
  52.7 3.7 %collective-permute-start.26 = (f32[8,128]{1,0:T(8,128)S(1)}, f32[8,128]{1,0:T(8,128)S(1)}, u32[]{:S(2)}, u32[]{:S(2)}) collective-permute-start(f32[8,128]{1,0:T(8,128)S(1)} %shard_map.121.rest_0_), channel_id=1, source_target_pairs={{0,24},{8,16},{16,8},{24,0},{1,25},{9,17},{17,9},{25,1},{2,26},{10... | collective-permute-start | bytes 12296 | tf_op jit(solution)/shard_map/ppermute | solution.py:680
  56.4 0.8 %collective-permute-start.24 = (f32[8,128]{1,0:T(8,128)S(1)}, f32[8,128]{1,0:T(8,128)S(1)}, u32[]{:S(2)}, u32[]{:S(2)}) collective-permute-start(f32[8,128]{1,0:T(8,128)S(1)} %shard_map.121.rest_0_), channel_id=1, source_target_pairs={{0,8},{8,0},{16,24},{24,16},{1,9},{9,1},{17,25},{25,17},{2,10},{10... | collective-permute-start | bytes 12296 | tf_op jit(solution)/shard_map/ppermute | solution.py:680
  58.2 2.7 %collective-permute-done.25.rest_2_ = f32[8,128]{1,0:T(8,128)S(1)} collective-permute-done((f32[8,128]{1,0:T(8,128)S(1)}, f32[8,128]{1,0:T(8,128)S(1)}, u32[]{:S(2)}, u32[]{:S(2)}) %collective-permute-start.25) | collective-permute-done | bytes 4128 | tf_op jit(solution)/shard_map/ppermute | solution.py:680
  60.9 1.2 %shard_map.123 = (f32[8,16,256]{2,1,0:T(8,128)}, f32[8,16,256]{2,1,0:T(8,128)}) custom-call(f32[8,128]{1,0:T(8,128)S(1)} %shard_map.121.rest_0_, f32[8,128]{1,0:T(8,128)S(1)} %collective-permute-done.24.rest_1_, f32[8,128]{1,0:T(8,128)S(1)} %collective-permute-done.25.rest_2_, f32[8,128]{1,0:T(8,128)S(1)} %collective-permute-done.26.rest_3_, ...), custom_call_target="tpu_custom_call" | custom-call | flops 4000000 | bytes 250000 | tf_op jit(solution)/shard_map/pallas_call | solution.py:538
  (44 shorter events, 9.6 us)
Async XLA Ops:
  1.7 1.5 %collective-permute-start.1 = (f32[36,8,128]{2,1,0:T(8,128)S(1)}, f32[36,8,128]{2,1,0:T(8,128)S(1)}, u32[]{:S(2)}, u32[]{:S(2)}) collective-permute-start(f32[36,8,128]{2,1,0:T(8,128)S(1)} %get-tuple-element.67), channel_id=1, source_target_pairs={{0,1},{1,0},{2,3},{3,2},{4,5},{5,4},{6,7},{7,6},{8,9},{9,8},{10,11... | collective-permute-start | bytes 442376 | tf_op jit(solution)/shard_map/ppermute | solution.py:581
  3.2 7.1 %collective-permute-start.2 = (f32[24,8,128]{2,1,0:T(8,128)S(1)}, f32[24,8,128]{2,1,0:T(8,128)S(1)}, u32[]{:S(2)}, u32[]{:S(2)}) collective-permute-start(f32[24,8,128]{2,1,0:T(8,128)S(1)} %get-tuple-element.68), channel_id=1, source_target_pairs={{0,6},{1,7},{2,4},{3,5},{4,2},{5,3},{6,0},{7,1},{8,14},{9,15},{10,... | collective-permute-start | bytes 294920 | tf_op jit(solution)/shard_map/ppermute | solution.py:581
  7.1 5.5 %collective-permute-start.3 = (f32[24,8,128]{2,1,0:T(8,128)S(1)}, f32[24,8,128]{2,1,0:T(8,128)S(1)}, u32[]{:S(2)}, u32[]{:S(2)}) collective-permute-start(f32[24,8,128]{2,1,0:T(8,128)S(1)} %get-tuple-element.69), channel_id=1, source_target_pairs={{0,2},{1,5},{2,0},{3,7},{4,6},{5,1},{6,4},{7,3},{8,10},{9,13},{10,... | collective-permute-start | bytes 294920 | tf_op jit(solution)/shard_map/ppermute | solution.py:581
  7.7 4.9 %collective-permute-start.4 = (f32[24,8,128]{2,1,0:T(8,128)S(1)}, f32[24,8,128]{2,1,0:T(8,128)S(1)}, u32[]{:S(2)}, u32[]{:S(2)}) collective-permute-start(f32[24,8,128]{2,1,0:T(8,128)S(1)} %get-tuple-element.70), channel_id=1, source_target_pairs={{0,4},{1,3},{2,6},{3,1},{4,0},{5,7},{6,2},{7,5},{8,12},{9,11},{10,... | collective-permute-start | bytes 294920 | tf_op jit(solution)/shard_map/ppermute | solution.py:581
  7.8 2.3 %collective-permute-start = (f32[12,8,128]{2,1,0:T(8,128)S(1)}, f32[12,8,128]{2,1,0:T(8,128)S(1)}, u32[]{:S(2)}, u32[]{:S(2)}) collective-permute-start(f32[12,8,128]{2,1,0:T(8,128)S(1)} %get-tuple-element.64), channel_id=1, source_target_pairs={{0,1},{1,0},{2,3},{3,2},{4,5},{5,4},{6,7},{7,6},{8,9},{9,8},{10,11... | collective-permute-start | bytes 147464 | tf_op jit(solution)/shard_map/ppermute | solution.py:581
  13.6 1.8 %collective-permute-start.6 = (f32[19,8,128]{2,1,0:T(8,128)S(1)}, f32[19,8,128]{2,1,0:T(8,128)S(1)}, u32[]{:S(2)}, u32[]{:S(2)}) collective-permute-start(f32[19,8,128]{2,1,0:T(8,128)S(1)} %get-tuple-element.78), channel_id=1, source_target_pairs={{0,1},{1,0},{2,3},{3,2},{4,5},{5,4},{6,7},{7,6},{8,9},{9,8},{10,11... | collective-permute-start | bytes 233480 | tf_op jit(solution)/shard_map/ppermute | solution.py:581
  14.9 6.7 %collective-permute-start.5 = (f32[6,8,128]{2,1,0:T(8,128)S(1)}, f32[6,8,128]{2,1,0:T(8,128)S(1)}, u32[]{:S(2)}, u32[]{:S(2)}) collective-permute-start(f32[6,8,128]{2,1,0:T(8,128)S(1)} %get-tuple-element.75), channel_id=1, source_target_pairs={{0,1},{1,0},{2,3},{3,2},{4,5},{5,4},{6,7},{7,6},{8,9},{9,8},{10,11... | collective-permute-start | bytes 73736 | tf_op jit(solution)/shard_map/ppermute | solution.py:581
  15.4 6.1 %collective-permute-start.7 = (f32[13,8,128]{2,1,0:T(8,128)S(1)}, f32[13,8,128]{2,1,0:T(8,128)S(1)}, u32[]{:S(2)}, u32[]{:S(2)}) collective-permute-start(f32[13,8,128]{2,1,0:T(8,128)S(1)} %get-tuple-element.79), channel_id=1, source_target_pairs={{0,6},{1,7},{2,4},{3,5},{4,2},{5,3},{6,0},{7,1},{8,14},{9,15},{10,... | collective-permute-start | bytes 159752 | tf_op jit(solution)/shard_map/ppermute | solution.py:581
  17.2 4.6 %collective-permute-start.8 = (f32[13,8,128]{2,1,0:T(8,128)S(1)}, f32[13,8,128]{2,1,0:T(8,128)S(1)}, u32[]{:S(2)}, u32[]{:S(2)}) collective-permute-start(f32[13,8,128]{2,1,0:T(8,128)S(1)} %get-tuple-element.80), channel_id=1, source_target_pairs={{0,2},{1,5},{2,0},{3,7},{4,6},{5,1},{6,4},{7,3},{8,10},{9,13},{10,... | collective-permute-start | bytes 159752 | tf_op jit(solution)/shard_map/ppermute | solution.py:581
  18.4 4.1 %collective-permute-start.9 = (f32[13,8,128]{2,1,0:T(8,128)S(1)}, f32[13,8,128]{2,1,0:T(8,128)S(1)}, u32[]{:S(2)}, u32[]{:S(2)}) collective-permute-start(f32[13,8,128]{2,1,0:T(8,128)S(1)} %get-tuple-element.81), channel_id=1, source_target_pairs={{0,4},{1,3},{2,6},{3,1},{4,0},{5,7},{6,2},{7,5},{8,12},{9,11},{10,... | collective-permute-start | bytes 159752 | tf_op jit(solution)/shard_map/ppermute | solution.py:581
  23.7 1.9 %collective-permute-start.11 = (f32[19,8,128]{2,1,0:T(8,128)S(1)}, f32[19,8,128]{2,1,0:T(8,128)S(1)}, u32[]{:S(2)}, u32[]{:S(2)}) collective-permute-start(f32[19,8,128]{2,1,0:T(8,128)S(1)} %get-tuple-element.91), channel_id=1, source_target_pairs={{0,1},{1,0},{2,3},{3,2},{4,5},{5,4},{6,7},{7,6},{8,9},{9,8},{10,11... | collective-permute-start | bytes 233480 | tf_op jit(solution)/shard_map/ppermute | solution.py:581
  25.0 4.4 %collective-permute-start.10 = (f32[6,8,128]{2,1,0:T(8,128)S(1)}, f32[6,8,128]{2,1,0:T(8,128)S(1)}, u32[]{:S(2)}, u32[]{:S(2)}) collective-permute-start(f32[6,8,128]{2,1,0:T(8,128)S(1)} %get-tuple-element.88), channel_id=1, source_target_pairs={{0,1},{1,0},{2,3},{3,2},{4,5},{5,4},{6,7},{7,6},{8,9},{9,8},{10,11... | collective-permute-start | bytes 73736 | tf_op jit(solution)/shard_map/ppermute | solution.py:581
  25.6 5.2 %collective-permute-start.12 = (f32[13,8,128]{2,1,0:T(8,128)S(1)}, f32[13,8,128]{2,1,0:T(8,128)S(1)}, u32[]{:S(2)}, u32[]{:S(2)}) collective-permute-start(f32[13,8,128]{2,1,0:T(8,128)S(1)} %get-tuple-element.92), channel_id=1, source_target_pairs={{0,6},{1,7},{2,4},{3,5},{4,2},{5,3},{6,0},{7,1},{8,14},{9,15},{10,... | collective-permute-start | bytes 159752 | tf_op jit(solution)/shard_map/ppermute | solution.py:581
  27.2 4.1 %collective-permute-start.13 = (f32[13,8,128]{2,1,0:T(8,128)S(1)}, f32[13,8,128]{2,1,0:T(8,128)S(1)}, u32[]{:S(2)}, u32[]{:S(2)}) collective-permute-start(f32[13,8,128]{2,1,0:T(8,128)S(1)} %get-tuple-element.93), channel_id=1, source_target_pairs={{0,2},{1,5},{2,0},{3,7},{4,6},{5,1},{6,4},{7,3},{8,10},{9,13},{10,... | collective-permute-start | bytes 159752 | tf_op jit(solution)/shard_map/ppermute | solution.py:581
  27.7 4.1 %collective-permute-start.14 = (f32[13,8,128]{2,1,0:T(8,128)S(1)}, f32[13,8,128]{2,1,0:T(8,128)S(1)}, u32[]{:S(2)}, u32[]{:S(2)}) collective-permute-start(f32[13,8,128]{2,1,0:T(8,128)S(1)} %get-tuple-element.94), channel_id=1, source_target_pairs={{0,4},{1,3},{2,6},{3,1},{4,0},{5,7},{6,2},{7,5},{8,12},{9,11},{10,... | collective-permute-start | bytes 159752 | tf_op jit(solution)/shard_map/ppermute | solution.py:581
  33.0 1.9 %collective-permute-start.16 = (f32[19,8,128]{2,1,0:T(8,128)S(1)}, f32[19,8,128]{2,1,0:T(8,128)S(1)}, u32[]{:S(2)}, u32[]{:S(2)}) collective-permute-start(f32[19,8,128]{2,1,0:T(8,128)S(1)} %get-tuple-element.103), channel_id=1, source_target_pairs={{0,1},{1,0},{2,3},{3,2},{4,5},{5,4},{6,7},{7,6},{8,9},{9,8},{10,11... | collective-permute-start | bytes 233480 | tf_op jit(solution)/shard_map/ppermute | solution.py:581
  34.3 4.4 %collective-permute-start.15 = (f32[6,8,128]{2,1,0:T(8,128)S(1)}, f32[6,8,128]{2,1,0:T(8,128)S(1)}, u32[]{:S(2)}, u32[]{:S(2)}) collective-permute-start(f32[6,8,128]{2,1,0:T(8,128)S(1)} %get-tuple-element.100), channel_id=1, source_target_pairs={{0,1},{1,0},{2,3},{3,2},{4,5},{5,4},{6,7},{7,6},{8,9},{9,8},{10,11... | collective-permute-start | bytes 73736 | tf_op jit(solution)/shard_map/ppermute | solution.py:581
  34.9 5.2 %collective-permute-start.17 = (f32[13,8,128]{2,1,0:T(8,128)S(1)}, f32[13,8,128]{2,1,0:T(8,128)S(1)}, u32[]{:S(2)}, u32[]{:S(2)}) collective-permute-start(f32[13,8,128]{2,1,0:T(8,128)S(1)} %get-tuple-element.104), channel_id=1, source_target_pairs={{0,6},{1,7},{2,4},{3,5},{4,2},{5,3},{6,0},{7,1},{8,14},{9,15},{10,... | collective-permute-start | bytes 159752 | tf_op jit(solution)/shard_map/ppermute | solution.py:581
  36.6 4.6 %collective-permute-start.18 = (f32[13,8,128]{2,1,0:T(8,128)S(1)}, f32[13,8,128]{2,1,0:T(8,128)S(1)}, u32[]{:S(2)}, u32[]{:S(2)}) collective-permute-start(f32[13,8,128]{2,1,0:T(8,128)S(1)} %get-tuple-element.105), channel_id=1, source_target_pairs={{0,2},{1,5},{2,0},{3,7},{4,6},{5,1},{6,4},{7,3},{8,10},{9,13},{10,... | collective-permute-start | bytes 159752 | tf_op jit(solution)/shard_map/ppermute | solution.py:581
  37.9 4.1 %collective-permute-start.19 = (f32[13,8,128]{2,1,0:T(8,128)S(1)}, f32[13,8,128]{2,1,0:T(8,128)S(1)}, u32[]{:S(2)}, u32[]{:S(2)}) collective-permute-start(f32[13,8,128]{2,1,0:T(8,128)S(1)} %get-tuple-element.106), channel_id=1, source_target_pairs={{0,4},{1,3},{2,6},{3,1},{4,0},{5,7},{6,2},{7,5},{8,12},{9,11},{10,... | collective-permute-start | bytes 159752 | tf_op jit(solution)/shard_map/ppermute | solution.py:581
  44.9 1.3 %collective-permute-start.20 = (f32[19,8,128]{2,1,0:T(8,128)S(1)}, f32[19,8,128]{2,1,0:T(8,128)S(1)}, u32[]{:S(2)}, u32[]{:S(2)}) collective-permute-start(f32[19,8,128]{2,1,0:T(8,128)S(1)} %get-tuple-element.108), channel_id=1, source_target_pairs={{0,1},{1,0},{2,3},{3,2},{4,5},{5,4},{6,7},{7,6},{8,9},{9,8},{10,11... | collective-permute-start | bytes 233480 | tf_op jit(solution)/shard_map/ppermute | solution.py:581
  46.2 5.2 %collective-permute-start.21 = (f32[13,8,128]{2,1,0:T(8,128)S(1)}, f32[13,8,128]{2,1,0:T(8,128)S(1)}, u32[]{:S(2)}, u32[]{:S(2)}) collective-permute-start(f32[13,8,128]{2,1,0:T(8,128)S(1)} %get-tuple-element.110), channel_id=1, source_target_pairs={{0,6},{1,7},{2,4},{3,5},{4,2},{5,3},{6,0},{7,1},{8,14},{9,15},{10,... | collective-permute-start | bytes 159752 | tf_op jit(solution)/shard_map/ppermute | solution.py:581
  47.8 4.1 %collective-permute-start.22 = (f32[13,8,128]{2,1,0:T(8,128)S(1)}, f32[13,8,128]{2,1,0:T(8,128)S(1)}, u32[]{:S(2)}, u32[]{:S(2)}) collective-permute-start(f32[13,8,128]{2,1,0:T(8,128)S(1)} %get-tuple-element.111), channel_id=1, source_target_pairs={{0,2},{1,5},{2,0},{3,7},{4,6},{5,1},{6,4},{7,3},{8,10},{9,13},{10,... | collective-permute-start | bytes 159752 | tf_op jit(solution)/shard_map/ppermute | solution.py:581
  48.3 4.1 %collective-permute-start.23 = (f32[13,8,128]{2,1,0:T(8,128)S(1)}, f32[13,8,128]{2,1,0:T(8,128)S(1)}, u32[]{:S(2)}, u32[]{:S(2)}) collective-permute-start(f32[13,8,128]{2,1,0:T(8,128)S(1)} %get-tuple-element.112), channel_id=1, source_target_pairs={{0,4},{1,3},{2,6},{3,1},{4,0},{5,7},{6,2},{7,5},{8,12},{9,11},{10,... | collective-permute-start | bytes 159752 | tf_op jit(solution)/shard_map/ppermute | solution.py:581
  49.7 7.4 %collective-permute-start.27 = (f32[6,8,128]{2,1,0:T(8,128)S(1)}, f32[6,8,128]{2,1,0:T(8,128)S(1)}, u32[]{:S(2)}, u32[]{:S(2)}) collective-permute-start(f32[6,8,128]{2,1,0:T(8,128)S(1)} %get-tuple-element.115), channel_id=1, source_target_pairs={{0,1},{1,0},{2,3},{3,2},{4,5},{5,4},{6,7},{7,6},{8,9},{9,8},{10,11... | collective-permute-start | bytes 73736 | tf_op jit(solution)/shard_map/ppermute | solution.py:581
  52.7 5.5 %collective-permute-start.26 = (f32[8,128]{1,0:T(8,128)S(1)}, f32[8,128]{1,0:T(8,128)S(1)}, u32[]{:S(2)}, u32[]{:S(2)}) collective-permute-start(f32[8,128]{1,0:T(8,128)S(1)} %shard_map.121.rest_0_), channel_id=1, source_target_pairs={{0,24},{8,16},{16,8},{24,0},{1,25},{9,17},{17,9},{25,1},{2,26},{10... | collective-permute-start | bytes 12296 | tf_op jit(solution)/shard_map/ppermute | solution.py:680
  56.4 4.5 %collective-permute-start.25 = (f32[8,128]{1,0:T(8,128)S(1)}, f32[8,128]{1,0:T(8,128)S(1)}, u32[]{:S(2)}, u32[]{:S(2)}) collective-permute-start(f32[8,128]{1,0:T(8,128)S(1)} %shard_map.121.rest_0_), channel_id=1, source_target_pairs={{0,16},{8,24},{16,0},{24,8},{1,17},{9,25},{17,1},{25,9},{2,18},{10... | collective-permute-start | bytes 12296 | tf_op jit(solution)/shard_map/ppermute | solution.py:680
  56.4 4.5 %collective-permute-start.24 = (f32[8,128]{1,0:T(8,128)S(1)}, f32[8,128]{1,0:T(8,128)S(1)}, u32[]{:S(2)}, u32[]{:S(2)}) collective-permute-start(f32[8,128]{1,0:T(8,128)S(1)} %shard_map.121.rest_0_), channel_id=1, source_target_pairs={{0,8},{8,0},{16,24},{24,16},{1,9},{9,1},{17,25},{25,17},{2,10},{10... | collective-permute-start | bytes 12296 | tf_op jit(solution)/shard_map/ppermute | solution.py:680

commit v8 on v7

v8 whole, which is shorter than its diff:
```python
import functools

import jax
import jax.numpy as jnp
from jax import lax
from jax.experimental import pallas as pl
from jax.experimental.pallas import tpu as pltpu
from jax.sharding import PartitionSpec as P

ITERS = 4
HIGH = lax.Precision.HIGHEST
F32 = jnp.float32
BF16 = jnp.bfloat16
VMEM = pl.BlockSpec(memory_space=pltpu.VMEM)
SMEM = pl.BlockSpec(memory_space=pltpu.SMEM)
HBM = pl.BlockSpec(memory_space=pltpu.HBM)
LIMIT = 24 * 1024 * 1024
LANES = 128
RR, DP, RP, PP = range(4)
NN = (((1,), (0,)), ((), ()))
NT = (((1,), (1,)), ((), ()))
TN = (((0,), (0,)), ((), ()))


def dot(a, b, dims):
    return lax.dot_general(a, b, dims, preferred_element_type=F32)


def dot_high(a, b, dims):
    return lax.dot_general(a, b, dims, precision=HIGH, preferred_element_type=F32)


def pad(a):
    return jnp.concatenate([a, jnp.zeros_like(a)], axis=0).astype(BF16)


def split(a):
    high = a.astype(BF16).astype(F32)
    return jnp.concatenate([high, a - high], axis=0).astype(BF16)


def fold(a):
    half = a.shape[0] // 2
    return a[:half] + a[half:]


def lane_ids(shape):
    return lax.broadcasted_iota(jnp.int32, shape, 1)


class Sizes:
    def __init__(self, load, corner_coupling, coarse_inverse, mesh):
        self.columns = load.shape[0]
        self.blocks = load.shape[1]
        self.width = load.shape[2]
        self.corners = corner_coupling.shape[0]
        assert self.corners == self.columns
        self.coarse = coarse_inverse.shape[1]
        self.peers = mesh["sub"]
        self.groups = mesh["group"]
        self.capacity = (self.blocks + self.peers - 2) // (self.peers - 1)
        self.all_corners = self.peers * self.corners
        self.extra_chunks = -(-self.all_corners // LANES)
        self.extra = self.extra_chunks * LANES
        self.halves = self.width // LANES
        evens = range(2, self.peers, 2)
        self.beyond = [m for m in evens if m & (m - 1)]
        self.beside = [m for m in evens if m & (m - 1) == 0]
        self.far = self.beyond + self.beside
        self.handed = [m + 1 for m in self.far]
        self.slots = self.peers * self.capacity
        self.inverse = self.slots
        self.pattern = self.inverse + self.blocks
        self.partner = self.pattern + self.blocks
        self.order = self.partner + self.blocks
        self.count = self.order + self.blocks + 1
        self.table = self.count + 1
        most = len(self.far) * self.capacity
        self.early = min(-(-most * 7 // 8), self.blocks)
        self.middle = max(self.early, min(most, self.blocks))

    def rows(self, kinds):
        return kinds * self.capacity * self.halves

    def near_rows(self, kinds):
        return len(self.handed) * self.rows(kinds)

    def at(self, k, core):
        first = len(self.beyond)
        return k if k < first else first + (k - first + core) % len(self.beside)

    def mine(self, k):
        core = lax.axis_index("sub") & 1
        at = [self.at(k, c) for c in range(2)]
        return tuple(
            jnp.where(core == 0, jnp.int32(a), jnp.int32(b))
            for a, b in [at, [self.far[n] for n in at]]
        )

    def sources(self):
        found = [(1, 0, 0)]
        for k in range(len(self.far)):
            _, m = self.mine(k)
            found += [(m + side, 1 + k, side) for side in range(2)]
        return found


def fill_table(z, partner, pattern, table, counts):
    me = lax.axis_index("sub")
    for entry in range(z.slots):
        table[entry] = z.blocks
    for m in range(z.peers):
        counts[m] = 0
    for i in range(z.blocks):
        mate = partner[0, i]
        source = pattern[0, i]
        m = mate ^ me
        rank = counts[m]
        table[m * z.capacity + rank] = i
        counts[m] = rank + 1
        table[z.inverse + source] = i
        table[z.pattern + i] = source
        table[z.partner + i] = mate
    place = jnp.int32(0)
    for m in z.handed + z.far + [1]:
        for r in range(z.capacity):
            block = table[m * z.capacity + r]
            table[z.order + place] = block
            place = place + (block < z.blocks).astype(jnp.int32)
        if m == z.handed[-1]:
            table[z.count] = place


def fill_piece(z, table, sources, m, piece, row):
    for source in sources:
        for r in range(z.capacity):
            value = source[jnp.minimum(table[m * z.capacity + r], z.blocks - 1)]
            for h in range(z.halves):
                piece[row] = value[:, h * LANES : (h + 1) * LANES]
                row += 1


def fill_near(z, table, sources, near):
    for k, m in enumerate(z.handed):
        fill_piece(z, table, sources, m, near, k * z.rows(len(sources)))


def store_extra(z, tile, piece, row):
    for j in range(z.extra_chunks):
        piece[row + j] = tile[:, j * LANES : (j + 1) * LANES]


def load_extra(z, piece, row):
    return jnp.concatenate([piece[row + j] for j in range(z.extra_chunks)], axis=1)


def relay(z, kinds, table, *rest):
    sources, rest = rest[:kinds], rest[kinds:]
    if kinds == 1:
        extra, rest = rest[0], rest[1:]
    near, pieces, beside = rest[0], rest[1:-1], rest[-1]
    rows = z.rows(kinds)
    fill_piece(z, table, sources, 1, beside, 0)
    if kinds == 1:
        tile = extra[...] + load_extra(z, near, z.near_rows(1))
    for k, piece in enumerate(pieces):
        which, m = z.mine(k)
        fill_piece(z, table, sources, m, piece, 0)
        for row in range(rows):
            piece[rows + row] = near[which * rows + row]
        if kinds == 1:
            store_extra(z, tile, piece, 2 * rows)


def place(z, table, arrived, kind, kinds, target):
    for m, transfer, piece in z.sources():
        row = piece * z.rows(kinds) + z.rows(kind)
        for r in range(z.capacity):
            block = table[m * z.capacity + r]
            for h in range(z.halves):
                target[block, :, h * LANES : (h + 1) * LANES] = arrived[transfer][row]
                row += 1


def begin(z, partner, pattern, load, scale, coupling, table, field, lift, wide, corners, near, *scratch):
    here, scale_here, coupling_here, partner_here, pattern_here, counts, sems = scratch
    copies = [
        pltpu.make_async_copy(a, b, sems.at[k])
        for k, (a, b) in enumerate(
            [
                (partner, partner_here),
                (pattern, pattern_here),
                (load, here),
                (scale, scale_here),
                (coupling, coupling_here),
            ]
        )
    ]
    for copy in copies:
        copy.start()
    copies[0].wait()
    copies[1].wait()
    fill_table(z, partner_here, pattern_here, table, counts)
    for copy in copies[2:]:
        copy.wait()
    for i in range(z.blocks):
        field[i] = here[:, i, :]
        row = jnp.broadcast_to(scale_here[i : i + 1, :], (z.columns, z.width))
        wide[i] = row
        part = coupling_here[:, i * z.width : (i + 1) * z.width].astype(F32)
        lift[i] = row * part
        corners[i] = jnp.concatenate([part, jnp.zeros_like(part)], axis=0).astype(BF16)
    fill_near(z, table, [field, lift], near)


def split3(a):
    high = a.astype(BF16).astype(F32)
    middle = (a - high).astype(BF16).astype(F32)
    return [high, middle, a - high - middle]


def prepare(z, index_in, inverse_in, diag, off, operator, diag_out, off_out, index, inverse, sems):
    copies = [
        pltpu.make_async_copy(a, b, sems.at[k])
        for k, (a, b) in enumerate(
            [(index_in, index), (inverse_in, inverse), (diag, diag_out), (off, off_out)]
        )
    ]
    for copy in copies:
        copy.start()
    copies[0].wait()
    copies[1].wait()
    rows = lax.broadcasted_iota(jnp.int32, (z.coarse, z.all_corners), 0)
    select = (rows == index[...]).astype(BF16)
    parts = jnp.concatenate(split3(inverse[...]), axis=0).astype(BF16)
    half = dot(parts, select, NN)
    half = sum(half[k * z.coarse : (k + 1) * z.coarse] for k in range(3))
    parts = jnp.concatenate(split3(half), axis=1).astype(BF16)
    full = dot(select, parts, TN)
    operator[...] = sum(full[:, k * z.all_corners : (k + 1) * z.all_corners] for k in range(3))
    copies[2].wait()
    copies[3].wait()


def build_lift(z, table, lift, *rest):
    count = 1 + len(z.far)
    arrived, (jump_lift, other, full) = rest[:count], rest[count:]
    place(z, table, [arrived[-1], *arrived[:-1]], 1, 2, other)
    me = lax.axis_index("sub")
    for i in range(z.blocks):
        full[i] = jnp.zeros((z.all_corners, z.width), F32)
        own = pl.multiple_of(me * z.corners, z.corners)
        theirs = pl.multiple_of(table[z.partner + i] * z.corners, z.corners)
        full[i, pl.ds(own, z.corners), :] = lift[i]
        full[i, pl.ds(theirs, z.corners), :] = -other[i]
        jump_lift[i] = split(full[i])


def extra_sum(z, own, near, *far):
    total = own[...] + load_extra(z, near, z.near_rows(1))
    for piece in far:
        total = total + load_extra(z, piece, 2 * z.rows(1))
    return total


def lane_sum(a):
    return jnp.sum(a, axis=1, keepdims=True)


def column(table, lane):
    return jnp.broadcast_to(table[:, lane : lane + 1], table.shape)


def scalars(z, gathered):
    shape = (z.columns, LANES)
    zero = jnp.zeros(shape, F32)
    count = gathered.shape[0]
    unroll = 32 if count % 32 == 0 else 1
    total = lax.fori_loop(0, count, lambda k, acc: acc + gathered[k], zero, unroll=unroll)
    norm = column(total, RR)
    alpha = norm / column(total, DP)

    def squares(k, acc):
        tile = gathered[k]
        step = alpha * pltpu.roll(tile, LANES // 2, 1)
        return acc + tile * step * step

    moved = lax.fori_loop(0, count, squares, zero, unroll=unroll)
    following = norm - 2.0 * alpha * column(total, RP) + column(moved, PP)
    return alpha, following / norm


def across_block(z, tile):
    return jnp.concatenate([tile] * z.halves, axis=1)


def couple(z, i, table, wide, diag, off, parts):
    source = table[z.inverse + i]
    mine = parts[i]
    coupled = dot(mine, diag[i], NT) + dot(mine, diag[i], NN)
    coupled = coupled + dot(parts[table[z.pattern + i]], off[i], NT)
    coupled = coupled + dot(parts[source], off[source], NN)
    return wide[i] * fold(coupled + mine.astype(F32))


def first_half(z, step, table, *rest):
    rest = list(rest)
    take = lambda n: [rest.pop(0) for _ in range(n)]
    wide, diag, off, corners = take(4)
    if step == 0:
        *far, beside, loaded = take(2 + len(z.far))
        residual, image, parts, extra, near_out, other = rest
        direction = residual
        place(z, table, [beside, *far], 0, 2, other)
    else:
        gathered, before, way, product = take(4)
        residual, direction, step_out, image, parts, extra, near_out = rest
        alpha, beta = scalars(z, gathered)
        step_out[...] = alpha
        alpha, beta = across_block(z, alpha), across_block(z, beta)
    partial = jnp.zeros((2 * z.columns, 2 * z.corners), F32)
    for i in range(z.blocks):
        if step == 0:
            value = loaded[i] - other[i]
            residual[i] = value
        else:
            value = before[i] - alpha * product[i]
            residual[i] = value
            value = value + beta * way[i]
            direction[i] = value
        mine = pad(wide[i] * value)
        parts[i] = mine
        partial = partial + dot(mine, corners[i], NT)
    refs = (table, wide, diag, off, parts)
    for position in range(z.early):
        i = table[z.order + position]
        image[i] = couple(z, i, *refs)

    @pl.when(table[z.count] > z.early)
    def _():
        for position in range(z.early, z.middle):
            i = table[z.order + position]
            image[i] = couple(z, i, *refs)

    fill_near(z, table, [image], near_out)
    sums = fold(partial)
    padded = jnp.concatenate(
        [sums, jnp.zeros((z.columns, z.extra - sums.shape[1]), F32)], axis=1
    )
    tile = pltpu.roll(padded, lax.axis_index("sub") * z.corners, 1)
    extra[...] = tile
    store_extra(z, tile, near_out, z.near_rows(1))


def second_half(z, step, table, wide, diag, off, parts, image_in, *rest):
    if step == 0:
        (image,) = rest
    elif step == 1:
        alpha, way, image, multipliers = rest
    else:
        alpha, way, before, image, multipliers = rest
    refs = (table, wide, diag, off, parts)
    for i in range(z.blocks):
        image[i] = image_in[i]

    @pl.when(table[z.count] <= z.early)
    def _():
        for position in range(z.early, z.middle):
            i = table[z.order + position]
            image[i] = couple(z, i, *refs)

    for position in range(z.middle, z.blocks):
        i = table[z.order + position]
        image[i] = couple(z, i, *refs)
    if step > 0:
        size = across_block(z, alpha[...])
        for i in range(z.blocks):
            value = size * way[i]
            multipliers[i] = value if step == 1 else before[i] + value


def finish_product(z, table, operator, image, own_extra, jump_lift, residual, direction, near, *rest):
    *far, beside, product, sent, other = rest
    place(z, table, [beside, *far], 0, 1, other)
    partials = extra_sum(z, own_extra, near, *far)[:, : z.all_corners]
    local = dot_high(partials, operator[...], NT)
    rows = pad(jnp.concatenate([local, local], axis=1))
    zero = jnp.zeros((z.columns, z.width), F32)
    sums = [zero] * 3
    top = zero
    for i in range(z.blocks):
        value = image[i] - other[i] + fold(dot(rows, jump_lift[i], NN))
        product[i] = value
        top = jnp.maximum(top, jnp.abs(value))
        r, d = residual[i], direction[i]
        sums = [s + a * b for s, (a, b) in zip(sums, [(r, r), (d, value), (r, value)])]
    top = jnp.max(top, axis=1, keepdims=True)
    shrink = jnp.where(top > 0.0, 1.0 / top, 0.0)
    squares = zero
    for i in range(z.blocks):
        value = product[i] * shrink
        squares = squares + value * value
    lanes = lane_ids((z.columns, LANES))
    tile = jnp.where(lanes == PP + LANES // 2, top, 0.0)
    for lane, value in zip([RR, DP, RP, PP], sums + [squares]):
        tile = jnp.where(lanes == lane, lane_sum(value), tile)
    for k in range(sent.shape[0]):
        sent[k] = tile


def finish(z, gathered, before, residual_in, direction, product, multipliers, residual):
    alpha, _ = scalars(z, gathered)
    for i in range(z.blocks):
        for h in range(z.halves):
            part = slice(h * LANES, (h + 1) * LANES)
            multipliers[:, i, part] = before[i, :, part] + alpha * direction[i, :, part]
            residual[:, i, part] = residual_in[i, :, part] - alpha * product[i, :, part]


def call(body, outs, scratch, cost, args, table=True, away=()):
    args = [
        pltpu.with_memory_space_constraint(a, pltpu.HBM) if k in away else a
        for k, a in enumerate(args)
    ]
    specs = [HBM if k in away else VMEM for k in range(len(args))]
    if table:
        specs[0] = SMEM
    shapes = [
        pltpu.SMEM(s, t) if t == jnp.int32 else jax.ShapeDtypeStruct(s, t) for s, t in outs
    ]
    return pl.pallas_call(
        body,
        out_shape=shapes,
        in_specs=specs,
        out_specs=[SMEM if t == jnp.int32 else VMEM for _, t in outs],
        scratch_shapes=scratch,
        compiler_params=pltpu.CompilerParams(vmem_limit_bytes=LIMIT),
        cost_estimate=pl.CostEstimate(flops=cost, bytes_accessed=cost // 16, transcendentals=0),
    )(*args)


def on_device(
    load,
    row_scale,
    diag_blocks,
    off_blocks,
    off_pattern,
    partner,
    corner_coupling,
    corner_index,
    coarse_inverse,
    *,
    mesh,
):
    z = Sizes(load, corner_coupling, coarse_inverse, mesh)
    cols, blocks, width = z.columns, z.blocks, z.width
    field = ((blocks, cols, width), F32)
    other = pltpu.VMEM((blocks + 1, cols, width), F32)
    extra = ((cols, z.extra), F32)
    light, heavy = 4_000_000, 600_000_000

    def shape(rows, kinds):
        return ((rows + (z.extra_chunks if kinds == 1 else 0), cols, LANES), F32)

    def kernel(body, *extra_args):
        return functools.partial(body, z, *extra_args)

    def across(piece, mask_of):
        pairs = [(t, t ^ mask_of(t & 1)) for t in range(z.peers)]
        return lax.ppermute(piece, "sub", pairs)

    def to_near(piece):
        return across(piece, lambda core: 1)

    def exchange(kinds, sources, near):
        *pieces, beside = call(
            kernel(relay, kinds),
            [shape(2 * z.rows(kinds), kinds)] * (len(z.far) + 1), [], light, [table, *sources, near],
        )
        far = [across(piece, lambda core: z.far[z.at(k, core)]) for k, piece in enumerate(pieces)]
        return [*far, to_near(beside)]

    table, loaded, lift, wide, corners, near = call(
        kernel(begin),
        [((z.table,), jnp.int32), field, field, field, ((blocks, 2 * z.corners, width), BF16)]
        + [shape(z.near_rows(2), 2)],
        [
            pltpu.VMEM(load.shape, F32),
            pltpu.VMEM(row_scale.shape, F32),
            pltpu.VMEM(corner_coupling.shape, BF16),
            pltpu.SMEM(partner.shape, jnp.int32),
            pltpu.SMEM(off_pattern.shape, jnp.int32),
            pltpu.SMEM((z.peers,), jnp.int32),
            pltpu.SemaphoreType.DMA((5,)),
        ],
        light,
        [partner, off_pattern, load, row_scale, corner_coupling],
        False, range(5),
    )
    arrived = exchange(2, [loaded, lift], to_near(near))
    weight = (diag_blocks.shape, BF16)
    operator, diag, off = call(
        kernel(prepare), [((z.all_corners, z.all_corners), F32), weight, weight],
        [
            pltpu.VMEM(corner_index.shape, jnp.int32),
            pltpu.VMEM(coarse_inverse.shape, F32),
            pltpu.SemaphoreType.DMA((4,)),
        ],
        heavy, [corner_index, coarse_inverse, diag_blocks, off_blocks], False, range(4),
    )
    half = ((blocks, 2 * cols, width), BF16)
    tile = ((cols, LANES), F32)
    devices = z.groups * z.peers
    fixed = [wide, diag, off, corners]
    multipliers = None
    for step in range(ITERS):
        early = [field, half, extra, shape(z.near_rows(1), 1)]
        if step == 0:
            residual, part, parts, own_extra, near = call(
                kernel(first_half, step), [field] + early, [other], heavy,
                [table, *fixed, *arrived, loaded],
            )
            direction = residual
            older = []
        else:
            way = direction
            residual, direction, alpha, part, parts, own_extra, near = call(
                kernel(first_half, step), [field, field, tile] + early, [], heavy,
                [table, *fixed, gathered, residual, way, product],
            )
            older = [alpha, way] + [multipliers] * (step > 1)
        near = to_near(near)
        image, *more = call(
            kernel(second_half, step), [field] + [field] * (step > 0), [], heavy,
            [table, wide, diag, off, parts, part, *older],
        )
        if more:
            (multipliers,) = more
        if step == 0:
            (jump_lift,) = call(
                kernel(build_lift), [((blocks, 2 * z.all_corners, width), BF16)],
                [other, pltpu.VMEM((blocks, z.all_corners, width), F32)], heavy,
                [table, lift, *arrived],
            )
        arrived = exchange(1, [image, own_extra], near)
        product, sent = call(
            kernel(finish_product), [field, ((devices, cols, LANES), F32)], [other], heavy,
            [table, operator, image, own_extra, jump_lift, residual, direction, near, *arrived],
        )
        gathered = lax.all_to_all(sent, ("group", "sub"), 0, 0, tiled=True)
    multipliers, residual = call(
        kernel(finish), [(load.shape, F32)] * 2, [], light,
        [gathered, multipliers, residual, direction, product], False,
    )
    return multipliers, residual


def solution(mesh):
    return jax.shard_map(
        functools.partial(on_device, mesh=dict(mesh.shape)),
        mesh=mesh,
        in_specs=(
            P(None, ("group", "sub"), None),
            P(("group", "sub"), None),
            P(("group", "sub"), None, None),
            P(("group", "sub"), None, None),
            P(("group", "sub"), None),
            P(("group", "sub"), None),
            P(("group", "sub"), None),
            P("group", None),
            P("group", None),
        ),
        out_specs=(P(None, ("group", "sub"), None), P(None, ("group", "sub"), None)),
        check_vma=False,
    )
```

time: 62.2 us -> 97.9 us (1.57)
  blocking collectives: 0 us -> 44.6 us
  starting transfers between devices: 25.4 us -> 19.9 us
  waiting for transfers between devices: 17.5 us -> 15.3 us
  Pallas kernels: 18.3 us -> 17.1 us
    all_to_all x0 -> x4, blocking collectives: none -> 44.6 us  [on_device(): gathered = lax.all_to_all(sent, ('group', 'sub'), 0, 0, tiled=True)]
    ppermute x3 -> x0, starting transfers between devices: 4.44 us -> none  [on_device(): lax.ppermute(own_gram, 'group', [(a, a ^ k if power else (a + k) % z.grou...]
    ppermute x3 -> x0, waiting for transfers between devices: 3.42 us -> none  [on_device(): lax.ppermute(own_gram, 'group', [(a, a ^ k if power else (a + k) % z.grou...]
    pallas_call x20 -> x21, Pallas kernels: 18.3 us -> 17.1 us  [call(): pl.pallas_call(body, out_shape=shapes, in_specs=specs, out_specs=[SMEM if...]
    ppermute x25, waiting for transfers between devices: 14.1 us -> 15.3 us  [across(): return lax.ppermute(piece, 'sub', pairs)]
    ppermute x25, starting transfers between devices: 21 us -> 19.9 us  [across(): return lax.ppermute(piece, 'sub', pairs)]
  transfers between devices with their start and end apart: 28 -> 25, of which waited for: 17 -> 13; matrix products, arithmetic and copies ran while one was open for 0% -> 0% of each run, Pallas kernels for 16% -> 7%
where the time goes in v8:
time: 97.9 us; the launch traced here: 97.7 us
  blocking collectives  44.6 us (46%)
  starting transfers between devices  19.9 us (20%)
  Pallas kernels  17.1 us (17%)
  waiting for transfers between devices  15.3 us (16%)
    all_to_all x4, blocking collectives, on_device(): gathered = lax.all_to_all(sent, ('group', 'sub'), 0, 0, tiled=True)  44.6 us
    ppermute x25, starting transfers between devices, across(): return lax.ppermute(piece, 'sub', pairs)  19.9 us
    pallas_call x21, Pallas kernels, call(): pl.pallas_call(body, out_shape=shapes, in_specs=specs, out_specs=[SMEM if...  17.1 us
    ppermute x25, waiting for transfers between devices, across(): return lax.ppermute(piece, 'sub', pairs)  15.3 us
  transfers between devices with their start and end apart: 25, of which 13 were waited for; matrix products, arithmetic and copies ran while one was open for 0% of the time, Pallas kernels for 7%

profile of v8, /device:TPU:0, one launch (start us, length us, event | category | flops | bytes accessed | tf_op | source)
XLA Modules:
  0.0 97.7 jit_solution(8853818668773929533)
XLA Ops:
  0.6 1.0 %shard_map.104 = (s32[90]{0:T(128)S(4)}, f32[16,8,256]{2,1,0:T(8,128)S(1)}, f32[16,8,256]{2,1,0:T(8,128)S(1)}, f32[16,8,256]{2,1,0:T(8,128)S(1)}, bf16[16,16,256...) custom-call(s32[1,16]{1,0:T(1,128)} %partner.1, s32[1,16]{1,0:T(1,128)} %pattern.1, f32[8,16,256]{2,1,0:T(8,128)} %load.1, ...), custom_call_target="tpu_custom_call" | custom-call | flops 4000000 | bytes 250000 | tf_op jit(solution)/shard_map/pallas_call | solution.py:431
  2.2 1.0 %collective-permute-done.rest_2_ = f32[36,8,128]{2,1,0:T(8,128)S(1)} collective-permute-done((f32[36,8,128]{2,1,0:T(8,128)S(1)}, f32[36,8,128]{2,1,0:T(8,128)S(1)}, u32[]{:S(2)}, u32[]{:S(2)}) %collective-permute-start) | collective-permute-done | bytes 147488 | tf_op jit(solution)/shard_map/ppermute | solution.py:470
  3.3 3.9 %collective-permute-start.1 = (f32[24,8,128]{2,1,0:T(8,128)S(1)}, f32[24,8,128]{2,1,0:T(8,128)S(1)}, u32[]{:S(2)}, u32[]{:S(2)}) collective-permute-start(f32[24,8,128]{2,1,0:T(8,128)S(1)} %get-tuple-element.80), channel_id=1, source_target_pairs={{0,6},{1,7},{2,4},{3,5},{4,2},{5,3},{6,0},{7,1},{8,14},{9,15},{10,... | collective-permute-start | bytes 294920 | tf_op jit(solution)/shard_map/ppermute | solution.py:470
  7.8 2.3 %shard_map.105 = (f32[64,64]{1,0:T(8,128)S(1)}, bf16[16,256,256]{2,1,0:T(8,128)(2,1)S(1)}, bf16[16,256,256]{2,1,0:T(8,128)(2,1)S(1)}) custom-call(s32[1,64]{1,0:T(1,128)} %index_in.1, f32[32,32]{1,0:T(8,128)} %inverse_in.1, bf16[16,256,256]{2,1,0:T(8,128)(2,1)} %diag.1, bf16[16,256,256]{2,1,0:T(8,128)(2,1)} %off.1), custom_call_target="tpu_custom_call" | custom-call | flops 600000000 | bytes 37500000 | tf_op jit(solution)/shard_map/pallas_call | solution.py:431
  10.3 2.3 %collective-permute-done.2.rest_5_.rest_1_ = f32[24,8,128]{2,1,0:T(8,128)S(1)} collective-permute-done((f32[24,8,128]{2,1,0:T(8,128)S(1)}, f32[24,8,128]{2,1,0:T(8,128)S(1)}, u32[]{:S(2)}, u32[]{:S(2)}) %collective-permute-start.2) | collective-permute-done | bytes 98336 | tf_op jit(solution)/shard_map/ppermute | solution.py:470
  12.6 1.1 %shard_map.107 = (f32[16,8,256]{2,1,0:T(8,128)S(1)}, f32[16,8,256]{2,1,0:T(8,128)S(1)}, bf16[16,16,256]{2,1,0:T(8,128)(2,1)S(1)}, f32[8,128]{1,0:T(8,128)S(1)}, f32[19,8,128]{2,1,0:T(8,128)S(1)}) custom-call(s32[90]{0:T(128)S(4)} %get-tuple-element.71.table, f32[16,8,256]{2,1,0:T(8,128)S(1)} %get-tuple-element.73.rest_0_.wide, ...), custom_call_target="tpu_custom_call" | custom-call | flops 600000000 | bytes 37500000 | tf_op jit(solution)/shard_map/pallas_call | solution.py:431
  13.7 1.1 %shard_map.108.rest_0_.image = f32[16,8,256]{2,1,0:T(8,128)S(1)} custom-call(s32[90]{0:T(128)S(4)} %get-tuple-element.71.table, f32[16,8,256]{2,1,0:T(8,128)S(1)} %get-tuple-element.73.rest_0_.wide, bf16[16,256,256]{2,1,0:T(8,128)(2,1)S(1)} %get-tuple-element.74.rest_1_.diag, bf16[16,256,256]{2,1,0:T(8,128)(2,1)S(1)} %get-tuple-element.75.rest_2_.off, ...), custom_call_target="tpu_custom_call" | custom-call | flops 600000000 | bytes 37500000 | tf_op jit(solution)/shard_map/pallas_call | solution.py:431
  15.0 1.7 %collective-permute-start.6 = (f32[13,8,128]{2,1,0:T(8,128)S(1)}, f32[13,8,128]{2,1,0:T(8,128)S(1)}, u32[]{:S(2)}, u32[]{:S(2)}) collective-permute-start(f32[13,8,128]{2,1,0:T(8,128)S(1)} %get-tuple-element.89), channel_id=1, source_target_pairs={{0,6},{1,7},{2,4},{3,5},{4,2},{5,3},{6,0},{7,1},{8,14},{9,15},{10,... | collective-permute-start | bytes 159752 | tf_op jit(solution)/shard_map/ppermute | solution.py:470
  16.8 1.3 %collective-permute-start.7 = (f32[13,8,128]{2,1,0:T(8,128)S(1)}, f32[13,8,128]{2,1,0:T(8,128)S(1)}, u32[]{:S(2)}, u32[]{:S(2)}) collective-permute-start(f32[13,8,128]{2,1,0:T(8,128)S(1)} %get-tuple-element.90), channel_id=1, source_target_pairs={{0,2},{1,5},{2,0},{3,7},{4,6},{5,1},{6,4},{7,3},{8,10},{9,13},{10,... | collective-permute-start | bytes 159752 | tf_op jit(solution)/shard_map/ppermute | solution.py:470
  18.8 1.4 %collective-permute-done.6.rest_0_ = f32[13,8,128]{2,1,0:T(8,128)S(1)} collective-permute-done((f32[13,8,128]{2,1,0:T(8,128)S(1)}, f32[13,8,128]{2,1,0:T(8,128)S(1)}, u32[]{:S(2)}, u32[]{:S(2)}) %collective-permute-start.6) | collective-permute-done | bytes 53280 | tf_op jit(solution)/shard_map/ppermute | solution.py:470
  20.2 1.1 %collective-permute-done.7.rest_1_ = f32[13,8,128]{2,1,0:T(8,128)S(1)} collective-permute-done((f32[13,8,128]{2,1,0:T(8,128)S(1)}, f32[13,8,128]{2,1,0:T(8,128)S(1)}, u32[]{:S(2)}, u32[]{:S(2)}) %collective-permute-start.7) | collective-permute-done | bytes 53280 | tf_op jit(solution)/shard_map/ppermute | solution.py:470
  22.9 13.0 %all_to_all.20.rest_4_ = f32[32,8,128]{2,1,0:T(8,128)S(1)} all-to-all(f32[32,8,128]{2,1,0:T(8,128)S(1)} %get-tuple-element.93), channel_id=1, replica_groups=mesh['group'=4,'sub'=8] {'group','sub'}, dimensions={0} | all-to-all | bytes 262144 | tf_op jit(solution)/shard_map/all_to_all | solution.py:550
  35.9 1.3 %shard_map.112 = (f32[16,8,256]{2,1,0:T(8,128)S(1)}, f32[16,8,256]{2,1,0:T(8,128)S(1)}, f32[8,128]{1,0:T(8,128)S(1)}, f32[16,8,256]{2,1,0:T(8,128)S(1)}, bf16[16...) custom-call(s32[90]{0:T(128)S(4)} %get-tuple-element.71.table, ...), custom_call_target="tpu_custom_call" | custom-call | flops 600000000 | bytes 37500000 | tf_op jit(solution)/shard_map/pallas_call | solution.py:431
  37.4 1.1 %shard_map.113 = (f32[16,8,256]{2,1,0:T(8,128)S(1)}, f32[16,8,256]{2,1,0:T(8,128)S(1)}) custom-call(s32[90]{0:T(128)S(4)} %get-tuple-element.71.table, f32[16,8,256]{2,1,0:T(8,128)S(1)} %get-tuple-element.73.rest_0_.wide, bf16[16,256,256]{2,1,0:T(8,128)(2,1)S(1)} %get-tuple-element.74.rest_1_.diag, bf16[16,256,256]{2,1,0:T(8,128)(2,1)S(1)} %get-tuple-element.75.rest_2_.off, ...), custom_call_target="tpu_custom_call" | custom-call | flops 600000000 | bytes 37500000 | tf_op jit(solution)/shard_map/pallas_call | solution.py:431
  39.5 1.3 %collective-permute-start.12 = (f32[13,8,128]{2,1,0:T(8,128)S(1)}, f32[13,8,128]{2,1,0:T(8,128)S(1)}, u32[]{:S(2)}, u32[]{:S(2)}) collective-permute-start(f32[13,8,128]{2,1,0:T(8,128)S(1)} %get-tuple-element.104), channel_id=1, source_target_pairs={{0,2},{1,5},{2,0},{3,7},{4,6},{5,1},{6,4},{7,3},{8,10},{9,13},{10,... | collective-permute-start | bytes 159752 | tf_op jit(solution)/shard_map/ppermute | solution.py:470
  40.7 1.4 %collective-permute-start.13 = (f32[13,8,128]{2,1,0:T(8,128)S(1)}, f32[13,8,128]{2,1,0:T(8,128)S(1)}, u32[]{:S(2)}, u32[]{:S(2)}) collective-permute-start(f32[13,8,128]{2,1,0:T(8,128)S(1)} %get-tuple-element.105), channel_id=1, source_target_pairs={{0,4},{1,3},{2,6},{3,1},{4,0},{5,7},{6,2},{7,5},{8,12},{9,11},{10,... | collective-permute-start | bytes 159752 | tf_op jit(solution)/shard_map/ppermute | solution.py:470
  42.1 1.9 %collective-permute-done.11.rest_0_ = f32[13,8,128]{2,1,0:T(8,128)S(1)} collective-permute-done((f32[13,8,128]{2,1,0:T(8,128)S(1)}, f32[13,8,128]{2,1,0:T(8,128)S(1)}, u32[]{:S(2)}, u32[]{:S(2)}) %collective-permute-start.11) | collective-permute-done | bytes 53280 | tf_op jit(solution)/shard_map/ppermute | solution.py:470
  45.6 10.5 %all_to_all.21.rest_4_ = f32[32,8,128]{2,1,0:T(8,128)S(1)} all-to-all(f32[32,8,128]{2,1,0:T(8,128)S(1)} %get-tuple-element.107), channel_id=1, replica_groups=mesh['group'=4,'sub'=8] {'group','sub'}, dimensions={0} | all-to-all | bytes 262144 | tf_op jit(solution)/shard_map/all_to_all | solution.py:550
  56.2 1.3 %shard_map.116 = (f32[16,8,256]{2,1,0:T(8,128)S(1)}, f32[16,8,256]{2,1,0:T(8,128)S(1)}, f32[8,128]{1,0:T(8,128)S(1)}, f32[16,8,256]{2,1,0:T(8,128)S(1)}, bf16[16...) custom-call(s32[90]{0:T(128)S(4)} %get-tuple-element.71.table, ...), custom_call_target="tpu_custom_call" | custom-call | flops 600000000 | bytes 37500000 | tf_op jit(solution)/shard_map/pallas_call | solution.py:431
  57.7 1.1 %shard_map.117 = (f32[16,8,256]{2,1,0:T(8,128)S(1)}, f32[16,8,256]{2,1,0:T(8,128)S(1)}) custom-call(s32[90]{0:T(128)S(4)} %get-tuple-element.71.table, f32[16,8,256]{2,1,0:T(8,128)S(1)} %get-tuple-element.73.rest_0_.wide, bf16[16,256,256]{2,1,0:T(8,128)(2,1)S(1)} %get-tuple-element.74.rest_1_.diag, bf16[16,256,256]{2,1,0:T(8,128)(2,1)S(1)} %get-tuple-element.75.rest_2_.off, ...), custom_call_target="tpu_custom_call" | custom-call | flops 600000000 | bytes 37500000 | tf_op jit(solution)/shard_map/pallas_call | solution.py:431
  59.7 1.3 %collective-permute-start.17 = (f32[13,8,128]{2,1,0:T(8,128)S(1)}, f32[13,8,128]{2,1,0:T(8,128)S(1)}, u32[]{:S(2)}, u32[]{:S(2)}) collective-permute-start(f32[13,8,128]{2,1,0:T(8,128)S(1)} %get-tuple-element.119), channel_id=1, source_target_pairs={{0,2},{1,5},{2,0},{3,7},{4,6},{5,1},{6,4},{7,3},{8,10},{9,13},{10,... | collective-permute-start | bytes 159752 | tf_op jit(solution)/shard_map/ppermute | solution.py:470
  61.0 1.4 %collective-permute-start.18 = (f32[13,8,128]{2,1,0:T(8,128)S(1)}, f32[13,8,128]{2,1,0:T(8,128)S(1)}, u32[]{:S(2)}, u32[]{:S(2)}) collective-permute-start(f32[13,8,128]{2,1,0:T(8,128)S(1)} %get-tuple-element.120), channel_id=1, source_target_pairs={{0,4},{1,3},{2,6},{3,1},{4,0},{5,7},{6,2},{7,5},{8,12},{9,11},{10,... | collective-permute-start | bytes 159752 | tf_op jit(solution)/shard_map/ppermute | solution.py:470
  62.4 1.9 %collective-permute-done.16.rest_0_ = f32[13,8,128]{2,1,0:T(8,128)S(1)} collective-permute-done((f32[13,8,128]{2,1,0:T(8,128)S(1)}, f32[13,8,128]{2,1,0:T(8,128)S(1)}, u32[]{:S(2)}, u32[]{:S(2)}) %collective-permute-start.16) | collective-permute-done | bytes 53280 | tf_op jit(solution)/shard_map/ppermute | solution.py:470
  65.9 10.5 %all_to_all.22.rest_4_ = f32[32,8,128]{2,1,0:T(8,128)S(1)} all-to-all(f32[32,8,128]{2,1,0:T(8,128)S(1)} %get-tuple-element.122), channel_id=1, replica_groups=mesh['group'=4,'sub'=8] {'group','sub'}, dimensions={0} | all-to-all | bytes 262144 | tf_op jit(solution)/shard_map/all_to_all | solution.py:550
  76.4 1.3 %shard_map.120 = (f32[16,8,256]{2,1,0:T(8,128)S(1)}, f32[16,8,256]{2,1,0:T(8,128)S(1)}, f32[8,128]{1,0:T(8,128)S(1)}, f32[16,8,256]{2,1,0:T(8,128)S(1)}, bf16[16...) custom-call(s32[90]{0:T(128)S(4)} %get-tuple-element.71.table, ...), custom_call_target="tpu_custom_call" | custom-call | flops 600000000 | bytes 37500000 | tf_op jit(solution)/shard_map/pallas_call | solution.py:431
  77.9 1.1 %shard_map.121 = (f32[16,8,256]{2,1,0:T(8,128)S(1)}, f32[16,8,256]{2,1,0:T(8,128)S(1)}) custom-call(s32[90]{0:T(128)S(4)} %get-tuple-element.71.table, f32[16,8,256]{2,1,0:T(8,128)S(1)} %get-tuple-element.73.rest_0_.wide, bf16[16,256,256]{2,1,0:T(8,128)(2,1)S(1)} %get-tuple-element.74.rest_1_.diag, bf16[16,256,256]{2,1,0:T(8,128)(2,1)S(1)} %get-tuple-element.75.rest_2_.off, ...), custom_call_target="tpu_custom_call" | custom-call | flops 600000000 | bytes 37500000 | tf_op jit(solution)/shard_map/pallas_call | solution.py:431
  79.1 0.9 collective-permute-start.21
  80.0 1.3 %collective-permute-start.22 = (f32[13,8,128]{2,1,0:T(8,128)S(1)}, f32[13,8,128]{2,1,0:T(8,128)S(1)}, u32[]{:S(2)}, u32[]{:S(2)}) collective-permute-start(f32[13,8,128]{2,1,0:T(8,128)S(1)} %get-tuple-element.134), channel_id=1, source_target_pairs={{0,2},{1,5},{2,0},{3,7},{4,6},{5,1},{6,4},{7,3},{8,10},{9,13},{10,... | collective-permute-start | bytes 159752 | tf_op jit(solution)/shard_map/ppermute | solution.py:470
  81.2 1.4 %collective-permute-start.23 = (f32[13,8,128]{2,1,0:T(8,128)S(1)}, f32[13,8,128]{2,1,0:T(8,128)S(1)}, u32[]{:S(2)}, u32[]{:S(2)}) collective-permute-start(f32[13,8,128]{2,1,0:T(8,128)S(1)} %get-tuple-element.135), channel_id=1, source_target_pairs={{0,4},{1,3},{2,6},{3,1},{4,0},{5,7},{6,2},{7,5},{8,12},{9,11},{10,... | collective-permute-start | bytes 159752 | tf_op jit(solution)/shard_map/ppermute | solution.py:470
  82.6 1.9 %collective-permute-done.21.rest_0_ = f32[13,8,128]{2,1,0:T(8,128)S(1)} collective-permute-done((f32[13,8,128]{2,1,0:T(8,128)S(1)}, f32[13,8,128]{2,1,0:T(8,128)S(1)}, u32[]{:S(2)}, u32[]{:S(2)}) %collective-permute-start.21) | collective-permute-done | bytes 53280 | tf_op jit(solution)/shard_map/ppermute | solution.py:470
  86.1 10.5 %all_to_all.23.gathered = f32[32,8,128]{2,1,0:T(8,128)S(1)} all-to-all(f32[32,8,128]{2,1,0:T(8,128)S(1)} %get-tuple-element.137), channel_id=1, replica_groups=mesh['group'=4,'sub'=8] {'group','sub'}, dimensions={0} | all-to-all | bytes 262144 | tf_op jit(solution)/shard_map/all_to_all | solution.py:550
  96.7 1.0 %shard_map.124 = (f32[8,16,256]{2,1,0:T(8,128)}, f32[8,16,256]{2,1,0:T(8,128)}) custom-call(f32[32,8,128]{2,1,0:T(8,128)S(1)} %all_to_all.23.gathered, f32[16,8,256]{2,1,0:T(8,128)S(1)} %get-tuple-element.138.before, f32[16,8,256]{2,1,0:T(8,128)S(1)} %get-tuple-element.130.residual.residual_in, f32[16,8,256]{2,1,0:T(8,128)S(1)} %get-tuple-element.131.direction, ...), custom_call_target="tpu_custom_call" | custom-call | flops 4000000 | bytes 250000 | tf_op jit(solution)/shard_map/pallas_call | solution.py:431
  (43 shorter events, 11.4 us)
Async XLA Ops:
  1.7 1.5 %collective-permute-start = (f32[36,8,128]{2,1,0:T(8,128)S(1)}, f32[36,8,128]{2,1,0:T(8,128)S(1)}, u32[]{:S(2)}, u32[]{:S(2)}) collective-permute-start(f32[36,8,128]{2,1,0:T(8,128)S(1)} %get-tuple-element.79), channel_id=1, source_target_pairs={{0,1},{1,0},{2,3},{3,2},{4,5},{5,4},{6,7},{7,6},{8,9},{9,8},{10,11... | collective-permute-start | bytes 442376 | tf_op jit(solution)/shard_map/ppermute | solution.py:470
  3.3 7.1 %collective-permute-start.1 = (f32[24,8,128]{2,1,0:T(8,128)S(1)}, f32[24,8,128]{2,1,0:T(8,128)S(1)}, u32[]{:S(2)}, u32[]{:S(2)}) collective-permute-start(f32[24,8,128]{2,1,0:T(8,128)S(1)} %get-tuple-element.80), channel_id=1, source_target_pairs={{0,6},{1,7},{2,4},{3,5},{4,2},{5,3},{6,0},{7,1},{8,14},{9,15},{10,... | collective-permute-start | bytes 294920 | tf_op jit(solution)/shard_map/ppermute | solution.py:470
  7.1 5.5 %collective-permute-start.2 = (f32[24,8,128]{2,1,0:T(8,128)S(1)}, f32[24,8,128]{2,1,0:T(8,128)S(1)}, u32[]{:S(2)}, u32[]{:S(2)}) collective-permute-start(f32[24,8,128]{2,1,0:T(8,128)S(1)} %get-tuple-element.81), channel_id=1, source_target_pairs={{0,2},{1,5},{2,0},{3,7},{4,6},{5,1},{6,4},{7,3},{8,10},{9,13},{10,... | collective-permute-start | bytes 294920 | tf_op jit(solution)/shard_map/ppermute | solution.py:470
  7.7 4.9 %collective-permute-start.3 = (f32[24,8,128]{2,1,0:T(8,128)S(1)}, f32[24,8,128]{2,1,0:T(8,128)S(1)}, u32[]{:S(2)}, u32[]{:S(2)}) collective-permute-start(f32[24,8,128]{2,1,0:T(8,128)S(1)} %get-tuple-element.82), channel_id=1, source_target_pairs={{0,4},{1,3},{2,6},{3,1},{4,0},{5,7},{6,2},{7,5},{8,12},{9,11},{10,... | collective-permute-start | bytes 294920 | tf_op jit(solution)/shard_map/ppermute | solution.py:470
  7.8 4.8 %collective-permute-start.4 = (f32[24,8,128]{2,1,0:T(8,128)S(1)}, f32[24,8,128]{2,1,0:T(8,128)S(1)}, u32[]{:S(2)}, u32[]{:S(2)}) collective-permute-start(f32[24,8,128]{2,1,0:T(8,128)S(1)} %get-tuple-element.83), channel_id=1, source_target_pairs={{0,1},{1,0},{2,3},{3,2},{4,5},{5,4},{6,7},{7,6},{8,9},{9,8},{10,11... | collective-permute-start | bytes 294920 | tf_op jit(solution)/shard_map/ppermute | solution.py:470
  13.7 1.3 %collective-permute-start.5 = (f32[19,8,128]{2,1,0:T(8,128)S(1)}, f32[19,8,128]{2,1,0:T(8,128)S(1)}, u32[]{:S(2)}, u32[]{:S(2)}) collective-permute-start(f32[19,8,128]{2,1,0:T(8,128)S(1)} %get-tuple-element.88), channel_id=1, source_target_pairs={{0,1},{1,0},{2,3},{3,2},{4,5},{5,4},{6,7},{7,6},{8,9},{9,8},{10,11... | collective-permute-start | bytes 233480 | tf_op jit(solution)/shard_map/ppermute | solution.py:470
  15.0 5.2 %collective-permute-start.6 = (f32[13,8,128]{2,1,0:T(8,128)S(1)}, f32[13,8,128]{2,1,0:T(8,128)S(1)}, u32[]{:S(2)}, u32[]{:S(2)}) collective-permute-start(f32[13,8,128]{2,1,0:T(8,128)S(1)} %get-tuple-element.89), channel_id=1, source_target_pairs={{0,6},{1,7},{2,4},{3,5},{4,2},{5,3},{6,0},{7,1},{8,14},{9,15},{10,... | collective-permute-start | bytes 159752 | tf_op jit(solution)/shard_map/ppermute | solution.py:470
  16.8 4.5 %collective-permute-start.7 = (f32[13,8,128]{2,1,0:T(8,128)S(1)}, f32[13,8,128]{2,1,0:T(8,128)S(1)}, u32[]{:S(2)}, u32[]{:S(2)}) collective-permute-start(f32[13,8,128]{2,1,0:T(8,128)S(1)} %get-tuple-element.90), channel_id=1, source_target_pairs={{0,2},{1,5},{2,0},{3,7},{4,6},{5,1},{6,4},{7,3},{8,10},{9,13},{10,... | collective-permute-start | bytes 159752 | tf_op jit(solution)/shard_map/ppermute | solution.py:470
  18.0 4.1 %collective-permute-start.8 = (f32[13,8,128]{2,1,0:T(8,128)S(1)}, f32[13,8,128]{2,1,0:T(8,128)S(1)}, u32[]{:S(2)}, u32[]{:S(2)}) collective-permute-start(f32[13,8,128]{2,1,0:T(8,128)S(1)} %get-tuple-element.91), channel_id=1, source_target_pairs={{0,4},{1,3},{2,6},{3,1},{4,0},{5,7},{6,2},{7,5},{8,12},{9,11},{10,... | collective-permute-start | bytes 159752 | tf_op jit(solution)/shard_map/ppermute | solution.py:470
  18.6 3.6 %collective-permute-start.9 = (f32[13,8,128]{2,1,0:T(8,128)S(1)}, f32[13,8,128]{2,1,0:T(8,128)S(1)}, u32[]{:S(2)}, u32[]{:S(2)}) collective-permute-start(f32[13,8,128]{2,1,0:T(8,128)S(1)} %get-tuple-element.92), channel_id=1, source_target_pairs={{0,1},{1,0},{2,3},{3,2},{4,5},{5,4},{6,7},{7,6},{8,9},{9,8},{10,11... | collective-permute-start | bytes 159752 | tf_op jit(solution)/shard_map/ppermute | solution.py:470
  37.2 1.3 %collective-permute-start.10 = (f32[19,8,128]{2,1,0:T(8,128)S(1)}, f32[19,8,128]{2,1,0:T(8,128)S(1)}, u32[]{:S(2)}, u32[]{:S(2)}) collective-permute-start(f32[19,8,128]{2,1,0:T(8,128)S(1)} %get-tuple-element.102), channel_id=1, source_target_pairs={{0,1},{1,0},{2,3},{3,2},{4,5},{5,4},{6,7},{7,6},{8,9},{9,8},{10,11... | collective-permute-start | bytes 233480 | tf_op jit(solution)/shard_map/ppermute | solution.py:470
  38.6 5.5 %collective-permute-start.11 = (f32[13,8,128]{2,1,0:T(8,128)S(1)}, f32[13,8,128]{2,1,0:T(8,128)S(1)}, u32[]{:S(2)}, u32[]{:S(2)}) collective-permute-start(f32[13,8,128]{2,1,0:T(8,128)S(1)} %get-tuple-element.103), channel_id=1, source_target_pairs={{0,6},{1,7},{2,4},{3,5},{4,2},{5,3},{6,0},{7,1},{8,14},{9,15},{10,... | collective-permute-start | bytes 159752 | tf_op jit(solution)/shard_map/ppermute | solution.py:470
  39.5 4.6 %collective-permute-start.12 = (f32[13,8,128]{2,1,0:T(8,128)S(1)}, f32[13,8,128]{2,1,0:T(8,128)S(1)}, u32[]{:S(2)}, u32[]{:S(2)}) collective-permute-start(f32[13,8,128]{2,1,0:T(8,128)S(1)} %get-tuple-element.104), channel_id=1, source_target_pairs={{0,2},{1,5},{2,0},{3,7},{4,6},{5,1},{6,4},{7,3},{8,10},{9,13},{10,... | collective-permute-start | bytes 159752 | tf_op jit(solution)/shard_map/ppermute | solution.py:470
  40.7 4.1 %collective-permute-start.13 = (f32[13,8,128]{2,1,0:T(8,128)S(1)}, f32[13,8,128]{2,1,0:T(8,128)S(1)}, u32[]{:S(2)}, u32[]{:S(2)}) collective-permute-start(f32[13,8,128]{2,1,0:T(8,128)S(1)} %get-tuple-element.105), channel_id=1, source_target_pairs={{0,4},{1,3},{2,6},{3,1},{4,0},{5,7},{6,2},{7,5},{8,12},{9,11},{10,... | collective-permute-start | bytes 159752 | tf_op jit(solution)/shard_map/ppermute | solution.py:470
  42.1 2.7 %collective-permute-start.14 = (f32[13,8,128]{2,1,0:T(8,128)S(1)}, f32[13,8,128]{2,1,0:T(8,128)S(1)}, u32[]{:S(2)}, u32[]{:S(2)}) collective-permute-start(f32[13,8,128]{2,1,0:T(8,128)S(1)} %get-tuple-element.106), channel_id=1, source_target_pairs={{0,1},{1,0},{2,3},{3,2},{4,5},{5,4},{6,7},{7,6},{8,9},{9,8},{10,11... | collective-permute-start | bytes 159752 | tf_op jit(solution)/shard_map/ppermute | solution.py:470
  57.5 1.3 %collective-permute-start.15 = (f32[19,8,128]{2,1,0:T(8,128)S(1)}, f32[19,8,128]{2,1,0:T(8,128)S(1)}, u32[]{:S(2)}, u32[]{:S(2)}) collective-permute-start(f32[19,8,128]{2,1,0:T(8,128)S(1)} %get-tuple-element.117), channel_id=1, source_target_pairs={{0,1},{1,0},{2,3},{3,2},{4,5},{5,4},{6,7},{7,6},{8,9},{9,8},{10,11... | collective-permute-start | bytes 233480 | tf_op jit(solution)/shard_map/ppermute | solution.py:470
  58.8 5.5 %collective-permute-start.16 = (f32[13,8,128]{2,1,0:T(8,128)S(1)}, f32[13,8,128]{2,1,0:T(8,128)S(1)}, u32[]{:S(2)}, u32[]{:S(2)}) collective-permute-start(f32[13,8,128]{2,1,0:T(8,128)S(1)} %get-tuple-element.118), channel_id=1, source_target_pairs={{0,6},{1,7},{2,4},{3,5},{4,2},{5,3},{6,0},{7,1},{8,14},{9,15},{10,... | collective-permute-start | bytes 159752 | tf_op jit(solution)/shard_map/ppermute | solution.py:470
  59.7 4.6 %collective-permute-start.17 = (f32[13,8,128]{2,1,0:T(8,128)S(1)}, f32[13,8,128]{2,1,0:T(8,128)S(1)}, u32[]{:S(2)}, u32[]{:S(2)}) collective-permute-start(f32[13,8,128]{2,1,0:T(8,128)S(1)} %get-tuple-element.119), channel_id=1, source_target_pairs={{0,2},{1,5},{2,0},{3,7},{4,6},{5,1},{6,4},{7,3},{8,10},{9,13},{10,... | collective-permute-start | bytes 159752 | tf_op jit(solution)/shard_map/ppermute | solution.py:470
  61.0 4.1 %collective-permute-start.18 = (f32[13,8,128]{2,1,0:T(8,128)S(1)}, f32[13,8,128]{2,1,0:T(8,128)S(1)}, u32[]{:S(2)}, u32[]{:S(2)}) collective-permute-start(f32[13,8,128]{2,1,0:T(8,128)S(1)} %get-tuple-element.120), channel_id=1, source_target_pairs={{0,4},{1,3},{2,6},{3,1},{4,0},{5,7},{6,2},{7,5},{8,12},{9,11},{10,... | collective-permute-start | bytes 159752 | tf_op jit(solution)/shard_map/ppermute | solution.py:470
  62.4 2.7 %collective-permute-start.19 = (f32[13,8,128]{2,1,0:T(8,128)S(1)}, f32[13,8,128]{2,1,0:T(8,128)S(1)}, u32[]{:S(2)}, u32[]{:S(2)}) collective-permute-start(f32[13,8,128]{2,1,0:T(8,128)S(1)} %get-tuple-element.121), channel_id=1, source_target_pairs={{0,1},{1,0},{2,3},{3,2},{4,5},{5,4},{6,7},{7,6},{8,9},{9,8},{10,11... | collective-permute-start | bytes 159752 | tf_op jit(solution)/shard_map/ppermute | solution.py:470
  77.7 1.3 %collective-permute-start.20 = (f32[19,8,128]{2,1,0:T(8,128)S(1)}, f32[19,8,128]{2,1,0:T(8,128)S(1)}, u32[]{:S(2)}, u32[]{:S(2)}) collective-permute-start(f32[19,8,128]{2,1,0:T(8,128)S(1)} %get-tuple-element.132), channel_id=1, source_target_pairs={{0,1},{1,0},{2,3},{3,2},{4,5},{5,4},{6,7},{7,6},{8,9},{9,8},{10,11... | collective-permute-start | bytes 233480 | tf_op jit(solution)/shard_map/ppermute | solution.py:470
  79.1 5.5 %collective-permute-start.21 = (f32[13,8,128]{2,1,0:T(8,128)S(1)}, f32[13,8,128]{2,1,0:T(8,128)S(1)}, u32[]{:S(2)}, u32[]{:S(2)}) collective-permute-start(f32[13,8,128]{2,1,0:T(8,128)S(1)} %get-tuple-element.133), channel_id=1, source_target_pairs={{0,6},{1,7},{2,4},{3,5},{4,2},{5,3},{6,0},{7,1},{8,14},{9,15},{10,... | collective-permute-start | bytes 159752 | tf_op jit(solution)/shard_map/ppermute | solution.py:470
  80.0 4.6 %collective-permute-start.22 = (f32[13,8,128]{2,1,0:T(8,128)S(1)}, f32[13,8,128]{2,1,0:T(8,128)S(1)}, u32[]{:S(2)}, u32[]{:S(2)}) collective-permute-start(f32[13,8,128]{2,1,0:T(8,128)S(1)} %get-tuple-element.134), channel_id=1, source_target_pairs={{0,2},{1,5},{2,0},{3,7},{4,6},{5,1},{6,4},{7,3},{8,10},{9,13},{10,... | collective-permute-start | bytes 159752 | tf_op jit(solution)/shard_map/ppermute | solution.py:470
  81.2 4.1 %collective-permute-start.23 = (f32[13,8,128]{2,1,0:T(8,128)S(1)}, f32[13,8,128]{2,1,0:T(8,128)S(1)}, u32[]{:S(2)}, u32[]{:S(2)}) collective-permute-start(f32[13,8,128]{2,1,0:T(8,128)S(1)} %get-tuple-element.135), channel_id=1, source_target_pairs={{0,4},{1,3},{2,6},{3,1},{4,0},{5,7},{6,2},{7,5},{8,12},{9,11},{10,... | collective-permute-start | bytes 159752 | tf_op jit(solution)/shard_map/ppermute | solution.py:470
  82.6 2.7 %collective-permute-start.24 = (f32[13,8,128]{2,1,0:T(8,128)S(1)}, f32[13,8,128]{2,1,0:T(8,128)S(1)}, u32[]{:S(2)}, u32[]{:S(2)}) collective-permute-start(f32[13,8,128]{2,1,0:T(8,128)S(1)} %get-tuple-element.136), channel_id=1, source_target_pairs={{0,1},{1,0},{2,3},{3,2},{4,5},{5,4},{6,7},{7,6},{8,9},{9,8},{10,11... | collective-permute-start | bytes 159752 | tf_op jit(solution)/shard_map/ppermute | solution.py:470

commit v9 on v8

--- a/solution.py
+++ b/solution.py
@@ -267,27 +267,44 @@
     return jnp.sum(a, axis=1, keepdims=True)
 
 
-def column(table, lane):
-    return jnp.broadcast_to(table[:, lane : lane + 1], table.shape)
+def to_row(z, values):
+    shape = (z.columns, LANES)
+    lanes = lane_ids(shape)
+    rows = lax.broadcasted_iota(jnp.int32, shape, 0)
+    tile = jnp.zeros(shape, F32)
+    for first, value in values:
+        tile = jnp.where(lanes == first + rows, value, tile)
+    return jnp.sum(tile, axis=0, keepdims=True)
+
+
+def to_tile(z, row):
+    shape = (z.columns, LANES)
+    rows = lax.broadcasted_iota(jnp.int32, shape, 0)
+    tile = jnp.where(lane_ids(shape) == rows, jnp.broadcast_to(row, shape), 0.0)
+    return jnp.broadcast_to(lane_sum(tile), shape)
 
 
 def scalars(z, gathered):
-    shape = (z.columns, LANES)
-    zero = jnp.zeros(shape, F32)
+    zero = jnp.zeros((1, LANES), F32)
     count = gathered.shape[0]
     unroll = 32 if count % 32 == 0 else 1
     total = lax.fori_loop(0, count, lambda k, acc: acc + gathered[k], zero, unroll=unroll)
-    norm = column(total, RR)
-    alpha = norm / column(total, DP)
+
+    def group(row, at):
+        return pltpu.roll(row, LANES - at * z.columns, 1) if at else row
+
+    norm = group(total, RR)
+    alpha = norm / group(total, DP)
+    placed = pltpu.roll(alpha, PP * z.columns, 1)
 
     def squares(k, acc):
-        tile = gathered[k]
-        step = alpha * pltpu.roll(tile, LANES // 2, 1)
-        return acc + tile * step * step
+        row = gathered[k]
+        step = placed * pltpu.roll(row, LANES // 2, 1)
+        return acc + row * step * step
 
     moved = lax.fori_loop(0, count, squares, zero, unroll=unroll)
-    following = norm - 2.0 * alpha * column(total, RP) + column(moved, PP)
-    return alpha, following / norm
+    following = norm - 2.0 * alpha * group(total, RP) + group(moved, PP)
+    return to_tile(z, alpha), to_tile(z, following / norm)
 
 
 def across_block(z, tile):
@@ -400,12 +417,10 @@
     for i in range(z.blocks):
         value = product[i] * shrink
         squares = squares + value * value
-    lanes = lane_ids((z.columns, LANES))
-    tile = jnp.where(lanes == PP + LANES // 2, top, 0.0)
-    for lane, value in zip([RR, DP, RP, PP], sums + [squares]):
-        tile = jnp.where(lanes == lane, lane_sum(value), tile)
+    values = [(k * z.columns, lane_sum(v)) for k, v in enumerate(sums + [squares])]
+    row = to_row(z, values + [(PP * z.columns + LANES // 2, top)])
     for k in range(sent.shape[0]):
-        sent[k] = tile
+        sent[k] = row
 
 
 def finish(z, gathered, before, residual_in, direction, product, multipliers, residual):
@@ -544,7 +559,7 @@
             )
         arrived = exchange(1, [image, own_extra], near)
         product, sent = call(
-            kernel(finish_product), [field, ((devices, cols, LANES), F32)], [other], heavy,
+            kernel(finish_product), [field, ((devices, 1, LANES), F32)], [other], heavy,
             [table, operator, image, own_extra, jump_lift, residual, direction, near, *arrived],
         )
         gathered = lax.all_to_all(sent, ("group", "sub"), 0, 0, tiled=True)

time: 97.9 us -> 92 us (0.940)
  blocking collectives: 44.6 us -> 38.4 us
    all_to_all x4, blocking collectives: 44.6 us -> 38.4 us  [on_device(): gathered = lax.all_to_all(sent, ('group', 'sub'), 0, 0, tiled=True)]
  transfers between devices with their start and end apart: 25 -> 25, of which waited for: 13 -> 16; matrix products, arithmetic and copies ran while one was open for 0% -> 0% of each run, Pallas kernels for 7% -> 7%
where the time goes in v9:
time: 92 us; the launch traced here: 91.8 us
  blocking collectives  38.4 us (42%)
  starting transfers between devices  19.3 us (21%)
  Pallas kernels  17.7 us (19%)
  waiting for transfers between devices  15.6 us (17%)
    all_to_all x4, blocking collectives, on_device(): gathered = lax.all_to_all(sent, ('group', 'sub'), 0, 0, tiled=True)  38.4 us
    ppermute x25, starting transfers between devices, across(): return lax.ppermute(piece, 'sub', pairs)  19.3 us
    pallas_call x21, Pallas kernels, call(): pl.pallas_call(body, out_shape=shapes, in_specs=specs, out_specs=[SMEM if...  17.7 us
    ppermute x25, waiting for transfers between devices, across(): return lax.ppermute(piece, 'sub', pairs)  15.6 us
  transfers between devices with their start and end apart: 25, of which 16 were waited for; matrix products, arithmetic and copies ran while one was open for 0% of the time, Pallas kernels for 7%

profile of v9, /device:TPU:0, one launch (start us, length us, event | category | flops | bytes accessed | tf_op | source)
XLA Modules:
  0.0 91.8 jit_solution(9946589109738164580)
XLA Ops:
  0.6 1.0 %shard_map.104 = (s32[90]{0:T(128)S(4)}, f32[16,8,256]{2,1,0:T(8,128)S(1)}, f32[16,8,256]{2,1,0:T(8,128)S(1)}, f32[16,8,256]{2,1,0:T(8,128)S(1)}, bf16[16,16,256...) custom-call(s32[1,16]{1,0:T(1,128)} %partner.1, s32[1,16]{1,0:T(1,128)} %pattern.1, f32[8,16,256]{2,1,0:T(8,128)} %load.1, ...), custom_call_target="tpu_custom_call" | custom-call | flops 4000000 | bytes 250000 | tf_op jit(solution)/shard_map/pallas_call | solution.py:446
  2.2 1.0 %collective-permute-done.rest_2_ = f32[36,8,128]{2,1,0:T(8,128)S(1)} collective-permute-done((f32[36,8,128]{2,1,0:T(8,128)S(1)}, f32[36,8,128]{2,1,0:T(8,128)S(1)}, u32[]{:S(2)}, u32[]{:S(2)}) %collective-permute-start) | collective-permute-done | bytes 147488 | tf_op jit(solution)/shard_map/ppermute | solution.py:485
  3.3 3.9 %collective-permute-start.1 = (f32[24,8,128]{2,1,0:T(8,128)S(1)}, f32[24,8,128]{2,1,0:T(8,128)S(1)}, u32[]{:S(2)}, u32[]{:S(2)}) collective-permute-start(f32[24,8,128]{2,1,0:T(8,128)S(1)} %get-tuple-element.80), channel_id=1, source_target_pairs={{0,6},{1,7},{2,4},{3,5},{4,2},{5,3},{6,0},{7,1},{8,14},{9,15},{10,... | collective-permute-start | bytes 294920 | tf_op jit(solution)/shard_map/ppermute | solution.py:485
  7.8 2.3 %shard_map.105 = (f32[64,64]{1,0:T(8,128)S(1)}, bf16[16,256,256]{2,1,0:T(8,128)(2,1)S(1)}, bf16[16,256,256]{2,1,0:T(8,128)(2,1)S(1)}) custom-call(s32[1,64]{1,0:T(1,128)} %index_in.1, f32[32,32]{1,0:T(8,128)} %inverse_in.1, bf16[16,256,256]{2,1,0:T(8,128)(2,1)} %diag.1, bf16[16,256,256]{2,1,0:T(8,128)(2,1)} %off.1), custom_call_target="tpu_custom_call" | custom-call | flops 600000000 | bytes 37500000 | tf_op jit(solution)/shard_map/pallas_call | solution.py:446
  10.3 2.3 %collective-permute-done.2.rest_5_.rest_1_ = f32[24,8,128]{2,1,0:T(8,128)S(1)} collective-permute-done((f32[24,8,128]{2,1,0:T(8,128)S(1)}, f32[24,8,128]{2,1,0:T(8,128)S(1)}, u32[]{:S(2)}, u32[]{:S(2)}) %collective-permute-start.2) | collective-permute-done | bytes 98336 | tf_op jit(solution)/shard_map/ppermute | solution.py:485
  12.6 1.1 %shard_map.107 = (f32[16,8,256]{2,1,0:T(8,128)S(1)}, f32[16,8,256]{2,1,0:T(8,128)S(1)}, bf16[16,16,256]{2,1,0:T(8,128)(2,1)S(1)}, f32[8,128]{1,0:T(8,128)S(1)}, f32[19,8,128]{2,1,0:T(8,128)S(1)}) custom-call(s32[90]{0:T(128)S(4)} %get-tuple-element.71.table, f32[16,8,256]{2,1,0:T(8,128)S(1)} %get-tuple-element.73.rest_0_.wide, ...), custom_call_target="tpu_custom_call" | custom-call | flops 600000000 | bytes 37500000 | tf_op jit(solution)/shard_map/pallas_call | solution.py:446
  13.7 1.1 %shard_map.108.rest_0_.image = f32[16,8,256]{2,1,0:T(8,128)S(1)} custom-call(s32[90]{0:T(128)S(4)} %get-tuple-element.71.table, f32[16,8,256]{2,1,0:T(8,128)S(1)} %get-tuple-element.73.rest_0_.wide, bf16[16,256,256]{2,1,0:T(8,128)(2,1)S(1)} %get-tuple-element.74.rest_1_.diag, bf16[16,256,256]{2,1,0:T(8,128)(2,1)S(1)} %get-tuple-element.75.rest_2_.off, ...), custom_call_target="tpu_custom_call" | custom-call | flops 600000000 | bytes 37500000 | tf_op jit(solution)/shard_map/pallas_call | solution.py:446
  15.0 1.7 %collective-permute-start.6 = (f32[13,8,128]{2,1,0:T(8,128)S(1)}, f32[13,8,128]{2,1,0:T(8,128)S(1)}, u32[]{:S(2)}, u32[]{:S(2)}) collective-permute-start(f32[13,8,128]{2,1,0:T(8,128)S(1)} %get-tuple-element.89), channel_id=1, source_target_pairs={{0,6},{1,7},{2,4},{3,5},{4,2},{5,3},{6,0},{7,1},{8,14},{9,15},{10,... | collective-permute-start | bytes 159752 | tf_op jit(solution)/shard_map/ppermute | solution.py:485
  16.8 1.3 %collective-permute-start.7 = (f32[13,8,128]{2,1,0:T(8,128)S(1)}, f32[13,8,128]{2,1,0:T(8,128)S(1)}, u32[]{:S(2)}, u32[]{:S(2)}) collective-permute-start(f32[13,8,128]{2,1,0:T(8,128)S(1)} %get-tuple-element.90), channel_id=1, source_target_pairs={{0,2},{1,5},{2,0},{3,7},{4,6},{5,1},{6,4},{7,3},{8,10},{9,13},{10,... | collective-permute-start | bytes 159752 | tf_op jit(solution)/shard_map/ppermute | solution.py:485
  18.8 1.4 %collective-permute-done.6.rest_0_ = f32[13,8,128]{2,1,0:T(8,128)S(1)} collective-permute-done((f32[13,8,128]{2,1,0:T(8,128)S(1)}, f32[13,8,128]{2,1,0:T(8,128)S(1)}, u32[]{:S(2)}, u32[]{:S(2)}) %collective-permute-start.6) | collective-permute-done | bytes 53280 | tf_op jit(solution)/shard_map/ppermute | solution.py:485
  20.2 1.1 %collective-permute-done.7.rest_1_ = f32[13,8,128]{2,1,0:T(8,128)S(1)} collective-permute-done((f32[13,8,128]{2,1,0:T(8,128)S(1)}, f32[13,8,128]{2,1,0:T(8,128)S(1)}, u32[]{:S(2)}, u32[]{:S(2)}) %collective-permute-start.7) | collective-permute-done | bytes 53280 | tf_op jit(solution)/shard_map/ppermute | solution.py:485
  21.3 0.9 collective-permute-done.8.rest_2_
  22.9 11.9 %all_to_all.20.rest_4_ = f32[32,1,128]{2,1,0:T(1,128)S(1)} all-to-all(f32[32,1,128]{2,1,0:T(1,128)S(1)} %get-tuple-element.93), channel_id=1, replica_groups=mesh['group'=4,'sub'=8] {'group','sub'}, dimensions={0} | all-to-all | bytes 32768 | tf_op jit(solution)/shard_map/all_to_all | solution.py:565
  34.8 1.5 %shard_map.112 = (f32[16,8,256]{2,1,0:T(8,128)S(1)}, f32[16,8,256]{2,1,0:T(8,128)S(1)}, f32[8,128]{1,0:T(8,128)S(1)}, f32[16,8,256]{2,1,0:T(8,128)S(1)}, bf16[16...) custom-call(s32[90]{0:T(128)S(4)} %get-tuple-element.71.table, ...), custom_call_target="tpu_custom_call" | custom-call | flops 600000000 | bytes 37500000 | tf_op jit(solution)/shard_map/pallas_call | solution.py:446
  36.3 1.1 %shard_map.113 = (f32[16,8,256]{2,1,0:T(8,128)S(1)}, f32[16,8,256]{2,1,0:T(8,128)S(1)}) custom-call(s32[90]{0:T(128)S(4)} %get-tuple-element.71.table, f32[16,8,256]{2,1,0:T(8,128)S(1)} %get-tuple-element.73.rest_0_.wide, bf16[16,256,256]{2,1,0:T(8,128)(2,1)S(1)} %get-tuple-element.74.rest_1_.diag, bf16[16,256,256]{2,1,0:T(8,128)(2,1)S(1)} %get-tuple-element.75.rest_2_.off, ...), custom_call_target="tpu_custom_call" | custom-call | flops 600000000 | bytes 37500000 | tf_op jit(solution)/shard_map/pallas_call | solution.py:446
  38.3 1.4 %collective-permute-start.12 = (f32[13,8,128]{2,1,0:T(8,128)S(1)}, f32[13,8,128]{2,1,0:T(8,128)S(1)}, u32[]{:S(2)}, u32[]{:S(2)}) collective-permute-start(f32[13,8,128]{2,1,0:T(8,128)S(1)} %get-tuple-element.104), channel_id=1, source_target_pairs={{0,2},{1,5},{2,0},{3,7},{4,6},{5,1},{6,4},{7,3},{8,10},{9,13},{10,... | collective-permute-start | bytes 159752 | tf_op jit(solution)/shard_map/ppermute | solution.py:485
  39.7 1.5 %collective-permute-start.13 = (f32[13,8,128]{2,1,0:T(8,128)S(1)}, f32[13,8,128]{2,1,0:T(8,128)S(1)}, u32[]{:S(2)}, u32[]{:S(2)}) collective-permute-start(f32[13,8,128]{2,1,0:T(8,128)S(1)} %get-tuple-element.105), channel_id=1, source_target_pairs={{0,4},{1,3},{2,6},{3,1},{4,0},{5,7},{6,2},{7,5},{8,12},{9,11},{10,... | collective-permute-start | bytes 159752 | tf_op jit(solution)/shard_map/ppermute | solution.py:485
  41.2 2.1 %collective-permute-done.11.rest_0_ = f32[13,8,128]{2,1,0:T(8,128)S(1)} collective-permute-done((f32[13,8,128]{2,1,0:T(8,128)S(1)}, f32[13,8,128]{2,1,0:T(8,128)S(1)}, u32[]{:S(2)}, u32[]{:S(2)}) %collective-permute-start.11) | collective-permute-done | bytes 53280 | tf_op jit(solution)/shard_map/ppermute | solution.py:485
  44.6 8.8 %all_to_all.21.rest_4_ = f32[32,1,128]{2,1,0:T(1,128)S(1)} all-to-all(f32[32,1,128]{2,1,0:T(1,128)S(1)} %get-tuple-element.107), channel_id=1, replica_groups=mesh['group'=4,'sub'=8] {'group','sub'}, dimensions={0} | all-to-all | bytes 32768 | tf_op jit(solution)/shard_map/all_to_all | solution.py:565
  53.4 1.5 %shard_map.116 = (f32[16,8,256]{2,1,0:T(8,128)S(1)}, f32[16,8,256]{2,1,0:T(8,128)S(1)}, f32[8,128]{1,0:T(8,128)S(1)}, f32[16,8,256]{2,1,0:T(8,128)S(1)}, bf16[16...) custom-call(s32[90]{0:T(128)S(4)} %get-tuple-element.71.table, ...), custom_call_target="tpu_custom_call" | custom-call | flops 600000000 | bytes 37500000 | tf_op jit(solution)/shard_map/pallas_call | solution.py:446
  54.9 1.1 %shard_map.117 = (f32[16,8,256]{2,1,0:T(8,128)S(1)}, f32[16,8,256]{2,1,0:T(8,128)S(1)}) custom-call(s32[90]{0:T(128)S(4)} %get-tuple-element.71.table, f32[16,8,256]{2,1,0:T(8,128)S(1)} %get-tuple-element.73.rest_0_.wide, bf16[16,256,256]{2,1,0:T(8,128)(2,1)S(1)} %get-tuple-element.74.rest_1_.diag, bf16[16,256,256]{2,1,0:T(8,128)(2,1)S(1)} %get-tuple-element.75.rest_2_.off, ...), custom_call_target="tpu_custom_call" | custom-call | flops 600000000 | bytes 37500000 | tf_op jit(solution)/shard_map/pallas_call | solution.py:446
  56.9 1.4 %collective-permute-start.17 = (f32[13,8,128]{2,1,0:T(8,128)S(1)}, f32[13,8,128]{2,1,0:T(8,128)S(1)}, u32[]{:S(2)}, u32[]{:S(2)}) collective-permute-start(f32[13,8,128]{2,1,0:T(8,128)S(1)} %get-tuple-element.119), channel_id=1, source_target_pairs={{0,2},{1,5},{2,0},{3,7},{4,6},{5,1},{6,4},{7,3},{8,10},{9,13},{10,... | collective-permute-start | bytes 159752 | tf_op jit(solution)/shard_map/ppermute | solution.py:485
  58.3 1.5 %collective-permute-start.18 = (f32[13,8,128]{2,1,0:T(8,128)S(1)}, f32[13,8,128]{2,1,0:T(8,128)S(1)}, u32[]{:S(2)}, u32[]{:S(2)}) collective-permute-start(f32[13,8,128]{2,1,0:T(8,128)S(1)} %get-tuple-element.120), channel_id=1, source_target_pairs={{0,4},{1,3},{2,6},{3,1},{4,0},{5,7},{6,2},{7,5},{8,12},{9,11},{10,... | collective-permute-start | bytes 159752 | tf_op jit(solution)/shard_map/ppermute | solution.py:485
  59.8 2.1 %collective-permute-done.16.rest_0_ = f32[13,8,128]{2,1,0:T(8,128)S(1)} collective-permute-done((f32[13,8,128]{2,1,0:T(8,128)S(1)}, f32[13,8,128]{2,1,0:T(8,128)S(1)}, u32[]{:S(2)}, u32[]{:S(2)}) %collective-permute-start.16) | collective-permute-done | bytes 53280 | tf_op jit(solution)/shard_map/ppermute | solution.py:485
  63.2 8.8 %all_to_all.22.rest_4_ = f32[32,1,128]{2,1,0:T(1,128)S(1)} all-to-all(f32[32,1,128]{2,1,0:T(1,128)S(1)} %get-tuple-element.122), channel_id=1, replica_groups=mesh['group'=4,'sub'=8] {'group','sub'}, dimensions={0} | all-to-all | bytes 32768 | tf_op jit(solution)/shard_map/all_to_all | solution.py:565
  72.1 1.5 %shard_map.120 = (f32[16,8,256]{2,1,0:T(8,128)S(1)}, f32[16,8,256]{2,1,0:T(8,128)S(1)}, f32[8,128]{1,0:T(8,128)S(1)}, f32[16,8,256]{2,1,0:T(8,128)S(1)}, bf16[16...) custom-call(s32[90]{0:T(128)S(4)} %get-tuple-element.71.table, ...), custom_call_target="tpu_custom_call" | custom-call | flops 600000000 | bytes 37500000 | tf_op jit(solution)/shard_map/pallas_call | solution.py:446
  73.5 1.1 %shard_map.121 = (f32[16,8,256]{2,1,0:T(8,128)S(1)}, f32[16,8,256]{2,1,0:T(8,128)S(1)}) custom-call(s32[90]{0:T(128)S(4)} %get-tuple-element.71.table, f32[16,8,256]{2,1,0:T(8,128)S(1)} %get-tuple-element.73.rest_0_.wide, bf16[16,256,256]{2,1,0:T(8,128)(2,1)S(1)} %get-tuple-element.74.rest_1_.diag, bf16[16,256,256]{2,1,0:T(8,128)(2,1)S(1)} %get-tuple-element.75.rest_2_.off, ...), custom_call_target="tpu_custom_call" | custom-call | flops 600000000 | bytes 37500000 | tf_op jit(solution)/shard_map/pallas_call | solution.py:446
  75.5 1.4 %collective-permute-start.22 = (f32[13,8,128]{2,1,0:T(8,128)S(1)}, f32[13,8,128]{2,1,0:T(8,128)S(1)}, u32[]{:S(2)}, u32[]{:S(2)}) collective-permute-start(f32[13,8,128]{2,1,0:T(8,128)S(1)} %get-tuple-element.134), channel_id=1, source_target_pairs={{0,2},{1,5},{2,0},{3,7},{4,6},{5,1},{6,4},{7,3},{8,10},{9,13},{10,... | collective-permute-start | bytes 159752 | tf_op jit(solution)/shard_map/ppermute | solution.py:485
  76.9 1.5 %collective-permute-start.23 = (f32[13,8,128]{2,1,0:T(8,128)S(1)}, f32[13,8,128]{2,1,0:T(8,128)S(1)}, u32[]{:S(2)}, u32[]{:S(2)}) collective-permute-start(f32[13,8,128]{2,1,0:T(8,128)S(1)} %get-tuple-element.135), channel_id=1, source_target_pairs={{0,4},{1,3},{2,6},{3,1},{4,0},{5,7},{6,2},{7,5},{8,12},{9,11},{10,... | collective-permute-start | bytes 159752 | tf_op jit(solution)/shard_map/ppermute | solution.py:485
  78.4 2.1 %collective-permute-done.21.rest_0_ = f32[13,8,128]{2,1,0:T(8,128)S(1)} collective-permute-done((f32[13,8,128]{2,1,0:T(8,128)S(1)}, f32[13,8,128]{2,1,0:T(8,128)S(1)}, u32[]{:S(2)}, u32[]{:S(2)}) %collective-permute-start.21) | collective-permute-done | bytes 53280 | tf_op jit(solution)/shard_map/ppermute | solution.py:485
  81.8 8.8 %all_to_all.23.gathered = f32[32,1,128]{2,1,0:T(1,128)S(1)} all-to-all(f32[32,1,128]{2,1,0:T(1,128)S(1)} %get-tuple-element.137), channel_id=1, replica_groups=mesh['group'=4,'sub'=8] {'group','sub'}, dimensions={0} | all-to-all | bytes 32768 | tf_op jit(solution)/shard_map/all_to_all | solution.py:565
  90.7 1.1 %shard_map.124 = (f32[8,16,256]{2,1,0:T(8,128)}, f32[8,16,256]{2,1,0:T(8,128)}) custom-call(f32[32,1,128]{2,1,0:T(1,128)S(1)} %all_to_all.23.gathered, f32[16,8,256]{2,1,0:T(8,128)S(1)} %get-tuple-element.138.before, f32[16,8,256]{2,1,0:T(8,128)S(1)} %get-tuple-element.130.residual.residual_in, f32[16,8,256]{2,1,0:T(8,128)S(1)} %get-tuple-element.131.direction, ...), custom_call_target="tpu_custom_call" | custom-call | flops 4000000 | bytes 250000 | tf_op jit(solution)/shard_map/pallas_call | solution.py:446
  (43 shorter events, 9.9 us)
Async XLA Ops:
  1.7 1.5 %collective-permute-start = (f32[36,8,128]{2,1,0:T(8,128)S(1)}, f32[36,8,128]{2,1,0:T(8,128)S(1)}, u32[]{:S(2)}, u32[]{:S(2)}) collective-permute-start(f32[36,8,128]{2,1,0:T(8,128)S(1)} %get-tuple-element.79), channel_id=1, source_target_pairs={{0,1},{1,0},{2,3},{3,2},{4,5},{5,4},{6,7},{7,6},{8,9},{9,8},{10,11... | collective-permute-start | bytes 442376 | tf_op jit(solution)/shard_map/ppermute | solution.py:485
  3.3 7.1 %collective-permute-start.1 = (f32[24,8,128]{2,1,0:T(8,128)S(1)}, f32[24,8,128]{2,1,0:T(8,128)S(1)}, u32[]{:S(2)}, u32[]{:S(2)}) collective-permute-start(f32[24,8,128]{2,1,0:T(8,128)S(1)} %get-tuple-element.80), channel_id=1, source_target_pairs={{0,6},{1,7},{2,4},{3,5},{4,2},{5,3},{6,0},{7,1},{8,14},{9,15},{10,... | collective-permute-start | bytes 294920 | tf_op jit(solution)/shard_map/ppermute | solution.py:485
  7.1 5.5 %collective-permute-start.2 = (f32[24,8,128]{2,1,0:T(8,128)S(1)}, f32[24,8,128]{2,1,0:T(8,128)S(1)}, u32[]{:S(2)}, u32[]{:S(2)}) collective-permute-start(f32[24,8,128]{2,1,0:T(8,128)S(1)} %get-tuple-element.81), channel_id=1, source_target_pairs={{0,2},{1,5},{2,0},{3,7},{4,6},{5,1},{6,4},{7,3},{8,10},{9,13},{10,... | collective-permute-start | bytes 294920 | tf_op jit(solution)/shard_map/ppermute | solution.py:485
  7.7 4.9 %collective-permute-start.3 = (f32[24,8,128]{2,1,0:T(8,128)S(1)}, f32[24,8,128]{2,1,0:T(8,128)S(1)}, u32[]{:S(2)}, u32[]{:S(2)}) collective-permute-start(f32[24,8,128]{2,1,0:T(8,128)S(1)} %get-tuple-element.82), channel_id=1, source_target_pairs={{0,4},{1,3},{2,6},{3,1},{4,0},{5,7},{6,2},{7,5},{8,12},{9,11},{10,... | collective-permute-start | bytes 294920 | tf_op jit(solution)/shard_map/ppermute | solution.py:485
  7.8 4.8 %collective-permute-start.4 = (f32[24,8,128]{2,1,0:T(8,128)S(1)}, f32[24,8,128]{2,1,0:T(8,128)S(1)}, u32[]{:S(2)}, u32[]{:S(2)}) collective-permute-start(f32[24,8,128]{2,1,0:T(8,128)S(1)} %get-tuple-element.83), channel_id=1, source_target_pairs={{0,1},{1,0},{2,3},{3,2},{4,5},{5,4},{6,7},{7,6},{8,9},{9,8},{10,11... | collective-permute-start | bytes 294920 | tf_op jit(solution)/shard_map/ppermute | solution.py:485
  13.7 1.3 %collective-permute-start.5 = (f32[19,8,128]{2,1,0:T(8,128)S(1)}, f32[19,8,128]{2,1,0:T(8,128)S(1)}, u32[]{:S(2)}, u32[]{:S(2)}) collective-permute-start(f32[19,8,128]{2,1,0:T(8,128)S(1)} %get-tuple-element.88), channel_id=1, source_target_pairs={{0,1},{1,0},{2,3},{3,2},{4,5},{5,4},{6,7},{7,6},{8,9},{9,8},{10,11... | collective-permute-start | bytes 233480 | tf_op jit(solution)/shard_map/ppermute | solution.py:485
  15.0 5.2 %collective-permute-start.6 = (f32[13,8,128]{2,1,0:T(8,128)S(1)}, f32[13,8,128]{2,1,0:T(8,128)S(1)}, u32[]{:S(2)}, u32[]{:S(2)}) collective-permute-start(f32[13,8,128]{2,1,0:T(8,128)S(1)} %get-tuple-element.89), channel_id=1, source_target_pairs={{0,6},{1,7},{2,4},{3,5},{4,2},{5,3},{6,0},{7,1},{8,14},{9,15},{10,... | collective-permute-start | bytes 159752 | tf_op jit(solution)/shard_map/ppermute | solution.py:485
  16.8 4.5 %collective-permute-start.7 = (f32[13,8,128]{2,1,0:T(8,128)S(1)}, f32[13,8,128]{2,1,0:T(8,128)S(1)}, u32[]{:S(2)}, u32[]{:S(2)}) collective-permute-start(f32[13,8,128]{2,1,0:T(8,128)S(1)} %get-tuple-element.90), channel_id=1, source_target_pairs={{0,2},{1,5},{2,0},{3,7},{4,6},{5,1},{6,4},{7,3},{8,10},{9,13},{10,... | collective-permute-start | bytes 159752 | tf_op jit(solution)/shard_map/ppermute | solution.py:485
  18.0 4.1 %collective-permute-start.8 = (f32[13,8,128]{2,1,0:T(8,128)S(1)}, f32[13,8,128]{2,1,0:T(8,128)S(1)}, u32[]{:S(2)}, u32[]{:S(2)}) collective-permute-start(f32[13,8,128]{2,1,0:T(8,128)S(1)} %get-tuple-element.91), channel_id=1, source_target_pairs={{0,4},{1,3},{2,6},{3,1},{4,0},{5,7},{6,2},{7,5},{8,12},{9,11},{10,... | collective-permute-start | bytes 159752 | tf_op jit(solution)/shard_map/ppermute | solution.py:485
  18.6 3.6 %collective-permute-start.9 = (f32[13,8,128]{2,1,0:T(8,128)S(1)}, f32[13,8,128]{2,1,0:T(8,128)S(1)}, u32[]{:S(2)}, u32[]{:S(2)}) collective-permute-start(f32[13,8,128]{2,1,0:T(8,128)S(1)} %get-tuple-element.92), channel_id=1, source_target_pairs={{0,1},{1,0},{2,3},{3,2},{4,5},{5,4},{6,7},{7,6},{8,9},{9,8},{10,11... | collective-permute-start | bytes 159752 | tf_op jit(solution)/shard_map/ppermute | solution.py:485
  36.3 1.3 %collective-permute-start.10 = (f32[19,8,128]{2,1,0:T(8,128)S(1)}, f32[19,8,128]{2,1,0:T(8,128)S(1)}, u32[]{:S(2)}, u32[]{:S(2)}) collective-permute-start(f32[19,8,128]{2,1,0:T(8,128)S(1)} %get-tuple-element.102), channel_id=1, source_target_pairs={{0,1},{1,0},{2,3},{3,2},{4,5},{5,4},{6,7},{7,6},{8,9},{9,8},{10,11... | collective-permute-start | bytes 233480 | tf_op jit(solution)/shard_map/ppermute | solution.py:485
  37.6 5.7 %collective-permute-start.11 = (f32[13,8,128]{2,1,0:T(8,128)S(1)}, f32[13,8,128]{2,1,0:T(8,128)S(1)}, u32[]{:S(2)}, u32[]{:S(2)}) collective-permute-start(f32[13,8,128]{2,1,0:T(8,128)S(1)} %get-tuple-element.103), channel_id=1, source_target_pairs={{0,6},{1,7},{2,4},{3,5},{4,2},{5,3},{6,0},{7,1},{8,14},{9,15},{10,... | collective-permute-start | bytes 159752 | tf_op jit(solution)/shard_map/ppermute | solution.py:485
  38.3 5.0 %collective-permute-start.12 = (f32[13,8,128]{2,1,0:T(8,128)S(1)}, f32[13,8,128]{2,1,0:T(8,128)S(1)}, u32[]{:S(2)}, u32[]{:S(2)}) collective-permute-start(f32[13,8,128]{2,1,0:T(8,128)S(1)} %get-tuple-element.104), channel_id=1, source_target_pairs={{0,2},{1,5},{2,0},{3,7},{4,6},{5,1},{6,4},{7,3},{8,10},{9,13},{10,... | collective-permute-start | bytes 159752 | tf_op jit(solution)/shard_map/ppermute | solution.py:485
  39.7 4.1 %collective-permute-start.13 = (f32[13,8,128]{2,1,0:T(8,128)S(1)}, f32[13,8,128]{2,1,0:T(8,128)S(1)}, u32[]{:S(2)}, u32[]{:S(2)}) collective-permute-start(f32[13,8,128]{2,1,0:T(8,128)S(1)} %get-tuple-element.105), channel_id=1, source_target_pairs={{0,4},{1,3},{2,6},{3,1},{4,0},{5,7},{6,2},{7,5},{8,12},{9,11},{10,... | collective-permute-start | bytes 159752 | tf_op jit(solution)/shard_map/ppermute | solution.py:485
  41.2 2.7 %collective-permute-start.14 = (f32[13,8,128]{2,1,0:T(8,128)S(1)}, f32[13,8,128]{2,1,0:T(8,128)S(1)}, u32[]{:S(2)}, u32[]{:S(2)}) collective-permute-start(f32[13,8,128]{2,1,0:T(8,128)S(1)} %get-tuple-element.106), channel_id=1, source_target_pairs={{0,1},{1,0},{2,3},{3,2},{4,5},{5,4},{6,7},{7,6},{8,9},{9,8},{10,11... | collective-permute-start | bytes 159752 | tf_op jit(solution)/shard_map/ppermute | solution.py:485
  54.9 1.3 %collective-permute-start.15 = (f32[19,8,128]{2,1,0:T(8,128)S(1)}, f32[19,8,128]{2,1,0:T(8,128)S(1)}, u32[]{:S(2)}, u32[]{:S(2)}) collective-permute-start(f32[19,8,128]{2,1,0:T(8,128)S(1)} %get-tuple-element.117), channel_id=1, source_target_pairs={{0,1},{1,0},{2,3},{3,2},{4,5},{5,4},{6,7},{7,6},{8,9},{9,8},{10,11... | collective-permute-start | bytes 233480 | tf_op jit(solution)/shard_map/ppermute | solution.py:485
  56.2 5.7 %collective-permute-start.16 = (f32[13,8,128]{2,1,0:T(8,128)S(1)}, f32[13,8,128]{2,1,0:T(8,128)S(1)}, u32[]{:S(2)}, u32[]{:S(2)}) collective-permute-start(f32[13,8,128]{2,1,0:T(8,128)S(1)} %get-tuple-element.118), channel_id=1, source_target_pairs={{0,6},{1,7},{2,4},{3,5},{4,2},{5,3},{6,0},{7,1},{8,14},{9,15},{10,... | collective-permute-start | bytes 159752 | tf_op jit(solution)/shard_map/ppermute | solution.py:485
  56.9 5.0 %collective-permute-start.17 = (f32[13,8,128]{2,1,0:T(8,128)S(1)}, f32[13,8,128]{2,1,0:T(8,128)S(1)}, u32[]{:S(2)}, u32[]{:S(2)}) collective-permute-start(f32[13,8,128]{2,1,0:T(8,128)S(1)} %get-tuple-element.119), channel_id=1, source_target_pairs={{0,2},{1,5},{2,0},{3,7},{4,6},{5,1},{6,4},{7,3},{8,10},{9,13},{10,... | collective-permute-start | bytes 159752 | tf_op jit(solution)/shard_map/ppermute | solution.py:485
  58.3 4.1 %collective-permute-start.18 = (f32[13,8,128]{2,1,0:T(8,128)S(1)}, f32[13,8,128]{2,1,0:T(8,128)S(1)}, u32[]{:S(2)}, u32[]{:S(2)}) collective-permute-start(f32[13,8,128]{2,1,0:T(8,128)S(1)} %get-tuple-element.120), channel_id=1, source_target_pairs={{0,4},{1,3},{2,6},{3,1},{4,0},{5,7},{6,2},{7,5},{8,12},{9,11},{10,... | collective-permute-start | bytes 159752 | tf_op jit(solution)/shard_map/ppermute | solution.py:485
  59.8 2.7 %collective-permute-start.19 = (f32[13,8,128]{2,1,0:T(8,128)S(1)}, f32[13,8,128]{2,1,0:T(8,128)S(1)}, u32[]{:S(2)}, u32[]{:S(2)}) collective-permute-start(f32[13,8,128]{2,1,0:T(8,128)S(1)} %get-tuple-element.121), channel_id=1, source_target_pairs={{0,1},{1,0},{2,3},{3,2},{4,5},{5,4},{6,7},{7,6},{8,9},{9,8},{10,11... | collective-permute-start | bytes 159752 | tf_op jit(solution)/shard_map/ppermute | solution.py:485
  73.5 1.3 %collective-permute-start.20 = (f32[19,8,128]{2,1,0:T(8,128)S(1)}, f32[19,8,128]{2,1,0:T(8,128)S(1)}, u32[]{:S(2)}, u32[]{:S(2)}) collective-permute-start(f32[19,8,128]{2,1,0:T(8,128)S(1)} %get-tuple-element.132), channel_id=1, source_target_pairs={{0,1},{1,0},{2,3},{3,2},{4,5},{5,4},{6,7},{7,6},{8,9},{9,8},{10,11... | collective-permute-start | bytes 233480 | tf_op jit(solution)/shard_map/ppermute | solution.py:485
  74.8 5.7 %collective-permute-start.21 = (f32[13,8,128]{2,1,0:T(8,128)S(1)}, f32[13,8,128]{2,1,0:T(8,128)S(1)}, u32[]{:S(2)}, u32[]{:S(2)}) collective-permute-start(f32[13,8,128]{2,1,0:T(8,128)S(1)} %get-tuple-element.133), channel_id=1, source_target_pairs={{0,6},{1,7},{2,4},{3,5},{4,2},{5,3},{6,0},{7,1},{8,14},{9,15},{10,... | collective-permute-start | bytes 159752 | tf_op jit(solution)/shard_map/ppermute | solution.py:485
  75.5 5.0 %collective-permute-start.22 = (f32[13,8,128]{2,1,0:T(8,128)S(1)}, f32[13,8,128]{2,1,0:T(8,128)S(1)}, u32[]{:S(2)}, u32[]{:S(2)}) collective-permute-start(f32[13,8,128]{2,1,0:T(8,128)S(1)} %get-tuple-element.134), channel_id=1, source_target_pairs={{0,2},{1,5},{2,0},{3,7},{4,6},{5,1},{6,4},{7,3},{8,10},{9,13},{10,... | collective-permute-start | bytes 159752 | tf_op jit(solution)/shard_map/ppermute | solution.py:485
  76.9 4.1 %collective-permute-start.23 = (f32[13,8,128]{2,1,0:T(8,128)S(1)}, f32[13,8,128]{2,1,0:T(8,128)S(1)}, u32[]{:S(2)}, u32[]{:S(2)}) collective-permute-start(f32[13,8,128]{2,1,0:T(8,128)S(1)} %get-tuple-element.135), channel_id=1, source_target_pairs={{0,4},{1,3},{2,6},{3,1},{4,0},{5,7},{6,2},{7,5},{8,12},{9,11},{10,... | collective-permute-start | bytes 159752 | tf_op jit(solution)/shard_map/ppermute | solution.py:485
  78.4 2.7 %collective-permute-start.24 = (f32[13,8,128]{2,1,0:T(8,128)S(1)}, f32[13,8,128]{2,1,0:T(8,128)S(1)}, u32[]{:S(2)}, u32[]{:S(2)}) collective-permute-start(f32[13,8,128]{2,1,0:T(8,128)S(1)} %get-tuple-element.136), channel_id=1, source_target_pairs={{0,1},{1,0},{2,3},{3,2},{4,5},{5,4},{6,7},{7,6},{8,9},{9,8},{10,11... | collective-permute-start | bytes 159752 | tf_op jit(solution)/shard_map/ppermute | solution.py:485

commit v10 on v9

--- a/solution.py
+++ b/solution.py
@@ -418,9 +418,7 @@
         value = product[i] * shrink
         squares = squares + value * value
     values = [(k * z.columns, lane_sum(v)) for k, v in enumerate(sums + [squares])]
-    row = to_row(z, values + [(PP * z.columns + LANES // 2, top)])
-    for k in range(sent.shape[0]):
-        sent[k] = row
+    sent[...] = to_row(z, values + [(PP * z.columns + LANES // 2, top)])
 
 
 def finish(z, gathered, before, residual_in, direction, product, multipliers, residual):
@@ -525,7 +523,6 @@
     )
     half = ((blocks, 2 * cols, width), BF16)
     tile = ((cols, LANES), F32)
-    devices = z.groups * z.peers
     fixed = [wide, diag, off, corners]
     multipliers = None
     for step in range(ITERS):
@@ -559,10 +556,10 @@
             )
         arrived = exchange(1, [image, own_extra], near)
         product, sent = call(
-            kernel(finish_product), [field, ((devices, 1, LANES), F32)], [other], heavy,
+            kernel(finish_product), [field, ((1, LANES), F32)], [other], heavy,
             [table, operator, image, own_extra, jump_lift, residual, direction, near, *arrived],
         )
-        gathered = lax.all_to_all(sent, ("group", "sub"), 0, 0, tiled=True)
+        gathered = lax.all_gather(sent, ("group", "sub"))
     multipliers, residual = call(
         kernel(finish), [(load.shape, F32)] * 2, [], light,
         [gathered, multipliers, residual, direction, product], False,

time: 92 us -> 205 us (2.23)
  blocking collectives: 38.4 us -> 151 us
    all_gather x0 -> x4, blocking collectives: none -> 151 us  [on_device(): gathered = lax.all_gather(sent, ('group', 'sub'))]
    all_to_all x4 -> x0, blocking collectives: 38.4 us -> none  [on_device(): gathered = lax.all_to_all(sent, ('group', 'sub'), 0, 0, tiled=True)]
  transfers between devices with their start and end apart: 25 -> 25, of which waited for: 16 -> 13; matrix products, arithmetic and copies ran while one was open for 0% -> 0% of each run, Pallas kernels for 7% -> 3%
where the time goes in v10:
time: 205 us; the launch traced here: 204 us
  blocking collectives  151 us (74%)
  starting transfers between devices  20.2 us (10%)
  Pallas kernels  17.6 us (9%)
  waiting for transfers between devices  14.3 us (7%)
    all_gather x4, blocking collectives, on_device(): gathered = lax.all_gather(sent, ('group', 'sub'))  151 us
    ppermute x25, starting transfers between devices, across(): return lax.ppermute(piece, 'sub', pairs)  20.2 us
    pallas_call x21, Pallas kernels, call(): pl.pallas_call(body, out_shape=shapes, in_specs=specs, out_specs=[SMEM if...  17.6 us
    ppermute x25, waiting for transfers between devices, across(): return lax.ppermute(piece, 'sub', pairs)  14.3 us
  transfers between devices with their start and end apart: 25, of which 13 were waited for; matrix products, arithmetic and copies ran while one was open for 0% of the time, Pallas kernels for 3%

profile of v10, /device:TPU:0, one launch (start us, length us, event | category | flops | bytes accessed | tf_op | source)
XLA Modules:
  0.0 204.3 jit_solution(17360794972058772843)
XLA Ops:
  0.6 1.0 shard_map.104
  2.2 1.0 collective-permute-done.rest_2_
  3.3 3.9 %collective-permute-start.1 = (f32[24,8,128]{2,1,0:T(8,128)S(1)}, f32[24,8,128]{2,1,0:T(8,128)S(1)}, u32[]{:S(2)}, u32[]{:S(2)}) collective-permute-start(f32[24,8,128]{2,1,0:T(8,128)S(1)} %get-tuple-element.80), channel_id=1, source_target_pairs={{0,6},{1,7},{2,4},{3,5},{4,2},{5,3},{6,0},{7,1},{8,14},{9,15},{10,... | collective-permute-start | bytes 294920 | tf_op jit(solution)/shard_map/ppermute | solution.py:483
  7.8 2.3 %shard_map.105 = (f32[64,64]{1,0:T(8,128)S(1)}, bf16[16,256,256]{2,1,0:T(8,128)(2,1)S(1)}, bf16[16,256,256]{2,1,0:T(8,128)(2,1)S(1)}) custom-call(s32[1,64]{1,0:T(1,128)} %index_in.1, f32[32,32]{1,0:T(8,128)} %inverse_in.1, bf16[16,256,256]{2,1,0:T(8,128)(2,1)} %diag.1, bf16[16,256,256]{2,1,0:T(8,128)(2,1)} %off.1), custom_call_target="tpu_custom_call" | custom-call | flops 600000000 | bytes 37500000 | tf_op jit(solution)/shard_map/pallas_call | solution.py:444
  10.3 2.3 %collective-permute-done.2.rest_5_.rest_1_ = f32[24,8,128]{2,1,0:T(8,128)S(1)} collective-permute-done((f32[24,8,128]{2,1,0:T(8,128)S(1)}, f32[24,8,128]{2,1,0:T(8,128)S(1)}, u32[]{:S(2)}, u32[]{:S(2)}) %collective-permute-start.2) | collective-permute-done | bytes 98336 | tf_op jit(solution)/shard_map/ppermute | solution.py:483
  12.6 1.1 shard_map.107
  13.7 1.1 shard_map.108.rest_0_.image
  15.0 1.7 collective-permute-start.6
  16.8 1.3 collective-permute-start.7
  18.8 1.4 collective-permute-done.6.rest_0_
  20.2 1.1 collective-permute-done.7.rest_1_
  21.3 0.9 collective-permute-done.8.rest_2_
  22.9 40.7 %all-gather.4.rest_4_ = f32[32,1,128]{2,1,0:T(1,128)S(1)} all-gather(f32[1,1,128]{2,1,0:T(1,128)S(1)} %bitcast.5), channel_id=2, replica_groups=mesh['group'=4,'sub'=8] {'group','sub'}, dimensions={0}, use_global_device_ids=true | all-gather | bytes 16896 | tf_op jit(solution)/shard_map/all_gather | solution.py:562
  63.6 1.5 shard_map.112
  65.3 1.1 shard_map.113
  66.6 3.4 %collective-permute-start.13 = (f32[13,8,128]{2,1,0:T(8,128)S(1)}, f32[13,8,128]{2,1,0:T(8,128)S(1)}, u32[]{:S(2)}, u32[]{:S(2)}) collective-permute-start(f32[13,8,128]{2,1,0:T(8,128)S(1)} %get-tuple-element.105), channel_id=1, source_target_pairs={{0,4},{1,3},{2,6},{3,1},{4,0},{5,7},{6,2},{7,5},{8,12},{9,11},{10,... | collective-permute-start | bytes 159752 | tf_op jit(solution)/shard_map/ppermute | solution.py:483
  70.0 2.0 collective-permute-done.11.rest_0_
  73.2 36.5 %all-gather.5.rest_4_ = f32[32,1,128]{2,1,0:T(1,128)S(1)} all-gather(f32[1,1,128]{2,1,0:T(1,128)S(1)} %bitcast.6), channel_id=3, replica_groups=mesh['group'=4,'sub'=8] {'group','sub'}, dimensions={0}, use_global_device_ids=true | all-gather | bytes 16896 | tf_op jit(solution)/shard_map/all_gather | solution.py:562
  109.6 1.5 shard_map.116
  111.4 1.1 shard_map.117
  112.6 1.7 collective-permute-start.17
  114.3 1.8 collective-permute-start.18
  116.1 1.6 collective-permute-done.16.rest_0_
  117.7 0.9 collective-permute-done.18.rest_2_
  118.6 0.8 shard_map.119
  119.3 37.6 %all-gather.6.rest_4_ = f32[32,1,128]{2,1,0:T(1,128)S(1)} all-gather(f32[1,1,128]{2,1,0:T(1,128)S(1)} %bitcast.7), channel_id=4, replica_groups=mesh['group'=4,'sub'=8] {'group','sub'}, dimensions={0}, use_global_device_ids=true | all-gather | bytes 16896 | tf_op jit(solution)/shard_map/all_gather | solution.py:562
  157.0 1.5 shard_map.120
  158.7 1.1 shard_map.121
  160.5 2.9 %collective-permute-start.23 = (f32[13,8,128]{2,1,0:T(8,128)S(1)}, f32[13,8,128]{2,1,0:T(8,128)S(1)}, u32[]{:S(2)}, u32[]{:S(2)}) collective-permute-start(f32[13,8,128]{2,1,0:T(8,128)S(1)} %get-tuple-element.135), channel_id=1, source_target_pairs={{0,4},{1,3},{2,6},{3,1},{4,0},{5,7},{6,2},{7,5},{8,12},{9,11},{10,... | collective-permute-start | bytes 159752 | tf_op jit(solution)/shard_map/ppermute | solution.py:483
  163.4 2.0 collective-permute-done.21.rest_0_
  166.6 36.7 %all-gather.7.gathered = f32[32,1,128]{2,1,0:T(1,128)S(1)} all-gather(f32[1,1,128]{2,1,0:T(1,128)S(1)} %bitcast.4), channel_id=5, replica_groups=mesh['group'=4,'sub'=8] {'group','sub'}, dimensions={0}, use_global_device_ids=true | all-gather | bytes 16896 | tf_op jit(solution)/shard_map/all_gather | solution.py:562
  203.2 1.1 shard_map.124
  (43 shorter events, 7.3 us)
Async XLA Ops:
  1.7 1.5 collective-permute-start
  3.3 7.1 %collective-permute-start.1 = (f32[24,8,128]{2,1,0:T(8,128)S(1)}, f32[24,8,128]{2,1,0:T(8,128)S(1)}, u32[]{:S(2)}, u32[]{:S(2)}) collective-permute-start(f32[24,8,128]{2,1,0:T(8,128)S(1)} %get-tuple-element.80), channel_id=1, source_target_pairs={{0,6},{1,7},{2,4},{3,5},{4,2},{5,3},{6,0},{7,1},{8,14},{9,15},{10,... | collective-permute-start | bytes 294920 | tf_op jit(solution)/shard_map/ppermute | solution.py:483
  7.1 5.5 %collective-permute-start.2 = (f32[24,8,128]{2,1,0:T(8,128)S(1)}, f32[24,8,128]{2,1,0:T(8,128)S(1)}, u32[]{:S(2)}, u32[]{:S(2)}) collective-permute-start(f32[24,8,128]{2,1,0:T(8,128)S(1)} %get-tuple-element.81), channel_id=1, source_target_pairs={{0,2},{1,5},{2,0},{3,7},{4,6},{5,1},{6,4},{7,3},{8,10},{9,13},{10,... | collective-permute-start | bytes 294920 | tf_op jit(solution)/shard_map/ppermute | solution.py:483
  7.7 4.9 %collective-permute-start.3 = (f32[24,8,128]{2,1,0:T(8,128)S(1)}, f32[24,8,128]{2,1,0:T(8,128)S(1)}, u32[]{:S(2)}, u32[]{:S(2)}) collective-permute-start(f32[24,8,128]{2,1,0:T(8,128)S(1)} %get-tuple-element.82), channel_id=1, source_target_pairs={{0,4},{1,3},{2,6},{3,1},{4,0},{5,7},{6,2},{7,5},{8,12},{9,11},{10,... | collective-permute-start | bytes 294920 | tf_op jit(solution)/shard_map/ppermute | solution.py:483
  7.8 4.8 %collective-permute-start.4 = (f32[24,8,128]{2,1,0:T(8,128)S(1)}, f32[24,8,128]{2,1,0:T(8,128)S(1)}, u32[]{:S(2)}, u32[]{:S(2)}) collective-permute-start(f32[24,8,128]{2,1,0:T(8,128)S(1)} %get-tuple-element.83), channel_id=1, source_target_pairs={{0,1},{1,0},{2,3},{3,2},{4,5},{5,4},{6,7},{7,6},{8,9},{9,8},{10,11... | collective-permute-start | bytes 294920 | tf_op jit(solution)/shard_map/ppermute | solution.py:483
  13.7 1.3 collective-permute-start.5
  15.0 5.2 %collective-permute-start.6 = (f32[13,8,128]{2,1,0:T(8,128)S(1)}, f32[13,8,128]{2,1,0:T(8,128)S(1)}, u32[]{:S(2)}, u32[]{:S(2)}) collective-permute-start(f32[13,8,128]{2,1,0:T(8,128)S(1)} %get-tuple-element.89), channel_id=1, source_target_pairs={{0,6},{1,7},{2,4},{3,5},{4,2},{5,3},{6,0},{7,1},{8,14},{9,15},{10,... | collective-permute-start | bytes 159752 | tf_op jit(solution)/shard_map/ppermute | solution.py:483
  16.8 4.5 %collective-permute-start.7 = (f32[13,8,128]{2,1,0:T(8,128)S(1)}, f32[13,8,128]{2,1,0:T(8,128)S(1)}, u32[]{:S(2)}, u32[]{:S(2)}) collective-permute-start(f32[13,8,128]{2,1,0:T(8,128)S(1)} %get-tuple-element.90), channel_id=1, source_target_pairs={{0,2},{1,5},{2,0},{3,7},{4,6},{5,1},{6,4},{7,3},{8,10},{9,13},{10,... | collective-permute-start | bytes 159752 | tf_op jit(solution)/shard_map/ppermute | solution.py:483
  18.0 4.1 %collective-permute-start.8 = (f32[13,8,128]{2,1,0:T(8,128)S(1)}, f32[13,8,128]{2,1,0:T(8,128)S(1)}, u32[]{:S(2)}, u32[]{:S(2)}) collective-permute-start(f32[13,8,128]{2,1,0:T(8,128)S(1)} %get-tuple-element.91), channel_id=1, source_target_pairs={{0,4},{1,3},{2,6},{3,1},{4,0},{5,7},{6,2},{7,5},{8,12},{9,11},{10,... | collective-permute-start | bytes 159752 | tf_op jit(solution)/shard_map/ppermute | solution.py:483
  18.6 3.6 %collective-permute-start.9 = (f32[13,8,128]{2,1,0:T(8,128)S(1)}, f32[13,8,128]{2,1,0:T(8,128)S(1)}, u32[]{:S(2)}, u32[]{:S(2)}) collective-permute-start(f32[13,8,128]{2,1,0:T(8,128)S(1)} %get-tuple-element.92), channel_id=1, source_target_pairs={{0,1},{1,0},{2,3},{3,2},{4,5},{5,4},{6,7},{7,6},{8,9},{9,8},{10,11... | collective-permute-start | bytes 159752 | tf_op jit(solution)/shard_map/ppermute | solution.py:483
  65.0 1.4 collective-permute-start.10
  66.5 5.6 %collective-permute-start.11 = (f32[13,8,128]{2,1,0:T(8,128)S(1)}, f32[13,8,128]{2,1,0:T(8,128)S(1)}, u32[]{:S(2)}, u32[]{:S(2)}) collective-permute-start(f32[13,8,128]{2,1,0:T(8,128)S(1)} %get-tuple-element.103), channel_id=1, source_target_pairs={{0,6},{1,7},{2,4},{3,5},{4,2},{5,3},{6,0},{7,1},{8,14},{9,15},{10,... | collective-permute-start | bytes 159752 | tf_op jit(solution)/shard_map/ppermute | solution.py:483
  66.6 5.5 %collective-permute-start.12 = (f32[13,8,128]{2,1,0:T(8,128)S(1)}, f32[13,8,128]{2,1,0:T(8,128)S(1)}, u32[]{:S(2)}, u32[]{:S(2)}) collective-permute-start(f32[13,8,128]{2,1,0:T(8,128)S(1)} %get-tuple-element.104), channel_id=1, source_target_pairs={{0,2},{1,5},{2,0},{3,7},{4,6},{5,1},{6,4},{7,3},{8,10},{9,13},{10,... | collective-permute-start | bytes 159752 | tf_op jit(solution)/shard_map/ppermute | solution.py:483
  66.6 5.8 %collective-permute-start.13 = (f32[13,8,128]{2,1,0:T(8,128)S(1)}, f32[13,8,128]{2,1,0:T(8,128)S(1)}, u32[]{:S(2)}, u32[]{:S(2)}) collective-permute-start(f32[13,8,128]{2,1,0:T(8,128)S(1)} %get-tuple-element.105), channel_id=1, source_target_pairs={{0,4},{1,3},{2,6},{3,1},{4,0},{5,7},{6,2},{7,5},{8,12},{9,11},{10,... | collective-permute-start | bytes 159752 | tf_op jit(solution)/shard_map/ppermute | solution.py:483
  70.0 2.4 %collective-permute-start.14 = (f32[13,8,128]{2,1,0:T(8,128)S(1)}, f32[13,8,128]{2,1,0:T(8,128)S(1)}, u32[]{:S(2)}, u32[]{:S(2)}) collective-permute-start(f32[13,8,128]{2,1,0:T(8,128)S(1)} %get-tuple-element.106), channel_id=1, source_target_pairs={{0,1},{1,0},{2,3},{3,2},{4,5},{5,4},{6,7},{7,6},{8,9},{9,8},{10,11... | collective-permute-start | bytes 159752 | tf_op jit(solution)/shard_map/ppermute | solution.py:483
  111.1 1.4 collective-permute-start.15
  112.5 5.2 %collective-permute-start.16 = (f32[13,8,128]{2,1,0:T(8,128)S(1)}, f32[13,8,128]{2,1,0:T(8,128)S(1)}, u32[]{:S(2)}, u32[]{:S(2)}) collective-permute-start(f32[13,8,128]{2,1,0:T(8,128)S(1)} %get-tuple-element.118), channel_id=1, source_target_pairs={{0,6},{1,7},{2,4},{3,5},{4,2},{5,3},{6,0},{7,1},{8,14},{9,15},{10,... | collective-permute-start | bytes 159752 | tf_op jit(solution)/shard_map/ppermute | solution.py:483
  112.6 5.1 %collective-permute-start.17 = (f32[13,8,128]{2,1,0:T(8,128)S(1)}, f32[13,8,128]{2,1,0:T(8,128)S(1)}, u32[]{:S(2)}, u32[]{:S(2)}) collective-permute-start(f32[13,8,128]{2,1,0:T(8,128)S(1)} %get-tuple-element.119), channel_id=1, source_target_pairs={{0,2},{1,5},{2,0},{3,7},{4,6},{5,1},{6,4},{7,3},{8,10},{9,13},{10,... | collective-permute-start | bytes 159752 | tf_op jit(solution)/shard_map/ppermute | solution.py:483
  114.3 4.2 %collective-permute-start.18 = (f32[13,8,128]{2,1,0:T(8,128)S(1)}, f32[13,8,128]{2,1,0:T(8,128)S(1)}, u32[]{:S(2)}, u32[]{:S(2)}) collective-permute-start(f32[13,8,128]{2,1,0:T(8,128)S(1)} %get-tuple-element.120), channel_id=1, source_target_pairs={{0,4},{1,3},{2,6},{3,1},{4,0},{5,7},{6,2},{7,5},{8,12},{9,11},{10,... | collective-permute-start | bytes 159752 | tf_op jit(solution)/shard_map/ppermute | solution.py:483
  116.1 2.5 %collective-permute-start.19 = (f32[13,8,128]{2,1,0:T(8,128)S(1)}, f32[13,8,128]{2,1,0:T(8,128)S(1)}, u32[]{:S(2)}, u32[]{:S(2)}) collective-permute-start(f32[13,8,128]{2,1,0:T(8,128)S(1)} %get-tuple-element.121), channel_id=1, source_target_pairs={{0,1},{1,0},{2,3},{3,2},{4,5},{5,4},{6,7},{7,6},{8,9},{9,8},{10,11... | collective-permute-start | bytes 159752 | tf_op jit(solution)/shard_map/ppermute | solution.py:483
  158.4 1.4 collective-permute-start.20
  159.9 5.6 %collective-permute-start.21 = (f32[13,8,128]{2,1,0:T(8,128)S(1)}, f32[13,8,128]{2,1,0:T(8,128)S(1)}, u32[]{:S(2)}, u32[]{:S(2)}) collective-permute-start(f32[13,8,128]{2,1,0:T(8,128)S(1)} %get-tuple-element.133), channel_id=1, source_target_pairs={{0,6},{1,7},{2,4},{3,5},{4,2},{5,3},{6,0},{7,1},{8,14},{9,15},{10,... | collective-permute-start | bytes 159752 | tf_op jit(solution)/shard_map/ppermute | solution.py:483
  159.9 5.5 %collective-permute-start.22 = (f32[13,8,128]{2,1,0:T(8,128)S(1)}, f32[13,8,128]{2,1,0:T(8,128)S(1)}, u32[]{:S(2)}, u32[]{:S(2)}) collective-permute-start(f32[13,8,128]{2,1,0:T(8,128)S(1)} %get-tuple-element.134), channel_id=1, source_target_pairs={{0,2},{1,5},{2,0},{3,7},{4,6},{5,1},{6,4},{7,3},{8,10},{9,13},{10,... | collective-permute-start | bytes 159752 | tf_op jit(solution)/shard_map/ppermute | solution.py:483
  160.5 5.3 %collective-permute-start.23 = (f32[13,8,128]{2,1,0:T(8,128)S(1)}, f32[13,8,128]{2,1,0:T(8,128)S(1)}, u32[]{:S(2)}, u32[]{:S(2)}) collective-permute-start(f32[13,8,128]{2,1,0:T(8,128)S(1)} %get-tuple-element.135), channel_id=1, source_target_pairs={{0,4},{1,3},{2,6},{3,1},{4,0},{5,7},{6,2},{7,5},{8,12},{9,11},{10,... | collective-permute-start | bytes 159752 | tf_op jit(solution)/shard_map/ppermute | solution.py:483
  163.4 2.4 %collective-permute-start.24 = (f32[13,8,128]{2,1,0:T(8,128)S(1)}, f32[13,8,128]{2,1,0:T(8,128)S(1)}, u32[]{:S(2)}, u32[]{:S(2)}) collective-permute-start(f32[13,8,128]{2,1,0:T(8,128)S(1)} %get-tuple-element.136), channel_id=1, source_target_pairs={{0,1},{1,0},{2,3},{3,2},{4,5},{5,4},{6,7},{7,6},{8,9},{9,8},{10,11... | collective-permute-start | bytes 159752 | tf_op jit(solution)/shard_map/ppermute | solution.py:483

commit v11 on v9

--- a/solution.py
+++ b/solution.py
@@ -277,34 +277,38 @@
     return jnp.sum(tile, axis=0, keepdims=True)
 
 
-def to_tile(z, row):
+def to_tile(z, row, first):
     shape = (z.columns, LANES)
     rows = lax.broadcasted_iota(jnp.int32, shape, 0)
-    tile = jnp.where(lane_ids(shape) == rows, jnp.broadcast_to(row, shape), 0.0)
+    tile = jnp.where(lane_ids(shape) == first + rows, jnp.broadcast_to(row, shape), 0.0)
     return jnp.broadcast_to(lane_sum(tile), shape)
 
 
-def scalars(z, gathered):
+def scalars(z, gathered, previous):
     zero = jnp.zeros((1, LANES), F32)
     count = gathered.shape[0]
     unroll = 32 if count % 32 == 0 else 1
     total = lax.fori_loop(0, count, lambda k, acc: acc + gathered[k], zero, unroll=unroll)
-
-    def group(row, at):
-        return pltpu.roll(row, LANES - at * z.columns, 1) if at else row
-
-    norm = group(total, RR)
-    alpha = norm / group(total, DP)
-    placed = pltpu.roll(alpha, PP * z.columns, 1)
-
-    def squares(k, acc):
-        row = gathered[k]
-        step = placed * pltpu.roll(row, LANES // 2, 1)
-        return acc + row * step * step
-
-    moved = lax.fori_loop(0, count, squares, zero, unroll=unroll)
-    following = norm - 2.0 * alpha * group(total, RP) + group(moved, PP)
-    return to_tile(z, alpha), to_tile(z, following / norm)
+    norm, way, rest = [to_tile(z, total, k * z.columns) for k in (RR, DP, RP)]
+    alpha = norm / way
+    if previous is None:
+        placed = to_row(z, [(PP * z.columns, alpha)])
+
+        def squares(k, acc):
+            row = gathered[k]
+            step = placed * pltpu.roll(row, LANES // 2, 1)
+            return acc + row * step * step
+
+        moved = lax.fori_loop(0, count, squares, zero, unroll=unroll)
+        moved = to_tile(z, moved, PP * z.columns)
+    else:
+        ratio = alpha / used_step(previous)
+        moved = to_tile(z, total, PP * z.columns) * ratio * ratio
+    return alpha, (norm - 2.0 * alpha * rest + moved) / norm
+
+
+def used_step(previous):
+    return jnp.where(previous == 0.0, 1.0, previous)
 
 
 def across_block(z, tile):
@@ -331,8 +335,9 @@
         place(z, table, [beside, *far], 0, 2, other)
     else:
         gathered, before, way, product = take(4)
+        previous = take(1)[0][...] if step > 1 else None
         residual, direction, step_out, image, parts, extra, near_out = rest
-        alpha, beta = scalars(z, gathered)
+        alpha, beta = scalars(z, gathered, previous)
         step_out[...] = alpha
         alpha, beta = across_block(z, alpha), across_block(z, beta)
     partial = jnp.zeros((2 * z.columns, 2 * z.corners), F32)
@@ -396,35 +401,46 @@
             multipliers[i] = value if step == 1 else before[i] + value
 
 
-def finish_product(z, table, operator, image, own_extra, jump_lift, residual, direction, near, *rest):
+def finish_product(z, step, table, operator, image, own_extra, jump_lift, residual, direction, near, *rest):
     *far, beside, product, sent, other = rest
+    if step > 0:
+        previous, far = far[0], far[1:]
+        scale = across_block(z, used_step(previous[...]))
     place(z, table, [beside, *far], 0, 1, other)
     partials = extra_sum(z, own_extra, near, *far)[:, : z.all_corners]
     local = dot_high(partials, operator[...], NT)
     rows = pad(jnp.concatenate([local, local], axis=1))
     zero = jnp.zeros((z.columns, z.width), F32)
-    sums = [zero] * 3
+    sums = [zero] * (4 if step > 0 else 3)
     top = zero
     for i in range(z.blocks):
         value = image[i] - other[i] + fold(dot(rows, jump_lift[i], NN))
         product[i] = value
-        top = jnp.maximum(top, jnp.abs(value))
         r, d = residual[i], direction[i]
-        sums = [s + a * b for s, (a, b) in zip(sums, [(r, r), (d, value), (r, value)])]
-    top = jnp.max(top, axis=1, keepdims=True)
-    shrink = jnp.where(top > 0.0, 1.0 / top, 0.0)
-    squares = zero
-    for i in range(z.blocks):
-        value = product[i] * shrink
-        squares = squares + value * value
-    values = [(k * z.columns, lane_sum(v)) for k, v in enumerate(sums + [squares])]
-    row = to_row(z, values + [(PP * z.columns + LANES // 2, top)])
+        pairs = [(r, r), (d, value), (r, value)]
+        if step > 0:
+            scaled = scale * value
+            pairs.append((scaled, scaled))
+        else:
+            top = jnp.maximum(top, jnp.abs(value))
+        sums = [s + a * b for s, (a, b) in zip(sums, pairs)]
+    more = []
+    if step == 0:
+        top = jnp.max(top, axis=1, keepdims=True)
+        shrink = jnp.where(top > 0.0, 1.0 / top, 0.0)
+        squares = zero
+        for i in range(z.blocks):
+            value = product[i] * shrink
+            squares = squares + value * value
+        sums.append(squares)
+        more.append((PP * z.columns + LANES // 2, top))
+    row = to_row(z, [(k * z.columns, lane_sum(v)) for k, v in enumerate(sums)] + more)
     for k in range(sent.shape[0]):
         sent[k] = row
 
 
-def finish(z, gathered, before, residual_in, direction, product, multipliers, residual):
-    alpha, _ = scalars(z, gathered)
+def finish(z, gathered, before, residual_in, direction, product, previous, multipliers, residual):
+    alpha, _ = scalars(z, gathered, previous[...])
     for i in range(z.blocks):
         for h in range(z.halves):
             part = slice(h * LANES, (h + 1) * LANES)
@@ -527,7 +543,7 @@
     tile = ((cols, LANES), F32)
     devices = z.groups * z.peers
     fixed = [wide, diag, off, corners]
-    multipliers = None
+    multipliers = alpha = None
     for step in range(ITERS):
         early = [field, half, extra, shape(z.near_rows(1), 1)]
         if step == 0:
@@ -541,7 +557,7 @@
             way = direction
             residual, direction, alpha, part, parts, own_extra, near = call(
                 kernel(first_half, step), [field, field, tile] + early, [], heavy,
-                [table, *fixed, gathered, residual, way, product],
+                [table, *fixed, gathered, residual, way, product] + [alpha] * (step > 1),
             )
             older = [alpha, way] + [multipliers] * (step > 1)
         near = to_near(near)
@@ -559,13 +575,14 @@
             )
         arrived = exchange(1, [image, own_extra], near)
         product, sent = call(
-            kernel(finish_product), [field, ((devices, 1, LANES), F32)], [other], heavy,
-            [table, operator, image, own_extra, jump_lift, residual, direction, near, *arrived],
+            kernel(finish_product, step), [field, ((devices, 1, LANES), F32)], [other], heavy,
+            [table, operator, image, own_extra, jump_lift, residual, direction, near]
+            + [alpha] * (step > 0) + arrived,
         )
         gathered = lax.all_to_all(sent, ("group", "sub"), 0, 0, tiled=True)
     multipliers, residual = call(
         kernel(finish), [(load.shape, F32)] * 2, [], light,
-        [gathered, multipliers, residual, direction, product], False,
+        [gathered, multipliers, residual, direction, product, alpha], False,
     )
     return multipliers, residual
 

time: 92 us -> 91.1 us (level)
  Pallas kernels: 17.7 us -> 16.7 us
where the time goes in v11:
time: 91.1 us; the launch traced here: 90.9 us
  blocking collectives  38.4 us (42%)
  starting transfers between devices  19.3 us (21%)
  Pallas kernels  16.7 us (18%)
  waiting for transfers between devices  15.6 us (17%)
    all_to_all x4, blocking collectives, on_device(): gathered = lax.all_to_all(sent, ('group', 'sub'), 0, 0, tiled=True)  38.4 us
    ppermute x25, starting transfers between devices, across(): return lax.ppermute(piece, 'sub', pairs)  19.3 us
    pallas_call x21, Pallas kernels, call(): pl.pallas_call(body, out_shape=shapes, in_specs=specs, out_specs=[SMEM if...  16.7 us
    ppermute x25, waiting for transfers between devices, across(): return lax.ppermute(piece, 'sub', pairs)  15.6 us
  transfers between devices with their start and end apart: 25, of which 16 were waited for; matrix products, arithmetic and copies ran while one was open for 0% of the time, Pallas kernels for 7%

profile of v11, /device:TPU:0, one launch (start us, length us, event | category | flops | bytes accessed | tf_op | source)
XLA Modules:
  0.0 90.9 jit_solution(16991663800702270623)
XLA Ops:
  0.6 1.0 %shard_map.104 = (s32[90]{0:T(128)S(4)}, f32[16,8,256]{2,1,0:T(8,128)S(1)}, f32[16,8,256]{2,1,0:T(8,128)S(1)}, f32[16,8,256]{2,1,0:T(8,128)S(1)}, bf16[16,16,256...) custom-call(s32[1,16]{1,0:T(1,128)} %partner.1, s32[1,16]{1,0:T(1,128)} %pattern.1, f32[8,16,256]{2,1,0:T(8,128)} %load.1, ...), custom_call_target="tpu_custom_call" | custom-call | flops 4000000 | bytes 250000 | tf_op jit(solution)/shard_map/pallas_call | solution.py:462
  2.2 1.0 %collective-permute-done.rest_2_ = f32[36,8,128]{2,1,0:T(8,128)S(1)} collective-permute-done((f32[36,8,128]{2,1,0:T(8,128)S(1)}, f32[36,8,128]{2,1,0:T(8,128)S(1)}, u32[]{:S(2)}, u32[]{:S(2)}) %collective-permute-start) | collective-permute-done | bytes 147488 | tf_op jit(solution)/shard_map/ppermute | solution.py:501
  3.3 3.9 %collective-permute-start.1 = (f32[24,8,128]{2,1,0:T(8,128)S(1)}, f32[24,8,128]{2,1,0:T(8,128)S(1)}, u32[]{:S(2)}, u32[]{:S(2)}) collective-permute-start(f32[24,8,128]{2,1,0:T(8,128)S(1)} %get-tuple-element.80), channel_id=1, source_target_pairs={{0,6},{1,7},{2,4},{3,5},{4,2},{5,3},{6,0},{7,1},{8,14},{9,15},{10,... | collective-permute-start | bytes 294920 | tf_op jit(solution)/shard_map/ppermute | solution.py:501
  7.8 2.3 %shard_map.105 = (f32[64,64]{1,0:T(8,128)S(1)}, bf16[16,256,256]{2,1,0:T(8,128)(2,1)S(1)}, bf16[16,256,256]{2,1,0:T(8,128)(2,1)S(1)}) custom-call(s32[1,64]{1,0:T(1,128)} %index_in.1, f32[32,32]{1,0:T(8,128)} %inverse_in.1, bf16[16,256,256]{2,1,0:T(8,128)(2,1)} %diag.1, bf16[16,256,256]{2,1,0:T(8,128)(2,1)} %off.1), custom_call_target="tpu_custom_call" | custom-call | flops 600000000 | bytes 37500000 | tf_op jit(solution)/shard_map/pallas_call | solution.py:462
  10.3 2.3 %collective-permute-done.2.rest_5_.rest_1_ = f32[24,8,128]{2,1,0:T(8,128)S(1)} collective-permute-done((f32[24,8,128]{2,1,0:T(8,128)S(1)}, f32[24,8,128]{2,1,0:T(8,128)S(1)}, u32[]{:S(2)}, u32[]{:S(2)}) %collective-permute-start.2) | collective-permute-done | bytes 98336 | tf_op jit(solution)/shard_map/ppermute | solution.py:501
  12.6 1.1 %shard_map.107 = (f32[16,8,256]{2,1,0:T(8,128)S(1)}, f32[16,8,256]{2,1,0:T(8,128)S(1)}, bf16[16,16,256]{2,1,0:T(8,128)(2,1)S(1)}, f32[8,128]{1,0:T(8,128)S(1)}, f32[19,8,128]{2,1,0:T(8,128)S(1)}) custom-call(s32[90]{0:T(128)S(4)} %get-tuple-element.71.table, f32[16,8,256]{2,1,0:T(8,128)S(1)} %get-tuple-element.73.rest_0_.wide, ...), custom_call_target="tpu_custom_call" | custom-call | flops 600000000 | bytes 37500000 | tf_op jit(solution)/shard_map/pallas_call | solution.py:462
  13.8 1.1 %shard_map.108.rest_0_.image = f32[16,8,256]{2,1,0:T(8,128)S(1)} custom-call(s32[90]{0:T(128)S(4)} %get-tuple-element.71.table, f32[16,8,256]{2,1,0:T(8,128)S(1)} %get-tuple-element.73.rest_0_.wide, bf16[16,256,256]{2,1,0:T(8,128)(2,1)S(1)} %get-tuple-element.74.rest_1_.diag, bf16[16,256,256]{2,1,0:T(8,128)(2,1)S(1)} %get-tuple-element.75.rest_2_.off, ...), custom_call_target="tpu_custom_call" | custom-call | flops 600000000 | bytes 37500000 | tf_op jit(solution)/shard_map/pallas_call | solution.py:462
  15.0 1.7 %collective-permute-start.6 = (f32[13,8,128]{2,1,0:T(8,128)S(1)}, f32[13,8,128]{2,1,0:T(8,128)S(1)}, u32[]{:S(2)}, u32[]{:S(2)}) collective-permute-start(f32[13,8,128]{2,1,0:T(8,128)S(1)} %get-tuple-element.89), channel_id=1, source_target_pairs={{0,6},{1,7},{2,4},{3,5},{4,2},{5,3},{6,0},{7,1},{8,14},{9,15},{10,... | collective-permute-start | bytes 159752 | tf_op jit(solution)/shard_map/ppermute | solution.py:501
  16.8 1.3 %collective-permute-start.7 = (f32[13,8,128]{2,1,0:T(8,128)S(1)}, f32[13,8,128]{2,1,0:T(8,128)S(1)}, u32[]{:S(2)}, u32[]{:S(2)}) collective-permute-start(f32[13,8,128]{2,1,0:T(8,128)S(1)} %get-tuple-element.90), channel_id=1, source_target_pairs={{0,2},{1,5},{2,0},{3,7},{4,6},{5,1},{6,4},{7,3},{8,10},{9,13},{10,... | collective-permute-start | bytes 159752 | tf_op jit(solution)/shard_map/ppermute | solution.py:501
  18.8 1.4 %collective-permute-done.6.rest_0_ = f32[13,8,128]{2,1,0:T(8,128)S(1)} collective-permute-done((f32[13,8,128]{2,1,0:T(8,128)S(1)}, f32[13,8,128]{2,1,0:T(8,128)S(1)}, u32[]{:S(2)}, u32[]{:S(2)}) %collective-permute-start.6) | collective-permute-done | bytes 53280 | tf_op jit(solution)/shard_map/ppermute | solution.py:501
  20.2 1.1 %collective-permute-done.7.rest_1_ = f32[13,8,128]{2,1,0:T(8,128)S(1)} collective-permute-done((f32[13,8,128]{2,1,0:T(8,128)S(1)}, f32[13,8,128]{2,1,0:T(8,128)S(1)}, u32[]{:S(2)}, u32[]{:S(2)}) %collective-permute-start.7) | collective-permute-done | bytes 53280 | tf_op jit(solution)/shard_map/ppermute | solution.py:501
  21.3 0.9 collective-permute-done.8.rest_2_
  22.9 11.9 %all_to_all.20.rest_4_ = f32[32,1,128]{2,1,0:T(1,128)S(1)} all-to-all(f32[32,1,128]{2,1,0:T(1,128)S(1)} %get-tuple-element.93), channel_id=1, replica_groups=mesh['group'=4,'sub'=8] {'group','sub'}, dimensions={0} | all-to-all | bytes 32768 | tf_op jit(solution)/shard_map/all_to_all | solution.py:582
  34.8 1.3 %shard_map.112 = (f32[16,8,256]{2,1,0:T(8,128)S(1)}, f32[16,8,256]{2,1,0:T(8,128)S(1)}, f32[8,128]{1,0:T(8,128)S(1)}, f32[16,8,256]{2,1,0:T(8,128)S(1)}, bf16[16...) custom-call(s32[90]{0:T(128)S(4)} %get-tuple-element.71.table, ...), custom_call_target="tpu_custom_call" | custom-call | flops 600000000 | bytes 37500000 | tf_op jit(solution)/shard_map/pallas_call | solution.py:462
  36.2 1.1 %shard_map.113 = (f32[16,8,256]{2,1,0:T(8,128)S(1)}, f32[16,8,256]{2,1,0:T(8,128)S(1)}) custom-call(s32[90]{0:T(128)S(4)} %get-tuple-element.71.table, f32[16,8,256]{2,1,0:T(8,128)S(1)} %get-tuple-element.73.rest_0_.wide, bf16[16,256,256]{2,1,0:T(8,128)(2,1)S(1)} %get-tuple-element.74.rest_1_.diag, bf16[16,256,256]{2,1,0:T(8,128)(2,1)S(1)} %get-tuple-element.75.rest_2_.off, ...), custom_call_target="tpu_custom_call" | custom-call | flops 600000000 | bytes 37500000 | tf_op jit(solution)/shard_map/pallas_call | solution.py:462
  38.2 1.4 %collective-permute-start.12 = (f32[13,8,128]{2,1,0:T(8,128)S(1)}, f32[13,8,128]{2,1,0:T(8,128)S(1)}, u32[]{:S(2)}, u32[]{:S(2)}) collective-permute-start(f32[13,8,128]{2,1,0:T(8,128)S(1)} %get-tuple-element.104), channel_id=1, source_target_pairs={{0,2},{1,5},{2,0},{3,7},{4,6},{5,1},{6,4},{7,3},{8,10},{9,13},{10,... | collective-permute-start | bytes 159752 | tf_op jit(solution)/shard_map/ppermute | solution.py:501
  39.6 1.5 %collective-permute-start.13 = (f32[13,8,128]{2,1,0:T(8,128)S(1)}, f32[13,8,128]{2,1,0:T(8,128)S(1)}, u32[]{:S(2)}, u32[]{:S(2)}) collective-permute-start(f32[13,8,128]{2,1,0:T(8,128)S(1)} %get-tuple-element.105), channel_id=1, source_target_pairs={{0,4},{1,3},{2,6},{3,1},{4,0},{5,7},{6,2},{7,5},{8,12},{9,11},{10,... | collective-permute-start | bytes 159752 | tf_op jit(solution)/shard_map/ppermute | solution.py:501
  41.1 2.1 %collective-permute-done.11.rest_1_ = f32[13,8,128]{2,1,0:T(8,128)S(1)} collective-permute-done((f32[13,8,128]{2,1,0:T(8,128)S(1)}, f32[13,8,128]{2,1,0:T(8,128)S(1)}, u32[]{:S(2)}, u32[]{:S(2)}) %collective-permute-start.11) | collective-permute-done | bytes 53280 | tf_op jit(solution)/shard_map/ppermute | solution.py:501
  44.4 8.8 %all_to_all.21.rest_4_ = f32[32,1,128]{2,1,0:T(1,128)S(1)} all-to-all(f32[32,1,128]{2,1,0:T(1,128)S(1)} %get-tuple-element.107), channel_id=1, replica_groups=mesh['group'=4,'sub'=8] {'group','sub'}, dimensions={0} | all-to-all | bytes 32768 | tf_op jit(solution)/shard_map/all_to_all | solution.py:582
  53.2 1.2 %shard_map.116 = (f32[16,8,256]{2,1,0:T(8,128)S(1)}, f32[16,8,256]{2,1,0:T(8,128)S(1)}, f32[8,128]{1,0:T(8,128)S(1)}, f32[16,8,256]{2,1,0:T(8,128)S(1)}, bf16[16...) custom-call(s32[90]{0:T(128)S(4)} %get-tuple-element.71.table, ...), custom_call_target="tpu_custom_call" | custom-call | flops 600000000 | bytes 37500000 | tf_op jit(solution)/shard_map/pallas_call | solution.py:462
  54.5 1.1 %shard_map.117 = (f32[16,8,256]{2,1,0:T(8,128)S(1)}, f32[16,8,256]{2,1,0:T(8,128)S(1)}) custom-call(s32[90]{0:T(128)S(4)} %get-tuple-element.71.table, f32[16,8,256]{2,1,0:T(8,128)S(1)} %get-tuple-element.73.rest_0_.wide, bf16[16,256,256]{2,1,0:T(8,128)(2,1)S(1)} %get-tuple-element.74.rest_1_.diag, bf16[16,256,256]{2,1,0:T(8,128)(2,1)S(1)} %get-tuple-element.75.rest_2_.off, ...), custom_call_target="tpu_custom_call" | custom-call | flops 600000000 | bytes 37500000 | tf_op jit(solution)/shard_map/pallas_call | solution.py:462
  56.5 1.4 %collective-permute-start.17 = (f32[13,8,128]{2,1,0:T(8,128)S(1)}, f32[13,8,128]{2,1,0:T(8,128)S(1)}, u32[]{:S(2)}, u32[]{:S(2)}) collective-permute-start(f32[13,8,128]{2,1,0:T(8,128)S(1)} %get-tuple-element.119), channel_id=1, source_target_pairs={{0,2},{1,5},{2,0},{3,7},{4,6},{5,1},{6,4},{7,3},{8,10},{9,13},{10,... | collective-permute-start | bytes 159752 | tf_op jit(solution)/shard_map/ppermute | solution.py:501
  57.9 1.5 %collective-permute-start.18 = (f32[13,8,128]{2,1,0:T(8,128)S(1)}, f32[13,8,128]{2,1,0:T(8,128)S(1)}, u32[]{:S(2)}, u32[]{:S(2)}) collective-permute-start(f32[13,8,128]{2,1,0:T(8,128)S(1)} %get-tuple-element.120), channel_id=1, source_target_pairs={{0,4},{1,3},{2,6},{3,1},{4,0},{5,7},{6,2},{7,5},{8,12},{9,11},{10,... | collective-permute-start | bytes 159752 | tf_op jit(solution)/shard_map/ppermute | solution.py:501
  59.3 2.2 %collective-permute-done.16.rest_1_ = f32[13,8,128]{2,1,0:T(8,128)S(1)} collective-permute-done((f32[13,8,128]{2,1,0:T(8,128)S(1)}, f32[13,8,128]{2,1,0:T(8,128)S(1)}, u32[]{:S(2)}, u32[]{:S(2)}) %collective-permute-start.16) | collective-permute-done | bytes 53280 | tf_op jit(solution)/shard_map/ppermute | solution.py:501
  62.7 8.8 %all_to_all.22.rest_4_ = f32[32,1,128]{2,1,0:T(1,128)S(1)} all-to-all(f32[32,1,128]{2,1,0:T(1,128)S(1)} %get-tuple-element.122), channel_id=1, replica_groups=mesh['group'=4,'sub'=8] {'group','sub'}, dimensions={0} | all-to-all | bytes 32768 | tf_op jit(solution)/shard_map/all_to_all | solution.py:582
  71.5 1.2 %shard_map.120 = (f32[16,8,256]{2,1,0:T(8,128)S(1)}, f32[16,8,256]{2,1,0:T(8,128)S(1)}, f32[8,128]{1,0:T(8,128)S(1)}, f32[16,8,256]{2,1,0:T(8,128)S(1)}, bf16[16...) custom-call(s32[90]{0:T(128)S(4)} %get-tuple-element.71.table, ...), custom_call_target="tpu_custom_call" | custom-call | flops 600000000 | bytes 37500000 | tf_op jit(solution)/shard_map/pallas_call | solution.py:462
  72.8 1.1 %shard_map.121 = (f32[16,8,256]{2,1,0:T(8,128)S(1)}, f32[16,8,256]{2,1,0:T(8,128)S(1)}) custom-call(s32[90]{0:T(128)S(4)} %get-tuple-element.71.table, f32[16,8,256]{2,1,0:T(8,128)S(1)} %get-tuple-element.73.rest_0_.wide, bf16[16,256,256]{2,1,0:T(8,128)(2,1)S(1)} %get-tuple-element.74.rest_1_.diag, bf16[16,256,256]{2,1,0:T(8,128)(2,1)S(1)} %get-tuple-element.75.rest_2_.off, ...), custom_call_target="tpu_custom_call" | custom-call | flops 600000000 | bytes 37500000 | tf_op jit(solution)/shard_map/pallas_call | solution.py:462
  74.8 1.4 %collective-permute-start.22 = (f32[13,8,128]{2,1,0:T(8,128)S(1)}, f32[13,8,128]{2,1,0:T(8,128)S(1)}, u32[]{:S(2)}, u32[]{:S(2)}) collective-permute-start(f32[13,8,128]{2,1,0:T(8,128)S(1)} %get-tuple-element.134), channel_id=1, source_target_pairs={{0,2},{1,5},{2,0},{3,7},{4,6},{5,1},{6,4},{7,3},{8,10},{9,13},{10,... | collective-permute-start | bytes 159752 | tf_op jit(solution)/shard_map/ppermute | solution.py:501
  76.2 1.5 %collective-permute-start.23 = (f32[13,8,128]{2,1,0:T(8,128)S(1)}, f32[13,8,128]{2,1,0:T(8,128)S(1)}, u32[]{:S(2)}, u32[]{:S(2)}) collective-permute-start(f32[13,8,128]{2,1,0:T(8,128)S(1)} %get-tuple-element.135), channel_id=1, source_target_pairs={{0,4},{1,3},{2,6},{3,1},{4,0},{5,7},{6,2},{7,5},{8,12},{9,11},{10,... | collective-permute-start | bytes 159752 | tf_op jit(solution)/shard_map/ppermute | solution.py:501
  77.6 2.2 %collective-permute-done.21.rest_1_ = f32[13,8,128]{2,1,0:T(8,128)S(1)} collective-permute-done((f32[13,8,128]{2,1,0:T(8,128)S(1)}, f32[13,8,128]{2,1,0:T(8,128)S(1)}, u32[]{:S(2)}, u32[]{:S(2)}) %collective-permute-start.21) | collective-permute-done | bytes 53280 | tf_op jit(solution)/shard_map/ppermute | solution.py:501
  81.0 8.8 %all_to_all.23.gathered = f32[32,1,128]{2,1,0:T(1,128)S(1)} all-to-all(f32[32,1,128]{2,1,0:T(1,128)S(1)} %get-tuple-element.137), channel_id=1, replica_groups=mesh['group'=4,'sub'=8] {'group','sub'}, dimensions={0} | all-to-all | bytes 32768 | tf_op jit(solution)/shard_map/all_to_all | solution.py:582
  89.8 1.0 %shard_map.124 = (f32[8,16,256]{2,1,0:T(8,128)}, f32[8,16,256]{2,1,0:T(8,128)}) custom-call(f32[32,1,128]{2,1,0:T(1,128)S(1)} %all_to_all.23.gathered, f32[16,8,256]{2,1,0:T(8,128)S(1)} %get-tuple-element.138.before, f32[16,8,256]{2,1,0:T(8,128)S(1)} %get-tuple-element.130.residual.residual_in, f32[16,8,256]{2,1,0:T(8,128)S(1)} %get-tuple-element.131.direction, ...), custom_call_target="tpu_custom_call" | custom-call | flops 4000000 | bytes 250000 | tf_op jit(solution)/shard_map/pallas_call | solution.py:462
  (43 shorter events, 9.4 us)
Async XLA Ops:
  1.7 1.5 %collective-permute-start = (f32[36,8,128]{2,1,0:T(8,128)S(1)}, f32[36,8,128]{2,1,0:T(8,128)S(1)}, u32[]{:S(2)}, u32[]{:S(2)}) collective-permute-start(f32[36,8,128]{2,1,0:T(8,128)S(1)} %get-tuple-element.79), channel_id=1, source_target_pairs={{0,1},{1,0},{2,3},{3,2},{4,5},{5,4},{6,7},{7,6},{8,9},{9,8},{10,11... | collective-permute-start | bytes 442376 | tf_op jit(solution)/shard_map/ppermute | solution.py:501
  3.3 7.1 %collective-permute-start.1 = (f32[24,8,128]{2,1,0:T(8,128)S(1)}, f32[24,8,128]{2,1,0:T(8,128)S(1)}, u32[]{:S(2)}, u32[]{:S(2)}) collective-permute-start(f32[24,8,128]{2,1,0:T(8,128)S(1)} %get-tuple-element.80), channel_id=1, source_target_pairs={{0,6},{1,7},{2,4},{3,5},{4,2},{5,3},{6,0},{7,1},{8,14},{9,15},{10,... | collective-permute-start | bytes 294920 | tf_op jit(solution)/shard_map/ppermute | solution.py:501
  7.1 5.5 %collective-permute-start.2 = (f32[24,8,128]{2,1,0:T(8,128)S(1)}, f32[24,8,128]{2,1,0:T(8,128)S(1)}, u32[]{:S(2)}, u32[]{:S(2)}) collective-permute-start(f32[24,8,128]{2,1,0:T(8,128)S(1)} %get-tuple-element.81), channel_id=1, source_target_pairs={{0,2},{1,5},{2,0},{3,7},{4,6},{5,1},{6,4},{7,3},{8,10},{9,13},{10,... | collective-permute-start | bytes 294920 | tf_op jit(solution)/shard_map/ppermute | solution.py:501
  7.7 4.9 %collective-permute-start.3 = (f32[24,8,128]{2,1,0:T(8,128)S(1)}, f32[24,8,128]{2,1,0:T(8,128)S(1)}, u32[]{:S(2)}, u32[]{:S(2)}) collective-permute-start(f32[24,8,128]{2,1,0:T(8,128)S(1)} %get-tuple-element.82), channel_id=1, source_target_pairs={{0,4},{1,3},{2,6},{3,1},{4,0},{5,7},{6,2},{7,5},{8,12},{9,11},{10,... | collective-permute-start | bytes 294920 | tf_op jit(solution)/shard_map/ppermute | solution.py:501
  7.8 4.8 %collective-permute-start.4 = (f32[24,8,128]{2,1,0:T(8,128)S(1)}, f32[24,8,128]{2,1,0:T(8,128)S(1)}, u32[]{:S(2)}, u32[]{:S(2)}) collective-permute-start(f32[24,8,128]{2,1,0:T(8,128)S(1)} %get-tuple-element.83), channel_id=1, source_target_pairs={{0,1},{1,0},{2,3},{3,2},{4,5},{5,4},{6,7},{7,6},{8,9},{9,8},{10,11... | collective-permute-start | bytes 294920 | tf_op jit(solution)/shard_map/ppermute | solution.py:501
  13.7 1.3 %collective-permute-start.5 = (f32[19,8,128]{2,1,0:T(8,128)S(1)}, f32[19,8,128]{2,1,0:T(8,128)S(1)}, u32[]{:S(2)}, u32[]{:S(2)}) collective-permute-start(f32[19,8,128]{2,1,0:T(8,128)S(1)} %get-tuple-element.88), channel_id=1, source_target_pairs={{0,1},{1,0},{2,3},{3,2},{4,5},{5,4},{6,7},{7,6},{8,9},{9,8},{10,11... | collective-permute-start | bytes 233480 | tf_op jit(solution)/shard_map/ppermute | solution.py:501
  15.0 5.2 %collective-permute-start.6 = (f32[13,8,128]{2,1,0:T(8,128)S(1)}, f32[13,8,128]{2,1,0:T(8,128)S(1)}, u32[]{:S(2)}, u32[]{:S(2)}) collective-permute-start(f32[13,8,128]{2,1,0:T(8,128)S(1)} %get-tuple-element.89), channel_id=1, source_target_pairs={{0,6},{1,7},{2,4},{3,5},{4,2},{5,3},{6,0},{7,1},{8,14},{9,15},{10,... | collective-permute-start | bytes 159752 | tf_op jit(solution)/shard_map/ppermute | solution.py:501
  16.8 4.5 %collective-permute-start.7 = (f32[13,8,128]{2,1,0:T(8,128)S(1)}, f32[13,8,128]{2,1,0:T(8,128)S(1)}, u32[]{:S(2)}, u32[]{:S(2)}) collective-permute-start(f32[13,8,128]{2,1,0:T(8,128)S(1)} %get-tuple-element.90), channel_id=1, source_target_pairs={{0,2},{1,5},{2,0},{3,7},{4,6},{5,1},{6,4},{7,3},{8,10},{9,13},{10,... | collective-permute-start | bytes 159752 | tf_op jit(solution)/shard_map/ppermute | solution.py:501
  18.0 4.1 %collective-permute-start.8 = (f32[13,8,128]{2,1,0:T(8,128)S(1)}, f32[13,8,128]{2,1,0:T(8,128)S(1)}, u32[]{:S(2)}, u32[]{:S(2)}) collective-permute-start(f32[13,8,128]{2,1,0:T(8,128)S(1)} %get-tuple-element.91), channel_id=1, source_target_pairs={{0,4},{1,3},{2,6},{3,1},{4,0},{5,7},{6,2},{7,5},{8,12},{9,11},{10,... | collective-permute-start | bytes 159752 | tf_op jit(solution)/shard_map/ppermute | solution.py:501
  18.6 3.6 %collective-permute-start.9 = (f32[13,8,128]{2,1,0:T(8,128)S(1)}, f32[13,8,128]{2,1,0:T(8,128)S(1)}, u32[]{:S(2)}, u32[]{:S(2)}) collective-permute-start(f32[13,8,128]{2,1,0:T(8,128)S(1)} %get-tuple-element.92), channel_id=1, source_target_pairs={{0,1},{1,0},{2,3},{3,2},{4,5},{5,4},{6,7},{7,6},{8,9},{9,8},{10,11... | collective-permute-start | bytes 159752 | tf_op jit(solution)/shard_map/ppermute | solution.py:501
  36.2 1.3 %collective-permute-start.10 = (f32[19,8,128]{2,1,0:T(8,128)S(1)}, f32[19,8,128]{2,1,0:T(8,128)S(1)}, u32[]{:S(2)}, u32[]{:S(2)}) collective-permute-start(f32[19,8,128]{2,1,0:T(8,128)S(1)} %get-tuple-element.102), channel_id=1, source_target_pairs={{0,1},{1,0},{2,3},{3,2},{4,5},{5,4},{6,7},{7,6},{8,9},{9,8},{10,11... | collective-permute-start | bytes 233480 | tf_op jit(solution)/shard_map/ppermute | solution.py:501
  37.5 5.7 %collective-permute-start.11 = (f32[13,8,128]{2,1,0:T(8,128)S(1)}, f32[13,8,128]{2,1,0:T(8,128)S(1)}, u32[]{:S(2)}, u32[]{:S(2)}) collective-permute-start(f32[13,8,128]{2,1,0:T(8,128)S(1)} %get-tuple-element.103), channel_id=1, source_target_pairs={{0,6},{1,7},{2,4},{3,5},{4,2},{5,3},{6,0},{7,1},{8,14},{9,15},{10,... | collective-permute-start | bytes 159752 | tf_op jit(solution)/shard_map/ppermute | solution.py:501
  38.2 5.0 %collective-permute-start.12 = (f32[13,8,128]{2,1,0:T(8,128)S(1)}, f32[13,8,128]{2,1,0:T(8,128)S(1)}, u32[]{:S(2)}, u32[]{:S(2)}) collective-permute-start(f32[13,8,128]{2,1,0:T(8,128)S(1)} %get-tuple-element.104), channel_id=1, source_target_pairs={{0,2},{1,5},{2,0},{3,7},{4,6},{5,1},{6,4},{7,3},{8,10},{9,13},{10,... | collective-permute-start | bytes 159752 | tf_op jit(solution)/shard_map/ppermute | solution.py:501
  39.6 4.1 %collective-permute-start.13 = (f32[13,8,128]{2,1,0:T(8,128)S(1)}, f32[13,8,128]{2,1,0:T(8,128)S(1)}, u32[]{:S(2)}, u32[]{:S(2)}) collective-permute-start(f32[13,8,128]{2,1,0:T(8,128)S(1)} %get-tuple-element.105), channel_id=1, source_target_pairs={{0,4},{1,3},{2,6},{3,1},{4,0},{5,7},{6,2},{7,5},{8,12},{9,11},{10,... | collective-permute-start | bytes 159752 | tf_op jit(solution)/shard_map/ppermute | solution.py:501
  41.1 2.7 %collective-permute-start.14 = (f32[13,8,128]{2,1,0:T(8,128)S(1)}, f32[13,8,128]{2,1,0:T(8,128)S(1)}, u32[]{:S(2)}, u32[]{:S(2)}) collective-permute-start(f32[13,8,128]{2,1,0:T(8,128)S(1)} %get-tuple-element.106), channel_id=1, source_target_pairs={{0,1},{1,0},{2,3},{3,2},{4,5},{5,4},{6,7},{7,6},{8,9},{9,8},{10,11... | collective-permute-start | bytes 159752 | tf_op jit(solution)/shard_map/ppermute | solution.py:501
  54.5 1.3 %collective-permute-start.15 = (f32[19,8,128]{2,1,0:T(8,128)S(1)}, f32[19,8,128]{2,1,0:T(8,128)S(1)}, u32[]{:S(2)}, u32[]{:S(2)}) collective-permute-start(f32[19,8,128]{2,1,0:T(8,128)S(1)} %get-tuple-element.117), channel_id=1, source_target_pairs={{0,1},{1,0},{2,3},{3,2},{4,5},{5,4},{6,7},{7,6},{8,9},{9,8},{10,11... | collective-permute-start | bytes 233480 | tf_op jit(solution)/shard_map/ppermute | solution.py:501
  55.8 5.8 %collective-permute-start.16 = (f32[13,8,128]{2,1,0:T(8,128)S(1)}, f32[13,8,128]{2,1,0:T(8,128)S(1)}, u32[]{:S(2)}, u32[]{:S(2)}) collective-permute-start(f32[13,8,128]{2,1,0:T(8,128)S(1)} %get-tuple-element.118), channel_id=1, source_target_pairs={{0,6},{1,7},{2,4},{3,5},{4,2},{5,3},{6,0},{7,1},{8,14},{9,15},{10,... | collective-permute-start | bytes 159752 | tf_op jit(solution)/shard_map/ppermute | solution.py:501
  56.5 5.1 %collective-permute-start.17 = (f32[13,8,128]{2,1,0:T(8,128)S(1)}, f32[13,8,128]{2,1,0:T(8,128)S(1)}, u32[]{:S(2)}, u32[]{:S(2)}) collective-permute-start(f32[13,8,128]{2,1,0:T(8,128)S(1)} %get-tuple-element.119), channel_id=1, source_target_pairs={{0,2},{1,5},{2,0},{3,7},{4,6},{5,1},{6,4},{7,3},{8,10},{9,13},{10,... | collective-permute-start | bytes 159752 | tf_op jit(solution)/shard_map/ppermute | solution.py:501
  57.9 4.2 %collective-permute-start.18 = (f32[13,8,128]{2,1,0:T(8,128)S(1)}, f32[13,8,128]{2,1,0:T(8,128)S(1)}, u32[]{:S(2)}, u32[]{:S(2)}) collective-permute-start(f32[13,8,128]{2,1,0:T(8,128)S(1)} %get-tuple-element.120), channel_id=1, source_target_pairs={{0,4},{1,3},{2,6},{3,1},{4,0},{5,7},{6,2},{7,5},{8,12},{9,11},{10,... | collective-permute-start | bytes 159752 | tf_op jit(solution)/shard_map/ppermute | solution.py:501
  59.3 2.7 %collective-permute-start.19 = (f32[13,8,128]{2,1,0:T(8,128)S(1)}, f32[13,8,128]{2,1,0:T(8,128)S(1)}, u32[]{:S(2)}, u32[]{:S(2)}) collective-permute-start(f32[13,8,128]{2,1,0:T(8,128)S(1)} %get-tuple-element.121), channel_id=1, source_target_pairs={{0,1},{1,0},{2,3},{3,2},{4,5},{5,4},{6,7},{7,6},{8,9},{9,8},{10,11... | collective-permute-start | bytes 159752 | tf_op jit(solution)/shard_map/ppermute | solution.py:501
  72.8 1.3 %collective-permute-start.20 = (f32[19,8,128]{2,1,0:T(8,128)S(1)}, f32[19,8,128]{2,1,0:T(8,128)S(1)}, u32[]{:S(2)}, u32[]{:S(2)}) collective-permute-start(f32[19,8,128]{2,1,0:T(8,128)S(1)} %get-tuple-element.132), channel_id=1, source_target_pairs={{0,1},{1,0},{2,3},{3,2},{4,5},{5,4},{6,7},{7,6},{8,9},{9,8},{10,11... | collective-permute-start | bytes 233480 | tf_op jit(solution)/shard_map/ppermute | solution.py:501
  74.1 5.8 %collective-permute-start.21 = (f32[13,8,128]{2,1,0:T(8,128)S(1)}, f32[13,8,128]{2,1,0:T(8,128)S(1)}, u32[]{:S(2)}, u32[]{:S(2)}) collective-permute-start(f32[13,8,128]{2,1,0:T(8,128)S(1)} %get-tuple-element.133), channel_id=1, source_target_pairs={{0,6},{1,7},{2,4},{3,5},{4,2},{5,3},{6,0},{7,1},{8,14},{9,15},{10,... | collective-permute-start | bytes 159752 | tf_op jit(solution)/shard_map/ppermute | solution.py:501
  74.8 5.1 %collective-permute-start.22 = (f32[13,8,128]{2,1,0:T(8,128)S(1)}, f32[13,8,128]{2,1,0:T(8,128)S(1)}, u32[]{:S(2)}, u32[]{:S(2)}) collective-permute-start(f32[13,8,128]{2,1,0:T(8,128)S(1)} %get-tuple-element.134), channel_id=1, source_target_pairs={{0,2},{1,5},{2,0},{3,7},{4,6},{5,1},{6,4},{7,3},{8,10},{9,13},{10,... | collective-permute-start | bytes 159752 | tf_op jit(solution)/shard_map/ppermute | solution.py:501
  76.2 4.2 %collective-permute-start.23 = (f32[13,8,128]{2,1,0:T(8,128)S(1)}, f32[13,8,128]{2,1,0:T(8,128)S(1)}, u32[]{:S(2)}, u32[]{:S(2)}) collective-permute-start(f32[13,8,128]{2,1,0:T(8,128)S(1)} %get-tuple-element.135), channel_id=1, source_target_pairs={{0,4},{1,3},{2,6},{3,1},{4,0},{5,7},{6,2},{7,5},{8,12},{9,11},{10,... | collective-permute-start | bytes 159752 | tf_op jit(solution)/shard_map/ppermute | solution.py:501
  77.6 2.7 %collective-permute-start.24 = (f32[13,8,128]{2,1,0:T(8,128)S(1)}, f32[13,8,128]{2,1,0:T(8,128)S(1)}, u32[]{:S(2)}, u32[]{:S(2)}) collective-permute-start(f32[13,8,128]{2,1,0:T(8,128)S(1)} %get-tuple-element.136), channel_id=1, source_target_pairs={{0,1},{1,0},{2,3},{3,2},{4,5},{5,4},{6,7},{7,6},{8,9},{9,8},{10,11... | collective-permute-start | bytes 159752 | tf_op jit(solution)/shard_map/ppermute | solution.py:501

commit v12 on v11

--- a/solution.py
+++ b/solution.py
@@ -86,8 +86,7 @@
         return len(self.handed) * self.rows(kinds)
 
     def at(self, k, core):
-        first = len(self.beyond)
-        return k if k < first else first + (k - first + core) % len(self.beside)
+        return (k + core) % len(self.far)
 
     def mine(self, k):
         core = lax.axis_index("sub") & 1

time: 91.1 us -> 92.2 us (1.012)
  transfers between devices with their start and end apart: 25 -> 25, of which waited for: 16 -> 17; matrix products, arithmetic and copies ran while one was open for 0% -> 0% of each run, Pallas kernels for 7% -> 7%
where the time goes in v12:
time: 92.2 us; the launch traced here: 92 us
  blocking collectives  39.3 us (43%)
  starting transfers between devices  19.3 us (21%)
  Pallas kernels  16.7 us (18%)
  waiting for transfers between devices  15.9 us (17%)
    all_to_all x4, blocking collectives, on_device(): gathered = lax.all_to_all(sent, ('group', 'sub'), 0, 0, tiled=True)  39.3 us
    ppermute x25, starting transfers between devices, across(): return lax.ppermute(piece, 'sub', pairs)  19.3 us
    pallas_call x21, Pallas kernels, call(): pl.pallas_call(body, out_shape=shapes, in_specs=specs, out_specs=[SMEM if...  16.7 us
    ppermute x25, waiting for transfers between devices, across(): return lax.ppermute(piece, 'sub', pairs)  15.9 us
  transfers between devices with their start and end apart: 25, of which 17 were waited for; matrix products, arithmetic and copies ran while one was open for 0% of the time, Pallas kernels for 7%

profile of v12, /device:TPU:0, one launch (start us, length us, event | category | flops | bytes accessed | tf_op | source)
XLA Modules:
  0.0 92.0 jit_solution(7122347248138247131)
XLA Ops:
  0.6 1.0 %shard_map.104 = (s32[90]{0:T(128)S(4)}, f32[16,8,256]{2,1,0:T(8,128)S(1)}, f32[16,8,256]{2,1,0:T(8,128)S(1)}, f32[16,8,256]{2,1,0:T(8,128)S(1)}, bf16[16,16,256...) custom-call(s32[1,16]{1,0:T(1,128)} %partner.1, s32[1,16]{1,0:T(1,128)} %pattern.1, f32[8,16,256]{2,1,0:T(8,128)} %load.1, ...), custom_call_target="tpu_custom_call" | custom-call | flops 4000000 | bytes 250000 | tf_op jit(solution)/shard_map/pallas_call | solution.py:461
  2.2 1.0 %collective-permute-done.rest_2_ = f32[36,8,128]{2,1,0:T(8,128)S(1)} collective-permute-done((f32[36,8,128]{2,1,0:T(8,128)S(1)}, f32[36,8,128]{2,1,0:T(8,128)S(1)}, u32[]{:S(2)}, u32[]{:S(2)}) %collective-permute-start) | collective-permute-done | bytes 147488 | tf_op jit(solution)/shard_map/ppermute | solution.py:500
  3.2 3.9 %collective-permute-start.1 = (f32[24,8,128]{2,1,0:T(8,128)S(1)}, f32[24,8,128]{2,1,0:T(8,128)S(1)}, u32[]{:S(2)}, u32[]{:S(2)}) collective-permute-start(f32[24,8,128]{2,1,0:T(8,128)S(1)} %get-tuple-element.80), channel_id=1, source_target_pairs={{0,6},{1,3},{2,4},{3,1},{4,2},{5,7},{6,0},{7,5},{8,14},{9,11},{10,... | collective-permute-start | bytes 294920 | tf_op jit(solution)/shard_map/ppermute | solution.py:500
  7.8 2.3 %shard_map.105 = (f32[64,64]{1,0:T(8,128)S(1)}, bf16[16,256,256]{2,1,0:T(8,128)(2,1)S(1)}, bf16[16,256,256]{2,1,0:T(8,128)(2,1)S(1)}) custom-call(s32[1,64]{1,0:T(1,128)} %index_in.1, f32[32,32]{1,0:T(8,128)} %inverse_in.1, bf16[16,256,256]{2,1,0:T(8,128)(2,1)} %diag.1, bf16[16,256,256]{2,1,0:T(8,128)(2,1)} %off.1), custom_call_target="tpu_custom_call" | custom-call | flops 600000000 | bytes 37500000 | tf_op jit(solution)/shard_map/pallas_call | solution.py:461
  10.6 1.8 %collective-permute-done.2.rest_5_.rest_1_ = f32[24,8,128]{2,1,0:T(8,128)S(1)} collective-permute-done((f32[24,8,128]{2,1,0:T(8,128)S(1)}, f32[24,8,128]{2,1,0:T(8,128)S(1)}, u32[]{:S(2)}, u32[]{:S(2)}) %collective-permute-start.2) | collective-permute-done | bytes 98336 | tf_op jit(solution)/shard_map/ppermute | solution.py:500
  13.1 1.1 %shard_map.107 = (f32[16,8,256]{2,1,0:T(8,128)S(1)}, f32[16,8,256]{2,1,0:T(8,128)S(1)}, bf16[16,16,256]{2,1,0:T(8,128)(2,1)S(1)}, f32[8,128]{1,0:T(8,128)S(1)}, f32[19,8,128]{2,1,0:T(8,128)S(1)}) custom-call(s32[90]{0:T(128)S(4)} %get-tuple-element.71.table, f32[16,8,256]{2,1,0:T(8,128)S(1)} %get-tuple-element.73.rest_0_.wide, ...), custom_call_target="tpu_custom_call" | custom-call | flops 600000000 | bytes 37500000 | tf_op jit(solution)/shard_map/pallas_call | solution.py:461
  14.3 1.1 %shard_map.108.rest_0_.image = f32[16,8,256]{2,1,0:T(8,128)S(1)} custom-call(s32[90]{0:T(128)S(4)} %get-tuple-element.71.table, f32[16,8,256]{2,1,0:T(8,128)S(1)} %get-tuple-element.73.rest_0_.wide, bf16[16,256,256]{2,1,0:T(8,128)(2,1)S(1)} %get-tuple-element.74.rest_1_.diag, bf16[16,256,256]{2,1,0:T(8,128)(2,1)S(1)} %get-tuple-element.75.rest_2_.off, ...), custom_call_target="tpu_custom_call" | custom-call | flops 600000000 | bytes 37500000 | tf_op jit(solution)/shard_map/pallas_call | solution.py:461
  15.5 1.3 %collective-permute-start.6 = (f32[13,8,128]{2,1,0:T(8,128)S(1)}, f32[13,8,128]{2,1,0:T(8,128)S(1)}, u32[]{:S(2)}, u32[]{:S(2)}) collective-permute-start(f32[13,8,128]{2,1,0:T(8,128)S(1)} %get-tuple-element.89), channel_id=1, source_target_pairs={{0,6},{1,3},{2,4},{3,1},{4,2},{5,7},{6,0},{7,5},{8,14},{9,11},{10,... | collective-permute-start | bytes 159752 | tf_op jit(solution)/shard_map/ppermute | solution.py:500
  16.8 1.5 %collective-permute-start.7 = (f32[13,8,128]{2,1,0:T(8,128)S(1)}, f32[13,8,128]{2,1,0:T(8,128)S(1)}, u32[]{:S(2)}, u32[]{:S(2)}) collective-permute-start(f32[13,8,128]{2,1,0:T(8,128)S(1)} %get-tuple-element.90), channel_id=1, source_target_pairs={{0,2},{1,5},{2,0},{3,7},{4,6},{5,1},{6,4},{7,3},{8,10},{9,13},{10,... | collective-permute-start | bytes 159752 | tf_op jit(solution)/shard_map/ppermute | solution.py:500
  19.3 1.3 %collective-permute-done.6.rest_0_ = f32[13,8,128]{2,1,0:T(8,128)S(1)} collective-permute-done((f32[13,8,128]{2,1,0:T(8,128)S(1)}, f32[13,8,128]{2,1,0:T(8,128)S(1)}, u32[]{:S(2)}, u32[]{:S(2)}) %collective-permute-start.6) | collective-permute-done | bytes 53280 | tf_op jit(solution)/shard_map/ppermute | solution.py:500
  20.6 0.9 %collective-permute-done.7.rest_1_ = f32[13,8,128]{2,1,0:T(8,128)S(1)} collective-permute-done((f32[13,8,128]{2,1,0:T(8,128)S(1)}, f32[13,8,128]{2,1,0:T(8,128)S(1)}, u32[]{:S(2)}, u32[]{:S(2)}) %collective-permute-start.7) | collective-permute-done | bytes 53280 | tf_op jit(solution)/shard_map/ppermute | solution.py:500
  21.6 0.9 collective-permute-done.8.rest_2_
  23.2 11.6 %all_to_all.20.rest_4_ = f32[32,1,128]{2,1,0:T(1,128)S(1)} all-to-all(f32[32,1,128]{2,1,0:T(1,128)S(1)} %get-tuple-element.93), channel_id=1, replica_groups=mesh['group'=4,'sub'=8] {'group','sub'}, dimensions={0} | all-to-all | bytes 32768 | tf_op jit(solution)/shard_map/all_to_all | solution.py:581
  34.8 1.3 %shard_map.112 = (f32[16,8,256]{2,1,0:T(8,128)S(1)}, f32[16,8,256]{2,1,0:T(8,128)S(1)}, f32[8,128]{1,0:T(8,128)S(1)}, f32[16,8,256]{2,1,0:T(8,128)S(1)}, bf16[16...) custom-call(s32[90]{0:T(128)S(4)} %get-tuple-element.71.table, ...), custom_call_target="tpu_custom_call" | custom-call | flops 600000000 | bytes 37500000 | tf_op jit(solution)/shard_map/pallas_call | solution.py:461
  36.2 1.1 %shard_map.113 = (f32[16,8,256]{2,1,0:T(8,128)S(1)}, f32[16,8,256]{2,1,0:T(8,128)S(1)}) custom-call(s32[90]{0:T(128)S(4)} %get-tuple-element.71.table, f32[16,8,256]{2,1,0:T(8,128)S(1)} %get-tuple-element.73.rest_0_.wide, bf16[16,256,256]{2,1,0:T(8,128)(2,1)S(1)} %get-tuple-element.74.rest_1_.diag, bf16[16,256,256]{2,1,0:T(8,128)(2,1)S(1)} %get-tuple-element.75.rest_2_.off, ...), custom_call_target="tpu_custom_call" | custom-call | flops 600000000 | bytes 37500000 | tf_op jit(solution)/shard_map/pallas_call | solution.py:461
  38.2 1.4 %collective-permute-start.12 = (f32[13,8,128]{2,1,0:T(8,128)S(1)}, f32[13,8,128]{2,1,0:T(8,128)S(1)}, u32[]{:S(2)}, u32[]{:S(2)}) collective-permute-start(f32[13,8,128]{2,1,0:T(8,128)S(1)} %get-tuple-element.104), channel_id=1, source_target_pairs={{0,2},{1,5},{2,0},{3,7},{4,6},{5,1},{6,4},{7,3},{8,10},{9,13},{10,... | collective-permute-start | bytes 159752 | tf_op jit(solution)/shard_map/ppermute | solution.py:500
  39.6 1.5 %collective-permute-start.13 = (f32[13,8,128]{2,1,0:T(8,128)S(1)}, f32[13,8,128]{2,1,0:T(8,128)S(1)}, u32[]{:S(2)}, u32[]{:S(2)}) collective-permute-start(f32[13,8,128]{2,1,0:T(8,128)S(1)} %get-tuple-element.105), channel_id=1, source_target_pairs={{0,4},{1,7},{2,6},{3,5},{4,0},{5,3},{6,2},{7,1},{8,12},{9,15},{10,... | collective-permute-start | bytes 159752 | tf_op jit(solution)/shard_map/ppermute | solution.py:500
  41.1 2.1 %collective-permute-done.11.rest_1_ = f32[13,8,128]{2,1,0:T(8,128)S(1)} collective-permute-done((f32[13,8,128]{2,1,0:T(8,128)S(1)}, f32[13,8,128]{2,1,0:T(8,128)S(1)}, u32[]{:S(2)}, u32[]{:S(2)}) %collective-permute-start.11) | collective-permute-done | bytes 53280 | tf_op jit(solution)/shard_map/ppermute | solution.py:500
  44.4 9.2 %all_to_all.21.rest_4_ = f32[32,1,128]{2,1,0:T(1,128)S(1)} all-to-all(f32[32,1,128]{2,1,0:T(1,128)S(1)} %get-tuple-element.107), channel_id=1, replica_groups=mesh['group'=4,'sub'=8] {'group','sub'}, dimensions={0} | all-to-all | bytes 32768 | tf_op jit(solution)/shard_map/all_to_all | solution.py:581
  53.6 1.2 %shard_map.116 = (f32[16,8,256]{2,1,0:T(8,128)S(1)}, f32[16,8,256]{2,1,0:T(8,128)S(1)}, f32[8,128]{1,0:T(8,128)S(1)}, f32[16,8,256]{2,1,0:T(8,128)S(1)}, bf16[16...) custom-call(s32[90]{0:T(128)S(4)} %get-tuple-element.71.table, ...), custom_call_target="tpu_custom_call" | custom-call | flops 600000000 | bytes 37500000 | tf_op jit(solution)/shard_map/pallas_call | solution.py:461
  54.9 1.1 %shard_map.117 = (f32[16,8,256]{2,1,0:T(8,128)S(1)}, f32[16,8,256]{2,1,0:T(8,128)S(1)}) custom-call(s32[90]{0:T(128)S(4)} %get-tuple-element.71.table, f32[16,8,256]{2,1,0:T(8,128)S(1)} %get-tuple-element.73.rest_0_.wide, bf16[16,256,256]{2,1,0:T(8,128)(2,1)S(1)} %get-tuple-element.74.rest_1_.diag, bf16[16,256,256]{2,1,0:T(8,128)(2,1)S(1)} %get-tuple-element.75.rest_2_.off, ...), custom_call_target="tpu_custom_call" | custom-call | flops 600000000 | bytes 37500000 | tf_op jit(solution)/shard_map/pallas_call | solution.py:461
  56.8 1.4 %collective-permute-start.17 = (f32[13,8,128]{2,1,0:T(8,128)S(1)}, f32[13,8,128]{2,1,0:T(8,128)S(1)}, u32[]{:S(2)}, u32[]{:S(2)}) collective-permute-start(f32[13,8,128]{2,1,0:T(8,128)S(1)} %get-tuple-element.119), channel_id=1, source_target_pairs={{0,2},{1,5},{2,0},{3,7},{4,6},{5,1},{6,4},{7,3},{8,10},{9,13},{10,... | collective-permute-start | bytes 159752 | tf_op jit(solution)/shard_map/ppermute | solution.py:500
  58.2 1.5 %collective-permute-start.18 = (f32[13,8,128]{2,1,0:T(8,128)S(1)}, f32[13,8,128]{2,1,0:T(8,128)S(1)}, u32[]{:S(2)}, u32[]{:S(2)}) collective-permute-start(f32[13,8,128]{2,1,0:T(8,128)S(1)} %get-tuple-element.120), channel_id=1, source_target_pairs={{0,4},{1,7},{2,6},{3,5},{4,0},{5,3},{6,2},{7,1},{8,12},{9,15},{10,... | collective-permute-start | bytes 159752 | tf_op jit(solution)/shard_map/ppermute | solution.py:500
  59.7 2.1 %collective-permute-done.16.rest_1_ = f32[13,8,128]{2,1,0:T(8,128)S(1)} collective-permute-done((f32[13,8,128]{2,1,0:T(8,128)S(1)}, f32[13,8,128]{2,1,0:T(8,128)S(1)}, u32[]{:S(2)}, u32[]{:S(2)}) %collective-permute-start.16) | collective-permute-done | bytes 53280 | tf_op jit(solution)/shard_map/ppermute | solution.py:500
  63.1 9.2 %all_to_all.22.rest_4_ = f32[32,1,128]{2,1,0:T(1,128)S(1)} all-to-all(f32[32,1,128]{2,1,0:T(1,128)S(1)} %get-tuple-element.122), channel_id=1, replica_groups=mesh['group'=4,'sub'=8] {'group','sub'}, dimensions={0} | all-to-all | bytes 32768 | tf_op jit(solution)/shard_map/all_to_all | solution.py:581
  72.3 1.2 %shard_map.120 = (f32[16,8,256]{2,1,0:T(8,128)S(1)}, f32[16,8,256]{2,1,0:T(8,128)S(1)}, f32[8,128]{1,0:T(8,128)S(1)}, f32[16,8,256]{2,1,0:T(8,128)S(1)}, bf16[16...) custom-call(s32[90]{0:T(128)S(4)} %get-tuple-element.71.table, ...), custom_call_target="tpu_custom_call" | custom-call | flops 600000000 | bytes 37500000 | tf_op jit(solution)/shard_map/pallas_call | solution.py:461
  73.5 1.1 %shard_map.121 = (f32[16,8,256]{2,1,0:T(8,128)S(1)}, f32[16,8,256]{2,1,0:T(8,128)S(1)}) custom-call(s32[90]{0:T(128)S(4)} %get-tuple-element.71.table, f32[16,8,256]{2,1,0:T(8,128)S(1)} %get-tuple-element.73.rest_0_.wide, bf16[16,256,256]{2,1,0:T(8,128)(2,1)S(1)} %get-tuple-element.74.rest_1_.diag, bf16[16,256,256]{2,1,0:T(8,128)(2,1)S(1)} %get-tuple-element.75.rest_2_.off, ...), custom_call_target="tpu_custom_call" | custom-call | flops 600000000 | bytes 37500000 | tf_op jit(solution)/shard_map/pallas_call | solution.py:461
  75.5 1.4 %collective-permute-start.22 = (f32[13,8,128]{2,1,0:T(8,128)S(1)}, f32[13,8,128]{2,1,0:T(8,128)S(1)}, u32[]{:S(2)}, u32[]{:S(2)}) collective-permute-start(f32[13,8,128]{2,1,0:T(8,128)S(1)} %get-tuple-element.134), channel_id=1, source_target_pairs={{0,2},{1,5},{2,0},{3,7},{4,6},{5,1},{6,4},{7,3},{8,10},{9,13},{10,... | collective-permute-start | bytes 159752 | tf_op jit(solution)/shard_map/ppermute | solution.py:500
  76.9 1.5 %collective-permute-start.23 = (f32[13,8,128]{2,1,0:T(8,128)S(1)}, f32[13,8,128]{2,1,0:T(8,128)S(1)}, u32[]{:S(2)}, u32[]{:S(2)}) collective-permute-start(f32[13,8,128]{2,1,0:T(8,128)S(1)} %get-tuple-element.135), channel_id=1, source_target_pairs={{0,4},{1,7},{2,6},{3,5},{4,0},{5,3},{6,2},{7,1},{8,12},{9,15},{10,... | collective-permute-start | bytes 159752 | tf_op jit(solution)/shard_map/ppermute | solution.py:500
  78.4 2.1 %collective-permute-done.21.rest_1_ = f32[13,8,128]{2,1,0:T(8,128)S(1)} collective-permute-done((f32[13,8,128]{2,1,0:T(8,128)S(1)}, f32[13,8,128]{2,1,0:T(8,128)S(1)}, u32[]{:S(2)}, u32[]{:S(2)}) %collective-permute-start.21) | collective-permute-done | bytes 53280 | tf_op jit(solution)/shard_map/ppermute | solution.py:500
  81.7 9.2 %all_to_all.23.gathered = f32[32,1,128]{2,1,0:T(1,128)S(1)} all-to-all(f32[32,1,128]{2,1,0:T(1,128)S(1)} %get-tuple-element.137), channel_id=1, replica_groups=mesh['group'=4,'sub'=8] {'group','sub'}, dimensions={0} | all-to-all | bytes 32768 | tf_op jit(solution)/shard_map/all_to_all | solution.py:581
  91.0 1.0 %shard_map.124 = (f32[8,16,256]{2,1,0:T(8,128)}, f32[8,16,256]{2,1,0:T(8,128)}) custom-call(f32[32,1,128]{2,1,0:T(1,128)S(1)} %all_to_all.23.gathered, f32[16,8,256]{2,1,0:T(8,128)S(1)} %get-tuple-element.138.before, f32[16,8,256]{2,1,0:T(8,128)S(1)} %get-tuple-element.130.residual.residual_in, f32[16,8,256]{2,1,0:T(8,128)S(1)} %get-tuple-element.131.direction, ...), custom_call_target="tpu_custom_call" | custom-call | flops 4000000 | bytes 250000 | tf_op jit(solution)/shard_map/pallas_call | solution.py:461
  (43 shorter events, 10.7 us)
Async XLA Ops:
  1.7 1.5 %collective-permute-start = (f32[36,8,128]{2,1,0:T(8,128)S(1)}, f32[36,8,128]{2,1,0:T(8,128)S(1)}, u32[]{:S(2)}, u32[]{:S(2)}) collective-permute-start(f32[36,8,128]{2,1,0:T(8,128)S(1)} %get-tuple-element.79), channel_id=1, source_target_pairs={{0,1},{1,0},{2,3},{3,2},{4,5},{5,4},{6,7},{7,6},{8,9},{9,8},{10,11... | collective-permute-start | bytes 442376 | tf_op jit(solution)/shard_map/ppermute | solution.py:500
  3.2 7.3 %collective-permute-start.1 = (f32[24,8,128]{2,1,0:T(8,128)S(1)}, f32[24,8,128]{2,1,0:T(8,128)S(1)}, u32[]{:S(2)}, u32[]{:S(2)}) collective-permute-start(f32[24,8,128]{2,1,0:T(8,128)S(1)} %get-tuple-element.80), channel_id=1, source_target_pairs={{0,6},{1,3},{2,4},{3,1},{4,2},{5,7},{6,0},{7,5},{8,14},{9,11},{10,... | collective-permute-start | bytes 294920 | tf_op jit(solution)/shard_map/ppermute | solution.py:500
  7.1 5.3 %collective-permute-start.2 = (f32[24,8,128]{2,1,0:T(8,128)S(1)}, f32[24,8,128]{2,1,0:T(8,128)S(1)}, u32[]{:S(2)}, u32[]{:S(2)}) collective-permute-start(f32[24,8,128]{2,1,0:T(8,128)S(1)} %get-tuple-element.81), channel_id=1, source_target_pairs={{0,2},{1,5},{2,0},{3,7},{4,6},{5,1},{6,4},{7,3},{8,10},{9,13},{10,... | collective-permute-start | bytes 294920 | tf_op jit(solution)/shard_map/ppermute | solution.py:500
  7.7 5.4 %collective-permute-start.3 = (f32[24,8,128]{2,1,0:T(8,128)S(1)}, f32[24,8,128]{2,1,0:T(8,128)S(1)}, u32[]{:S(2)}, u32[]{:S(2)}) collective-permute-start(f32[24,8,128]{2,1,0:T(8,128)S(1)} %get-tuple-element.82), channel_id=1, source_target_pairs={{0,4},{1,7},{2,6},{3,5},{4,0},{5,3},{6,2},{7,1},{8,12},{9,15},{10,... | collective-permute-start | bytes 294920 | tf_op jit(solution)/shard_map/ppermute | solution.py:500
  7.8 5.3 %collective-permute-start.4 = (f32[24,8,128]{2,1,0:T(8,128)S(1)}, f32[24,8,128]{2,1,0:T(8,128)S(1)}, u32[]{:S(2)}, u32[]{:S(2)}) collective-permute-start(f32[24,8,128]{2,1,0:T(8,128)S(1)} %get-tuple-element.83), channel_id=1, source_target_pairs={{0,1},{1,0},{2,3},{3,2},{4,5},{5,4},{6,7},{7,6},{8,9},{9,8},{10,11... | collective-permute-start | bytes 294920 | tf_op jit(solution)/shard_map/ppermute | solution.py:500
  14.2 1.3 %collective-permute-start.5 = (f32[19,8,128]{2,1,0:T(8,128)S(1)}, f32[19,8,128]{2,1,0:T(8,128)S(1)}, u32[]{:S(2)}, u32[]{:S(2)}) collective-permute-start(f32[19,8,128]{2,1,0:T(8,128)S(1)} %get-tuple-element.88), channel_id=1, source_target_pairs={{0,1},{1,0},{2,3},{3,2},{4,5},{5,4},{6,7},{7,6},{8,9},{9,8},{10,11... | collective-permute-start | bytes 233480 | tf_op jit(solution)/shard_map/ppermute | solution.py:500
  15.5 5.1 %collective-permute-start.6 = (f32[13,8,128]{2,1,0:T(8,128)S(1)}, f32[13,8,128]{2,1,0:T(8,128)S(1)}, u32[]{:S(2)}, u32[]{:S(2)}) collective-permute-start(f32[13,8,128]{2,1,0:T(8,128)S(1)} %get-tuple-element.89), channel_id=1, source_target_pairs={{0,6},{1,3},{2,4},{3,1},{4,2},{5,7},{6,0},{7,5},{8,14},{9,11},{10,... | collective-permute-start | bytes 159752 | tf_op jit(solution)/shard_map/ppermute | solution.py:500
  16.8 4.7 %collective-permute-start.7 = (f32[13,8,128]{2,1,0:T(8,128)S(1)}, f32[13,8,128]{2,1,0:T(8,128)S(1)}, u32[]{:S(2)}, u32[]{:S(2)}) collective-permute-start(f32[13,8,128]{2,1,0:T(8,128)S(1)} %get-tuple-element.90), channel_id=1, source_target_pairs={{0,2},{1,5},{2,0},{3,7},{4,6},{5,1},{6,4},{7,3},{8,10},{9,13},{10,... | collective-permute-start | bytes 159752 | tf_op jit(solution)/shard_map/ppermute | solution.py:500
  18.3 4.1 %collective-permute-start.8 = (f32[13,8,128]{2,1,0:T(8,128)S(1)}, f32[13,8,128]{2,1,0:T(8,128)S(1)}, u32[]{:S(2)}, u32[]{:S(2)}) collective-permute-start(f32[13,8,128]{2,1,0:T(8,128)S(1)} %get-tuple-element.91), channel_id=1, source_target_pairs={{0,4},{1,7},{2,6},{3,5},{4,0},{5,3},{6,2},{7,1},{8,12},{9,15},{10,... | collective-permute-start | bytes 159752 | tf_op jit(solution)/shard_map/ppermute | solution.py:500
  19.1 3.4 %collective-permute-start.9 = (f32[13,8,128]{2,1,0:T(8,128)S(1)}, f32[13,8,128]{2,1,0:T(8,128)S(1)}, u32[]{:S(2)}, u32[]{:S(2)}) collective-permute-start(f32[13,8,128]{2,1,0:T(8,128)S(1)} %get-tuple-element.92), channel_id=1, source_target_pairs={{0,1},{1,0},{2,3},{3,2},{4,5},{5,4},{6,7},{7,6},{8,9},{9,8},{10,11... | collective-permute-start | bytes 159752 | tf_op jit(solution)/shard_map/ppermute | solution.py:500
  36.2 1.3 %collective-permute-start.10 = (f32[19,8,128]{2,1,0:T(8,128)S(1)}, f32[19,8,128]{2,1,0:T(8,128)S(1)}, u32[]{:S(2)}, u32[]{:S(2)}) collective-permute-start(f32[19,8,128]{2,1,0:T(8,128)S(1)} %get-tuple-element.102), channel_id=1, source_target_pairs={{0,1},{1,0},{2,3},{3,2},{4,5},{5,4},{6,7},{7,6},{8,9},{9,8},{10,11... | collective-permute-start | bytes 233480 | tf_op jit(solution)/shard_map/ppermute | solution.py:500
  37.5 5.7 %collective-permute-start.11 = (f32[13,8,128]{2,1,0:T(8,128)S(1)}, f32[13,8,128]{2,1,0:T(8,128)S(1)}, u32[]{:S(2)}, u32[]{:S(2)}) collective-permute-start(f32[13,8,128]{2,1,0:T(8,128)S(1)} %get-tuple-element.103), channel_id=1, source_target_pairs={{0,6},{1,3},{2,4},{3,1},{4,2},{5,7},{6,0},{7,5},{8,14},{9,11},{10,... | collective-permute-start | bytes 159752 | tf_op jit(solution)/shard_map/ppermute | solution.py:500
  38.2 5.0 %collective-permute-start.12 = (f32[13,8,128]{2,1,0:T(8,128)S(1)}, f32[13,8,128]{2,1,0:T(8,128)S(1)}, u32[]{:S(2)}, u32[]{:S(2)}) collective-permute-start(f32[13,8,128]{2,1,0:T(8,128)S(1)} %get-tuple-element.104), channel_id=1, source_target_pairs={{0,2},{1,5},{2,0},{3,7},{4,6},{5,1},{6,4},{7,3},{8,10},{9,13},{10,... | collective-permute-start | bytes 159752 | tf_op jit(solution)/shard_map/ppermute | solution.py:500
  39.6 4.1 %collective-permute-start.13 = (f32[13,8,128]{2,1,0:T(8,128)S(1)}, f32[13,8,128]{2,1,0:T(8,128)S(1)}, u32[]{:S(2)}, u32[]{:S(2)}) collective-permute-start(f32[13,8,128]{2,1,0:T(8,128)S(1)} %get-tuple-element.105), channel_id=1, source_target_pairs={{0,4},{1,7},{2,6},{3,5},{4,0},{5,3},{6,2},{7,1},{8,12},{9,15},{10,... | collective-permute-start | bytes 159752 | tf_op jit(solution)/shard_map/ppermute | solution.py:500
  41.0 2.7 %collective-permute-start.14 = (f32[13,8,128]{2,1,0:T(8,128)S(1)}, f32[13,8,128]{2,1,0:T(8,128)S(1)}, u32[]{:S(2)}, u32[]{:S(2)}) collective-permute-start(f32[13,8,128]{2,1,0:T(8,128)S(1)} %get-tuple-element.106), channel_id=1, source_target_pairs={{0,1},{1,0},{2,3},{3,2},{4,5},{5,4},{6,7},{7,6},{8,9},{9,8},{10,11... | collective-permute-start | bytes 159752 | tf_op jit(solution)/shard_map/ppermute | solution.py:500
  54.9 1.3 %collective-permute-start.15 = (f32[19,8,128]{2,1,0:T(8,128)S(1)}, f32[19,8,128]{2,1,0:T(8,128)S(1)}, u32[]{:S(2)}, u32[]{:S(2)}) collective-permute-start(f32[19,8,128]{2,1,0:T(8,128)S(1)} %get-tuple-element.117), channel_id=1, source_target_pairs={{0,1},{1,0},{2,3},{3,2},{4,5},{5,4},{6,7},{7,6},{8,9},{9,8},{10,11... | collective-permute-start | bytes 233480 | tf_op jit(solution)/shard_map/ppermute | solution.py:500
  56.2 5.7 %collective-permute-start.16 = (f32[13,8,128]{2,1,0:T(8,128)S(1)}, f32[13,8,128]{2,1,0:T(8,128)S(1)}, u32[]{:S(2)}, u32[]{:S(2)}) collective-permute-start(f32[13,8,128]{2,1,0:T(8,128)S(1)} %get-tuple-element.118), channel_id=1, source_target_pairs={{0,6},{1,3},{2,4},{3,1},{4,2},{5,7},{6,0},{7,5},{8,14},{9,11},{10,... | collective-permute-start | bytes 159752 | tf_op jit(solution)/shard_map/ppermute | solution.py:500
  56.8 5.0 %collective-permute-start.17 = (f32[13,8,128]{2,1,0:T(8,128)S(1)}, f32[13,8,128]{2,1,0:T(8,128)S(1)}, u32[]{:S(2)}, u32[]{:S(2)}) collective-permute-start(f32[13,8,128]{2,1,0:T(8,128)S(1)} %get-tuple-element.119), channel_id=1, source_target_pairs={{0,2},{1,5},{2,0},{3,7},{4,6},{5,1},{6,4},{7,3},{8,10},{9,13},{10,... | collective-permute-start | bytes 159752 | tf_op jit(solution)/shard_map/ppermute | solution.py:500
  58.2 4.1 %collective-permute-start.18 = (f32[13,8,128]{2,1,0:T(8,128)S(1)}, f32[13,8,128]{2,1,0:T(8,128)S(1)}, u32[]{:S(2)}, u32[]{:S(2)}) collective-permute-start(f32[13,8,128]{2,1,0:T(8,128)S(1)} %get-tuple-element.120), channel_id=1, source_target_pairs={{0,4},{1,7},{2,6},{3,5},{4,0},{5,3},{6,2},{7,1},{8,12},{9,15},{10,... | collective-permute-start | bytes 159752 | tf_op jit(solution)/shard_map/ppermute | solution.py:500
  59.7 2.7 %collective-permute-start.19 = (f32[13,8,128]{2,1,0:T(8,128)S(1)}, f32[13,8,128]{2,1,0:T(8,128)S(1)}, u32[]{:S(2)}, u32[]{:S(2)}) collective-permute-start(f32[13,8,128]{2,1,0:T(8,128)S(1)} %get-tuple-element.121), channel_id=1, source_target_pairs={{0,1},{1,0},{2,3},{3,2},{4,5},{5,4},{6,7},{7,6},{8,9},{9,8},{10,11... | collective-permute-start | bytes 159752 | tf_op jit(solution)/shard_map/ppermute | solution.py:500
  73.5 1.3 %collective-permute-start.20 = (f32[19,8,128]{2,1,0:T(8,128)S(1)}, f32[19,8,128]{2,1,0:T(8,128)S(1)}, u32[]{:S(2)}, u32[]{:S(2)}) collective-permute-start(f32[19,8,128]{2,1,0:T(8,128)S(1)} %get-tuple-element.132), channel_id=1, source_target_pairs={{0,1},{1,0},{2,3},{3,2},{4,5},{5,4},{6,7},{7,6},{8,9},{9,8},{10,11... | collective-permute-start | bytes 233480 | tf_op jit(solution)/shard_map/ppermute | solution.py:500
  74.8 5.7 %collective-permute-start.21 = (f32[13,8,128]{2,1,0:T(8,128)S(1)}, f32[13,8,128]{2,1,0:T(8,128)S(1)}, u32[]{:S(2)}, u32[]{:S(2)}) collective-permute-start(f32[13,8,128]{2,1,0:T(8,128)S(1)} %get-tuple-element.133), channel_id=1, source_target_pairs={{0,6},{1,3},{2,4},{3,1},{4,2},{5,7},{6,0},{7,5},{8,14},{9,11},{10,... | collective-permute-start | bytes 159752 | tf_op jit(solution)/shard_map/ppermute | solution.py:500
  75.5 5.0 %collective-permute-start.22 = (f32[13,8,128]{2,1,0:T(8,128)S(1)}, f32[13,8,128]{2,1,0:T(8,128)S(1)}, u32[]{:S(2)}, u32[]{:S(2)}) collective-permute-start(f32[13,8,128]{2,1,0:T(8,128)S(1)} %get-tuple-element.134), channel_id=1, source_target_pairs={{0,2},{1,5},{2,0},{3,7},{4,6},{5,1},{6,4},{7,3},{8,10},{9,13},{10,... | collective-permute-start | bytes 159752 | tf_op jit(solution)/shard_map/ppermute | solution.py:500
  76.9 4.1 %collective-permute-start.23 = (f32[13,8,128]{2,1,0:T(8,128)S(1)}, f32[13,8,128]{2,1,0:T(8,128)S(1)}, u32[]{:S(2)}, u32[]{:S(2)}) collective-permute-start(f32[13,8,128]{2,1,0:T(8,128)S(1)} %get-tuple-element.135), channel_id=1, source_target_pairs={{0,4},{1,7},{2,6},{3,5},{4,0},{5,3},{6,2},{7,1},{8,12},{9,15},{10,... | collective-permute-start | bytes 159752 | tf_op jit(solution)/shard_map/ppermute | solution.py:500
  78.4 2.7 %collective-permute-start.24 = (f32[13,8,128]{2,1,0:T(8,128)S(1)}, f32[13,8,128]{2,1,0:T(8,128)S(1)}, u32[]{:S(2)}, u32[]{:S(2)}) collective-permute-start(f32[13,8,128]{2,1,0:T(8,128)S(1)} %get-tuple-element.136), channel_id=1, source_target_pairs={{0,1},{1,0},{2,3},{3,2},{4,5},{5,4},{6,7},{7,6},{8,9},{9,8},{10,11... | collective-permute-start | bytes 159752 | tf_op jit(solution)/shard_map/ppermute | solution.py:500

commit v13 on v11

--- a/solution.py
+++ b/solution.py
@@ -76,7 +76,7 @@
         self.count = self.order + self.blocks + 1
         self.table = self.count + 1
         most = len(self.far) * self.capacity
-        self.early = min(-(-most * 7 // 8), self.blocks)
+        self.early = min(-(-most * 3 // 4), self.blocks)
         self.middle = max(self.early, min(most, self.blocks))
 
     def rows(self, kinds):
@@ -358,9 +358,10 @@
         i = table[z.order + position]
         image[i] = couple(z, i, *refs)
 
-    @pl.when(table[z.count] > z.early)
-    def _():
-        for position in range(z.early, z.middle):
+    for position in range(z.early, z.middle):
+
+        @pl.when(table[z.count] > position)
+        def _():
             i = table[z.order + position]
             image[i] = couple(z, i, *refs)
 
@@ -385,9 +386,10 @@
     for i in range(z.blocks):
         image[i] = image_in[i]
 
-    @pl.when(table[z.count] <= z.early)
-    def _():
-        for position in range(z.early, z.middle):
+    for position in range(z.early, z.middle):
+
+        @pl.when(table[z.count] <= position)
+        def _():
             i = table[z.order + position]
             image[i] = couple(z, i, *refs)
 
@@ -579,7 +581,7 @@
             [table, operator, image, own_extra, jump_lift, residual, direction, near]
             + [alpha] * (step > 0) + arrived,
         )
-        gathered = lax.all_to_all(sent, ("group", "sub"), 0, 0, tiled=True)
+        gathered = lax.all_to_all(sent, ("sub", "group"), 0, 0, tiled=True)
     multipliers, residual = call(
         kernel(finish), [(load.shape, F32)] * 2, [], light,
         [gathered, multipliers, residual, direction, product, alpha], False,

time: 91.1 us -> 91.1 us (level)
  transfers between devices with their start and end apart: 25 -> 25, of which waited for: 16 -> 12; matrix products, arithmetic and copies ran while one was open for 0% -> 0% of each run, Pallas kernels for 7% -> 8%
where the time goes in v13:
time: 91.1 us; the launch traced here: 90.9 us
  blocking collectives  38.5 us (42%)
  starting transfers between devices  19.3 us (21%)
  Pallas kernels  17.3 us (19%)
  waiting for transfers between devices  15 us (16%)
    all_to_all x4, blocking collectives, on_device(): gathered = lax.all_to_all(sent, ('sub', 'group'), 0, 0, tiled=True)  38.5 us
    ppermute x25, starting transfers between devices, across(): return lax.ppermute(piece, 'sub', pairs)  19.3 us
    pallas_call x21, Pallas kernels, call(): pl.pallas_call(body, out_shape=shapes, in_specs=specs, out_specs=[SMEM if...  17.3 us
    ppermute x25, waiting for transfers between devices, across(): return lax.ppermute(piece, 'sub', pairs)  15 us
  transfers between devices with their start and end apart: 25, of which 12 were waited for; matrix products, arithmetic and copies ran while one was open for 0% of the time, Pallas kernels for 8%

profile of v13, /device:TPU:0, one launch (start us, length us, event | category | flops | bytes accessed | tf_op | source)
XLA Modules:
  0.0 90.9 jit_solution(8977431116598969064)
XLA Ops:
  0.6 1.0 %shard_map.104 = (s32[90]{0:T(128)S(4)}, f32[16,8,256]{2,1,0:T(8,128)S(1)}, f32[16,8,256]{2,1,0:T(8,128)S(1)}, f32[16,8,256]{2,1,0:T(8,128)S(1)}, bf16[16,16,256...) custom-call(s32[1,16]{1,0:T(1,128)} %partner.1, s32[1,16]{1,0:T(1,128)} %pattern.1, f32[8,16,256]{2,1,0:T(8,128)} %load.1, ...), custom_call_target="tpu_custom_call" | custom-call | flops 4000000 | bytes 250000 | tf_op jit(solution)/shard_map/pallas_call | solution.py:464
  2.2 1.0 %collective-permute-done.rest_2_ = f32[36,8,128]{2,1,0:T(8,128)S(1)} collective-permute-done((f32[36,8,128]{2,1,0:T(8,128)S(1)}, f32[36,8,128]{2,1,0:T(8,128)S(1)}, u32[]{:S(2)}, u32[]{:S(2)}) %collective-permute-start) | collective-permute-done | bytes 147488 | tf_op jit(solution)/shard_map/ppermute | solution.py:503
  3.3 3.9 %collective-permute-start.1 = (f32[24,8,128]{2,1,0:T(8,128)S(1)}, f32[24,8,128]{2,1,0:T(8,128)S(1)}, u32[]{:S(2)}, u32[]{:S(2)}) collective-permute-start(f32[24,8,128]{2,1,0:T(8,128)S(1)} %get-tuple-element.80), channel_id=1, source_target_pairs={{0,6},{1,7},{2,4},{3,5},{4,2},{5,3},{6,0},{7,1},{8,14},{9,15},{10,... | collective-permute-start | bytes 294920 | tf_op jit(solution)/shard_map/ppermute | solution.py:503
  7.8 2.3 %shard_map.105 = (f32[64,64]{1,0:T(8,128)S(1)}, bf16[16,256,256]{2,1,0:T(8,128)(2,1)S(1)}, bf16[16,256,256]{2,1,0:T(8,128)(2,1)S(1)}) custom-call(s32[1,64]{1,0:T(1,128)} %index_in.1, f32[32,32]{1,0:T(8,128)} %inverse_in.1, bf16[16,256,256]{2,1,0:T(8,128)(2,1)} %diag.1, bf16[16,256,256]{2,1,0:T(8,128)(2,1)} %off.1), custom_call_target="tpu_custom_call" | custom-call | flops 600000000 | bytes 37500000 | tf_op jit(solution)/shard_map/pallas_call | solution.py:464
  10.3 2.3 %collective-permute-done.2.rest_5_.rest_1_ = f32[24,8,128]{2,1,0:T(8,128)S(1)} collective-permute-done((f32[24,8,128]{2,1,0:T(8,128)S(1)}, f32[24,8,128]{2,1,0:T(8,128)S(1)}, u32[]{:S(2)}, u32[]{:S(2)}) %collective-permute-start.2) | collective-permute-done | bytes 98336 | tf_op jit(solution)/shard_map/ppermute | solution.py:503
  12.6 1.0 %shard_map.107 = (f32[16,8,256]{2,1,0:T(8,128)S(1)}, f32[16,8,256]{2,1,0:T(8,128)S(1)}, bf16[16,16,256]{2,1,0:T(8,128)(2,1)S(1)}, f32[8,128]{1,0:T(8,128)S(1)}, f32[19,8,128]{2,1,0:T(8,128)S(1)}) custom-call(s32[90]{0:T(128)S(4)} %get-tuple-element.71.table, f32[16,8,256]{2,1,0:T(8,128)S(1)} %get-tuple-element.73.rest_0_.wide, ...), custom_call_target="tpu_custom_call" | custom-call | flops 600000000 | bytes 37500000 | tf_op jit(solution)/shard_map/pallas_call | solution.py:464
  13.7 1.3 %shard_map.108.rest_0_.image = f32[16,8,256]{2,1,0:T(8,128)S(1)} custom-call(s32[90]{0:T(128)S(4)} %get-tuple-element.71.table, f32[16,8,256]{2,1,0:T(8,128)S(1)} %get-tuple-element.73.rest_0_.wide, bf16[16,256,256]{2,1,0:T(8,128)(2,1)S(1)} %get-tuple-element.74.rest_1_.diag, bf16[16,256,256]{2,1,0:T(8,128)(2,1)S(1)} %get-tuple-element.75.rest_2_.off, ...), custom_call_target="tpu_custom_call" | custom-call | flops 600000000 | bytes 37500000 | tf_op jit(solution)/shard_map/pallas_call | solution.py:464
  15.0 1.7 %collective-permute-start.6 = (f32[13,8,128]{2,1,0:T(8,128)S(1)}, f32[13,8,128]{2,1,0:T(8,128)S(1)}, u32[]{:S(2)}, u32[]{:S(2)}) collective-permute-start(f32[13,8,128]{2,1,0:T(8,128)S(1)} %get-tuple-element.89), channel_id=1, source_target_pairs={{0,6},{1,7},{2,4},{3,5},{4,2},{5,3},{6,0},{7,1},{8,14},{9,15},{10,... | collective-permute-start | bytes 159752 | tf_op jit(solution)/shard_map/ppermute | solution.py:503
  16.7 1.3 %collective-permute-start.7 = (f32[13,8,128]{2,1,0:T(8,128)S(1)}, f32[13,8,128]{2,1,0:T(8,128)S(1)}, u32[]{:S(2)}, u32[]{:S(2)}) collective-permute-start(f32[13,8,128]{2,1,0:T(8,128)S(1)} %get-tuple-element.90), channel_id=1, source_target_pairs={{0,2},{1,5},{2,0},{3,7},{4,6},{5,1},{6,4},{7,3},{8,10},{9,13},{10,... | collective-permute-start | bytes 159752 | tf_op jit(solution)/shard_map/ppermute | solution.py:503
  18.8 1.5 %collective-permute-done.6.rest_0_ = f32[13,8,128]{2,1,0:T(8,128)S(1)} collective-permute-done((f32[13,8,128]{2,1,0:T(8,128)S(1)}, f32[13,8,128]{2,1,0:T(8,128)S(1)}, u32[]{:S(2)}, u32[]{:S(2)}) %collective-permute-start.6) | collective-permute-done | bytes 53280 | tf_op jit(solution)/shard_map/ppermute | solution.py:503
  20.3 0.8 collective-permute-done.7.rest_1_
  21.1 1.0 %collective-permute-done.8.rest_2_ = f32[13,8,128]{2,1,0:T(8,128)S(1)} collective-permute-done((f32[13,8,128]{2,1,0:T(8,128)S(1)}, f32[13,8,128]{2,1,0:T(8,128)S(1)}, u32[]{:S(2)}, u32[]{:S(2)}) %collective-permute-start.8) | collective-permute-done | bytes 53280 | tf_op jit(solution)/shard_map/ppermute | solution.py:503
  22.9 11.9 %all_to_all.20.rest_4_ = f32[32,1,128]{2,1,0:T(1,128)S(1)} all-to-all(f32[32,1,128]{2,1,0:T(1,128)S(1)} %get-tuple-element.93), channel_id=1, replica_groups=mesh['group'=4,'sub'=8] {'sub','group'}, dimensions={0} | all-to-all | bytes 32768 | tf_op jit(solution)/shard_map/all_to_all | solution.py:584
  34.8 1.2 %shard_map.112 = (f32[16,8,256]{2,1,0:T(8,128)S(1)}, f32[16,8,256]{2,1,0:T(8,128)S(1)}, f32[8,128]{1,0:T(8,128)S(1)}, f32[16,8,256]{2,1,0:T(8,128)S(1)}, bf16[16...) custom-call(s32[90]{0:T(128)S(4)} %get-tuple-element.71.table, ...), custom_call_target="tpu_custom_call" | custom-call | flops 600000000 | bytes 37500000 | tf_op jit(solution)/shard_map/pallas_call | solution.py:464
  36.1 1.3 %shard_map.113 = (f32[16,8,256]{2,1,0:T(8,128)S(1)}, f32[16,8,256]{2,1,0:T(8,128)S(1)}) custom-call(s32[90]{0:T(128)S(4)} %get-tuple-element.71.table, f32[16,8,256]{2,1,0:T(8,128)S(1)} %get-tuple-element.73.rest_0_.wide, bf16[16,256,256]{2,1,0:T(8,128)(2,1)S(1)} %get-tuple-element.74.rest_1_.diag, bf16[16,256,256]{2,1,0:T(8,128)(2,1)S(1)} %get-tuple-element.75.rest_2_.off, ...), custom_call_target="tpu_custom_call" | custom-call | flops 600000000 | bytes 37500000 | tf_op jit(solution)/shard_map/pallas_call | solution.py:464
  38.1 1.5 %collective-permute-start.12 = (f32[13,8,128]{2,1,0:T(8,128)S(1)}, f32[13,8,128]{2,1,0:T(8,128)S(1)}, u32[]{:S(2)}, u32[]{:S(2)}) collective-permute-start(f32[13,8,128]{2,1,0:T(8,128)S(1)} %get-tuple-element.104), channel_id=1, source_target_pairs={{0,2},{1,5},{2,0},{3,7},{4,6},{5,1},{6,4},{7,3},{8,10},{9,13},{10,... | collective-permute-start | bytes 159752 | tf_op jit(solution)/shard_map/ppermute | solution.py:503
  39.6 1.4 %collective-permute-start.13 = (f32[13,8,128]{2,1,0:T(8,128)S(1)}, f32[13,8,128]{2,1,0:T(8,128)S(1)}, u32[]{:S(2)}, u32[]{:S(2)}) collective-permute-start(f32[13,8,128]{2,1,0:T(8,128)S(1)} %get-tuple-element.105), channel_id=1, source_target_pairs={{0,4},{1,3},{2,6},{3,1},{4,0},{5,7},{6,2},{7,5},{8,12},{9,11},{10,... | collective-permute-start | bytes 159752 | tf_op jit(solution)/shard_map/ppermute | solution.py:503
  41.0 2.0 %collective-permute-done.11.rest_1_ = f32[13,8,128]{2,1,0:T(8,128)S(1)} collective-permute-done((f32[13,8,128]{2,1,0:T(8,128)S(1)}, f32[13,8,128]{2,1,0:T(8,128)S(1)}, u32[]{:S(2)}, u32[]{:S(2)}) %collective-permute-start.11) | collective-permute-done | bytes 53280 | tf_op jit(solution)/shard_map/ppermute | solution.py:503
  44.4 8.9 %all_to_all.21.rest_4_ = f32[32,1,128]{2,1,0:T(1,128)S(1)} all-to-all(f32[32,1,128]{2,1,0:T(1,128)S(1)} %get-tuple-element.107), channel_id=1, replica_groups=mesh['group'=4,'sub'=8] {'sub','group'}, dimensions={0} | all-to-all | bytes 32768 | tf_op jit(solution)/shard_map/all_to_all | solution.py:584
  53.3 1.1 %shard_map.116 = (f32[16,8,256]{2,1,0:T(8,128)S(1)}, f32[16,8,256]{2,1,0:T(8,128)S(1)}, f32[8,128]{1,0:T(8,128)S(1)}, f32[16,8,256]{2,1,0:T(8,128)S(1)}, bf16[16...) custom-call(s32[90]{0:T(128)S(4)} %get-tuple-element.71.table, ...), custom_call_target="tpu_custom_call" | custom-call | flops 600000000 | bytes 37500000 | tf_op jit(solution)/shard_map/pallas_call | solution.py:464
  54.4 1.3 %shard_map.117 = (f32[16,8,256]{2,1,0:T(8,128)S(1)}, f32[16,8,256]{2,1,0:T(8,128)S(1)}) custom-call(s32[90]{0:T(128)S(4)} %get-tuple-element.71.table, f32[16,8,256]{2,1,0:T(8,128)S(1)} %get-tuple-element.73.rest_0_.wide, bf16[16,256,256]{2,1,0:T(8,128)(2,1)S(1)} %get-tuple-element.74.rest_1_.diag, bf16[16,256,256]{2,1,0:T(8,128)(2,1)S(1)} %get-tuple-element.75.rest_2_.off, ...), custom_call_target="tpu_custom_call" | custom-call | flops 600000000 | bytes 37500000 | tf_op jit(solution)/shard_map/pallas_call | solution.py:464
  56.4 1.5 %collective-permute-start.17 = (f32[13,8,128]{2,1,0:T(8,128)S(1)}, f32[13,8,128]{2,1,0:T(8,128)S(1)}, u32[]{:S(2)}, u32[]{:S(2)}) collective-permute-start(f32[13,8,128]{2,1,0:T(8,128)S(1)} %get-tuple-element.119), channel_id=1, source_target_pairs={{0,2},{1,5},{2,0},{3,7},{4,6},{5,1},{6,4},{7,3},{8,10},{9,13},{10,... | collective-permute-start | bytes 159752 | tf_op jit(solution)/shard_map/ppermute | solution.py:503
  57.9 1.4 %collective-permute-start.18 = (f32[13,8,128]{2,1,0:T(8,128)S(1)}, f32[13,8,128]{2,1,0:T(8,128)S(1)}, u32[]{:S(2)}, u32[]{:S(2)}) collective-permute-start(f32[13,8,128]{2,1,0:T(8,128)S(1)} %get-tuple-element.120), channel_id=1, source_target_pairs={{0,4},{1,3},{2,6},{3,1},{4,0},{5,7},{6,2},{7,5},{8,12},{9,11},{10,... | collective-permute-start | bytes 159752 | tf_op jit(solution)/shard_map/ppermute | solution.py:503
  59.3 2.0 %collective-permute-done.16.rest_1_ = f32[13,8,128]{2,1,0:T(8,128)S(1)} collective-permute-done((f32[13,8,128]{2,1,0:T(8,128)S(1)}, f32[13,8,128]{2,1,0:T(8,128)S(1)}, u32[]{:S(2)}, u32[]{:S(2)}) %collective-permute-start.16) | collective-permute-done | bytes 53280 | tf_op jit(solution)/shard_map/ppermute | solution.py:503
  62.7 8.9 %all_to_all.22.rest_4_ = f32[32,1,128]{2,1,0:T(1,128)S(1)} all-to-all(f32[32,1,128]{2,1,0:T(1,128)S(1)} %get-tuple-element.122), channel_id=1, replica_groups=mesh['group'=4,'sub'=8] {'sub','group'}, dimensions={0} | all-to-all | bytes 32768 | tf_op jit(solution)/shard_map/all_to_all | solution.py:584
  71.6 1.1 %shard_map.120 = (f32[16,8,256]{2,1,0:T(8,128)S(1)}, f32[16,8,256]{2,1,0:T(8,128)S(1)}, f32[8,128]{1,0:T(8,128)S(1)}, f32[16,8,256]{2,1,0:T(8,128)S(1)}, bf16[16...) custom-call(s32[90]{0:T(128)S(4)} %get-tuple-element.71.table, ...), custom_call_target="tpu_custom_call" | custom-call | flops 600000000 | bytes 37500000 | tf_op jit(solution)/shard_map/pallas_call | solution.py:464
  72.7 1.3 %shard_map.121 = (f32[16,8,256]{2,1,0:T(8,128)S(1)}, f32[16,8,256]{2,1,0:T(8,128)S(1)}) custom-call(s32[90]{0:T(128)S(4)} %get-tuple-element.71.table, f32[16,8,256]{2,1,0:T(8,128)S(1)} %get-tuple-element.73.rest_0_.wide, bf16[16,256,256]{2,1,0:T(8,128)(2,1)S(1)} %get-tuple-element.74.rest_1_.diag, bf16[16,256,256]{2,1,0:T(8,128)(2,1)S(1)} %get-tuple-element.75.rest_2_.off, ...), custom_call_target="tpu_custom_call" | custom-call | flops 600000000 | bytes 37500000 | tf_op jit(solution)/shard_map/pallas_call | solution.py:464
  74.7 1.5 %collective-permute-start.22 = (f32[13,8,128]{2,1,0:T(8,128)S(1)}, f32[13,8,128]{2,1,0:T(8,128)S(1)}, u32[]{:S(2)}, u32[]{:S(2)}) collective-permute-start(f32[13,8,128]{2,1,0:T(8,128)S(1)} %get-tuple-element.134), channel_id=1, source_target_pairs={{0,2},{1,5},{2,0},{3,7},{4,6},{5,1},{6,4},{7,3},{8,10},{9,13},{10,... | collective-permute-start | bytes 159752 | tf_op jit(solution)/shard_map/ppermute | solution.py:503
  76.2 1.4 %collective-permute-start.23 = (f32[13,8,128]{2,1,0:T(8,128)S(1)}, f32[13,8,128]{2,1,0:T(8,128)S(1)}, u32[]{:S(2)}, u32[]{:S(2)}) collective-permute-start(f32[13,8,128]{2,1,0:T(8,128)S(1)} %get-tuple-element.135), channel_id=1, source_target_pairs={{0,4},{1,3},{2,6},{3,1},{4,0},{5,7},{6,2},{7,5},{8,12},{9,11},{10,... | collective-permute-start | bytes 159752 | tf_op jit(solution)/shard_map/ppermute | solution.py:503
  77.7 2.0 %collective-permute-done.21.rest_1_ = f32[13,8,128]{2,1,0:T(8,128)S(1)} collective-permute-done((f32[13,8,128]{2,1,0:T(8,128)S(1)}, f32[13,8,128]{2,1,0:T(8,128)S(1)}, u32[]{:S(2)}, u32[]{:S(2)}) %collective-permute-start.21) | collective-permute-done | bytes 53280 | tf_op jit(solution)/shard_map/ppermute | solution.py:503
  81.0 8.9 %all_to_all.23.gathered = f32[32,1,128]{2,1,0:T(1,128)S(1)} all-to-all(f32[32,1,128]{2,1,0:T(1,128)S(1)} %get-tuple-element.137), channel_id=1, replica_groups=mesh['group'=4,'sub'=8] {'sub','group'}, dimensions={0} | all-to-all | bytes 32768 | tf_op jit(solution)/shard_map/all_to_all | solution.py:584
  89.9 1.0 %shard_map.124 = (f32[8,16,256]{2,1,0:T(8,128)}, f32[8,16,256]{2,1,0:T(8,128)}) custom-call(f32[32,1,128]{2,1,0:T(1,128)S(1)} %all_to_all.23.gathered, f32[16,8,256]{2,1,0:T(8,128)S(1)} %get-tuple-element.138.before, f32[16,8,256]{2,1,0:T(8,128)S(1)} %get-tuple-element.130.residual.residual_in, f32[16,8,256]{2,1,0:T(8,128)S(1)} %get-tuple-element.131.direction, ...), custom_call_target="tpu_custom_call" | custom-call | flops 4000000 | bytes 250000 | tf_op jit(solution)/shard_map/pallas_call | solution.py:464
  (43 shorter events, 9.1 us)
Async XLA Ops:
  1.7 1.5 %collective-permute-start = (f32[36,8,128]{2,1,0:T(8,128)S(1)}, f32[36,8,128]{2,1,0:T(8,128)S(1)}, u32[]{:S(2)}, u32[]{:S(2)}) collective-permute-start(f32[36,8,128]{2,1,0:T(8,128)S(1)} %get-tuple-element.79), channel_id=1, source_target_pairs={{0,1},{1,0},{2,3},{3,2},{4,5},{5,4},{6,7},{7,6},{8,9},{9,8},{10,11... | collective-permute-start | bytes 442376 | tf_op jit(solution)/shard_map/ppermute | solution.py:503
  3.3 7.1 %collective-permute-start.1 = (f32[24,8,128]{2,1,0:T(8,128)S(1)}, f32[24,8,128]{2,1,0:T(8,128)S(1)}, u32[]{:S(2)}, u32[]{:S(2)}) collective-permute-start(f32[24,8,128]{2,1,0:T(8,128)S(1)} %get-tuple-element.80), channel_id=1, source_target_pairs={{0,6},{1,7},{2,4},{3,5},{4,2},{5,3},{6,0},{7,1},{8,14},{9,15},{10,... | collective-permute-start | bytes 294920 | tf_op jit(solution)/shard_map/ppermute | solution.py:503
  7.1 5.5 %collective-permute-start.2 = (f32[24,8,128]{2,1,0:T(8,128)S(1)}, f32[24,8,128]{2,1,0:T(8,128)S(1)}, u32[]{:S(2)}, u32[]{:S(2)}) collective-permute-start(f32[24,8,128]{2,1,0:T(8,128)S(1)} %get-tuple-element.81), channel_id=1, source_target_pairs={{0,2},{1,5},{2,0},{3,7},{4,6},{5,1},{6,4},{7,3},{8,10},{9,13},{10,... | collective-permute-start | bytes 294920 | tf_op jit(solution)/shard_map/ppermute | solution.py:503
  7.7 4.9 %collective-permute-start.3 = (f32[24,8,128]{2,1,0:T(8,128)S(1)}, f32[24,8,128]{2,1,0:T(8,128)S(1)}, u32[]{:S(2)}, u32[]{:S(2)}) collective-permute-start(f32[24,8,128]{2,1,0:T(8,128)S(1)} %get-tuple-element.82), channel_id=1, source_target_pairs={{0,4},{1,3},{2,6},{3,1},{4,0},{5,7},{6,2},{7,5},{8,12},{9,11},{10,... | collective-permute-start | bytes 294920 | tf_op jit(solution)/shard_map/ppermute | solution.py:503
  7.8 4.8 %collective-permute-start.4 = (f32[24,8,128]{2,1,0:T(8,128)S(1)}, f32[24,8,128]{2,1,0:T(8,128)S(1)}, u32[]{:S(2)}, u32[]{:S(2)}) collective-permute-start(f32[24,8,128]{2,1,0:T(8,128)S(1)} %get-tuple-element.83), channel_id=1, source_target_pairs={{0,1},{1,0},{2,3},{3,2},{4,5},{5,4},{6,7},{7,6},{8,9},{9,8},{10,11... | collective-permute-start | bytes 294920 | tf_op jit(solution)/shard_map/ppermute | solution.py:503
  13.6 1.3 %collective-permute-start.5 = (f32[19,8,128]{2,1,0:T(8,128)S(1)}, f32[19,8,128]{2,1,0:T(8,128)S(1)}, u32[]{:S(2)}, u32[]{:S(2)}) collective-permute-start(f32[19,8,128]{2,1,0:T(8,128)S(1)} %get-tuple-element.88), channel_id=1, source_target_pairs={{0,1},{1,0},{2,3},{3,2},{4,5},{5,4},{6,7},{7,6},{8,9},{9,8},{10,11... | collective-permute-start | bytes 233480 | tf_op jit(solution)/shard_map/ppermute | solution.py:503
  15.0 5.3 %collective-permute-start.6 = (f32[13,8,128]{2,1,0:T(8,128)S(1)}, f32[13,8,128]{2,1,0:T(8,128)S(1)}, u32[]{:S(2)}, u32[]{:S(2)}) collective-permute-start(f32[13,8,128]{2,1,0:T(8,128)S(1)} %get-tuple-element.89), channel_id=1, source_target_pairs={{0,6},{1,7},{2,4},{3,5},{4,2},{5,3},{6,0},{7,1},{8,14},{9,15},{10,... | collective-permute-start | bytes 159752 | tf_op jit(solution)/shard_map/ppermute | solution.py:503
  16.7 4.4 %collective-permute-start.7 = (f32[13,8,128]{2,1,0:T(8,128)S(1)}, f32[13,8,128]{2,1,0:T(8,128)S(1)}, u32[]{:S(2)}, u32[]{:S(2)}) collective-permute-start(f32[13,8,128]{2,1,0:T(8,128)S(1)} %get-tuple-element.90), channel_id=1, source_target_pairs={{0,2},{1,5},{2,0},{3,7},{4,6},{5,1},{6,4},{7,3},{8,10},{9,13},{10,... | collective-permute-start | bytes 159752 | tf_op jit(solution)/shard_map/ppermute | solution.py:503
  18.0 4.1 %collective-permute-start.8 = (f32[13,8,128]{2,1,0:T(8,128)S(1)}, f32[13,8,128]{2,1,0:T(8,128)S(1)}, u32[]{:S(2)}, u32[]{:S(2)}) collective-permute-start(f32[13,8,128]{2,1,0:T(8,128)S(1)} %get-tuple-element.91), channel_id=1, source_target_pairs={{0,4},{1,3},{2,6},{3,1},{4,0},{5,7},{6,2},{7,5},{8,12},{9,11},{10,... | collective-permute-start | bytes 159752 | tf_op jit(solution)/shard_map/ppermute | solution.py:503
  18.6 3.6 %collective-permute-start.9 = (f32[13,8,128]{2,1,0:T(8,128)S(1)}, f32[13,8,128]{2,1,0:T(8,128)S(1)}, u32[]{:S(2)}, u32[]{:S(2)}) collective-permute-start(f32[13,8,128]{2,1,0:T(8,128)S(1)} %get-tuple-element.92), channel_id=1, source_target_pairs={{0,1},{1,0},{2,3},{3,2},{4,5},{5,4},{6,7},{7,6},{8,9},{9,8},{10,11... | collective-permute-start | bytes 159752 | tf_op jit(solution)/shard_map/ppermute | solution.py:503
  36.1 1.3 %collective-permute-start.10 = (f32[19,8,128]{2,1,0:T(8,128)S(1)}, f32[19,8,128]{2,1,0:T(8,128)S(1)}, u32[]{:S(2)}, u32[]{:S(2)}) collective-permute-start(f32[19,8,128]{2,1,0:T(8,128)S(1)} %get-tuple-element.102), channel_id=1, source_target_pairs={{0,1},{1,0},{2,3},{3,2},{4,5},{5,4},{6,7},{7,6},{8,9},{9,8},{10,11... | collective-permute-start | bytes 233480 | tf_op jit(solution)/shard_map/ppermute | solution.py:503
  37.5 5.6 %collective-permute-start.11 = (f32[13,8,128]{2,1,0:T(8,128)S(1)}, f32[13,8,128]{2,1,0:T(8,128)S(1)}, u32[]{:S(2)}, u32[]{:S(2)}) collective-permute-start(f32[13,8,128]{2,1,0:T(8,128)S(1)} %get-tuple-element.103), channel_id=1, source_target_pairs={{0,6},{1,7},{2,4},{3,5},{4,2},{5,3},{6,0},{7,1},{8,14},{9,15},{10,... | collective-permute-start | bytes 159752 | tf_op jit(solution)/shard_map/ppermute | solution.py:503
  38.1 5.0 %collective-permute-start.12 = (f32[13,8,128]{2,1,0:T(8,128)S(1)}, f32[13,8,128]{2,1,0:T(8,128)S(1)}, u32[]{:S(2)}, u32[]{:S(2)}) collective-permute-start(f32[13,8,128]{2,1,0:T(8,128)S(1)} %get-tuple-element.104), channel_id=1, source_target_pairs={{0,2},{1,5},{2,0},{3,7},{4,6},{5,1},{6,4},{7,3},{8,10},{9,13},{10,... | collective-permute-start | bytes 159752 | tf_op jit(solution)/shard_map/ppermute | solution.py:503
  39.6 4.1 %collective-permute-start.13 = (f32[13,8,128]{2,1,0:T(8,128)S(1)}, f32[13,8,128]{2,1,0:T(8,128)S(1)}, u32[]{:S(2)}, u32[]{:S(2)}) collective-permute-start(f32[13,8,128]{2,1,0:T(8,128)S(1)} %get-tuple-element.105), channel_id=1, source_target_pairs={{0,4},{1,3},{2,6},{3,1},{4,0},{5,7},{6,2},{7,5},{8,12},{9,11},{10,... | collective-permute-start | bytes 159752 | tf_op jit(solution)/shard_map/ppermute | solution.py:503
  41.0 2.7 %collective-permute-start.14 = (f32[13,8,128]{2,1,0:T(8,128)S(1)}, f32[13,8,128]{2,1,0:T(8,128)S(1)}, u32[]{:S(2)}, u32[]{:S(2)}) collective-permute-start(f32[13,8,128]{2,1,0:T(8,128)S(1)} %get-tuple-element.106), channel_id=1, source_target_pairs={{0,1},{1,0},{2,3},{3,2},{4,5},{5,4},{6,7},{7,6},{8,9},{9,8},{10,11... | collective-permute-start | bytes 159752 | tf_op jit(solution)/shard_map/ppermute | solution.py:503
  54.4 1.3 %collective-permute-start.15 = (f32[19,8,128]{2,1,0:T(8,128)S(1)}, f32[19,8,128]{2,1,0:T(8,128)S(1)}, u32[]{:S(2)}, u32[]{:S(2)}) collective-permute-start(f32[19,8,128]{2,1,0:T(8,128)S(1)} %get-tuple-element.117), channel_id=1, source_target_pairs={{0,1},{1,0},{2,3},{3,2},{4,5},{5,4},{6,7},{7,6},{8,9},{9,8},{10,11... | collective-permute-start | bytes 233480 | tf_op jit(solution)/shard_map/ppermute | solution.py:503
  55.8 5.6 %collective-permute-start.16 = (f32[13,8,128]{2,1,0:T(8,128)S(1)}, f32[13,8,128]{2,1,0:T(8,128)S(1)}, u32[]{:S(2)}, u32[]{:S(2)}) collective-permute-start(f32[13,8,128]{2,1,0:T(8,128)S(1)} %get-tuple-element.118), channel_id=1, source_target_pairs={{0,6},{1,7},{2,4},{3,5},{4,2},{5,3},{6,0},{7,1},{8,14},{9,15},{10,... | collective-permute-start | bytes 159752 | tf_op jit(solution)/shard_map/ppermute | solution.py:503
  56.4 5.0 %collective-permute-start.17 = (f32[13,8,128]{2,1,0:T(8,128)S(1)}, f32[13,8,128]{2,1,0:T(8,128)S(1)}, u32[]{:S(2)}, u32[]{:S(2)}) collective-permute-start(f32[13,8,128]{2,1,0:T(8,128)S(1)} %get-tuple-element.119), channel_id=1, source_target_pairs={{0,2},{1,5},{2,0},{3,7},{4,6},{5,1},{6,4},{7,3},{8,10},{9,13},{10,... | collective-permute-start | bytes 159752 | tf_op jit(solution)/shard_map/ppermute | solution.py:503
  57.9 4.1 %collective-permute-start.18 = (f32[13,8,128]{2,1,0:T(8,128)S(1)}, f32[13,8,128]{2,1,0:T(8,128)S(1)}, u32[]{:S(2)}, u32[]{:S(2)}) collective-permute-start(f32[13,8,128]{2,1,0:T(8,128)S(1)} %get-tuple-element.120), channel_id=1, source_target_pairs={{0,4},{1,3},{2,6},{3,1},{4,0},{5,7},{6,2},{7,5},{8,12},{9,11},{10,... | collective-permute-start | bytes 159752 | tf_op jit(solution)/shard_map/ppermute | solution.py:503
  59.3 2.7 %collective-permute-start.19 = (f32[13,8,128]{2,1,0:T(8,128)S(1)}, f32[13,8,128]{2,1,0:T(8,128)S(1)}, u32[]{:S(2)}, u32[]{:S(2)}) collective-permute-start(f32[13,8,128]{2,1,0:T(8,128)S(1)} %get-tuple-element.121), channel_id=1, source_target_pairs={{0,1},{1,0},{2,3},{3,2},{4,5},{5,4},{6,7},{7,6},{8,9},{9,8},{10,11... | collective-permute-start | bytes 159752 | tf_op jit(solution)/shard_map/ppermute | solution.py:503
  72.7 1.3 %collective-permute-start.20 = (f32[19,8,128]{2,1,0:T(8,128)S(1)}, f32[19,8,128]{2,1,0:T(8,128)S(1)}, u32[]{:S(2)}, u32[]{:S(2)}) collective-permute-start(f32[19,8,128]{2,1,0:T(8,128)S(1)} %get-tuple-element.132), channel_id=1, source_target_pairs={{0,1},{1,0},{2,3},{3,2},{4,5},{5,4},{6,7},{7,6},{8,9},{9,8},{10,11... | collective-permute-start | bytes 233480 | tf_op jit(solution)/shard_map/ppermute | solution.py:503
  74.1 5.6 %collective-permute-start.21 = (f32[13,8,128]{2,1,0:T(8,128)S(1)}, f32[13,8,128]{2,1,0:T(8,128)S(1)}, u32[]{:S(2)}, u32[]{:S(2)}) collective-permute-start(f32[13,8,128]{2,1,0:T(8,128)S(1)} %get-tuple-element.133), channel_id=1, source_target_pairs={{0,6},{1,7},{2,4},{3,5},{4,2},{5,3},{6,0},{7,1},{8,14},{9,15},{10,... | collective-permute-start | bytes 159752 | tf_op jit(solution)/shard_map/ppermute | solution.py:503
  74.7 5.0 %collective-permute-start.22 = (f32[13,8,128]{2,1,0:T(8,128)S(1)}, f32[13,8,128]{2,1,0:T(8,128)S(1)}, u32[]{:S(2)}, u32[]{:S(2)}) collective-permute-start(f32[13,8,128]{2,1,0:T(8,128)S(1)} %get-tuple-element.134), channel_id=1, source_target_pairs={{0,2},{1,5},{2,0},{3,7},{4,6},{5,1},{6,4},{7,3},{8,10},{9,13},{10,... | collective-permute-start | bytes 159752 | tf_op jit(solution)/shard_map/ppermute | solution.py:503
  76.2 4.1 %collective-permute-start.23 = (f32[13,8,128]{2,1,0:T(8,128)S(1)}, f32[13,8,128]{2,1,0:T(8,128)S(1)}, u32[]{:S(2)}, u32[]{:S(2)}) collective-permute-start(f32[13,8,128]{2,1,0:T(8,128)S(1)} %get-tuple-element.135), channel_id=1, source_target_pairs={{0,4},{1,3},{2,6},{3,1},{4,0},{5,7},{6,2},{7,5},{8,12},{9,11},{10,... | collective-permute-start | bytes 159752 | tf_op jit(solution)/shard_map/ppermute | solution.py:503
  77.7 2.7 %collective-permute-start.24 = (f32[13,8,128]{2,1,0:T(8,128)S(1)}, f32[13,8,128]{2,1,0:T(8,128)S(1)}, u32[]{:S(2)}, u32[]{:S(2)}) collective-permute-start(f32[13,8,128]{2,1,0:T(8,128)S(1)} %get-tuple-element.136), channel_id=1, source_target_pairs={{0,1},{1,0},{2,3},{3,2},{4,5},{5,4},{6,7},{7,6},{8,9},{9,8},{10,11... | collective-permute-start | bytes 159752 | tf_op jit(solution)/shard_map/ppermute | solution.py:503

commit v14 on v12

--- a/solution.py
+++ b/solution.py
@@ -66,8 +66,8 @@
         evens = range(2, self.peers, 2)
         self.beyond = [m for m in evens if m & (m - 1)]
         self.beside = [m for m in evens if m & (m - 1) == 0]
-        self.far = self.beyond + self.beside
-        self.handed = [m + 1 for m in self.far]
+        assert len(self.beside) % 2 == 0
+        self.turns = len(self.beside) // 2
         self.slots = self.peers * self.capacity
         self.inverse = self.slots
         self.pattern = self.inverse + self.blocks
@@ -75,7 +75,7 @@
         self.order = self.partner + self.blocks
         self.count = self.order + self.blocks + 1
         self.table = self.count + 1
-        most = len(self.far) * self.capacity
+        most = (len(self.beside) + len(self.beyond)) * self.capacity
         self.early = min(-(-most * 7 // 8), self.blocks)
         self.middle = max(self.early, min(most, self.blocks))
 
@@ -83,25 +83,43 @@
         return kinds * self.capacity * self.halves
 
     def near_rows(self, kinds):
-        return len(self.handed) * self.rows(kinds)
-
-    def at(self, k, core):
-        return (k + core) % len(self.far)
+        return (len(self.beside) + len(self.beyond)) * self.rows(kinds)
+
+    def beside_rows(self, kinds):
+        return 4 * self.rows(kinds)
+
+    def beyond_rows(self, kinds):
+        return 2 * self.rows(kinds)
+
+    def on_rows(self, kinds):
+        return (1 + len(self.beside)) * self.rows(kinds)
+
+    def carried(self, k, core):
+        return self.beside[2 * k + core]
 
     def mine(self, k):
         core = lax.axis_index("sub") & 1
-        at = [self.at(k, c) for c in range(2)]
-        return tuple(
-            jnp.where(core == 0, jnp.int32(a), jnp.int32(b))
-            for a, b in [at, [self.far[n] for n in at]]
-        )
+        masks = [jnp.int32(self.carried(k, c)) for c in range(2)]
+        return tuple(jnp.where(core == c, masks[0], masks[1]) for c in range(2))
+
+    def handed(self):
+        theirs = [self.mine(k)[1] for k in range(self.turns)]
+        return [m + side for m in theirs for side in range(2)] + [m + 1 for m in self.beyond]
+
+    def kept(self):
+        own = [self.mine(k)[0] for k in range(self.turns)]
+        return [m + side for m in own for side in range(2)] + self.beyond + [1]
 
     def sources(self):
-        found = [(1, 0, 0)]
-        for k in range(len(self.far)):
-            _, m = self.mine(k)
-            found += [(m + side, 1 + k, side) for side in range(2)]
-        return found
+        found = []
+        last = self.turns + len(self.beyond)
+        for k in range(self.turns):
+            own, other = self.mine(k)
+            found += [(own, k, 0), (own + 1, k, 2)]
+            found += [(other + 1, last, 1 + 2 * k), (other, last, 2 + 2 * k)]
+        for k, m in enumerate(self.beyond):
+            found += [(m, self.turns + k, 0), (m + 1, self.turns + k, 1)]
+        return found + [(1, last, 0)]
 
 
 def fill_table(z, partner, pattern, table, counts):
@@ -121,13 +139,18 @@
         table[z.pattern + i] = source
         table[z.partner + i] = mate
     place = jnp.int32(0)
-    for m in z.handed + z.far + [1]:
-        for r in range(z.capacity):
-            block = table[m * z.capacity + r]
-            table[z.order + place] = block
-            place = place + (block < z.blocks).astype(jnp.int32)
-        if m == z.handed[-1]:
-            table[z.count] = place
+
+    def follow(masks, place):
+        for m in masks:
+            for r in range(z.capacity):
+                block = table[m * z.capacity + r]
+                table[z.order + place] = block
+                place = place + (block < z.blocks).astype(jnp.int32)
+        return place
+
+    place = follow(z.handed(), place)
+    table[z.count] = place
+    follow(z.kept(), place)
 
 
 def fill_piece(z, table, sources, m, piece, row):
@@ -140,7 +163,7 @@
 
 
 def fill_near(z, table, sources, near):
-    for k, m in enumerate(z.handed):
+    for k, m in enumerate(z.handed()):
         fill_piece(z, table, sources, m, near, k * z.rows(len(sources)))
 
 
@@ -151,24 +174,50 @@
 
 def load_extra(z, piece, row):
     return jnp.concatenate([piece[row + j] for j in range(z.extra_chunks)], axis=1)
+
+
+def copy_piece(rows, source, at, target, to):
+    for row in range(rows):
+        target[to * rows + row] = source[at * rows + row]
 
 
 def relay(z, kinds, table, *rest):
     sources, rest = rest[:kinds], rest[kinds:]
     if kinds == 1:
         extra, rest = rest[0], rest[1:]
-    near, pieces, beside = rest[0], rest[1:-1], rest[-1]
+    near, pieces = rest[0], rest[1:]
     rows = z.rows(kinds)
-    fill_piece(z, table, sources, 1, beside, 0)
     if kinds == 1:
         tile = extra[...] + load_extra(z, near, z.near_rows(1))
-    for k, piece in enumerate(pieces):
-        which, m = z.mine(k)
+    for k, piece in enumerate(pieces[: z.turns]):
+        m, _ = z.mine(k)
         fill_piece(z, table, sources, m, piece, 0)
-        for row in range(rows):
-            piece[rows + row] = near[which * rows + row]
+        fill_piece(z, table, sources, m + 1, piece, rows)
+        copy_piece(rows, near, 2 * k + 1, piece, 2)
+        copy_piece(rows, near, 2 * k, piece, 3)
         if kinds == 1:
-            store_extra(z, tile, piece, 2 * rows)
+            store_extra(z, tile, piece, z.beside_rows(1))
+    for k, (m, piece) in enumerate(zip(z.beyond, pieces[z.turns :])):
+        fill_piece(z, table, sources, m, piece, 0)
+        copy_piece(rows, near, len(z.beside) + k, piece, 1)
+        if kinds == 1:
+            store_extra(z, tile, piece, z.beyond_rows(1))
+
+
+def keep(z, source, target):
+    target[...] = source[...]
+
+
+def hand_on(z, kinds, table, *rest):
+    sources, arrived, piece = rest[:kinds], rest[kinds:-1], rest[-1]
+    rows = z.rows(kinds)
+    fill_piece(z, table, sources, 1, piece, 0)
+    for k, source in enumerate(arrived):
+        copy_piece(rows, source, 1, piece, 1 + 2 * k)
+        copy_piece(rows, source, 3, piece, 2 + 2 * k)
+        if kinds == 1:
+            tile = load_extra(z, source, z.beside_rows(1))
+            store_extra(z, tile, piece, z.on_rows(1) + k * z.extra_chunks)
 
 
 def place(z, table, arrived, kind, kinds, target):
@@ -242,9 +291,8 @@
 
 
 def build_lift(z, table, lift, *rest):
-    count = 1 + len(z.far)
-    arrived, (jump_lift, other, full) = rest[:count], rest[count:]
-    place(z, table, [arrived[-1], *arrived[:-1]], 1, 2, other)
+    arrived, (jump_lift, other, full) = rest[:-3], rest[-3:]
+    place(z, table, arrived, 1, 2, other)
     me = lax.axis_index("sub")
     for i in range(z.blocks):
         full[i] = jnp.zeros((z.all_corners, z.width), F32)
@@ -255,10 +303,13 @@
         jump_lift[i] = split(full[i])
 
 
-def extra_sum(z, own, near, *far):
+def extra_sum(z, own, near, arrived):
     total = own[...] + load_extra(z, near, z.near_rows(1))
-    for piece in far:
-        total = total + load_extra(z, piece, 2 * z.rows(1))
+    for k in range(z.turns):
+        total = total + load_extra(z, arrived[k], z.beside_rows(1))
+        total = total + load_extra(z, arrived[-1], z.on_rows(1) + k * z.extra_chunks)
+    for piece in arrived[z.turns : -1]:
+        total = total + load_extra(z, piece, z.beyond_rows(1))
     return total
 
 
@@ -328,10 +379,10 @@
     take = lambda n: [rest.pop(0) for _ in range(n)]
     wide, diag, off, corners = take(4)
     if step == 0:
-        *far, beside, loaded = take(2 + len(z.far))
+        *arrived, loaded = take(2 + z.turns + len(z.beyond))
         residual, image, parts, extra, near_out, other = rest
         direction = residual
-        place(z, table, [beside, *far], 0, 2, other)
+        place(z, table, arrived, 0, 2, other)
     else:
         gathered, before, way, product = take(4)
         previous = take(1)[0][...] if step > 1 else None
@@ -401,12 +452,12 @@
 
 
 def finish_product(z, step, table, operator, image, own_extra, jump_lift, residual, direction, near, *rest):
-    *far, beside, product, sent, other = rest
+    *arrived, product, sent, other = rest
     if step > 0:
-        previous, far = far[0], far[1:]
+        previous, arrived = arrived[0], arrived[1:]
         scale = across_block(z, used_step(previous[...]))
-    place(z, table, [beside, *far], 0, 1, other)
-    partials = extra_sum(z, own_extra, near, *far)[:, : z.all_corners]
+    place(z, table, arrived, 0, 1, other)
+    partials = extra_sum(z, own_extra, near, arrived)[:, : z.all_corners]
     local = dot_high(partials, operator[...], NT)
     rows = pad(jnp.concatenate([local, local], axis=1))
     zero = jnp.zeros((z.columns, z.width), F32)
@@ -489,8 +540,8 @@
     extra = ((cols, z.extra), F32)
     light, heavy = 4_000_000, 600_000_000
 
-    def shape(rows, kinds):
-        return ((rows + (z.extra_chunks if kinds == 1 else 0), cols, LANES), F32)
+    def shape(rows, kinds, chunks=1):
+        return ((rows + (chunks * z.extra_chunks if kinds == 1 else 0), cols, LANES), F32)
 
     def kernel(body, *extra_args):
         return functools.partial(body, z, *extra_args)
@@ -503,12 +554,25 @@
         return across(piece, lambda core: 1)
 
     def exchange(kinds, sources, near):
-        *pieces, beside = call(
+        fields = sources[:kinds]
+        pieces = call(
             kernel(relay, kinds),
-            [shape(2 * z.rows(kinds), kinds)] * (len(z.far) + 1), [], light, [table, *sources, near],
+            [shape(z.beside_rows(kinds), kinds)] * z.turns
+            + [shape(z.beyond_rows(kinds), kinds)] * len(z.beyond),
+            [], light, [table, *sources, near],
         )
-        far = [across(piece, lambda core: z.far[z.at(k, core)]) for k, piece in enumerate(pieces)]
-        return [*far, to_near(beside)]
+        beside = [
+            across(piece, lambda core: z.carried(k, core)) for k, piece in enumerate(pieces[: z.turns])
+        ]
+        beyond = [across(piece, lambda core: m) for m, piece in zip(z.beyond, pieces[z.turns :])]
+        beyond = [
+            call(kernel(keep), [(piece.shape, F32)], [], heavy, [piece], False)[0] for piece in beyond
+        ]
+        (piece,) = call(
+            kernel(hand_on, kinds), [shape(z.on_rows(kinds), kinds, z.turns)], [], light,
+            [table, *fields, *beside],
+        )
+        return [*beside, *beyond, to_near(piece)]
 
     table, loaded, lift, wide, corners, near = call(
         kernel(begin),

time: 92.2 us -> 94.3 us (1.023)
  waiting for transfers between devices: 15.9 us -> 21.8 us
  starting transfers between devices: 19.3 us -> 15.5 us
    ppermute x25 -> x20, waiting for transfers between devices: 15.9 us -> 21.8 us  [across(): return lax.ppermute(piece, 'sub', pairs)]
    ppermute x25 -> x20, starting transfers between devices: 19.3 us -> 15.5 us  [across(): return lax.ppermute(piece, 'sub', pairs)]
    pallas_call x21 -> x31, Pallas kernels: 16.7 us -> 16.8 us  [call(): pl.pallas_call(body, out_shape=shapes, in_specs=specs, out_specs=[SMEM if...]
  transfers between devices with their start and end apart: 25 -> 20, of which waited for: 17 -> 17; matrix products, arithmetic and copies ran while one was open for 0% -> 0% of each run, Pallas kernels for 7% -> 7%
where the time goes in v14:
time: 94.3 us; the launch traced here: 94.1 us
  blocking collectives  39.2 us (42%)
  waiting for transfers between devices  21.8 us (23%)
  Pallas kernels  16.8 us (18%)
  starting transfers between devices  15.5 us (16%)
    all_to_all x4, blocking collectives, on_device(): gathered = lax.all_to_all(sent, ('group', 'sub'), 0, 0, tiled=True)  39.2 us
    ppermute x20, waiting for transfers between devices, across(): return lax.ppermute(piece, 'sub', pairs)  21.8 us
    pallas_call x31, Pallas kernels, call(): pl.pallas_call(body, out_shape=shapes, in_specs=specs, out_specs=[SMEM if...  16.8 us
    ppermute x20, starting transfers between devices, across(): return lax.ppermute(piece, 'sub', pairs)  15.5 us
  transfers between devices with their start and end apart: 20, of which 17 were waited for; matrix products, arithmetic and copies ran while one was open for 0% of the time, Pallas kernels for 7%

profile of v14, /device:TPU:0, one launch (start us, length us, event | category | flops | bytes accessed | tf_op | source)
XLA Modules:
  0.0 94.1 jit_solution(4664762678716952223)
XLA Ops:
  0.6 1.0 %shard_map.104 = (s32[90]{0:T(128)S(4)}, f32[16,8,256]{2,1,0:T(8,128)S(1)}, f32[16,8,256]{2,1,0:T(8,128)S(1)}, f32[16,8,256]{2,1,0:T(8,128)S(1)}, bf16[16,16,256...) custom-call(s32[1,16]{1,0:T(1,128)} %partner.1, s32[1,16]{1,0:T(1,128)} %pattern.1, f32[8,16,256]{2,1,0:T(8,128)} %load.1, ...), custom_call_target="tpu_custom_call" | custom-call | flops 4000000 | bytes 250000 | tf_op jit(solution)/shard_map/pallas_call | solution.py:512
  2.2 1.0 %collective-permute-done.rest_2_ = f32[36,8,128]{2,1,0:T(8,128)S(1)} collective-permute-done((f32[36,8,128]{2,1,0:T(8,128)S(1)}, f32[36,8,128]{2,1,0:T(8,128)S(1)}, u32[]{:S(2)}, u32[]{:S(2)}) %collective-permute-start) | collective-permute-done | bytes 147488 | tf_op jit(solution)/shard_map/ppermute | solution.py:551
  3.2 2.9 %collective-permute-start.1 = (f32[48,8,128]{2,1,0:T(8,128)S(1)}, f32[48,8,128]{2,1,0:T(8,128)S(1)}, u32[]{:S(2)}, u32[]{:S(2)}) collective-permute-start(f32[48,8,128]{2,1,0:T(8,128)S(1)} %get-tuple-element.70), channel_id=1, source_target_pairs={{0,2},{1,5},{2,0},{3,7},{4,6},{5,1},{6,4},{7,3},{8,10},{9,13},{10,... | collective-permute-start | bytes 589832 | tf_op jit(solution)/shard_map/ppermute | solution.py:551
  6.2 1.5 %collective-permute-start.2 = (f32[24,8,128]{2,1,0:T(8,128)S(1)}, f32[24,8,128]{2,1,0:T(8,128)S(1)}, u32[]{:S(2)}, u32[]{:S(2)}) collective-permute-start(f32[24,8,128]{2,1,0:T(8,128)S(1)} %get-tuple-element.71), channel_id=1, source_target_pairs={{0,6},{1,7},{2,4},{3,5},{4,2},{5,3},{6,0},{7,1},{8,14},{9,15},{10,... | collective-permute-start | bytes 294920 | tf_op jit(solution)/shard_map/ppermute | solution.py:551
  7.6 3.2 %collective-permute-done.1.rest_2_.rest_4_.rest_0_ = f32[48,8,128]{2,1,0:T(8,128)S(1)} collective-permute-done((f32[48,8,128]{2,1,0:T(8,128)S(1)}, f32[48,8,128]{2,1,0:T(8,128)S(1)}, u32[]{:S(2)}, u32[]{:S(2)}) %collective-permute-start.1) | collective-permute-done | bytes 196640 | tf_op jit(solution)/shard_map/ppermute | solution.py:551
  11.0 2.3 %shard_map.105 = (f32[64,64]{1,0:T(8,128)S(1)}, bf16[16,256,256]{2,1,0:T(8,128)(2,1)S(1)}, bf16[16,256,256]{2,1,0:T(8,128)(2,1)S(1)}) custom-call(s32[1,64]{1,0:T(1,128)} %index_in.1, f32[32,32]{1,0:T(8,128)} %inverse_in.1, bf16[16,256,256]{2,1,0:T(8,128)(2,1)} %diag.1, bf16[16,256,256]{2,1,0:T(8,128)(2,1)} %off.1), custom_call_target="tpu_custom_call" | custom-call | flops 600000000 | bytes 37500000 | tf_op jit(solution)/shard_map/pallas_call | solution.py:512
  13.4 1.1 %shard_map.109 = (f32[16,8,256]{2,1,0:T(8,128)S(1)}, f32[16,8,256]{2,1,0:T(8,128)S(1)}, bf16[16,16,256]{2,1,0:T(8,128)(2,1)S(1)}, f32[8,128]{1,0:T(8,128)S(1)}, f32[19,8,128]{2,1,0:T(8,128)S(1)}) custom-call(s32[90]{0:T(128)S(4)} %get-tuple-element.61.table, f32[16,8,256]{2,1,0:T(8,128)S(1)} %get-tuple-element.63.rest_0_.wide, ...), custom_call_target="tpu_custom_call" | custom-call | flops 600000000 | bytes 37500000 | tf_op jit(solution)/shard_map/pallas_call | solution.py:512
  14.9 1.1 %shard_map.110.rest_0_.image = f32[16,8,256]{2,1,0:T(8,128)S(1)} custom-call(s32[90]{0:T(128)S(4)} %get-tuple-element.61.table, f32[16,8,256]{2,1,0:T(8,128)S(1)} %get-tuple-element.63.rest_0_.wide, bf16[16,256,256]{2,1,0:T(8,128)(2,1)S(1)} %get-tuple-element.64.rest_1_.diag, bf16[16,256,256]{2,1,0:T(8,128)(2,1)S(1)} %get-tuple-element.65.rest_2_.off, ...), custom_call_target="tpu_custom_call" | custom-call | flops 600000000 | bytes 37500000 | tf_op jit(solution)/shard_map/pallas_call | solution.py:512
  16.1 2.1 %collective-permute-start.5 = (f32[25,8,128]{2,1,0:T(8,128)S(1)}, f32[25,8,128]{2,1,0:T(8,128)S(1)}, u32[]{:S(2)}, u32[]{:S(2)}) collective-permute-start(f32[25,8,128]{2,1,0:T(8,128)S(1)} %get-tuple-element.77), channel_id=1, source_target_pairs={{0,2},{1,5},{2,0},{3,7},{4,6},{5,1},{6,4},{7,3},{8,10},{9,13},{10,... | collective-permute-start | bytes 307208 | tf_op jit(solution)/shard_map/ppermute | solution.py:551
  18.1 1.5 %collective-permute-start.6 = (f32[13,8,128]{2,1,0:T(8,128)S(1)}, f32[13,8,128]{2,1,0:T(8,128)S(1)}, u32[]{:S(2)}, u32[]{:S(2)}) collective-permute-start(f32[13,8,128]{2,1,0:T(8,128)S(1)} %get-tuple-element.78), channel_id=1, source_target_pairs={{0,6},{1,7},{2,4},{3,5},{4,2},{5,3},{6,0},{7,1},{8,14},{9,15},{10,... | collective-permute-start | bytes 159752 | tf_op jit(solution)/shard_map/ppermute | solution.py:551
  19.6 1.5 %collective-permute-done.5.rest_1_.rest_0_ = f32[25,8,128]{2,1,0:T(8,128)S(1)} collective-permute-done((f32[25,8,128]{2,1,0:T(8,128)S(1)}, f32[25,8,128]{2,1,0:T(8,128)S(1)}, u32[]{:S(2)}, u32[]{:S(2)}) %collective-permute-start.5) | collective-permute-done | bytes 102432 | tf_op jit(solution)/shard_map/ppermute | solution.py:551
  21.4 2.0 %collective-permute-done.6.source = f32[13,8,128]{2,1,0:T(8,128)S(1)} collective-permute-done((f32[13,8,128]{2,1,0:T(8,128)S(1)}, f32[13,8,128]{2,1,0:T(8,128)S(1)}, u32[]{:S(2)}, u32[]{:S(2)}) %collective-permute-start.6) | collective-permute-done | bytes 53280 | tf_op jit(solution)/shard_map/ppermute | solution.py:551
  24.2 12.6 %all_to_all.20.rest_4_ = f32[32,1,128]{2,1,0:T(1,128)S(1)} all-to-all(f32[32,1,128]{2,1,0:T(1,128)S(1)} %get-tuple-element.79), channel_id=1, replica_groups=mesh['group'=4,'sub'=8] {'group','sub'}, dimensions={0} | all-to-all | bytes 32768 | tf_op jit(solution)/shard_map/all_to_all | solution.py:645
  36.8 1.3 %shard_map.116 = (f32[16,8,256]{2,1,0:T(8,128)S(1)}, f32[16,8,256]{2,1,0:T(8,128)S(1)}, f32[8,128]{1,0:T(8,128)S(1)}, f32[16,8,256]{2,1,0:T(8,128)S(1)}, bf16[16...) custom-call(s32[90]{0:T(128)S(4)} %get-tuple-element.61.table, ...), custom_call_target="tpu_custom_call" | custom-call | flops 600000000 | bytes 37500000 | tf_op jit(solution)/shard_map/pallas_call | solution.py:512
  38.2 1.1 %shard_map.117 = (f32[16,8,256]{2,1,0:T(8,128)S(1)}, f32[16,8,256]{2,1,0:T(8,128)S(1)}) custom-call(s32[90]{0:T(128)S(4)} %get-tuple-element.61.table, f32[16,8,256]{2,1,0:T(8,128)S(1)} %get-tuple-element.63.rest_0_.wide, bf16[16,256,256]{2,1,0:T(8,128)(2,1)S(1)} %get-tuple-element.64.rest_1_.diag, bf16[16,256,256]{2,1,0:T(8,128)(2,1)S(1)} %get-tuple-element.65.rest_2_.off, ...), custom_call_target="tpu_custom_call" | custom-call | flops 600000000 | bytes 37500000 | tf_op jit(solution)/shard_map/pallas_call | solution.py:512
  40.1 1.5 %collective-permute-start.10 = (f32[13,8,128]{2,1,0:T(8,128)S(1)}, f32[13,8,128]{2,1,0:T(8,128)S(1)}, u32[]{:S(2)}, u32[]{:S(2)}) collective-permute-start(f32[13,8,128]{2,1,0:T(8,128)S(1)} %get-tuple-element.90), channel_id=1, source_target_pairs={{0,6},{1,7},{2,4},{3,5},{4,2},{5,3},{6,0},{7,1},{8,14},{9,15},{10,... | collective-permute-start | bytes 159752 | tf_op jit(solution)/shard_map/ppermute | solution.py:551
  41.5 3.2 %collective-permute-done.9.rest_1_ = f32[25,8,128]{2,1,0:T(8,128)S(1)} collective-permute-done((f32[25,8,128]{2,1,0:T(8,128)S(1)}, f32[25,8,128]{2,1,0:T(8,128)S(1)}, u32[]{:S(2)}, u32[]{:S(2)}) %collective-permute-start.9) | collective-permute-done | bytes 102432 | tf_op jit(solution)/shard_map/ppermute | solution.py:551
  45.3 0.8 collective-permute-done.11.rest_3_
  46.8 8.8 %all_to_all.21.rest_4_ = f32[32,1,128]{2,1,0:T(1,128)S(1)} all-to-all(f32[32,1,128]{2,1,0:T(1,128)S(1)} %get-tuple-element.91), channel_id=1, replica_groups=mesh['group'=4,'sub'=8] {'group','sub'}, dimensions={0} | all-to-all | bytes 32768 | tf_op jit(solution)/shard_map/all_to_all | solution.py:645
  55.6 1.2 %shard_map.122 = (f32[16,8,256]{2,1,0:T(8,128)S(1)}, f32[16,8,256]{2,1,0:T(8,128)S(1)}, f32[8,128]{1,0:T(8,128)S(1)}, f32[16,8,256]{2,1,0:T(8,128)S(1)}, bf16[16...) custom-call(s32[90]{0:T(128)S(4)} %get-tuple-element.61.table, ...), custom_call_target="tpu_custom_call" | custom-call | flops 600000000 | bytes 37500000 | tf_op jit(solution)/shard_map/pallas_call | solution.py:512
  56.9 1.1 %shard_map.123 = (f32[16,8,256]{2,1,0:T(8,128)S(1)}, f32[16,8,256]{2,1,0:T(8,128)S(1)}) custom-call(s32[90]{0:T(128)S(4)} %get-tuple-element.61.table, f32[16,8,256]{2,1,0:T(8,128)S(1)} %get-tuple-element.63.rest_0_.wide, bf16[16,256,256]{2,1,0:T(8,128)(2,1)S(1)} %get-tuple-element.64.rest_1_.diag, bf16[16,256,256]{2,1,0:T(8,128)(2,1)S(1)} %get-tuple-element.65.rest_2_.off, ...), custom_call_target="tpu_custom_call" | custom-call | flops 600000000 | bytes 37500000 | tf_op jit(solution)/shard_map/pallas_call | solution.py:512
  58.8 1.5 %collective-permute-start.14 = (f32[13,8,128]{2,1,0:T(8,128)S(1)}, f32[13,8,128]{2,1,0:T(8,128)S(1)}, u32[]{:S(2)}, u32[]{:S(2)}) collective-permute-start(f32[13,8,128]{2,1,0:T(8,128)S(1)} %get-tuple-element.103), channel_id=1, source_target_pairs={{0,6},{1,7},{2,4},{3,5},{4,2},{5,3},{6,0},{7,1},{8,14},{9,15},{10,... | collective-permute-start | bytes 159752 | tf_op jit(solution)/shard_map/ppermute | solution.py:551
  60.2 3.2 %collective-permute-done.13.rest_1_ = f32[25,8,128]{2,1,0:T(8,128)S(1)} collective-permute-done((f32[25,8,128]{2,1,0:T(8,128)S(1)}, f32[25,8,128]{2,1,0:T(8,128)S(1)}, u32[]{:S(2)}, u32[]{:S(2)}) %collective-permute-start.13) | collective-permute-done | bytes 102432 | tf_op jit(solution)/shard_map/ppermute | solution.py:551
  64.0 0.8 collective-permute-done.15.rest_3_
  65.5 8.8 %all_to_all.22.rest_4_ = f32[32,1,128]{2,1,0:T(1,128)S(1)} all-to-all(f32[32,1,128]{2,1,0:T(1,128)S(1)} %get-tuple-element.104), channel_id=1, replica_groups=mesh['group'=4,'sub'=8] {'group','sub'}, dimensions={0} | all-to-all | bytes 32768 | tf_op jit(solution)/shard_map/all_to_all | solution.py:645
  74.3 1.2 %shard_map.128 = (f32[16,8,256]{2,1,0:T(8,128)S(1)}, f32[16,8,256]{2,1,0:T(8,128)S(1)}, f32[8,128]{1,0:T(8,128)S(1)}, f32[16,8,256]{2,1,0:T(8,128)S(1)}, bf16[16...) custom-call(s32[90]{0:T(128)S(4)} %get-tuple-element.61.table, ...), custom_call_target="tpu_custom_call" | custom-call | flops 600000000 | bytes 37500000 | tf_op jit(solution)/shard_map/pallas_call | solution.py:512
  75.6 1.1 %shard_map.129 = (f32[16,8,256]{2,1,0:T(8,128)S(1)}, f32[16,8,256]{2,1,0:T(8,128)S(1)}) custom-call(s32[90]{0:T(128)S(4)} %get-tuple-element.61.table, f32[16,8,256]{2,1,0:T(8,128)S(1)} %get-tuple-element.63.rest_0_.wide, bf16[16,256,256]{2,1,0:T(8,128)(2,1)S(1)} %get-tuple-element.64.rest_1_.diag, bf16[16,256,256]{2,1,0:T(8,128)(2,1)S(1)} %get-tuple-element.65.rest_2_.off, ...), custom_call_target="tpu_custom_call" | custom-call | flops 600000000 | bytes 37500000 | tf_op jit(solution)/shard_map/pallas_call | solution.py:512
  77.5 1.5 %collective-permute-start.18 = (f32[13,8,128]{2,1,0:T(8,128)S(1)}, f32[13,8,128]{2,1,0:T(8,128)S(1)}, u32[]{:S(2)}, u32[]{:S(2)}) collective-permute-start(f32[13,8,128]{2,1,0:T(8,128)S(1)} %get-tuple-element.116), channel_id=1, source_target_pairs={{0,6},{1,7},{2,4},{3,5},{4,2},{5,3},{6,0},{7,1},{8,14},{9,15},{10,... | collective-permute-start | bytes 159752 | tf_op jit(solution)/shard_map/ppermute | solution.py:551
  78.9 3.2 %collective-permute-done.17.rest_1_ = f32[25,8,128]{2,1,0:T(8,128)S(1)} collective-permute-done((f32[25,8,128]{2,1,0:T(8,128)S(1)}, f32[25,8,128]{2,1,0:T(8,128)S(1)}, u32[]{:S(2)}, u32[]{:S(2)}) %collective-permute-start.17) | collective-permute-done | bytes 102432 | tf_op jit(solution)/shard_map/ppermute | solution.py:551
  82.7 0.8 collective-permute-done.19.rest_3_
  84.2 8.8 %all_to_all.23.gathered = f32[32,1,128]{2,1,0:T(1,128)S(1)} all-to-all(f32[32,1,128]{2,1,0:T(1,128)S(1)} %get-tuple-element.117), channel_id=1, replica_groups=mesh['group'=4,'sub'=8] {'group','sub'}, dimensions={0} | all-to-all | bytes 32768 | tf_op jit(solution)/shard_map/all_to_all | solution.py:645
  93.0 1.0 %shard_map.134 = (f32[8,16,256]{2,1,0:T(8,128)}, f32[8,16,256]{2,1,0:T(8,128)}) custom-call(f32[32,1,128]{2,1,0:T(1,128)S(1)} %all_to_all.23.gathered, f32[16,8,256]{2,1,0:T(8,128)S(1)} %get-tuple-element.118.before, f32[16,8,256]{2,1,0:T(8,128)S(1)} %get-tuple-element.112.residual.residual_in, f32[16,8,256]{2,1,0:T(8,128)S(1)} %get-tuple-element.113.direction, ...), custom_call_target="tpu_custom_call" | custom-call | flops 4000000 | bytes 250000 | tf_op jit(solution)/shard_map/pallas_call | solution.py:512
  (43 shorter events, 8.3 us)
Async XLA Ops:
  1.7 1.5 %collective-permute-start = (f32[36,8,128]{2,1,0:T(8,128)S(1)}, f32[36,8,128]{2,1,0:T(8,128)S(1)}, u32[]{:S(2)}, u32[]{:S(2)}) collective-permute-start(f32[36,8,128]{2,1,0:T(8,128)S(1)} %get-tuple-element.69), channel_id=1, source_target_pairs={{0,1},{1,0},{2,3},{3,2},{4,5},{5,4},{6,7},{7,6},{8,9},{9,8},{10,11... | collective-permute-start | bytes 442376 | tf_op jit(solution)/shard_map/ppermute | solution.py:551
  3.2 7.6 %collective-permute-start.1 = (f32[48,8,128]{2,1,0:T(8,128)S(1)}, f32[48,8,128]{2,1,0:T(8,128)S(1)}, u32[]{:S(2)}, u32[]{:S(2)}) collective-permute-start(f32[48,8,128]{2,1,0:T(8,128)S(1)} %get-tuple-element.70), channel_id=1, source_target_pairs={{0,2},{1,5},{2,0},{3,7},{4,6},{5,1},{6,4},{7,3},{8,10},{9,13},{10,... | collective-permute-start | bytes 589832 | tf_op jit(solution)/shard_map/ppermute | solution.py:551
  6.2 7.2 %collective-permute-start.2 = (f32[24,8,128]{2,1,0:T(8,128)S(1)}, f32[24,8,128]{2,1,0:T(8,128)S(1)}, u32[]{:S(2)}, u32[]{:S(2)}) collective-permute-start(f32[24,8,128]{2,1,0:T(8,128)S(1)} %get-tuple-element.71), channel_id=1, source_target_pairs={{0,6},{1,7},{2,4},{3,5},{4,2},{5,3},{6,0},{7,1},{8,14},{9,15},{10,... | collective-permute-start | bytes 294920 | tf_op jit(solution)/shard_map/ppermute | solution.py:551
  10.9 2.5 %collective-permute-start.3 = (f32[36,8,128]{2,1,0:T(8,128)S(1)}, f32[36,8,128]{2,1,0:T(8,128)S(1)}, u32[]{:S(2)}, u32[]{:S(2)}) collective-permute-start(f32[36,8,128]{2,1,0:T(8,128)S(1)} %shard_map.108), channel_id=1, source_target_pairs={{0,1},{1,0},{2,3},{3,2},{4,5},{5,4},{6,7},{7,6},{8,9},{9,8},{10,11... | collective-permute-start | bytes 442376 | tf_op jit(solution)/shard_map/ppermute | solution.py:551
  14.6 1.5 %collective-permute-start.4 = (f32[19,8,128]{2,1,0:T(8,128)S(1)}, f32[19,8,128]{2,1,0:T(8,128)S(1)}, u32[]{:S(2)}, u32[]{:S(2)}) collective-permute-start(f32[19,8,128]{2,1,0:T(8,128)S(1)} %get-tuple-element.76), channel_id=1, source_target_pairs={{0,1},{1,0},{2,3},{3,2},{4,5},{5,4},{6,7},{7,6},{8,9},{9,8},{10,11... | collective-permute-start | bytes 233480 | tf_op jit(solution)/shard_map/ppermute | solution.py:551
  16.1 5.1 %collective-permute-start.5 = (f32[25,8,128]{2,1,0:T(8,128)S(1)}, f32[25,8,128]{2,1,0:T(8,128)S(1)}, u32[]{:S(2)}, u32[]{:S(2)}) collective-permute-start(f32[25,8,128]{2,1,0:T(8,128)S(1)} %get-tuple-element.77), channel_id=1, source_target_pairs={{0,2},{1,5},{2,0},{3,7},{4,6},{5,1},{6,4},{7,3},{8,10},{9,13},{10,... | collective-permute-start | bytes 307208 | tf_op jit(solution)/shard_map/ppermute | solution.py:551
  18.1 5.3 %collective-permute-start.6 = (f32[13,8,128]{2,1,0:T(8,128)S(1)}, f32[13,8,128]{2,1,0:T(8,128)S(1)}, u32[]{:S(2)}, u32[]{:S(2)}) collective-permute-start(f32[13,8,128]{2,1,0:T(8,128)S(1)} %get-tuple-element.78), channel_id=1, source_target_pairs={{0,6},{1,7},{2,4},{3,5},{4,2},{5,3},{6,0},{7,1},{8,14},{9,15},{10,... | collective-permute-start | bytes 159752 | tf_op jit(solution)/shard_map/ppermute | solution.py:551
  21.1 2.3 %collective-permute-start.7 = (f32[19,8,128]{2,1,0:T(8,128)S(1)}, f32[19,8,128]{2,1,0:T(8,128)S(1)}, u32[]{:S(2)}, u32[]{:S(2)}) collective-permute-start(f32[19,8,128]{2,1,0:T(8,128)S(1)} %shard_map.114), channel_id=1, source_target_pairs={{0,1},{1,0},{2,3},{3,2},{4,5},{5,4},{6,7},{7,6},{8,9},{9,8},{10,11... | collective-permute-start | bytes 233480 | tf_op jit(solution)/shard_map/ppermute | solution.py:551
  38.2 1.3 %collective-permute-start.8 = (f32[19,8,128]{2,1,0:T(8,128)S(1)}, f32[19,8,128]{2,1,0:T(8,128)S(1)}, u32[]{:S(2)}, u32[]{:S(2)}) collective-permute-start(f32[19,8,128]{2,1,0:T(8,128)S(1)} %get-tuple-element.88), channel_id=1, source_target_pairs={{0,1},{1,0},{2,3},{3,2},{4,5},{5,4},{6,7},{7,6},{8,9},{9,8},{10,11... | collective-permute-start | bytes 233480 | tf_op jit(solution)/shard_map/ppermute | solution.py:551
  39.5 5.3 %collective-permute-start.9 = (f32[25,8,128]{2,1,0:T(8,128)S(1)}, f32[25,8,128]{2,1,0:T(8,128)S(1)}, u32[]{:S(2)}, u32[]{:S(2)}) collective-permute-start(f32[25,8,128]{2,1,0:T(8,128)S(1)} %get-tuple-element.89), channel_id=1, source_target_pairs={{0,2},{1,5},{2,0},{3,7},{4,6},{5,1},{6,4},{7,3},{8,10},{9,13},{10,... | collective-permute-start | bytes 307208 | tf_op jit(solution)/shard_map/ppermute | solution.py:551
  40.1 5.3 %collective-permute-start.10 = (f32[13,8,128]{2,1,0:T(8,128)S(1)}, f32[13,8,128]{2,1,0:T(8,128)S(1)}, u32[]{:S(2)}, u32[]{:S(2)}) collective-permute-start(f32[13,8,128]{2,1,0:T(8,128)S(1)} %get-tuple-element.90), channel_id=1, source_target_pairs={{0,6},{1,7},{2,4},{3,5},{4,2},{5,3},{6,0},{7,1},{8,14},{9,15},{10,... | collective-permute-start | bytes 159752 | tf_op jit(solution)/shard_map/ppermute | solution.py:551
  44.8 1.3 %collective-permute-start.11 = (f32[19,8,128]{2,1,0:T(8,128)S(1)}, f32[19,8,128]{2,1,0:T(8,128)S(1)}, u32[]{:S(2)}, u32[]{:S(2)}) collective-permute-start(f32[19,8,128]{2,1,0:T(8,128)S(1)} %shard_map.120), channel_id=1, source_target_pairs={{0,1},{1,0},{2,3},{3,2},{4,5},{5,4},{6,7},{7,6},{8,9},{9,8},{10,11... | collective-permute-start | bytes 233480 | tf_op jit(solution)/shard_map/ppermute | solution.py:551
  56.9 1.3 %collective-permute-start.12 = (f32[19,8,128]{2,1,0:T(8,128)S(1)}, f32[19,8,128]{2,1,0:T(8,128)S(1)}, u32[]{:S(2)}, u32[]{:S(2)}) collective-permute-start(f32[19,8,128]{2,1,0:T(8,128)S(1)} %get-tuple-element.101), channel_id=1, source_target_pairs={{0,1},{1,0},{2,3},{3,2},{4,5},{5,4},{6,7},{7,6},{8,9},{9,8},{10,11... | collective-permute-start | bytes 233480 | tf_op jit(solution)/shard_map/ppermute | solution.py:551
  58.2 5.3 %collective-permute-start.13 = (f32[25,8,128]{2,1,0:T(8,128)S(1)}, f32[25,8,128]{2,1,0:T(8,128)S(1)}, u32[]{:S(2)}, u32[]{:S(2)}) collective-permute-start(f32[25,8,128]{2,1,0:T(8,128)S(1)} %get-tuple-element.102), channel_id=1, source_target_pairs={{0,2},{1,5},{2,0},{3,7},{4,6},{5,1},{6,4},{7,3},{8,10},{9,13},{10,... | collective-permute-start | bytes 307208 | tf_op jit(solution)/shard_map/ppermute | solution.py:551
  58.8 5.3 %collective-permute-start.14 = (f32[13,8,128]{2,1,0:T(8,128)S(1)}, f32[13,8,128]{2,1,0:T(8,128)S(1)}, u32[]{:S(2)}, u32[]{:S(2)}) collective-permute-start(f32[13,8,128]{2,1,0:T(8,128)S(1)} %get-tuple-element.103), channel_id=1, source_target_pairs={{0,6},{1,7},{2,4},{3,5},{4,2},{5,3},{6,0},{7,1},{8,14},{9,15},{10,... | collective-permute-start | bytes 159752 | tf_op jit(solution)/shard_map/ppermute | solution.py:551
  63.5 1.3 %collective-permute-start.15 = (f32[19,8,128]{2,1,0:T(8,128)S(1)}, f32[19,8,128]{2,1,0:T(8,128)S(1)}, u32[]{:S(2)}, u32[]{:S(2)}) collective-permute-start(f32[19,8,128]{2,1,0:T(8,128)S(1)} %shard_map.126), channel_id=1, source_target_pairs={{0,1},{1,0},{2,3},{3,2},{4,5},{5,4},{6,7},{7,6},{8,9},{9,8},{10,11... | collective-permute-start | bytes 233480 | tf_op jit(solution)/shard_map/ppermute | solution.py:551
  75.6 1.3 %collective-permute-start.16 = (f32[19,8,128]{2,1,0:T(8,128)S(1)}, f32[19,8,128]{2,1,0:T(8,128)S(1)}, u32[]{:S(2)}, u32[]{:S(2)}) collective-permute-start(f32[19,8,128]{2,1,0:T(8,128)S(1)} %get-tuple-element.114), channel_id=1, source_target_pairs={{0,1},{1,0},{2,3},{3,2},{4,5},{5,4},{6,7},{7,6},{8,9},{9,8},{10,11... | collective-permute-start | bytes 233480 | tf_op jit(solution)/shard_map/ppermute | solution.py:551
  76.9 5.3 %collective-permute-start.17 = (f32[25,8,128]{2,1,0:T(8,128)S(1)}, f32[25,8,128]{2,1,0:T(8,128)S(1)}, u32[]{:S(2)}, u32[]{:S(2)}) collective-permute-start(f32[25,8,128]{2,1,0:T(8,128)S(1)} %get-tuple-element.115), channel_id=1, source_target_pairs={{0,2},{1,5},{2,0},{3,7},{4,6},{5,1},{6,4},{7,3},{8,10},{9,13},{10,... | collective-permute-start | bytes 307208 | tf_op jit(solution)/shard_map/ppermute | solution.py:551
  77.5 5.2 %collective-permute-start.18 = (f32[13,8,128]{2,1,0:T(8,128)S(1)}, f32[13,8,128]{2,1,0:T(8,128)S(1)}, u32[]{:S(2)}, u32[]{:S(2)}) collective-permute-start(f32[13,8,128]{2,1,0:T(8,128)S(1)} %get-tuple-element.116), channel_id=1, source_target_pairs={{0,6},{1,7},{2,4},{3,5},{4,2},{5,3},{6,0},{7,1},{8,14},{9,15},{10,... | collective-permute-start | bytes 159752 | tf_op jit(solution)/shard_map/ppermute | solution.py:551
  82.2 1.3 %collective-permute-start.19 = (f32[19,8,128]{2,1,0:T(8,128)S(1)}, f32[19,8,128]{2,1,0:T(8,128)S(1)}, u32[]{:S(2)}, u32[]{:S(2)}) collective-permute-start(f32[19,8,128]{2,1,0:T(8,128)S(1)} %shard_map.132), channel_id=1, source_target_pairs={{0,1},{1,0},{2,3},{3,2},{4,5},{5,4},{6,7},{7,6},{8,9},{9,8},{10,11... | collective-permute-start | bytes 233480 | tf_op jit(solution)/shard_map/ppermute | solution.py:551

commit v15 on v12

--- a/solution.py
+++ b/solution.py
@@ -86,7 +86,7 @@
         return len(self.handed) * self.rows(kinds)
 
     def at(self, k, core):
-        return (k + core) % len(self.far)
+        return k
 
     def mine(self, k):
         core = lax.axis_index("sub") & 1

time: 92.2 us -> 91 us (0.987)
  transfers between devices with their start and end apart: 25 -> 25, of which waited for: 17 -> 16; matrix products, arithmetic and copies ran while one was open for 0% -> 0% of each run, Pallas kernels for 7% -> 8%
where the time goes in v15:
time: 91 us; the launch traced here: 90.8 us
  blocking collectives  38.4 us (42%)
  starting transfers between devices  19.3 us (21%)
  Pallas kernels  16.7 us (18%)
  waiting for transfers between devices  15.6 us (17%)
    all_to_all x4, blocking collectives, on_device(): gathered = lax.all_to_all(sent, ('group', 'sub'), 0, 0, tiled=True)  38.4 us
    ppermute x25, starting transfers between devices, across(): return lax.ppermute(piece, 'sub', pairs)  19.3 us
    pallas_call x21, Pallas kernels, call(): pl.pallas_call(body, out_shape=shapes, in_specs=specs, out_specs=[SMEM if...  16.7 us
    ppermute x25, waiting for transfers between devices, across(): return lax.ppermute(piece, 'sub', pairs)  15.6 us
  transfers between devices with their start and end apart: 25, of which 16 were waited for; matrix products, arithmetic and copies ran while one was open for 0% of the time, Pallas kernels for 8%

profile of v15, /device:TPU:0, one launch (start us, length us, event | category | flops | bytes accessed | tf_op | source)
XLA Modules:
  0.0 90.8 jit_solution(6969788712927237595)
XLA Ops:
  0.6 1.0 %shard_map.104 = (s32[90]{0:T(128)S(4)}, f32[16,8,256]{2,1,0:T(8,128)S(1)}, f32[16,8,256]{2,1,0:T(8,128)S(1)}, f32[16,8,256]{2,1,0:T(8,128)S(1)}, bf16[16,16,256...) custom-call(s32[1,16]{1,0:T(1,128)} %partner.1, s32[1,16]{1,0:T(1,128)} %pattern.1, f32[8,16,256]{2,1,0:T(8,128)} %load.1, ...), custom_call_target="tpu_custom_call" | custom-call | flops 4000000 | bytes 250000 | tf_op jit(solution)/shard_map/pallas_call | solution.py:461
  2.2 1.0 %collective-permute-done.rest_2_ = f32[36,8,128]{2,1,0:T(8,128)S(1)} collective-permute-done((f32[36,8,128]{2,1,0:T(8,128)S(1)}, f32[36,8,128]{2,1,0:T(8,128)S(1)}, u32[]{:S(2)}, u32[]{:S(2)}) %collective-permute-start) | collective-permute-done | bytes 147488 | tf_op jit(solution)/shard_map/ppermute | solution.py:500
  3.2 3.9 %collective-permute-start.1 = (f32[24,8,128]{2,1,0:T(8,128)S(1)}, f32[24,8,128]{2,1,0:T(8,128)S(1)}, u32[]{:S(2)}, u32[]{:S(2)}) collective-permute-start(f32[24,8,128]{2,1,0:T(8,128)S(1)} %get-tuple-element.80), channel_id=1, source_target_pairs={{0,6},{1,7},{2,4},{3,5},{4,2},{5,3},{6,0},{7,1},{8,14},{9,15},{10,... | collective-permute-start | bytes 294920 | tf_op jit(solution)/shard_map/ppermute | solution.py:500
  7.8 2.3 %shard_map.105 = (f32[64,64]{1,0:T(8,128)S(1)}, bf16[16,256,256]{2,1,0:T(8,128)(2,1)S(1)}, bf16[16,256,256]{2,1,0:T(8,128)(2,1)S(1)}) custom-call(s32[1,64]{1,0:T(1,128)} %index_in.1, f32[32,32]{1,0:T(8,128)} %inverse_in.1, bf16[16,256,256]{2,1,0:T(8,128)(2,1)} %diag.1, bf16[16,256,256]{2,1,0:T(8,128)(2,1)} %off.1), custom_call_target="tpu_custom_call" | custom-call | flops 600000000 | bytes 37500000 | tf_op jit(solution)/shard_map/pallas_call | solution.py:461
  10.7 1.9 %collective-permute-done.2.rest_5_.rest_1_ = f32[24,8,128]{2,1,0:T(8,128)S(1)} collective-permute-done((f32[24,8,128]{2,1,0:T(8,128)S(1)}, f32[24,8,128]{2,1,0:T(8,128)S(1)}, u32[]{:S(2)}, u32[]{:S(2)}) %collective-permute-start.2) | collective-permute-done | bytes 98336 | tf_op jit(solution)/shard_map/ppermute | solution.py:500
  12.6 1.1 %shard_map.107 = (f32[16,8,256]{2,1,0:T(8,128)S(1)}, f32[16,8,256]{2,1,0:T(8,128)S(1)}, bf16[16,16,256]{2,1,0:T(8,128)(2,1)S(1)}, f32[8,128]{1,0:T(8,128)S(1)}, f32[19,8,128]{2,1,0:T(8,128)S(1)}) custom-call(s32[90]{0:T(128)S(4)} %get-tuple-element.71.table, f32[16,8,256]{2,1,0:T(8,128)S(1)} %get-tuple-element.73.rest_0_.wide, ...), custom_call_target="tpu_custom_call" | custom-call | flops 600000000 | bytes 37500000 | tf_op jit(solution)/shard_map/pallas_call | solution.py:461
  13.7 1.1 %shard_map.108.rest_0_.image = f32[16,8,256]{2,1,0:T(8,128)S(1)} custom-call(s32[90]{0:T(128)S(4)} %get-tuple-element.71.table, f32[16,8,256]{2,1,0:T(8,128)S(1)} %get-tuple-element.73.rest_0_.wide, bf16[16,256,256]{2,1,0:T(8,128)(2,1)S(1)} %get-tuple-element.74.rest_1_.diag, bf16[16,256,256]{2,1,0:T(8,128)(2,1)S(1)} %get-tuple-element.75.rest_2_.off, ...), custom_call_target="tpu_custom_call" | custom-call | flops 600000000 | bytes 37500000 | tf_op jit(solution)/shard_map/pallas_call | solution.py:461
  15.0 2.5 %collective-permute-start.6 = (f32[13,8,128]{2,1,0:T(8,128)S(1)}, f32[13,8,128]{2,1,0:T(8,128)S(1)}, u32[]{:S(2)}, u32[]{:S(2)}) collective-permute-start(f32[13,8,128]{2,1,0:T(8,128)S(1)} %get-tuple-element.89), channel_id=1, source_target_pairs={{0,6},{1,7},{2,4},{3,5},{4,2},{5,3},{6,0},{7,1},{8,14},{9,15},{10,... | collective-permute-start | bytes 159752 | tf_op jit(solution)/shard_map/ppermute | solution.py:500
  18.8 1.3 %collective-permute-done.6.rest_0_ = f32[13,8,128]{2,1,0:T(8,128)S(1)} collective-permute-done((f32[13,8,128]{2,1,0:T(8,128)S(1)}, f32[13,8,128]{2,1,0:T(8,128)S(1)}, u32[]{:S(2)}, u32[]{:S(2)}) %collective-permute-start.6) | collective-permute-done | bytes 53280 | tf_op jit(solution)/shard_map/ppermute | solution.py:500
  20.1 1.5 %collective-permute-done.7.rest_1_ = f32[13,8,128]{2,1,0:T(8,128)S(1)} collective-permute-done((f32[13,8,128]{2,1,0:T(8,128)S(1)}, f32[13,8,128]{2,1,0:T(8,128)S(1)}, u32[]{:S(2)}, u32[]{:S(2)}) %collective-permute-start.7) | collective-permute-done | bytes 53280 | tf_op jit(solution)/shard_map/ppermute | solution.py:500
  22.2 0.8 shard_map.111
  22.9 11.9 %all_to_all.20.rest_4_ = f32[32,1,128]{2,1,0:T(1,128)S(1)} all-to-all(f32[32,1,128]{2,1,0:T(1,128)S(1)} %get-tuple-element.93), channel_id=1, replica_groups=mesh['group'=4,'sub'=8] {'group','sub'}, dimensions={0} | all-to-all | bytes 32768 | tf_op jit(solution)/shard_map/all_to_all | solution.py:581
  34.8 1.3 %shard_map.112 = (f32[16,8,256]{2,1,0:T(8,128)S(1)}, f32[16,8,256]{2,1,0:T(8,128)S(1)}, f32[8,128]{1,0:T(8,128)S(1)}, f32[16,8,256]{2,1,0:T(8,128)S(1)}, bf16[16...) custom-call(s32[90]{0:T(128)S(4)} %get-tuple-element.71.table, ...), custom_call_target="tpu_custom_call" | custom-call | flops 600000000 | bytes 37500000 | tf_op jit(solution)/shard_map/pallas_call | solution.py:461
  36.2 1.1 %shard_map.113 = (f32[16,8,256]{2,1,0:T(8,128)S(1)}, f32[16,8,256]{2,1,0:T(8,128)S(1)}) custom-call(s32[90]{0:T(128)S(4)} %get-tuple-element.71.table, f32[16,8,256]{2,1,0:T(8,128)S(1)} %get-tuple-element.73.rest_0_.wide, bf16[16,256,256]{2,1,0:T(8,128)(2,1)S(1)} %get-tuple-element.74.rest_1_.diag, bf16[16,256,256]{2,1,0:T(8,128)(2,1)S(1)} %get-tuple-element.75.rest_2_.off, ...), custom_call_target="tpu_custom_call" | custom-call | flops 600000000 | bytes 37500000 | tf_op jit(solution)/shard_map/pallas_call | solution.py:461
  38.2 1.4 %collective-permute-start.12 = (f32[13,8,128]{2,1,0:T(8,128)S(1)}, f32[13,8,128]{2,1,0:T(8,128)S(1)}, u32[]{:S(2)}, u32[]{:S(2)}) collective-permute-start(f32[13,8,128]{2,1,0:T(8,128)S(1)} %get-tuple-element.104), channel_id=1, source_target_pairs={{0,2},{1,3},{2,0},{3,1},{4,6},{5,7},{6,4},{7,5},{8,10},{9,11},{10,... | collective-permute-start | bytes 159752 | tf_op jit(solution)/shard_map/ppermute | solution.py:500
  39.6 1.5 %collective-permute-start.13 = (f32[13,8,128]{2,1,0:T(8,128)S(1)}, f32[13,8,128]{2,1,0:T(8,128)S(1)}, u32[]{:S(2)}, u32[]{:S(2)}) collective-permute-start(f32[13,8,128]{2,1,0:T(8,128)S(1)} %get-tuple-element.105), channel_id=1, source_target_pairs={{0,4},{1,5},{2,6},{3,7},{4,0},{5,1},{6,2},{7,3},{8,12},{9,13},{10,... | collective-permute-start | bytes 159752 | tf_op jit(solution)/shard_map/ppermute | solution.py:500
  41.0 2.0 %collective-permute-done.11.rest_1_ = f32[13,8,128]{2,1,0:T(8,128)S(1)} collective-permute-done((f32[13,8,128]{2,1,0:T(8,128)S(1)}, f32[13,8,128]{2,1,0:T(8,128)S(1)}, u32[]{:S(2)}, u32[]{:S(2)}) %collective-permute-start.11) | collective-permute-done | bytes 53280 | tf_op jit(solution)/shard_map/ppermute | solution.py:500
  44.4 8.8 %all_to_all.21.rest_4_ = f32[32,1,128]{2,1,0:T(1,128)S(1)} all-to-all(f32[32,1,128]{2,1,0:T(1,128)S(1)} %get-tuple-element.107), channel_id=1, replica_groups=mesh['group'=4,'sub'=8] {'group','sub'}, dimensions={0} | all-to-all | bytes 32768 | tf_op jit(solution)/shard_map/all_to_all | solution.py:581
  53.2 1.2 %shard_map.116 = (f32[16,8,256]{2,1,0:T(8,128)S(1)}, f32[16,8,256]{2,1,0:T(8,128)S(1)}, f32[8,128]{1,0:T(8,128)S(1)}, f32[16,8,256]{2,1,0:T(8,128)S(1)}, bf16[16...) custom-call(s32[90]{0:T(128)S(4)} %get-tuple-element.71.table, ...), custom_call_target="tpu_custom_call" | custom-call | flops 600000000 | bytes 37500000 | tf_op jit(solution)/shard_map/pallas_call | solution.py:461
  54.5 1.1 %shard_map.117 = (f32[16,8,256]{2,1,0:T(8,128)S(1)}, f32[16,8,256]{2,1,0:T(8,128)S(1)}) custom-call(s32[90]{0:T(128)S(4)} %get-tuple-element.71.table, f32[16,8,256]{2,1,0:T(8,128)S(1)} %get-tuple-element.73.rest_0_.wide, bf16[16,256,256]{2,1,0:T(8,128)(2,1)S(1)} %get-tuple-element.74.rest_1_.diag, bf16[16,256,256]{2,1,0:T(8,128)(2,1)S(1)} %get-tuple-element.75.rest_2_.off, ...), custom_call_target="tpu_custom_call" | custom-call | flops 600000000 | bytes 37500000 | tf_op jit(solution)/shard_map/pallas_call | solution.py:461
  56.4 1.4 %collective-permute-start.17 = (f32[13,8,128]{2,1,0:T(8,128)S(1)}, f32[13,8,128]{2,1,0:T(8,128)S(1)}, u32[]{:S(2)}, u32[]{:S(2)}) collective-permute-start(f32[13,8,128]{2,1,0:T(8,128)S(1)} %get-tuple-element.119), channel_id=1, source_target_pairs={{0,2},{1,3},{2,0},{3,1},{4,6},{5,7},{6,4},{7,5},{8,10},{9,11},{10,... | collective-permute-start | bytes 159752 | tf_op jit(solution)/shard_map/ppermute | solution.py:500
  57.8 1.5 %collective-permute-start.18 = (f32[13,8,128]{2,1,0:T(8,128)S(1)}, f32[13,8,128]{2,1,0:T(8,128)S(1)}, u32[]{:S(2)}, u32[]{:S(2)}) collective-permute-start(f32[13,8,128]{2,1,0:T(8,128)S(1)} %get-tuple-element.120), channel_id=1, source_target_pairs={{0,4},{1,5},{2,6},{3,7},{4,0},{5,1},{6,2},{7,3},{8,12},{9,13},{10,... | collective-permute-start | bytes 159752 | tf_op jit(solution)/shard_map/ppermute | solution.py:500
  59.3 2.0 %collective-permute-done.16.rest_1_ = f32[13,8,128]{2,1,0:T(8,128)S(1)} collective-permute-done((f32[13,8,128]{2,1,0:T(8,128)S(1)}, f32[13,8,128]{2,1,0:T(8,128)S(1)}, u32[]{:S(2)}, u32[]{:S(2)}) %collective-permute-start.16) | collective-permute-done | bytes 53280 | tf_op jit(solution)/shard_map/ppermute | solution.py:500
  62.0 0.7 shard_map.119
  62.7 8.8 %all_to_all.22.rest_4_ = f32[32,1,128]{2,1,0:T(1,128)S(1)} all-to-all(f32[32,1,128]{2,1,0:T(1,128)S(1)} %get-tuple-element.122), channel_id=1, replica_groups=mesh['group'=4,'sub'=8] {'group','sub'}, dimensions={0} | all-to-all | bytes 32768 | tf_op jit(solution)/shard_map/all_to_all | solution.py:581
  71.5 1.2 %shard_map.120 = (f32[16,8,256]{2,1,0:T(8,128)S(1)}, f32[16,8,256]{2,1,0:T(8,128)S(1)}, f32[8,128]{1,0:T(8,128)S(1)}, f32[16,8,256]{2,1,0:T(8,128)S(1)}, bf16[16...) custom-call(s32[90]{0:T(128)S(4)} %get-tuple-element.71.table, ...), custom_call_target="tpu_custom_call" | custom-call | flops 600000000 | bytes 37500000 | tf_op jit(solution)/shard_map/pallas_call | solution.py:461
  72.8 1.1 %shard_map.121 = (f32[16,8,256]{2,1,0:T(8,128)S(1)}, f32[16,8,256]{2,1,0:T(8,128)S(1)}) custom-call(s32[90]{0:T(128)S(4)} %get-tuple-element.71.table, f32[16,8,256]{2,1,0:T(8,128)S(1)} %get-tuple-element.73.rest_0_.wide, bf16[16,256,256]{2,1,0:T(8,128)(2,1)S(1)} %get-tuple-element.74.rest_1_.diag, bf16[16,256,256]{2,1,0:T(8,128)(2,1)S(1)} %get-tuple-element.75.rest_2_.off, ...), custom_call_target="tpu_custom_call" | custom-call | flops 600000000 | bytes 37500000 | tf_op jit(solution)/shard_map/pallas_call | solution.py:461
  74.7 1.4 %collective-permute-start.22 = (f32[13,8,128]{2,1,0:T(8,128)S(1)}, f32[13,8,128]{2,1,0:T(8,128)S(1)}, u32[]{:S(2)}, u32[]{:S(2)}) collective-permute-start(f32[13,8,128]{2,1,0:T(8,128)S(1)} %get-tuple-element.134), channel_id=1, source_target_pairs={{0,2},{1,3},{2,0},{3,1},{4,6},{5,7},{6,4},{7,5},{8,10},{9,11},{10,... | collective-permute-start | bytes 159752 | tf_op jit(solution)/shard_map/ppermute | solution.py:500
  76.1 1.5 %collective-permute-start.23 = (f32[13,8,128]{2,1,0:T(8,128)S(1)}, f32[13,8,128]{2,1,0:T(8,128)S(1)}, u32[]{:S(2)}, u32[]{:S(2)}) collective-permute-start(f32[13,8,128]{2,1,0:T(8,128)S(1)} %get-tuple-element.135), channel_id=1, source_target_pairs={{0,4},{1,5},{2,6},{3,7},{4,0},{5,1},{6,2},{7,3},{8,12},{9,13},{10,... | collective-permute-start | bytes 159752 | tf_op jit(solution)/shard_map/ppermute | solution.py:500
  77.6 2.0 %collective-permute-done.21.rest_1_ = f32[13,8,128]{2,1,0:T(8,128)S(1)} collective-permute-done((f32[13,8,128]{2,1,0:T(8,128)S(1)}, f32[13,8,128]{2,1,0:T(8,128)S(1)}, u32[]{:S(2)}, u32[]{:S(2)}) %collective-permute-start.21) | collective-permute-done | bytes 53280 | tf_op jit(solution)/shard_map/ppermute | solution.py:500
  80.9 8.8 %all_to_all.23.gathered = f32[32,1,128]{2,1,0:T(1,128)S(1)} all-to-all(f32[32,1,128]{2,1,0:T(1,128)S(1)} %get-tuple-element.137), channel_id=1, replica_groups=mesh['group'=4,'sub'=8] {'group','sub'}, dimensions={0} | all-to-all | bytes 32768 | tf_op jit(solution)/shard_map/all_to_all | solution.py:581
  89.8 1.0 %shard_map.124 = (f32[8,16,256]{2,1,0:T(8,128)}, f32[8,16,256]{2,1,0:T(8,128)}) custom-call(f32[32,1,128]{2,1,0:T(1,128)S(1)} %all_to_all.23.gathered, f32[16,8,256]{2,1,0:T(8,128)S(1)} %get-tuple-element.138.before, f32[16,8,256]{2,1,0:T(8,128)S(1)} %get-tuple-element.130.residual.residual_in, f32[16,8,256]{2,1,0:T(8,128)S(1)} %get-tuple-element.131.direction, ...), custom_call_target="tpu_custom_call" | custom-call | flops 4000000 | bytes 250000 | tf_op jit(solution)/shard_map/pallas_call | solution.py:461
  (43 shorter events, 9.7 us)
Async XLA Ops:
  1.7 1.5 %collective-permute-start = (f32[36,8,128]{2,1,0:T(8,128)S(1)}, f32[36,8,128]{2,1,0:T(8,128)S(1)}, u32[]{:S(2)}, u32[]{:S(2)}) collective-permute-start(f32[36,8,128]{2,1,0:T(8,128)S(1)} %get-tuple-element.79), channel_id=1, source_target_pairs={{0,1},{1,0},{2,3},{3,2},{4,5},{5,4},{6,7},{7,6},{8,9},{9,8},{10,11... | collective-permute-start | bytes 442376 | tf_op jit(solution)/shard_map/ppermute | solution.py:500
  3.2 7.5 %collective-permute-start.1 = (f32[24,8,128]{2,1,0:T(8,128)S(1)}, f32[24,8,128]{2,1,0:T(8,128)S(1)}, u32[]{:S(2)}, u32[]{:S(2)}) collective-permute-start(f32[24,8,128]{2,1,0:T(8,128)S(1)} %get-tuple-element.80), channel_id=1, source_target_pairs={{0,6},{1,7},{2,4},{3,5},{4,2},{5,3},{6,0},{7,1},{8,14},{9,15},{10,... | collective-permute-start | bytes 294920 | tf_op jit(solution)/shard_map/ppermute | solution.py:500
  7.1 5.5 %collective-permute-start.2 = (f32[24,8,128]{2,1,0:T(8,128)S(1)}, f32[24,8,128]{2,1,0:T(8,128)S(1)}, u32[]{:S(2)}, u32[]{:S(2)}) collective-permute-start(f32[24,8,128]{2,1,0:T(8,128)S(1)} %get-tuple-element.81), channel_id=1, source_target_pairs={{0,2},{1,3},{2,0},{3,1},{4,6},{5,7},{6,4},{7,5},{8,10},{9,11},{10,... | collective-permute-start | bytes 294920 | tf_op jit(solution)/shard_map/ppermute | solution.py:500
  7.7 4.9 %collective-permute-start.3 = (f32[24,8,128]{2,1,0:T(8,128)S(1)}, f32[24,8,128]{2,1,0:T(8,128)S(1)}, u32[]{:S(2)}, u32[]{:S(2)}) collective-permute-start(f32[24,8,128]{2,1,0:T(8,128)S(1)} %get-tuple-element.82), channel_id=1, source_target_pairs={{0,4},{1,5},{2,6},{3,7},{4,0},{5,1},{6,2},{7,3},{8,12},{9,13},{10,... | collective-permute-start | bytes 294920 | tf_op jit(solution)/shard_map/ppermute | solution.py:500
  7.8 4.8 %collective-permute-start.4 = (f32[24,8,128]{2,1,0:T(8,128)S(1)}, f32[24,8,128]{2,1,0:T(8,128)S(1)}, u32[]{:S(2)}, u32[]{:S(2)}) collective-permute-start(f32[24,8,128]{2,1,0:T(8,128)S(1)} %get-tuple-element.83), channel_id=1, source_target_pairs={{0,1},{1,0},{2,3},{3,2},{4,5},{5,4},{6,7},{7,6},{8,9},{9,8},{10,11... | collective-permute-start | bytes 294920 | tf_op jit(solution)/shard_map/ppermute | solution.py:500
  13.7 1.3 %collective-permute-start.5 = (f32[19,8,128]{2,1,0:T(8,128)S(1)}, f32[19,8,128]{2,1,0:T(8,128)S(1)}, u32[]{:S(2)}, u32[]{:S(2)}) collective-permute-start(f32[19,8,128]{2,1,0:T(8,128)S(1)} %get-tuple-element.88), channel_id=1, source_target_pairs={{0,1},{1,0},{2,3},{3,2},{4,5},{5,4},{6,7},{7,6},{8,9},{9,8},{10,11... | collective-permute-start | bytes 233480 | tf_op jit(solution)/shard_map/ppermute | solution.py:500
  15.0 5.1 %collective-permute-start.6 = (f32[13,8,128]{2,1,0:T(8,128)S(1)}, f32[13,8,128]{2,1,0:T(8,128)S(1)}, u32[]{:S(2)}, u32[]{:S(2)}) collective-permute-start(f32[13,8,128]{2,1,0:T(8,128)S(1)} %get-tuple-element.89), channel_id=1, source_target_pairs={{0,6},{1,7},{2,4},{3,5},{4,2},{5,3},{6,0},{7,1},{8,14},{9,15},{10,... | collective-permute-start | bytes 159752 | tf_op jit(solution)/shard_map/ppermute | solution.py:500
  17.5 4.1 %collective-permute-start.7 = (f32[13,8,128]{2,1,0:T(8,128)S(1)}, f32[13,8,128]{2,1,0:T(8,128)S(1)}, u32[]{:S(2)}, u32[]{:S(2)}) collective-permute-start(f32[13,8,128]{2,1,0:T(8,128)S(1)} %get-tuple-element.90), channel_id=1, source_target_pairs={{0,2},{1,3},{2,0},{3,1},{4,6},{5,7},{6,4},{7,5},{8,10},{9,11},{10,... | collective-permute-start | bytes 159752 | tf_op jit(solution)/shard_map/ppermute | solution.py:500
  18.0 4.1 %collective-permute-start.8 = (f32[13,8,128]{2,1,0:T(8,128)S(1)}, f32[13,8,128]{2,1,0:T(8,128)S(1)}, u32[]{:S(2)}, u32[]{:S(2)}) collective-permute-start(f32[13,8,128]{2,1,0:T(8,128)S(1)} %get-tuple-element.91), channel_id=1, source_target_pairs={{0,4},{1,5},{2,6},{3,7},{4,0},{5,1},{6,2},{7,3},{8,12},{9,13},{10,... | collective-permute-start | bytes 159752 | tf_op jit(solution)/shard_map/ppermute | solution.py:500
  18.6 3.6 %collective-permute-start.9 = (f32[13,8,128]{2,1,0:T(8,128)S(1)}, f32[13,8,128]{2,1,0:T(8,128)S(1)}, u32[]{:S(2)}, u32[]{:S(2)}) collective-permute-start(f32[13,8,128]{2,1,0:T(8,128)S(1)} %get-tuple-element.92), channel_id=1, source_target_pairs={{0,1},{1,0},{2,3},{3,2},{4,5},{5,4},{6,7},{7,6},{8,9},{9,8},{10,11... | collective-permute-start | bytes 159752 | tf_op jit(solution)/shard_map/ppermute | solution.py:500
  36.2 1.3 %collective-permute-start.10 = (f32[19,8,128]{2,1,0:T(8,128)S(1)}, f32[19,8,128]{2,1,0:T(8,128)S(1)}, u32[]{:S(2)}, u32[]{:S(2)}) collective-permute-start(f32[19,8,128]{2,1,0:T(8,128)S(1)} %get-tuple-element.102), channel_id=1, source_target_pairs={{0,1},{1,0},{2,3},{3,2},{4,5},{5,4},{6,7},{7,6},{8,9},{9,8},{10,11... | collective-permute-start | bytes 233480 | tf_op jit(solution)/shard_map/ppermute | solution.py:500
  37.5 5.6 %collective-permute-start.11 = (f32[13,8,128]{2,1,0:T(8,128)S(1)}, f32[13,8,128]{2,1,0:T(8,128)S(1)}, u32[]{:S(2)}, u32[]{:S(2)}) collective-permute-start(f32[13,8,128]{2,1,0:T(8,128)S(1)} %get-tuple-element.103), channel_id=1, source_target_pairs={{0,6},{1,7},{2,4},{3,5},{4,2},{5,3},{6,0},{7,1},{8,14},{9,15},{10,... | collective-permute-start | bytes 159752 | tf_op jit(solution)/shard_map/ppermute | solution.py:500
  38.2 4.9 %collective-permute-start.12 = (f32[13,8,128]{2,1,0:T(8,128)S(1)}, f32[13,8,128]{2,1,0:T(8,128)S(1)}, u32[]{:S(2)}, u32[]{:S(2)}) collective-permute-start(f32[13,8,128]{2,1,0:T(8,128)S(1)} %get-tuple-element.104), channel_id=1, source_target_pairs={{0,2},{1,3},{2,0},{3,1},{4,6},{5,7},{6,4},{7,5},{8,10},{9,11},{10,... | collective-permute-start | bytes 159752 | tf_op jit(solution)/shard_map/ppermute | solution.py:500
  39.6 4.1 %collective-permute-start.13 = (f32[13,8,128]{2,1,0:T(8,128)S(1)}, f32[13,8,128]{2,1,0:T(8,128)S(1)}, u32[]{:S(2)}, u32[]{:S(2)}) collective-permute-start(f32[13,8,128]{2,1,0:T(8,128)S(1)} %get-tuple-element.105), channel_id=1, source_target_pairs={{0,4},{1,5},{2,6},{3,7},{4,0},{5,1},{6,2},{7,3},{8,12},{9,13},{10,... | collective-permute-start | bytes 159752 | tf_op jit(solution)/shard_map/ppermute | solution.py:500
  41.0 2.7 %collective-permute-start.14 = (f32[13,8,128]{2,1,0:T(8,128)S(1)}, f32[13,8,128]{2,1,0:T(8,128)S(1)}, u32[]{:S(2)}, u32[]{:S(2)}) collective-permute-start(f32[13,8,128]{2,1,0:T(8,128)S(1)} %get-tuple-element.106), channel_id=1, source_target_pairs={{0,1},{1,0},{2,3},{3,2},{4,5},{5,4},{6,7},{7,6},{8,9},{9,8},{10,11... | collective-permute-start | bytes 159752 | tf_op jit(solution)/shard_map/ppermute | solution.py:500
  54.5 1.3 %collective-permute-start.15 = (f32[19,8,128]{2,1,0:T(8,128)S(1)}, f32[19,8,128]{2,1,0:T(8,128)S(1)}, u32[]{:S(2)}, u32[]{:S(2)}) collective-permute-start(f32[19,8,128]{2,1,0:T(8,128)S(1)} %get-tuple-element.117), channel_id=1, source_target_pairs={{0,1},{1,0},{2,3},{3,2},{4,5},{5,4},{6,7},{7,6},{8,9},{9,8},{10,11... | collective-permute-start | bytes 233480 | tf_op jit(solution)/shard_map/ppermute | solution.py:500
  55.8 5.6 %collective-permute-start.16 = (f32[13,8,128]{2,1,0:T(8,128)S(1)}, f32[13,8,128]{2,1,0:T(8,128)S(1)}, u32[]{:S(2)}, u32[]{:S(2)}) collective-permute-start(f32[13,8,128]{2,1,0:T(8,128)S(1)} %get-tuple-element.118), channel_id=1, source_target_pairs={{0,6},{1,7},{2,4},{3,5},{4,2},{5,3},{6,0},{7,1},{8,14},{9,15},{10,... | collective-permute-start | bytes 159752 | tf_op jit(solution)/shard_map/ppermute | solution.py:500
  56.4 4.9 %collective-permute-start.17 = (f32[13,8,128]{2,1,0:T(8,128)S(1)}, f32[13,8,128]{2,1,0:T(8,128)S(1)}, u32[]{:S(2)}, u32[]{:S(2)}) collective-permute-start(f32[13,8,128]{2,1,0:T(8,128)S(1)} %get-tuple-element.119), channel_id=1, source_target_pairs={{0,2},{1,3},{2,0},{3,1},{4,6},{5,7},{6,4},{7,5},{8,10},{9,11},{10,... | collective-permute-start | bytes 159752 | tf_op jit(solution)/shard_map/ppermute | solution.py:500
  57.8 4.1 %collective-permute-start.18 = (f32[13,8,128]{2,1,0:T(8,128)S(1)}, f32[13,8,128]{2,1,0:T(8,128)S(1)}, u32[]{:S(2)}, u32[]{:S(2)}) collective-permute-start(f32[13,8,128]{2,1,0:T(8,128)S(1)} %get-tuple-element.120), channel_id=1, source_target_pairs={{0,4},{1,5},{2,6},{3,7},{4,0},{5,1},{6,2},{7,3},{8,12},{9,13},{10,... | collective-permute-start | bytes 159752 | tf_op jit(solution)/shard_map/ppermute | solution.py:500
  59.3 2.7 %collective-permute-start.19 = (f32[13,8,128]{2,1,0:T(8,128)S(1)}, f32[13,8,128]{2,1,0:T(8,128)S(1)}, u32[]{:S(2)}, u32[]{:S(2)}) collective-permute-start(f32[13,8,128]{2,1,0:T(8,128)S(1)} %get-tuple-element.121), channel_id=1, source_target_pairs={{0,1},{1,0},{2,3},{3,2},{4,5},{5,4},{6,7},{7,6},{8,9},{9,8},{10,11... | collective-permute-start | bytes 159752 | tf_op jit(solution)/shard_map/ppermute | solution.py:500
  72.7 1.3 %collective-permute-start.20 = (f32[19,8,128]{2,1,0:T(8,128)S(1)}, f32[19,8,128]{2,1,0:T(8,128)S(1)}, u32[]{:S(2)}, u32[]{:S(2)}) collective-permute-start(f32[19,8,128]{2,1,0:T(8,128)S(1)} %get-tuple-element.132), channel_id=1, source_target_pairs={{0,1},{1,0},{2,3},{3,2},{4,5},{5,4},{6,7},{7,6},{8,9},{9,8},{10,11... | collective-permute-start | bytes 233480 | tf_op jit(solution)/shard_map/ppermute | solution.py:500
  74.0 5.6 %collective-permute-start.21 = (f32[13,8,128]{2,1,0:T(8,128)S(1)}, f32[13,8,128]{2,1,0:T(8,128)S(1)}, u32[]{:S(2)}, u32[]{:S(2)}) collective-permute-start(f32[13,8,128]{2,1,0:T(8,128)S(1)} %get-tuple-element.133), channel_id=1, source_target_pairs={{0,6},{1,7},{2,4},{3,5},{4,2},{5,3},{6,0},{7,1},{8,14},{9,15},{10,... | collective-permute-start | bytes 159752 | tf_op jit(solution)/shard_map/ppermute | solution.py:500
  74.7 4.9 %collective-permute-start.22 = (f32[13,8,128]{2,1,0:T(8,128)S(1)}, f32[13,8,128]{2,1,0:T(8,128)S(1)}, u32[]{:S(2)}, u32[]{:S(2)}) collective-permute-start(f32[13,8,128]{2,1,0:T(8,128)S(1)} %get-tuple-element.134), channel_id=1, source_target_pairs={{0,2},{1,3},{2,0},{3,1},{4,6},{5,7},{6,4},{7,5},{8,10},{9,11},{10,... | collective-permute-start | bytes 159752 | tf_op jit(solution)/shard_map/ppermute | solution.py:500
  76.1 4.1 %collective-permute-start.23 = (f32[13,8,128]{2,1,0:T(8,128)S(1)}, f32[13,8,128]{2,1,0:T(8,128)S(1)}, u32[]{:S(2)}, u32[]{:S(2)}) collective-permute-start(f32[13,8,128]{2,1,0:T(8,128)S(1)} %get-tuple-element.135), channel_id=1, source_target_pairs={{0,4},{1,5},{2,6},{3,7},{4,0},{5,1},{6,2},{7,3},{8,12},{9,13},{10,... | collective-permute-start | bytes 159752 | tf_op jit(solution)/shard_map/ppermute | solution.py:500
  77.6 2.7 %collective-permute-start.24 = (f32[13,8,128]{2,1,0:T(8,128)S(1)}, f32[13,8,128]{2,1,0:T(8,128)S(1)}, u32[]{:S(2)}, u32[]{:S(2)}) collective-permute-start(f32[13,8,128]{2,1,0:T(8,128)S(1)} %get-tuple-element.136), channel_id=1, source_target_pairs={{0,1},{1,0},{2,3},{3,2},{4,5},{5,4},{6,7},{7,6},{8,9},{9,8},{10,11... | collective-permute-start | bytes 159752 | tf_op jit(solution)/shard_map/ppermute | solution.py:500

commit v16 on v11

--- a/solution.py
+++ b/solution.py
@@ -232,9 +232,7 @@
     copies[1].wait()
     rows = lax.broadcasted_iota(jnp.int32, (z.coarse, z.all_corners), 0)
     select = (rows == index[...]).astype(BF16)
-    parts = jnp.concatenate(split3(inverse[...]), axis=0).astype(BF16)
-    half = dot(parts, select, NN)
-    half = sum(half[k * z.coarse : (k + 1) * z.coarse] for k in range(3))
+    half = sum(dot(part.astype(BF16), select, TN) for part in split3(inverse[...]))
     parts = jnp.concatenate(split3(half), axis=1).astype(BF16)
     full = dot(select, parts, TN)
     operator[...] = sum(full[:, k * z.all_corners : (k + 1) * z.all_corners] for k in range(3))
@@ -291,6 +289,7 @@
     total = lax.fori_loop(0, count, lambda k, acc: acc + gathered[k], zero, unroll=unroll)
     norm, way, rest = [to_tile(z, total, k * z.columns) for k in (RR, DP, RP)]
     alpha = norm / way
+    turn = 1.0 / norm
     if previous is None:
         placed = to_row(z, [(PP * z.columns, alpha)])
 
@@ -304,7 +303,7 @@
     else:
         ratio = alpha / used_step(previous)
         moved = to_tile(z, total, PP * z.columns) * ratio * ratio
-    return alpha, (norm - 2.0 * alpha * rest + moved) / norm
+    return alpha, (norm - 2.0 * alpha * rest + moved) * turn
 
 
 def used_step(previous):
@@ -408,7 +407,7 @@
         scale = across_block(z, used_step(previous[...]))
     place(z, table, [beside, *far], 0, 1, other)
     partials = extra_sum(z, own_extra, near, *far)[:, : z.all_corners]
-    local = dot_high(partials, operator[...], NT)
+    local = dot_high(partials, operator[...], NN)
     rows = pad(jnp.concatenate([local, local], axis=1))
     zero = jnp.zeros((z.columns, z.width), F32)
     sums = [zero] * (4 if step > 0 else 3)

time: 91.1 us -> 90.7 us (level)
  transfers between devices with their start and end apart: 25 -> 25, of which waited for: 16 -> 16; matrix products, arithmetic and copies ran while one was open for 0% -> 0% of each run, Pallas kernels for 7% -> 8%
where the time goes in v16:
time: 90.7 us; the launch traced here: 90.5 us
  blocking collectives  38.4 us (42%)
  starting transfers between devices  19.3 us (21%)
  Pallas kernels  16.4 us (18%)
  waiting for transfers between devices  15.6 us (17%)
    all_to_all x4, blocking collectives, on_device(): gathered = lax.all_to_all(sent, ('group', 'sub'), 0, 0, tiled=True)  38.4 us
    ppermute x25, starting transfers between devices, across(): return lax.ppermute(piece, 'sub', pairs)  19.3 us
    pallas_call x21, Pallas kernels, call(): pl.pallas_call(body, out_shape=shapes, in_specs=specs, out_specs=[SMEM if...  16.4 us
    ppermute x25, waiting for transfers between devices, across(): return lax.ppermute(piece, 'sub', pairs)  15.6 us
  transfers between devices with their start and end apart: 25, of which 16 were waited for; matrix products, arithmetic and copies ran while one was open for 0% of the time, Pallas kernels for 8%

profile of v16, /device:TPU:0, one launch (start us, length us, event | category | flops | bytes accessed | tf_op | source)
XLA Modules:
  0.0 90.5 jit_solution(7497789212190752432)
XLA Ops:
  0.6 1.0 %shard_map.104 = (s32[90]{0:T(128)S(4)}, f32[16,8,256]{2,1,0:T(8,128)S(1)}, f32[16,8,256]{2,1,0:T(8,128)S(1)}, f32[16,8,256]{2,1,0:T(8,128)S(1)}, bf16[16,16,256...) custom-call(s32[1,16]{1,0:T(1,128)} %partner.1, s32[1,16]{1,0:T(1,128)} %pattern.1, f32[8,16,256]{2,1,0:T(8,128)} %load.1, ...), custom_call_target="tpu_custom_call" | custom-call | flops 4000000 | bytes 250000 | tf_op jit(solution)/shard_map/pallas_call | solution.py:461
  2.2 1.0 %collective-permute-done.rest_2_ = f32[36,8,128]{2,1,0:T(8,128)S(1)} collective-permute-done((f32[36,8,128]{2,1,0:T(8,128)S(1)}, f32[36,8,128]{2,1,0:T(8,128)S(1)}, u32[]{:S(2)}, u32[]{:S(2)}) %collective-permute-start) | collective-permute-done | bytes 147488 | tf_op jit(solution)/shard_map/ppermute | solution.py:500
  3.3 3.9 %collective-permute-start.1 = (f32[24,8,128]{2,1,0:T(8,128)S(1)}, f32[24,8,128]{2,1,0:T(8,128)S(1)}, u32[]{:S(2)}, u32[]{:S(2)}) collective-permute-start(f32[24,8,128]{2,1,0:T(8,128)S(1)} %get-tuple-element.80), channel_id=1, source_target_pairs={{0,6},{1,7},{2,4},{3,5},{4,2},{5,3},{6,0},{7,1},{8,14},{9,15},{10,... | collective-permute-start | bytes 294920 | tf_op jit(solution)/shard_map/ppermute | solution.py:500
  7.8 2.3 %shard_map.105 = (f32[64,64]{1,0:T(8,128)S(1)}, bf16[16,256,256]{2,1,0:T(8,128)(2,1)S(1)}, bf16[16,256,256]{2,1,0:T(8,128)(2,1)S(1)}) custom-call(s32[1,64]{1,0:T(1,128)} %index_in.1, f32[32,32]{1,0:T(8,128)} %inverse_in.1, bf16[16,256,256]{2,1,0:T(8,128)(2,1)} %diag.1, bf16[16,256,256]{2,1,0:T(8,128)(2,1)} %off.1), custom_call_target="tpu_custom_call" | custom-call | flops 600000000 | bytes 37500000 | tf_op jit(solution)/shard_map/pallas_call | solution.py:461
  10.3 2.3 %collective-permute-done.2.rest_5_.rest_1_ = f32[24,8,128]{2,1,0:T(8,128)S(1)} collective-permute-done((f32[24,8,128]{2,1,0:T(8,128)S(1)}, f32[24,8,128]{2,1,0:T(8,128)S(1)}, u32[]{:S(2)}, u32[]{:S(2)}) %collective-permute-start.2) | collective-permute-done | bytes 98336 | tf_op jit(solution)/shard_map/ppermute | solution.py:500
  12.6 1.1 %shard_map.107 = (f32[16,8,256]{2,1,0:T(8,128)S(1)}, f32[16,8,256]{2,1,0:T(8,128)S(1)}, bf16[16,16,256]{2,1,0:T(8,128)(2,1)S(1)}, f32[8,128]{1,0:T(8,128)S(1)}, f32[19,8,128]{2,1,0:T(8,128)S(1)}) custom-call(s32[90]{0:T(128)S(4)} %get-tuple-element.71.table, f32[16,8,256]{2,1,0:T(8,128)S(1)} %get-tuple-element.73.rest_0_.wide, ...), custom_call_target="tpu_custom_call" | custom-call | flops 600000000 | bytes 37500000 | tf_op jit(solution)/shard_map/pallas_call | solution.py:461
  13.8 1.1 %shard_map.108.rest_0_.image = f32[16,8,256]{2,1,0:T(8,128)S(1)} custom-call(s32[90]{0:T(128)S(4)} %get-tuple-element.71.table, f32[16,8,256]{2,1,0:T(8,128)S(1)} %get-tuple-element.73.rest_0_.wide, bf16[16,256,256]{2,1,0:T(8,128)(2,1)S(1)} %get-tuple-element.74.rest_1_.diag, bf16[16,256,256]{2,1,0:T(8,128)(2,1)S(1)} %get-tuple-element.75.rest_2_.off, ...), custom_call_target="tpu_custom_call" | custom-call | flops 600000000 | bytes 37500000 | tf_op jit(solution)/shard_map/pallas_call | solution.py:461
  15.0 1.7 %collective-permute-start.6 = (f32[13,8,128]{2,1,0:T(8,128)S(1)}, f32[13,8,128]{2,1,0:T(8,128)S(1)}, u32[]{:S(2)}, u32[]{:S(2)}) collective-permute-start(f32[13,8,128]{2,1,0:T(8,128)S(1)} %get-tuple-element.89), channel_id=1, source_target_pairs={{0,6},{1,7},{2,4},{3,5},{4,2},{5,3},{6,0},{7,1},{8,14},{9,15},{10,... | collective-permute-start | bytes 159752 | tf_op jit(solution)/shard_map/ppermute | solution.py:500
  16.8 1.3 %collective-permute-start.7 = (f32[13,8,128]{2,1,0:T(8,128)S(1)}, f32[13,8,128]{2,1,0:T(8,128)S(1)}, u32[]{:S(2)}, u32[]{:S(2)}) collective-permute-start(f32[13,8,128]{2,1,0:T(8,128)S(1)} %get-tuple-element.90), channel_id=1, source_target_pairs={{0,2},{1,5},{2,0},{3,7},{4,6},{5,1},{6,4},{7,3},{8,10},{9,13},{10,... | collective-permute-start | bytes 159752 | tf_op jit(solution)/shard_map/ppermute | solution.py:500
  18.8 1.4 %collective-permute-done.6.rest_0_ = f32[13,8,128]{2,1,0:T(8,128)S(1)} collective-permute-done((f32[13,8,128]{2,1,0:T(8,128)S(1)}, f32[13,8,128]{2,1,0:T(8,128)S(1)}, u32[]{:S(2)}, u32[]{:S(2)}) %collective-permute-start.6) | collective-permute-done | bytes 53280 | tf_op jit(solution)/shard_map/ppermute | solution.py:500
  20.2 1.1 %collective-permute-done.7.rest_1_ = f32[13,8,128]{2,1,0:T(8,128)S(1)} collective-permute-done((f32[13,8,128]{2,1,0:T(8,128)S(1)}, f32[13,8,128]{2,1,0:T(8,128)S(1)}, u32[]{:S(2)}, u32[]{:S(2)}) %collective-permute-start.7) | collective-permute-done | bytes 53280 | tf_op jit(solution)/shard_map/ppermute | solution.py:500
  21.3 0.9 collective-permute-done.8.rest_2_
  22.9 11.9 %all_to_all.20.rest_4_ = f32[32,1,128]{2,1,0:T(1,128)S(1)} all-to-all(f32[32,1,128]{2,1,0:T(1,128)S(1)} %get-tuple-element.93), channel_id=1, replica_groups=mesh['group'=4,'sub'=8] {'group','sub'}, dimensions={0} | all-to-all | bytes 32768 | tf_op jit(solution)/shard_map/all_to_all | solution.py:581
  34.8 1.3 %shard_map.112 = (f32[16,8,256]{2,1,0:T(8,128)S(1)}, f32[16,8,256]{2,1,0:T(8,128)S(1)}, f32[8,128]{1,0:T(8,128)S(1)}, f32[16,8,256]{2,1,0:T(8,128)S(1)}, bf16[16...) custom-call(s32[90]{0:T(128)S(4)} %get-tuple-element.71.table, ...), custom_call_target="tpu_custom_call" | custom-call | flops 600000000 | bytes 37500000 | tf_op jit(solution)/shard_map/pallas_call | solution.py:461
  36.1 1.1 %shard_map.113 = (f32[16,8,256]{2,1,0:T(8,128)S(1)}, f32[16,8,256]{2,1,0:T(8,128)S(1)}) custom-call(s32[90]{0:T(128)S(4)} %get-tuple-element.71.table, f32[16,8,256]{2,1,0:T(8,128)S(1)} %get-tuple-element.73.rest_0_.wide, bf16[16,256,256]{2,1,0:T(8,128)(2,1)S(1)} %get-tuple-element.74.rest_1_.diag, bf16[16,256,256]{2,1,0:T(8,128)(2,1)S(1)} %get-tuple-element.75.rest_2_.off, ...), custom_call_target="tpu_custom_call" | custom-call | flops 600000000 | bytes 37500000 | tf_op jit(solution)/shard_map/pallas_call | solution.py:461
  38.1 1.4 %collective-permute-start.12 = (f32[13,8,128]{2,1,0:T(8,128)S(1)}, f32[13,8,128]{2,1,0:T(8,128)S(1)}, u32[]{:S(2)}, u32[]{:S(2)}) collective-permute-start(f32[13,8,128]{2,1,0:T(8,128)S(1)} %get-tuple-element.104), channel_id=1, source_target_pairs={{0,2},{1,5},{2,0},{3,7},{4,6},{5,1},{6,4},{7,3},{8,10},{9,13},{10,... | collective-permute-start | bytes 159752 | tf_op jit(solution)/shard_map/ppermute | solution.py:500
  39.5 1.5 %collective-permute-start.13 = (f32[13,8,128]{2,1,0:T(8,128)S(1)}, f32[13,8,128]{2,1,0:T(8,128)S(1)}, u32[]{:S(2)}, u32[]{:S(2)}) collective-permute-start(f32[13,8,128]{2,1,0:T(8,128)S(1)} %get-tuple-element.105), channel_id=1, source_target_pairs={{0,4},{1,3},{2,6},{3,1},{4,0},{5,7},{6,2},{7,5},{8,12},{9,11},{10,... | collective-permute-start | bytes 159752 | tf_op jit(solution)/shard_map/ppermute | solution.py:500
  41.0 2.1 %collective-permute-done.11.rest_1_ = f32[13,8,128]{2,1,0:T(8,128)S(1)} collective-permute-done((f32[13,8,128]{2,1,0:T(8,128)S(1)}, f32[13,8,128]{2,1,0:T(8,128)S(1)}, u32[]{:S(2)}, u32[]{:S(2)}) %collective-permute-start.11) | collective-permute-done | bytes 53280 | tf_op jit(solution)/shard_map/ppermute | solution.py:500
  44.2 8.8 %all_to_all.21.rest_4_ = f32[32,1,128]{2,1,0:T(1,128)S(1)} all-to-all(f32[32,1,128]{2,1,0:T(1,128)S(1)} %get-tuple-element.107), channel_id=1, replica_groups=mesh['group'=4,'sub'=8] {'group','sub'}, dimensions={0} | all-to-all | bytes 32768 | tf_op jit(solution)/shard_map/all_to_all | solution.py:581
  53.1 1.2 %shard_map.116 = (f32[16,8,256]{2,1,0:T(8,128)S(1)}, f32[16,8,256]{2,1,0:T(8,128)S(1)}, f32[8,128]{1,0:T(8,128)S(1)}, f32[16,8,256]{2,1,0:T(8,128)S(1)}, bf16[16...) custom-call(s32[90]{0:T(128)S(4)} %get-tuple-element.71.table, ...), custom_call_target="tpu_custom_call" | custom-call | flops 600000000 | bytes 37500000 | tf_op jit(solution)/shard_map/pallas_call | solution.py:461
  54.3 1.1 %shard_map.117 = (f32[16,8,256]{2,1,0:T(8,128)S(1)}, f32[16,8,256]{2,1,0:T(8,128)S(1)}) custom-call(s32[90]{0:T(128)S(4)} %get-tuple-element.71.table, f32[16,8,256]{2,1,0:T(8,128)S(1)} %get-tuple-element.73.rest_0_.wide, bf16[16,256,256]{2,1,0:T(8,128)(2,1)S(1)} %get-tuple-element.74.rest_1_.diag, bf16[16,256,256]{2,1,0:T(8,128)(2,1)S(1)} %get-tuple-element.75.rest_2_.off, ...), custom_call_target="tpu_custom_call" | custom-call | flops 600000000 | bytes 37500000 | tf_op jit(solution)/shard_map/pallas_call | solution.py:461
  56.3 1.4 %collective-permute-start.17 = (f32[13,8,128]{2,1,0:T(8,128)S(1)}, f32[13,8,128]{2,1,0:T(8,128)S(1)}, u32[]{:S(2)}, u32[]{:S(2)}) collective-permute-start(f32[13,8,128]{2,1,0:T(8,128)S(1)} %get-tuple-element.119), channel_id=1, source_target_pairs={{0,2},{1,5},{2,0},{3,7},{4,6},{5,1},{6,4},{7,3},{8,10},{9,13},{10,... | collective-permute-start | bytes 159752 | tf_op jit(solution)/shard_map/ppermute | solution.py:500
  57.7 1.5 %collective-permute-start.18 = (f32[13,8,128]{2,1,0:T(8,128)S(1)}, f32[13,8,128]{2,1,0:T(8,128)S(1)}, u32[]{:S(2)}, u32[]{:S(2)}) collective-permute-start(f32[13,8,128]{2,1,0:T(8,128)S(1)} %get-tuple-element.120), channel_id=1, source_target_pairs={{0,4},{1,3},{2,6},{3,1},{4,0},{5,7},{6,2},{7,5},{8,12},{9,11},{10,... | collective-permute-start | bytes 159752 | tf_op jit(solution)/shard_map/ppermute | solution.py:500
  59.2 2.1 %collective-permute-done.16.rest_1_ = f32[13,8,128]{2,1,0:T(8,128)S(1)} collective-permute-done((f32[13,8,128]{2,1,0:T(8,128)S(1)}, f32[13,8,128]{2,1,0:T(8,128)S(1)}, u32[]{:S(2)}, u32[]{:S(2)}) %collective-permute-start.16) | collective-permute-done | bytes 53280 | tf_op jit(solution)/shard_map/ppermute | solution.py:500
  62.4 8.8 %all_to_all.22.rest_4_ = f32[32,1,128]{2,1,0:T(1,128)S(1)} all-to-all(f32[32,1,128]{2,1,0:T(1,128)S(1)} %get-tuple-element.122), channel_id=1, replica_groups=mesh['group'=4,'sub'=8] {'group','sub'}, dimensions={0} | all-to-all | bytes 32768 | tf_op jit(solution)/shard_map/all_to_all | solution.py:581
  71.3 1.2 %shard_map.120 = (f32[16,8,256]{2,1,0:T(8,128)S(1)}, f32[16,8,256]{2,1,0:T(8,128)S(1)}, f32[8,128]{1,0:T(8,128)S(1)}, f32[16,8,256]{2,1,0:T(8,128)S(1)}, bf16[16...) custom-call(s32[90]{0:T(128)S(4)} %get-tuple-element.71.table, ...), custom_call_target="tpu_custom_call" | custom-call | flops 600000000 | bytes 37500000 | tf_op jit(solution)/shard_map/pallas_call | solution.py:461
  72.5 1.1 %shard_map.121 = (f32[16,8,256]{2,1,0:T(8,128)S(1)}, f32[16,8,256]{2,1,0:T(8,128)S(1)}) custom-call(s32[90]{0:T(128)S(4)} %get-tuple-element.71.table, f32[16,8,256]{2,1,0:T(8,128)S(1)} %get-tuple-element.73.rest_0_.wide, bf16[16,256,256]{2,1,0:T(8,128)(2,1)S(1)} %get-tuple-element.74.rest_1_.diag, bf16[16,256,256]{2,1,0:T(8,128)(2,1)S(1)} %get-tuple-element.75.rest_2_.off, ...), custom_call_target="tpu_custom_call" | custom-call | flops 600000000 | bytes 37500000 | tf_op jit(solution)/shard_map/pallas_call | solution.py:461
  74.5 1.4 %collective-permute-start.22 = (f32[13,8,128]{2,1,0:T(8,128)S(1)}, f32[13,8,128]{2,1,0:T(8,128)S(1)}, u32[]{:S(2)}, u32[]{:S(2)}) collective-permute-start(f32[13,8,128]{2,1,0:T(8,128)S(1)} %get-tuple-element.134), channel_id=1, source_target_pairs={{0,2},{1,5},{2,0},{3,7},{4,6},{5,1},{6,4},{7,3},{8,10},{9,13},{10,... | collective-permute-start | bytes 159752 | tf_op jit(solution)/shard_map/ppermute | solution.py:500
  75.9 1.5 %collective-permute-start.23 = (f32[13,8,128]{2,1,0:T(8,128)S(1)}, f32[13,8,128]{2,1,0:T(8,128)S(1)}, u32[]{:S(2)}, u32[]{:S(2)}) collective-permute-start(f32[13,8,128]{2,1,0:T(8,128)S(1)} %get-tuple-element.135), channel_id=1, source_target_pairs={{0,4},{1,3},{2,6},{3,1},{4,0},{5,7},{6,2},{7,5},{8,12},{9,11},{10,... | collective-permute-start | bytes 159752 | tf_op jit(solution)/shard_map/ppermute | solution.py:500
  77.4 2.1 %collective-permute-done.21.rest_1_ = f32[13,8,128]{2,1,0:T(8,128)S(1)} collective-permute-done((f32[13,8,128]{2,1,0:T(8,128)S(1)}, f32[13,8,128]{2,1,0:T(8,128)S(1)}, u32[]{:S(2)}, u32[]{:S(2)}) %collective-permute-start.21) | collective-permute-done | bytes 53280 | tf_op jit(solution)/shard_map/ppermute | solution.py:500
  80.6 8.8 %all_to_all.23.gathered = f32[32,1,128]{2,1,0:T(1,128)S(1)} all-to-all(f32[32,1,128]{2,1,0:T(1,128)S(1)} %get-tuple-element.137), channel_id=1, replica_groups=mesh['group'=4,'sub'=8] {'group','sub'}, dimensions={0} | all-to-all | bytes 32768 | tf_op jit(solution)/shard_map/all_to_all | solution.py:581
  89.5 1.0 %shard_map.124 = (f32[8,16,256]{2,1,0:T(8,128)}, f32[8,16,256]{2,1,0:T(8,128)}) custom-call(f32[32,1,128]{2,1,0:T(1,128)S(1)} %all_to_all.23.gathered, f32[16,8,256]{2,1,0:T(8,128)S(1)} %get-tuple-element.138.before, f32[16,8,256]{2,1,0:T(8,128)S(1)} %get-tuple-element.130.residual.residual_in, f32[16,8,256]{2,1,0:T(8,128)S(1)} %get-tuple-element.131.direction, ...), custom_call_target="tpu_custom_call" | custom-call | flops 4000000 | bytes 250000 | tf_op jit(solution)/shard_map/pallas_call | solution.py:461
  (43 shorter events, 9.2 us)
Async XLA Ops:
  1.7 1.5 %collective-permute-start = (f32[36,8,128]{2,1,0:T(8,128)S(1)}, f32[36,8,128]{2,1,0:T(8,128)S(1)}, u32[]{:S(2)}, u32[]{:S(2)}) collective-permute-start(f32[36,8,128]{2,1,0:T(8,128)S(1)} %get-tuple-element.79), channel_id=1, source_target_pairs={{0,1},{1,0},{2,3},{3,2},{4,5},{5,4},{6,7},{7,6},{8,9},{9,8},{10,11... | collective-permute-start | bytes 442376 | tf_op jit(solution)/shard_map/ppermute | solution.py:500
  3.3 7.1 %collective-permute-start.1 = (f32[24,8,128]{2,1,0:T(8,128)S(1)}, f32[24,8,128]{2,1,0:T(8,128)S(1)}, u32[]{:S(2)}, u32[]{:S(2)}) collective-permute-start(f32[24,8,128]{2,1,0:T(8,128)S(1)} %get-tuple-element.80), channel_id=1, source_target_pairs={{0,6},{1,7},{2,4},{3,5},{4,2},{5,3},{6,0},{7,1},{8,14},{9,15},{10,... | collective-permute-start | bytes 294920 | tf_op jit(solution)/shard_map/ppermute | solution.py:500
  7.1 5.5 %collective-permute-start.2 = (f32[24,8,128]{2,1,0:T(8,128)S(1)}, f32[24,8,128]{2,1,0:T(8,128)S(1)}, u32[]{:S(2)}, u32[]{:S(2)}) collective-permute-start(f32[24,8,128]{2,1,0:T(8,128)S(1)} %get-tuple-element.81), channel_id=1, source_target_pairs={{0,2},{1,5},{2,0},{3,7},{4,6},{5,1},{6,4},{7,3},{8,10},{9,13},{10,... | collective-permute-start | bytes 294920 | tf_op jit(solution)/shard_map/ppermute | solution.py:500
  7.7 4.9 %collective-permute-start.3 = (f32[24,8,128]{2,1,0:T(8,128)S(1)}, f32[24,8,128]{2,1,0:T(8,128)S(1)}, u32[]{:S(2)}, u32[]{:S(2)}) collective-permute-start(f32[24,8,128]{2,1,0:T(8,128)S(1)} %get-tuple-element.82), channel_id=1, source_target_pairs={{0,4},{1,3},{2,6},{3,1},{4,0},{5,7},{6,2},{7,5},{8,12},{9,11},{10,... | collective-permute-start | bytes 294920 | tf_op jit(solution)/shard_map/ppermute | solution.py:500
  7.8 4.8 %collective-permute-start.4 = (f32[24,8,128]{2,1,0:T(8,128)S(1)}, f32[24,8,128]{2,1,0:T(8,128)S(1)}, u32[]{:S(2)}, u32[]{:S(2)}) collective-permute-start(f32[24,8,128]{2,1,0:T(8,128)S(1)} %get-tuple-element.83), channel_id=1, source_target_pairs={{0,1},{1,0},{2,3},{3,2},{4,5},{5,4},{6,7},{7,6},{8,9},{9,8},{10,11... | collective-permute-start | bytes 294920 | tf_op jit(solution)/shard_map/ppermute | solution.py:500
  13.7 1.3 %collective-permute-start.5 = (f32[19,8,128]{2,1,0:T(8,128)S(1)}, f32[19,8,128]{2,1,0:T(8,128)S(1)}, u32[]{:S(2)}, u32[]{:S(2)}) collective-permute-start(f32[19,8,128]{2,1,0:T(8,128)S(1)} %get-tuple-element.88), channel_id=1, source_target_pairs={{0,1},{1,0},{2,3},{3,2},{4,5},{5,4},{6,7},{7,6},{8,9},{9,8},{10,11... | collective-permute-start | bytes 233480 | tf_op jit(solution)/shard_map/ppermute | solution.py:500
  15.0 5.2 %collective-permute-start.6 = (f32[13,8,128]{2,1,0:T(8,128)S(1)}, f32[13,8,128]{2,1,0:T(8,128)S(1)}, u32[]{:S(2)}, u32[]{:S(2)}) collective-permute-start(f32[13,8,128]{2,1,0:T(8,128)S(1)} %get-tuple-element.89), channel_id=1, source_target_pairs={{0,6},{1,7},{2,4},{3,5},{4,2},{5,3},{6,0},{7,1},{8,14},{9,15},{10,... | collective-permute-start | bytes 159752 | tf_op jit(solution)/shard_map/ppermute | solution.py:500
  16.8 4.5 %collective-permute-start.7 = (f32[13,8,128]{2,1,0:T(8,128)S(1)}, f32[13,8,128]{2,1,0:T(8,128)S(1)}, u32[]{:S(2)}, u32[]{:S(2)}) collective-permute-start(f32[13,8,128]{2,1,0:T(8,128)S(1)} %get-tuple-element.90), channel_id=1, source_target_pairs={{0,2},{1,5},{2,0},{3,7},{4,6},{5,1},{6,4},{7,3},{8,10},{9,13},{10,... | collective-permute-start | bytes 159752 | tf_op jit(solution)/shard_map/ppermute | solution.py:500
  18.0 4.1 %collective-permute-start.8 = (f32[13,8,128]{2,1,0:T(8,128)S(1)}, f32[13,8,128]{2,1,0:T(8,128)S(1)}, u32[]{:S(2)}, u32[]{:S(2)}) collective-permute-start(f32[13,8,128]{2,1,0:T(8,128)S(1)} %get-tuple-element.91), channel_id=1, source_target_pairs={{0,4},{1,3},{2,6},{3,1},{4,0},{5,7},{6,2},{7,5},{8,12},{9,11},{10,... | collective-permute-start | bytes 159752 | tf_op jit(solution)/shard_map/ppermute | solution.py:500
  18.6 3.6 %collective-permute-start.9 = (f32[13,8,128]{2,1,0:T(8,128)S(1)}, f32[13,8,128]{2,1,0:T(8,128)S(1)}, u32[]{:S(2)}, u32[]{:S(2)}) collective-permute-start(f32[13,8,128]{2,1,0:T(8,128)S(1)} %get-tuple-element.92), channel_id=1, source_target_pairs={{0,1},{1,0},{2,3},{3,2},{4,5},{5,4},{6,7},{7,6},{8,9},{9,8},{10,11... | collective-permute-start | bytes 159752 | tf_op jit(solution)/shard_map/ppermute | solution.py:500
  36.1 1.3 %collective-permute-start.10 = (f32[19,8,128]{2,1,0:T(8,128)S(1)}, f32[19,8,128]{2,1,0:T(8,128)S(1)}, u32[]{:S(2)}, u32[]{:S(2)}) collective-permute-start(f32[19,8,128]{2,1,0:T(8,128)S(1)} %get-tuple-element.102), channel_id=1, source_target_pairs={{0,1},{1,0},{2,3},{3,2},{4,5},{5,4},{6,7},{7,6},{8,9},{9,8},{10,11... | collective-permute-start | bytes 233480 | tf_op jit(solution)/shard_map/ppermute | solution.py:500
  37.4 5.7 %collective-permute-start.11 = (f32[13,8,128]{2,1,0:T(8,128)S(1)}, f32[13,8,128]{2,1,0:T(8,128)S(1)}, u32[]{:S(2)}, u32[]{:S(2)}) collective-permute-start(f32[13,8,128]{2,1,0:T(8,128)S(1)} %get-tuple-element.103), channel_id=1, source_target_pairs={{0,6},{1,7},{2,4},{3,5},{4,2},{5,3},{6,0},{7,1},{8,14},{9,15},{10,... | collective-permute-start | bytes 159752 | tf_op jit(solution)/shard_map/ppermute | solution.py:500
  38.1 5.0 %collective-permute-start.12 = (f32[13,8,128]{2,1,0:T(8,128)S(1)}, f32[13,8,128]{2,1,0:T(8,128)S(1)}, u32[]{:S(2)}, u32[]{:S(2)}) collective-permute-start(f32[13,8,128]{2,1,0:T(8,128)S(1)} %get-tuple-element.104), channel_id=1, source_target_pairs={{0,2},{1,5},{2,0},{3,7},{4,6},{5,1},{6,4},{7,3},{8,10},{9,13},{10,... | collective-permute-start | bytes 159752 | tf_op jit(solution)/shard_map/ppermute | solution.py:500
  39.5 4.1 %collective-permute-start.13 = (f32[13,8,128]{2,1,0:T(8,128)S(1)}, f32[13,8,128]{2,1,0:T(8,128)S(1)}, u32[]{:S(2)}, u32[]{:S(2)}) collective-permute-start(f32[13,8,128]{2,1,0:T(8,128)S(1)} %get-tuple-element.105), channel_id=1, source_target_pairs={{0,4},{1,3},{2,6},{3,1},{4,0},{5,7},{6,2},{7,5},{8,12},{9,11},{10,... | collective-permute-start | bytes 159752 | tf_op jit(solution)/shard_map/ppermute | solution.py:500
  41.0 2.7 %collective-permute-start.14 = (f32[13,8,128]{2,1,0:T(8,128)S(1)}, f32[13,8,128]{2,1,0:T(8,128)S(1)}, u32[]{:S(2)}, u32[]{:S(2)}) collective-permute-start(f32[13,8,128]{2,1,0:T(8,128)S(1)} %get-tuple-element.106), channel_id=1, source_target_pairs={{0,1},{1,0},{2,3},{3,2},{4,5},{5,4},{6,7},{7,6},{8,9},{9,8},{10,11... | collective-permute-start | bytes 159752 | tf_op jit(solution)/shard_map/ppermute | solution.py:500
  54.3 1.3 %collective-permute-start.15 = (f32[19,8,128]{2,1,0:T(8,128)S(1)}, f32[19,8,128]{2,1,0:T(8,128)S(1)}, u32[]{:S(2)}, u32[]{:S(2)}) collective-permute-start(f32[19,8,128]{2,1,0:T(8,128)S(1)} %get-tuple-element.117), channel_id=1, source_target_pairs={{0,1},{1,0},{2,3},{3,2},{4,5},{5,4},{6,7},{7,6},{8,9},{9,8},{10,11... | collective-permute-start | bytes 233480 | tf_op jit(solution)/shard_map/ppermute | solution.py:500
  55.6 5.7 %collective-permute-start.16 = (f32[13,8,128]{2,1,0:T(8,128)S(1)}, f32[13,8,128]{2,1,0:T(8,128)S(1)}, u32[]{:S(2)}, u32[]{:S(2)}) collective-permute-start(f32[13,8,128]{2,1,0:T(8,128)S(1)} %get-tuple-element.118), channel_id=1, source_target_pairs={{0,6},{1,7},{2,4},{3,5},{4,2},{5,3},{6,0},{7,1},{8,14},{9,15},{10,... | collective-permute-start | bytes 159752 | tf_op jit(solution)/shard_map/ppermute | solution.py:500
  56.3 5.0 %collective-permute-start.17 = (f32[13,8,128]{2,1,0:T(8,128)S(1)}, f32[13,8,128]{2,1,0:T(8,128)S(1)}, u32[]{:S(2)}, u32[]{:S(2)}) collective-permute-start(f32[13,8,128]{2,1,0:T(8,128)S(1)} %get-tuple-element.119), channel_id=1, source_target_pairs={{0,2},{1,5},{2,0},{3,7},{4,6},{5,1},{6,4},{7,3},{8,10},{9,13},{10,... | collective-permute-start | bytes 159752 | tf_op jit(solution)/shard_map/ppermute | solution.py:500
  57.7 4.1 %collective-permute-start.18 = (f32[13,8,128]{2,1,0:T(8,128)S(1)}, f32[13,8,128]{2,1,0:T(8,128)S(1)}, u32[]{:S(2)}, u32[]{:S(2)}) collective-permute-start(f32[13,8,128]{2,1,0:T(8,128)S(1)} %get-tuple-element.120), channel_id=1, source_target_pairs={{0,4},{1,3},{2,6},{3,1},{4,0},{5,7},{6,2},{7,5},{8,12},{9,11},{10,... | collective-permute-start | bytes 159752 | tf_op jit(solution)/shard_map/ppermute | solution.py:500
  59.2 2.7 %collective-permute-start.19 = (f32[13,8,128]{2,1,0:T(8,128)S(1)}, f32[13,8,128]{2,1,0:T(8,128)S(1)}, u32[]{:S(2)}, u32[]{:S(2)}) collective-permute-start(f32[13,8,128]{2,1,0:T(8,128)S(1)} %get-tuple-element.121), channel_id=1, source_target_pairs={{0,1},{1,0},{2,3},{3,2},{4,5},{5,4},{6,7},{7,6},{8,9},{9,8},{10,11... | collective-permute-start | bytes 159752 | tf_op jit(solution)/shard_map/ppermute | solution.py:500
  72.5 1.3 %collective-permute-start.20 = (f32[19,8,128]{2,1,0:T(8,128)S(1)}, f32[19,8,128]{2,1,0:T(8,128)S(1)}, u32[]{:S(2)}, u32[]{:S(2)}) collective-permute-start(f32[19,8,128]{2,1,0:T(8,128)S(1)} %get-tuple-element.132), channel_id=1, source_target_pairs={{0,1},{1,0},{2,3},{3,2},{4,5},{5,4},{6,7},{7,6},{8,9},{9,8},{10,11... | collective-permute-start | bytes 233480 | tf_op jit(solution)/shard_map/ppermute | solution.py:500
  73.8 5.7 %collective-permute-start.21 = (f32[13,8,128]{2,1,0:T(8,128)S(1)}, f32[13,8,128]{2,1,0:T(8,128)S(1)}, u32[]{:S(2)}, u32[]{:S(2)}) collective-permute-start(f32[13,8,128]{2,1,0:T(8,128)S(1)} %get-tuple-element.133), channel_id=1, source_target_pairs={{0,6},{1,7},{2,4},{3,5},{4,2},{5,3},{6,0},{7,1},{8,14},{9,15},{10,... | collective-permute-start | bytes 159752 | tf_op jit(solution)/shard_map/ppermute | solution.py:500
  74.5 5.0 %collective-permute-start.22 = (f32[13,8,128]{2,1,0:T(8,128)S(1)}, f32[13,8,128]{2,1,0:T(8,128)S(1)}, u32[]{:S(2)}, u32[]{:S(2)}) collective-permute-start(f32[13,8,128]{2,1,0:T(8,128)S(1)} %get-tuple-element.134), channel_id=1, source_target_pairs={{0,2},{1,5},{2,0},{3,7},{4,6},{5,1},{6,4},{7,3},{8,10},{9,13},{10,... | collective-permute-start | bytes 159752 | tf_op jit(solution)/shard_map/ppermute | solution.py:500
  75.9 4.1 %collective-permute-start.23 = (f32[13,8,128]{2,1,0:T(8,128)S(1)}, f32[13,8,128]{2,1,0:T(8,128)S(1)}, u32[]{:S(2)}, u32[]{:S(2)}) collective-permute-start(f32[13,8,128]{2,1,0:T(8,128)S(1)} %get-tuple-element.135), channel_id=1, source_target_pairs={{0,4},{1,3},{2,6},{3,1},{4,0},{5,7},{6,2},{7,5},{8,12},{9,11},{10,... | collective-permute-start | bytes 159752 | tf_op jit(solution)/shard_map/ppermute | solution.py:500
  77.4 2.7 %collective-permute-start.24 = (f32[13,8,128]{2,1,0:T(8,128)S(1)}, f32[13,8,128]{2,1,0:T(8,128)S(1)}, u32[]{:S(2)}, u32[]{:S(2)}) collective-permute-start(f32[13,8,128]{2,1,0:T(8,128)S(1)} %get-tuple-element.136), channel_id=1, source_target_pairs={{0,1},{1,0},{2,3},{3,2},{4,5},{5,4},{6,7},{7,6},{8,9},{9,8},{10,11... | collective-permute-start | bytes 159752 | tf_op jit(solution)/shard_map/ppermute | solution.py:500

commit v17 on v16

--- a/solution.py
+++ b/solution.py
@@ -209,7 +209,7 @@
         wide[i] = row
         part = coupling_here[:, i * z.width : (i + 1) * z.width].astype(F32)
         lift[i] = row * part
-        corners[i] = jnp.concatenate([part, jnp.zeros_like(part)], axis=0).astype(BF16)
+        corners[:, i * z.width : (i + 1) * z.width] = pad(part)
     fill_near(z, table, [field, lift], near)
 
 
@@ -339,7 +339,7 @@
         alpha, beta = scalars(z, gathered, previous)
         step_out[...] = alpha
         alpha, beta = across_block(z, alpha), across_block(z, beta)
-    partial = jnp.zeros((2 * z.columns, 2 * z.corners), F32)
+    pieces = []
     for i in range(z.blocks):
         if step == 0:
             value = loaded[i] - other[i]
@@ -351,7 +351,8 @@
             direction[i] = value
         mine = pad(wide[i] * value)
         parts[i] = mine
-        partial = partial + dot(mine, corners[i], NT)
+        pieces.append(mine)
+    partial = dot(jnp.concatenate(pieces, axis=1), corners[...], NT)
     refs = (table, wide, diag, off, parts)
     for position in range(z.early):
         i = table[z.order + position]
@@ -512,7 +513,7 @@
 
     table, loaded, lift, wide, corners, near = call(
         kernel(begin),
-        [((z.table,), jnp.int32), field, field, field, ((blocks, 2 * z.corners, width), BF16)]
+        [((z.table,), jnp.int32), field, field, field, ((2 * z.corners, blocks * width), BF16)]
         + [shape(z.near_rows(2), 2)],
         [
             pltpu.VMEM(load.shape, F32),

time: 90.7 us -> 90.7 us (level)
  no operation moved by 1% of the time
where the time goes in v17:
time: 90.7 us; the launch traced here: 90.5 us
  blocking collectives  38.4 us (42%)
  starting transfers between devices  19.3 us (21%)
  Pallas kernels  16.4 us (18%)
  waiting for transfers between devices  15.6 us (17%)
    all_to_all x4, blocking collectives, on_device(): gathered = lax.all_to_all(sent, ('group', 'sub'), 0, 0, tiled=True)  38.4 us
    ppermute x25, starting transfers between devices, across(): return lax.ppermute(piece, 'sub', pairs)  19.3 us
    pallas_call x21, Pallas kernels, call(): pl.pallas_call(body, out_shape=shapes, in_specs=specs, out_specs=[SMEM if...  16.4 us
    ppermute x25, waiting for transfers between devices, across(): return lax.ppermute(piece, 'sub', pairs)  15.6 us
  transfers between devices with their start and end apart: 25, of which 16 were waited for; matrix products, arithmetic and copies ran while one was open for 0% of the time, Pallas kernels for 8%

profile of v17, /device:TPU:0, one launch (start us, length us, event | category | flops | bytes accessed | tf_op | source)
XLA Modules:
  0.0 90.5 jit_solution(4410245910101463830)
XLA Ops:
  0.6 1.0 %shard_map.104 = (s32[90]{0:T(128)S(4)}, f32[16,8,256]{2,1,0:T(8,128)S(1)}, f32[16,8,256]{2,1,0:T(8,128)S(1)}, f32[16,8,256]{2,1,0:T(8,128)S(1)}, bf16[16,4096]{...) custom-call(s32[1,16]{1,0:T(1,128)} %partner.1, s32[1,16]{1,0:T(1,128)} %pattern.1, f32[8,16,256]{2,1,0:T(8,128)} %load.1, ...), custom_call_target="tpu_custom_call" | custom-call | flops 4000000 | bytes 250000 | tf_op jit(solution)/shard_map/pallas_call | solution.py:462
  2.2 1.0 %collective-permute-done.rest_2_ = f32[36,8,128]{2,1,0:T(8,128)S(1)} collective-permute-done((f32[36,8,128]{2,1,0:T(8,128)S(1)}, f32[36,8,128]{2,1,0:T(8,128)S(1)}, u32[]{:S(2)}, u32[]{:S(2)}) %collective-permute-start) | collective-permute-done | bytes 147488 | tf_op jit(solution)/shard_map/ppermute | solution.py:501
  3.3 3.9 %collective-permute-start.1 = (f32[24,8,128]{2,1,0:T(8,128)S(1)}, f32[24,8,128]{2,1,0:T(8,128)S(1)}, u32[]{:S(2)}, u32[]{:S(2)}) collective-permute-start(f32[24,8,128]{2,1,0:T(8,128)S(1)} %get-tuple-element.80), channel_id=1, source_target_pairs={{0,6},{1,7},{2,4},{3,5},{4,2},{5,3},{6,0},{7,1},{8,14},{9,15},{10,... | collective-permute-start | bytes 294920 | tf_op jit(solution)/shard_map/ppermute | solution.py:501
  7.8 2.3 %shard_map.105 = (f32[64,64]{1,0:T(8,128)S(1)}, bf16[16,256,256]{2,1,0:T(8,128)(2,1)S(1)}, bf16[16,256,256]{2,1,0:T(8,128)(2,1)S(1)}) custom-call(s32[1,64]{1,0:T(1,128)} %index_in.1, f32[32,32]{1,0:T(8,128)} %inverse_in.1, bf16[16,256,256]{2,1,0:T(8,128)(2,1)} %diag.1, bf16[16,256,256]{2,1,0:T(8,128)(2,1)} %off.1), custom_call_target="tpu_custom_call" | custom-call | flops 600000000 | bytes 37500000 | tf_op jit(solution)/shard_map/pallas_call | solution.py:462
  10.3 2.3 %collective-permute-done.2.rest_5_.rest_1_ = f32[24,8,128]{2,1,0:T(8,128)S(1)} collective-permute-done((f32[24,8,128]{2,1,0:T(8,128)S(1)}, f32[24,8,128]{2,1,0:T(8,128)S(1)}, u32[]{:S(2)}, u32[]{:S(2)}) %collective-permute-start.2) | collective-permute-done | bytes 98336 | tf_op jit(solution)/shard_map/ppermute | solution.py:501
  12.6 1.1 %shard_map.107 = (f32[16,8,256]{2,1,0:T(8,128)S(1)}, f32[16,8,256]{2,1,0:T(8,128)S(1)}, bf16[16,16,256]{2,1,0:T(8,128)(2,1)S(1)}, f32[8,128]{1,0:T(8,128)S(1)}, f32[19,8,128]{2,1,0:T(8,128)S(1)}) custom-call(s32[90]{0:T(128)S(4)} %get-tuple-element.71.table, f32[16,8,256]{2,1,0:T(8,128)S(1)} %get-tuple-element.73.rest_0_.wide, ...), custom_call_target="tpu_custom_call" | custom-call | flops 600000000 | bytes 37500000 | tf_op jit(solution)/shard_map/pallas_call | solution.py:462
  13.8 1.1 %shard_map.108.rest_0_.image = f32[16,8,256]{2,1,0:T(8,128)S(1)} custom-call(s32[90]{0:T(128)S(4)} %get-tuple-element.71.table, f32[16,8,256]{2,1,0:T(8,128)S(1)} %get-tuple-element.73.rest_0_.wide, bf16[16,256,256]{2,1,0:T(8,128)(2,1)S(1)} %get-tuple-element.74.rest_1_.diag, bf16[16,256,256]{2,1,0:T(8,128)(2,1)S(1)} %get-tuple-element.75.rest_2_.off, ...), custom_call_target="tpu_custom_call" | custom-call | flops 600000000 | bytes 37500000 | tf_op jit(solution)/shard_map/pallas_call | solution.py:462
  15.0 1.7 %collective-permute-start.6 = (f32[13,8,128]{2,1,0:T(8,128)S(1)}, f32[13,8,128]{2,1,0:T(8,128)S(1)}, u32[]{:S(2)}, u32[]{:S(2)}) collective-permute-start(f32[13,8,128]{2,1,0:T(8,128)S(1)} %get-tuple-element.89), channel_id=1, source_target_pairs={{0,6},{1,7},{2,4},{3,5},{4,2},{5,3},{6,0},{7,1},{8,14},{9,15},{10,... | collective-permute-start | bytes 159752 | tf_op jit(solution)/shard_map/ppermute | solution.py:501
  16.8 1.3 %collective-permute-start.7 = (f32[13,8,128]{2,1,0:T(8,128)S(1)}, f32[13,8,128]{2,1,0:T(8,128)S(1)}, u32[]{:S(2)}, u32[]{:S(2)}) collective-permute-start(f32[13,8,128]{2,1,0:T(8,128)S(1)} %get-tuple-element.90), channel_id=1, source_target_pairs={{0,2},{1,5},{2,0},{3,7},{4,6},{5,1},{6,4},{7,3},{8,10},{9,13},{10,... | collective-permute-start | bytes 159752 | tf_op jit(solution)/shard_map/ppermute | solution.py:501
  18.8 1.4 %collective-permute-done.6.rest_0_ = f32[13,8,128]{2,1,0:T(8,128)S(1)} collective-permute-done((f32[13,8,128]{2,1,0:T(8,128)S(1)}, f32[13,8,128]{2,1,0:T(8,128)S(1)}, u32[]{:S(2)}, u32[]{:S(2)}) %collective-permute-start.6) | collective-permute-done | bytes 53280 | tf_op jit(solution)/shard_map/ppermute | solution.py:501
  20.2 1.1 %collective-permute-done.7.rest_1_ = f32[13,8,128]{2,1,0:T(8,128)S(1)} collective-permute-done((f32[13,8,128]{2,1,0:T(8,128)S(1)}, f32[13,8,128]{2,1,0:T(8,128)S(1)}, u32[]{:S(2)}, u32[]{:S(2)}) %collective-permute-start.7) | collective-permute-done | bytes 53280 | tf_op jit(solution)/shard_map/ppermute | solution.py:501
  21.3 0.9 collective-permute-done.8.rest_2_
  22.9 11.9 %all_to_all.20.rest_4_ = f32[32,1,128]{2,1,0:T(1,128)S(1)} all-to-all(f32[32,1,128]{2,1,0:T(1,128)S(1)} %get-tuple-element.93), channel_id=1, replica_groups=mesh['group'=4,'sub'=8] {'group','sub'}, dimensions={0} | all-to-all | bytes 32768 | tf_op jit(solution)/shard_map/all_to_all | solution.py:582
  34.8 1.3 %shard_map.112 = (f32[16,8,256]{2,1,0:T(8,128)S(1)}, f32[16,8,256]{2,1,0:T(8,128)S(1)}, f32[8,128]{1,0:T(8,128)S(1)}, f32[16,8,256]{2,1,0:T(8,128)S(1)}, bf16[16...) custom-call(s32[90]{0:T(128)S(4)} %get-tuple-element.71.table, ...), custom_call_target="tpu_custom_call" | custom-call | flops 600000000 | bytes 37500000 | tf_op jit(solution)/shard_map/pallas_call | solution.py:462
  36.1 1.1 %shard_map.113 = (f32[16,8,256]{2,1,0:T(8,128)S(1)}, f32[16,8,256]{2,1,0:T(8,128)S(1)}) custom-call(s32[90]{0:T(128)S(4)} %get-tuple-element.71.table, f32[16,8,256]{2,1,0:T(8,128)S(1)} %get-tuple-element.73.rest_0_.wide, bf16[16,256,256]{2,1,0:T(8,128)(2,1)S(1)} %get-tuple-element.74.rest_1_.diag, bf16[16,256,256]{2,1,0:T(8,128)(2,1)S(1)} %get-tuple-element.75.rest_2_.off, ...), custom_call_target="tpu_custom_call" | custom-call | flops 600000000 | bytes 37500000 | tf_op jit(solution)/shard_map/pallas_call | solution.py:462
  38.1 1.4 %collective-permute-start.12 = (f32[13,8,128]{2,1,0:T(8,128)S(1)}, f32[13,8,128]{2,1,0:T(8,128)S(1)}, u32[]{:S(2)}, u32[]{:S(2)}) collective-permute-start(f32[13,8,128]{2,1,0:T(8,128)S(1)} %get-tuple-element.104), channel_id=1, source_target_pairs={{0,2},{1,5},{2,0},{3,7},{4,6},{5,1},{6,4},{7,3},{8,10},{9,13},{10,... | collective-permute-start | bytes 159752 | tf_op jit(solution)/shard_map/ppermute | solution.py:501
  39.5 1.5 %collective-permute-start.13 = (f32[13,8,128]{2,1,0:T(8,128)S(1)}, f32[13,8,128]{2,1,0:T(8,128)S(1)}, u32[]{:S(2)}, u32[]{:S(2)}) collective-permute-start(f32[13,8,128]{2,1,0:T(8,128)S(1)} %get-tuple-element.105), channel_id=1, source_target_pairs={{0,4},{1,3},{2,6},{3,1},{4,0},{5,7},{6,2},{7,5},{8,12},{9,11},{10,... | collective-permute-start | bytes 159752 | tf_op jit(solution)/shard_map/ppermute | solution.py:501
  41.0 2.1 %collective-permute-done.11.rest_1_ = f32[13,8,128]{2,1,0:T(8,128)S(1)} collective-permute-done((f32[13,8,128]{2,1,0:T(8,128)S(1)}, f32[13,8,128]{2,1,0:T(8,128)S(1)}, u32[]{:S(2)}, u32[]{:S(2)}) %collective-permute-start.11) | collective-permute-done | bytes 53280 | tf_op jit(solution)/shard_map/ppermute | solution.py:501
  44.2 8.8 %all_to_all.21.rest_4_ = f32[32,1,128]{2,1,0:T(1,128)S(1)} all-to-all(f32[32,1,128]{2,1,0:T(1,128)S(1)} %get-tuple-element.107), channel_id=1, replica_groups=mesh['group'=4,'sub'=8] {'group','sub'}, dimensions={0} | all-to-all | bytes 32768 | tf_op jit(solution)/shard_map/all_to_all | solution.py:582
  53.1 1.2 %shard_map.116 = (f32[16,8,256]{2,1,0:T(8,128)S(1)}, f32[16,8,256]{2,1,0:T(8,128)S(1)}, f32[8,128]{1,0:T(8,128)S(1)}, f32[16,8,256]{2,1,0:T(8,128)S(1)}, bf16[16...) custom-call(s32[90]{0:T(128)S(4)} %get-tuple-element.71.table, ...), custom_call_target="tpu_custom_call" | custom-call | flops 600000000 | bytes 37500000 | tf_op jit(solution)/shard_map/pallas_call | solution.py:462
  54.3 1.1 %shard_map.117 = (f32[16,8,256]{2,1,0:T(8,128)S(1)}, f32[16,8,256]{2,1,0:T(8,128)S(1)}) custom-call(s32[90]{0:T(128)S(4)} %get-tuple-element.71.table, f32[16,8,256]{2,1,0:T(8,128)S(1)} %get-tuple-element.73.rest_0_.wide, bf16[16,256,256]{2,1,0:T(8,128)(2,1)S(1)} %get-tuple-element.74.rest_1_.diag, bf16[16,256,256]{2,1,0:T(8,128)(2,1)S(1)} %get-tuple-element.75.rest_2_.off, ...), custom_call_target="tpu_custom_call" | custom-call | flops 600000000 | bytes 37500000 | tf_op jit(solution)/shard_map/pallas_call | solution.py:462
  56.3 1.4 %collective-permute-start.17 = (f32[13,8,128]{2,1,0:T(8,128)S(1)}, f32[13,8,128]{2,1,0:T(8,128)S(1)}, u32[]{:S(2)}, u32[]{:S(2)}) collective-permute-start(f32[13,8,128]{2,1,0:T(8,128)S(1)} %get-tuple-element.119), channel_id=1, source_target_pairs={{0,2},{1,5},{2,0},{3,7},{4,6},{5,1},{6,4},{7,3},{8,10},{9,13},{10,... | collective-permute-start | bytes 159752 | tf_op jit(solution)/shard_map/ppermute | solution.py:501
  57.7 1.5 %collective-permute-start.18 = (f32[13,8,128]{2,1,0:T(8,128)S(1)}, f32[13,8,128]{2,1,0:T(8,128)S(1)}, u32[]{:S(2)}, u32[]{:S(2)}) collective-permute-start(f32[13,8,128]{2,1,0:T(8,128)S(1)} %get-tuple-element.120), channel_id=1, source_target_pairs={{0,4},{1,3},{2,6},{3,1},{4,0},{5,7},{6,2},{7,5},{8,12},{9,11},{10,... | collective-permute-start | bytes 159752 | tf_op jit(solution)/shard_map/ppermute | solution.py:501
  59.2 2.1 %collective-permute-done.16.rest_1_ = f32[13,8,128]{2,1,0:T(8,128)S(1)} collective-permute-done((f32[13,8,128]{2,1,0:T(8,128)S(1)}, f32[13,8,128]{2,1,0:T(8,128)S(1)}, u32[]{:S(2)}, u32[]{:S(2)}) %collective-permute-start.16) | collective-permute-done | bytes 53280 | tf_op jit(solution)/shard_map/ppermute | solution.py:501
  62.4 8.8 %all_to_all.22.rest_4_ = f32[32,1,128]{2,1,0:T(1,128)S(1)} all-to-all(f32[32,1,128]{2,1,0:T(1,128)S(1)} %get-tuple-element.122), channel_id=1, replica_groups=mesh['group'=4,'sub'=8] {'group','sub'}, dimensions={0} | all-to-all | bytes 32768 | tf_op jit(solution)/shard_map/all_to_all | solution.py:582
  71.3 1.2 %shard_map.120 = (f32[16,8,256]{2,1,0:T(8,128)S(1)}, f32[16,8,256]{2,1,0:T(8,128)S(1)}, f32[8,128]{1,0:T(8,128)S(1)}, f32[16,8,256]{2,1,0:T(8,128)S(1)}, bf16[16...) custom-call(s32[90]{0:T(128)S(4)} %get-tuple-element.71.table, ...), custom_call_target="tpu_custom_call" | custom-call | flops 600000000 | bytes 37500000 | tf_op jit(solution)/shard_map/pallas_call | solution.py:462
  72.5 1.1 %shard_map.121 = (f32[16,8,256]{2,1,0:T(8,128)S(1)}, f32[16,8,256]{2,1,0:T(8,128)S(1)}) custom-call(s32[90]{0:T(128)S(4)} %get-tuple-element.71.table, f32[16,8,256]{2,1,0:T(8,128)S(1)} %get-tuple-element.73.rest_0_.wide, bf16[16,256,256]{2,1,0:T(8,128)(2,1)S(1)} %get-tuple-element.74.rest_1_.diag, bf16[16,256,256]{2,1,0:T(8,128)(2,1)S(1)} %get-tuple-element.75.rest_2_.off, ...), custom_call_target="tpu_custom_call" | custom-call | flops 600000000 | bytes 37500000 | tf_op jit(solution)/shard_map/pallas_call | solution.py:462
  74.5 1.4 %collective-permute-start.22 = (f32[13,8,128]{2,1,0:T(8,128)S(1)}, f32[13,8,128]{2,1,0:T(8,128)S(1)}, u32[]{:S(2)}, u32[]{:S(2)}) collective-permute-start(f32[13,8,128]{2,1,0:T(8,128)S(1)} %get-tuple-element.134), channel_id=1, source_target_pairs={{0,2},{1,5},{2,0},{3,7},{4,6},{5,1},{6,4},{7,3},{8,10},{9,13},{10,... | collective-permute-start | bytes 159752 | tf_op jit(solution)/shard_map/ppermute | solution.py:501
  75.9 1.5 %collective-permute-start.23 = (f32[13,8,128]{2,1,0:T(8,128)S(1)}, f32[13,8,128]{2,1,0:T(8,128)S(1)}, u32[]{:S(2)}, u32[]{:S(2)}) collective-permute-start(f32[13,8,128]{2,1,0:T(8,128)S(1)} %get-tuple-element.135), channel_id=1, source_target_pairs={{0,4},{1,3},{2,6},{3,1},{4,0},{5,7},{6,2},{7,5},{8,12},{9,11},{10,... | collective-permute-start | bytes 159752 | tf_op jit(solution)/shard_map/ppermute | solution.py:501
  77.4 2.1 %collective-permute-done.21.rest_1_ = f32[13,8,128]{2,1,0:T(8,128)S(1)} collective-permute-done((f32[13,8,128]{2,1,0:T(8,128)S(1)}, f32[13,8,128]{2,1,0:T(8,128)S(1)}, u32[]{:S(2)}, u32[]{:S(2)}) %collective-permute-start.21) | collective-permute-done | bytes 53280 | tf_op jit(solution)/shard_map/ppermute | solution.py:501
  80.6 8.8 %all_to_all.23.gathered = f32[32,1,128]{2,1,0:T(1,128)S(1)} all-to-all(f32[32,1,128]{2,1,0:T(1,128)S(1)} %get-tuple-element.137), channel_id=1, replica_groups=mesh['group'=4,'sub'=8] {'group','sub'}, dimensions={0} | all-to-all | bytes 32768 | tf_op jit(solution)/shard_map/all_to_all | solution.py:582
  89.5 1.0 %shard_map.124 = (f32[8,16,256]{2,1,0:T(8,128)}, f32[8,16,256]{2,1,0:T(8,128)}) custom-call(f32[32,1,128]{2,1,0:T(1,128)S(1)} %all_to_all.23.gathered, f32[16,8,256]{2,1,0:T(8,128)S(1)} %get-tuple-element.138.before, f32[16,8,256]{2,1,0:T(8,128)S(1)} %get-tuple-element.130.residual.residual_in, f32[16,8,256]{2,1,0:T(8,128)S(1)} %get-tuple-element.131.direction, ...), custom_call_target="tpu_custom_call" | custom-call | flops 4000000 | bytes 250000 | tf_op jit(solution)/shard_map/pallas_call | solution.py:462
  (43 shorter events, 9.2 us)
Async XLA Ops:
  1.7 1.5 %collective-permute-start = (f32[36,8,128]{2,1,0:T(8,128)S(1)}, f32[36,8,128]{2,1,0:T(8,128)S(1)}, u32[]{:S(2)}, u32[]{:S(2)}) collective-permute-start(f32[36,8,128]{2,1,0:T(8,128)S(1)} %get-tuple-element.79), channel_id=1, source_target_pairs={{0,1},{1,0},{2,3},{3,2},{4,5},{5,4},{6,7},{7,6},{8,9},{9,8},{10,11... | collective-permute-start | bytes 442376 | tf_op jit(solution)/shard_map/ppermute | solution.py:501
  3.3 7.1 %collective-permute-start.1 = (f32[24,8,128]{2,1,0:T(8,128)S(1)}, f32[24,8,128]{2,1,0:T(8,128)S(1)}, u32[]{:S(2)}, u32[]{:S(2)}) collective-permute-start(f32[24,8,128]{2,1,0:T(8,128)S(1)} %get-tuple-element.80), channel_id=1, source_target_pairs={{0,6},{1,7},{2,4},{3,5},{4,2},{5,3},{6,0},{7,1},{8,14},{9,15},{10,... | collective-permute-start | bytes 294920 | tf_op jit(solution)/shard_map/ppermute | solution.py:501
  7.1 5.5 %collective-permute-start.2 = (f32[24,8,128]{2,1,0:T(8,128)S(1)}, f32[24,8,128]{2,1,0:T(8,128)S(1)}, u32[]{:S(2)}, u32[]{:S(2)}) collective-permute-start(f32[24,8,128]{2,1,0:T(8,128)S(1)} %get-tuple-element.81), channel_id=1, source_target_pairs={{0,2},{1,5},{2,0},{3,7},{4,6},{5,1},{6,4},{7,3},{8,10},{9,13},{10,... | collective-permute-start | bytes 294920 | tf_op jit(solution)/shard_map/ppermute | solution.py:501
  7.7 4.9 %collective-permute-start.3 = (f32[24,8,128]{2,1,0:T(8,128)S(1)}, f32[24,8,128]{2,1,0:T(8,128)S(1)}, u32[]{:S(2)}, u32[]{:S(2)}) collective-permute-start(f32[24,8,128]{2,1,0:T(8,128)S(1)} %get-tuple-element.82), channel_id=1, source_target_pairs={{0,4},{1,3},{2,6},{3,1},{4,0},{5,7},{6,2},{7,5},{8,12},{9,11},{10,... | collective-permute-start | bytes 294920 | tf_op jit(solution)/shard_map/ppermute | solution.py:501
  7.8 4.8 %collective-permute-start.4 = (f32[24,8,128]{2,1,0:T(8,128)S(1)}, f32[24,8,128]{2,1,0:T(8,128)S(1)}, u32[]{:S(2)}, u32[]{:S(2)}) collective-permute-start(f32[24,8,128]{2,1,0:T(8,128)S(1)} %get-tuple-element.83), channel_id=1, source_target_pairs={{0,1},{1,0},{2,3},{3,2},{4,5},{5,4},{6,7},{7,6},{8,9},{9,8},{10,11... | collective-permute-start | bytes 294920 | tf_op jit(solution)/shard_map/ppermute | solution.py:501
  13.7 1.3 %collective-permute-start.5 = (f32[19,8,128]{2,1,0:T(8,128)S(1)}, f32[19,8,128]{2,1,0:T(8,128)S(1)}, u32[]{:S(2)}, u32[]{:S(2)}) collective-permute-start(f32[19,8,128]{2,1,0:T(8,128)S(1)} %get-tuple-element.88), channel_id=1, source_target_pairs={{0,1},{1,0},{2,3},{3,2},{4,5},{5,4},{6,7},{7,6},{8,9},{9,8},{10,11... | collective-permute-start | bytes 233480 | tf_op jit(solution)/shard_map/ppermute | solution.py:501
  15.0 5.2 %collective-permute-start.6 = (f32[13,8,128]{2,1,0:T(8,128)S(1)}, f32[13,8,128]{2,1,0:T(8,128)S(1)}, u32[]{:S(2)}, u32[]{:S(2)}) collective-permute-start(f32[13,8,128]{2,1,0:T(8,128)S(1)} %get-tuple-element.89), channel_id=1, source_target_pairs={{0,6},{1,7},{2,4},{3,5},{4,2},{5,3},{6,0},{7,1},{8,14},{9,15},{10,... | collective-permute-start | bytes 159752 | tf_op jit(solution)/shard_map/ppermute | solution.py:501
  16.8 4.5 %collective-permute-start.7 = (f32[13,8,128]{2,1,0:T(8,128)S(1)}, f32[13,8,128]{2,1,0:T(8,128)S(1)}, u32[]{:S(2)}, u32[]{:S(2)}) collective-permute-start(f32[13,8,128]{2,1,0:T(8,128)S(1)} %get-tuple-element.90), channel_id=1, source_target_pairs={{0,2},{1,5},{2,0},{3,7},{4,6},{5,1},{6,4},{7,3},{8,10},{9,13},{10,... | collective-permute-start | bytes 159752 | tf_op jit(solution)/shard_map/ppermute | solution.py:501
  18.0 4.1 %collective-permute-start.8 = (f32[13,8,128]{2,1,0:T(8,128)S(1)}, f32[13,8,128]{2,1,0:T(8,128)S(1)}, u32[]{:S(2)}, u32[]{:S(2)}) collective-permute-start(f32[13,8,128]{2,1,0:T(8,128)S(1)} %get-tuple-element.91), channel_id=1, source_target_pairs={{0,4},{1,3},{2,6},{3,1},{4,0},{5,7},{6,2},{7,5},{8,12},{9,11},{10,... | collective-permute-start | bytes 159752 | tf_op jit(solution)/shard_map/ppermute | solution.py:501
  18.6 3.6 %collective-permute-start.9 = (f32[13,8,128]{2,1,0:T(8,128)S(1)}, f32[13,8,128]{2,1,0:T(8,128)S(1)}, u32[]{:S(2)}, u32[]{:S(2)}) collective-permute-start(f32[13,8,128]{2,1,0:T(8,128)S(1)} %get-tuple-element.92), channel_id=1, source_target_pairs={{0,1},{1,0},{2,3},{3,2},{4,5},{5,4},{6,7},{7,6},{8,9},{9,8},{10,11... | collective-permute-start | bytes 159752 | tf_op jit(solution)/shard_map/ppermute | solution.py:501
  36.1 1.3 %collective-permute-start.10 = (f32[19,8,128]{2,1,0:T(8,128)S(1)}, f32[19,8,128]{2,1,0:T(8,128)S(1)}, u32[]{:S(2)}, u32[]{:S(2)}) collective-permute-start(f32[19,8,128]{2,1,0:T(8,128)S(1)} %get-tuple-element.102), channel_id=1, source_target_pairs={{0,1},{1,0},{2,3},{3,2},{4,5},{5,4},{6,7},{7,6},{8,9},{9,8},{10,11... | collective-permute-start | bytes 233480 | tf_op jit(solution)/shard_map/ppermute | solution.py:501
  37.4 5.7 %collective-permute-start.11 = (f32[13,8,128]{2,1,0:T(8,128)S(1)}, f32[13,8,128]{2,1,0:T(8,128)S(1)}, u32[]{:S(2)}, u32[]{:S(2)}) collective-permute-start(f32[13,8,128]{2,1,0:T(8,128)S(1)} %get-tuple-element.103), channel_id=1, source_target_pairs={{0,6},{1,7},{2,4},{3,5},{4,2},{5,3},{6,0},{7,1},{8,14},{9,15},{10,... | collective-permute-start | bytes 159752 | tf_op jit(solution)/shard_map/ppermute | solution.py:501
  38.1 5.0 %collective-permute-start.12 = (f32[13,8,128]{2,1,0:T(8,128)S(1)}, f32[13,8,128]{2,1,0:T(8,128)S(1)}, u32[]{:S(2)}, u32[]{:S(2)}) collective-permute-start(f32[13,8,128]{2,1,0:T(8,128)S(1)} %get-tuple-element.104), channel_id=1, source_target_pairs={{0,2},{1,5},{2,0},{3,7},{4,6},{5,1},{6,4},{7,3},{8,10},{9,13},{10,... | collective-permute-start | bytes 159752 | tf_op jit(solution)/shard_map/ppermute | solution.py:501
  39.5 4.1 %collective-permute-start.13 = (f32[13,8,128]{2,1,0:T(8,128)S(1)}, f32[13,8,128]{2,1,0:T(8,128)S(1)}, u32[]{:S(2)}, u32[]{:S(2)}) collective-permute-start(f32[13,8,128]{2,1,0:T(8,128)S(1)} %get-tuple-element.105), channel_id=1, source_target_pairs={{0,4},{1,3},{2,6},{3,1},{4,0},{5,7},{6,2},{7,5},{8,12},{9,11},{10,... | collective-permute-start | bytes 159752 | tf_op jit(solution)/shard_map/ppermute | solution.py:501
  41.0 2.7 %collective-permute-start.14 = (f32[13,8,128]{2,1,0:T(8,128)S(1)}, f32[13,8,128]{2,1,0:T(8,128)S(1)}, u32[]{:S(2)}, u32[]{:S(2)}) collective-permute-start(f32[13,8,128]{2,1,0:T(8,128)S(1)} %get-tuple-element.106), channel_id=1, source_target_pairs={{0,1},{1,0},{2,3},{3,2},{4,5},{5,4},{6,7},{7,6},{8,9},{9,8},{10,11... | collective-permute-start | bytes 159752 | tf_op jit(solution)/shard_map/ppermute | solution.py:501
  54.3 1.3 %collective-permute-start.15 = (f32[19,8,128]{2,1,0:T(8,128)S(1)}, f32[19,8,128]{2,1,0:T(8,128)S(1)}, u32[]{:S(2)}, u32[]{:S(2)}) collective-permute-start(f32[19,8,128]{2,1,0:T(8,128)S(1)} %get-tuple-element.117), channel_id=1, source_target_pairs={{0,1},{1,0},{2,3},{3,2},{4,5},{5,4},{6,7},{7,6},{8,9},{9,8},{10,11... | collective-permute-start | bytes 233480 | tf_op jit(solution)/shard_map/ppermute | solution.py:501
  55.6 5.7 %collective-permute-start.16 = (f32[13,8,128]{2,1,0:T(8,128)S(1)}, f32[13,8,128]{2,1,0:T(8,128)S(1)}, u32[]{:S(2)}, u32[]{:S(2)}) collective-permute-start(f32[13,8,128]{2,1,0:T(8,128)S(1)} %get-tuple-element.118), channel_id=1, source_target_pairs={{0,6},{1,7},{2,4},{3,5},{4,2},{5,3},{6,0},{7,1},{8,14},{9,15},{10,... | collective-permute-start | bytes 159752 | tf_op jit(solution)/shard_map/ppermute | solution.py:501
  56.3 5.0 %collective-permute-start.17 = (f32[13,8,128]{2,1,0:T(8,128)S(1)}, f32[13,8,128]{2,1,0:T(8,128)S(1)}, u32[]{:S(2)}, u32[]{:S(2)}) collective-permute-start(f32[13,8,128]{2,1,0:T(8,128)S(1)} %get-tuple-element.119), channel_id=1, source_target_pairs={{0,2},{1,5},{2,0},{3,7},{4,6},{5,1},{6,4},{7,3},{8,10},{9,13},{10,... | collective-permute-start | bytes 159752 | tf_op jit(solution)/shard_map/ppermute | solution.py:501
  57.7 4.1 %collective-permute-start.18 = (f32[13,8,128]{2,1,0:T(8,128)S(1)}, f32[13,8,128]{2,1,0:T(8,128)S(1)}, u32[]{:S(2)}, u32[]{:S(2)}) collective-permute-start(f32[13,8,128]{2,1,0:T(8,128)S(1)} %get-tuple-element.120), channel_id=1, source_target_pairs={{0,4},{1,3},{2,6},{3,1},{4,0},{5,7},{6,2},{7,5},{8,12},{9,11},{10,... | collective-permute-start | bytes 159752 | tf_op jit(solution)/shard_map/ppermute | solution.py:501
  59.2 2.7 %collective-permute-start.19 = (f32[13,8,128]{2,1,0:T(8,128)S(1)}, f32[13,8,128]{2,1,0:T(8,128)S(1)}, u32[]{:S(2)}, u32[]{:S(2)}) collective-permute-start(f32[13,8,128]{2,1,0:T(8,128)S(1)} %get-tuple-element.121), channel_id=1, source_target_pairs={{0,1},{1,0},{2,3},{3,2},{4,5},{5,4},{6,7},{7,6},{8,9},{9,8},{10,11... | collective-permute-start | bytes 159752 | tf_op jit(solution)/shard_map/ppermute | solution.py:501
  72.5 1.3 %collective-permute-start.20 = (f32[19,8,128]{2,1,0:T(8,128)S(1)}, f32[19,8,128]{2,1,0:T(8,128)S(1)}, u32[]{:S(2)}, u32[]{:S(2)}) collective-permute-start(f32[19,8,128]{2,1,0:T(8,128)S(1)} %get-tuple-element.132), channel_id=1, source_target_pairs={{0,1},{1,0},{2,3},{3,2},{4,5},{5,4},{6,7},{7,6},{8,9},{9,8},{10,11... | collective-permute-start | bytes 233480 | tf_op jit(solution)/shard_map/ppermute | solution.py:501
  73.8 5.7 %collective-permute-start.21 = (f32[13,8,128]{2,1,0:T(8,128)S(1)}, f32[13,8,128]{2,1,0:T(8,128)S(1)}, u32[]{:S(2)}, u32[]{:S(2)}) collective-permute-start(f32[13,8,128]{2,1,0:T(8,128)S(1)} %get-tuple-element.133), channel_id=1, source_target_pairs={{0,6},{1,7},{2,4},{3,5},{4,2},{5,3},{6,0},{7,1},{8,14},{9,15},{10,... | collective-permute-start | bytes 159752 | tf_op jit(solution)/shard_map/ppermute | solution.py:501
  74.5 5.0 %collective-permute-start.22 = (f32[13,8,128]{2,1,0:T(8,128)S(1)}, f32[13,8,128]{2,1,0:T(8,128)S(1)}, u32[]{:S(2)}, u32[]{:S(2)}) collective-permute-start(f32[13,8,128]{2,1,0:T(8,128)S(1)} %get-tuple-element.134), channel_id=1, source_target_pairs={{0,2},{1,5},{2,0},{3,7},{4,6},{5,1},{6,4},{7,3},{8,10},{9,13},{10,... | collective-permute-start | bytes 159752 | tf_op jit(solution)/shard_map/ppermute | solution.py:501
  75.9 4.1 %collective-permute-start.23 = (f32[13,8,128]{2,1,0:T(8,128)S(1)}, f32[13,8,128]{2,1,0:T(8,128)S(1)}, u32[]{:S(2)}, u32[]{:S(2)}) collective-permute-start(f32[13,8,128]{2,1,0:T(8,128)S(1)} %get-tuple-element.135), channel_id=1, source_target_pairs={{0,4},{1,3},{2,6},{3,1},{4,0},{5,7},{6,2},{7,5},{8,12},{9,11},{10,... | collective-permute-start | bytes 159752 | tf_op jit(solution)/shard_map/ppermute | solution.py:501
  77.4 2.7 %collective-permute-start.24 = (f32[13,8,128]{2,1,0:T(8,128)S(1)}, f32[13,8,128]{2,1,0:T(8,128)S(1)}, u32[]{:S(2)}, u32[]{:S(2)}) collective-permute-start(f32[13,8,128]{2,1,0:T(8,128)S(1)} %get-tuple-element.136), channel_id=1, source_target_pairs={{0,1},{1,0},{2,3},{3,2},{4,5},{5,4},{6,7},{7,6},{8,9},{9,8},{10,11... | collective-permute-start | bytes 159752 | tf_op jit(solution)/shard_map/ppermute | solution.py:501
